TPU v7x, 32 devices: a whole 2x2x4 slice. The times are simulated.
32 devices in a mesh: replica: 4 (over y, x), fsdp: 4 (over z), tensor: 2 (over core).
Axes of the slice: x: 2, y: 2, z: 4, core: 2. Of those that a mesh axis runs over, the one named last changes fastest.
Arguments:
- tokens: bfloat16 [4, 16, 4096], P('replica', ('fsdp', 'tensor')), may hold values from -6 to 6
- d_out: bfloat16 [4, 16, 4096], P('replica', ('fsdp', 'tensor')), may hold values from -6 to 6
- w_gate: bfloat16 [4096, 15360], P(None, ('fsdp', 'tensor')), may hold values from -0.09375 to 0.09375
- w_up: bfloat16 [4096, 15360], P(None, ('fsdp', 'tensor')), may hold values from -0.09375 to 0.09375
- w_down: bfloat16 [15360, 4096], P(('fsdp', 'tensor')), may hold values from -0.046875 to 0.046875
- failed: int32 [8], P(('fsdp', 'tensor')), may hold values from 0 to 3
- master: float32 [2, 15360, 4096], P(None, ('fsdp', 'tensor'), 'replica'), may hold values from -6 to 6
- moment1: float32 [2, 15360, 4096], P(None, ('fsdp', 'tensor'), 'replica'), may hold values from -4 to 4
- moment2: float32 [2, 15360, 4096], P(None, ('fsdp', 'tensor'), 'replica'), may hold values from 0.1 to 1
Outputs:
- d_tokens: bfloat16 [4, 16, 4096], P('replica', ('fsdp', 'tensor'))
- master_new: float32 [15360, 4096], P(('fsdp', 'tensor'), 'replica')
- moment1_new: float32 [15360, 4096], P(('fsdp', 'tensor'), 'replica')
- moment2_new: float32 [15360, 4096], P(('fsdp', 'tensor'), 'replica')
All inputs are finite; a program needn't handle non-finite values.
Results may differ from a plain program's by a relative error of at most 0.0049.
Values may be sent and summed in bfloat16 or wider, within the bound.
No kernel may reach another device: no remote copies, remote signals or barrier semaphores. Data moves between devices by JAX's collectives and lax.ppermute only.
A program may use at most 256 MiB of HBM per device.

v0:
```python
import functools

import jax
import jax.numpy as jnp
from jax import lax
from jax.experimental import pallas as pl
from jax.experimental.pallas import tpu as pltpu
from jax.sharding import PartitionSpec as P

BF16, F32 = jnp.bfloat16, jnp.float32
LAG = 2
MOST_CHUNKS = 24
TILE = 16
BUFFERS = 3
FETCHED = 4
VMEM = 50 << 20

ANY = pl.BlockSpec(memory_space=pl.ANY)
SMEM = pl.BlockSpec(memory_space=pltpu.SMEM)
WHOLE = pl.BlockSpec(memory_space=pltpu.VMEM)
PARAMS = pltpu.CompilerParams(vmem_limit_bytes=VMEM)


def ring_order(n):
    return [0, 1, 3, 2] if n == 4 else list(range(n))


def entry(table, index):
    found = jnp.int32(0)
    for at, value in enumerate(table):
        found = jnp.where(index == at, jnp.int32(value), found)
    return found


class Roles:
    def __init__(self, failed, n):
        self.n = n
        self.order = ring_order(n)
        self.spots = [self.order.index(i) for i in range(n)]
        self.me = lax.axis_index("replica").astype(jnp.int32)
        self.failed = failed[0]
        self.source = lax.rem(self.failed + 1, n)
        self.lost = self.me == self.failed

    def ahead(self):
        apart = entry(self.spots, self.failed) - entry(self.spots, self.source)
        return lax.rem(apart + self.n, self.n)

    def neighbour(self, hops):
        spot = lax.rem(entry(self.spots, self.me) + hops, self.n)
        return entry(self.order, spot)


def largest(options, default):
    options = list(options)
    return max(options) if options else default


def shares(total, parts):
    parts = min(parts, total)
    edges = [total * i // parts for i in range(parts + 1)]
    return [(a, b - a) for a, b in zip(edges, edges[1:])]


def row_group(rows):
    return largest((g for g in (16, 32) if rows % g == 0), rows)


def cost(flops, bytes_accessed, transcendentals=0):
    return pl.CostEstimate(
        flops=flops, bytes_accessed=bytes_accessed, transcendentals=transcendentals
    )


def updated(master_old, first_old, second_old, total, healthy):
    first_new = 0.9 * first_old + (0.1 / healthy) * total
    second_new = 0.95 * second_old + (0.05 / healthy**2) * (total * total)
    root = second_new * lax.rsqrt(second_new)
    step = first_new * pl.reciprocal(root + 1e-08)
    return master_old - 0.01 * step, first_new, second_new


def column_pieces(lengths, width):
    moves, column = [], 0
    for part, length in enumerate(lengths):
        begin = 0
        while begin < length:
            piece, to = divmod(column, width)
            run = min(length - begin, width - to)
            moves.append((part, begin, piece, to, run))
            begin, column = begin + run, column + run
    return moves


def pack_body(*refs, n, places, chunk, slabs, passed, counts):
    count_seen, count_parts, count_after = counts
    if count_seen:
        roles, refs = Roles(refs[0], n), refs[1:]
    state = refs[0:3]
    seen = refs[3 : 3 + count_seen]
    rest = refs[3 + count_seen :]
    if count_parts:
        both, parts, rest = rest[0], rest[1 : 1 + count_parts], rest[1 + count_parts :]
    sends = rest[count_after : count_after + 2]
    held, made, sem, out_sem, below_sem = rest[count_after + 2 :]
    width = held.shape[2]
    size = 3 * chunk

    def rows_of(j):
        way, k = divmod(j, 3)
        return way, pl.ds(k * chunk, chunk)

    def fetch(j):
        way, k = divmod(j, 3)
        rows = pl.ds(places[way] * chunk, chunk)
        return pltpu.make_async_copy(state[k].at[1, rows], held.at[j], sem.at[j])

    def take(j):
        way, rows = rows_of(j)
        return pltpu.make_async_copy(seen[way].at[rows], made.at[way, rows], sem.at[j])

    def store(j):
        way, rows = rows_of(j)
        return pltpu.make_async_copy(
            made.at[way, rows], sends[way].at[rows], out_sem.at[j]
        )

    def convert():
        for j in range(6):
            fetch(j).start()
        for j in range(6):
            way, rows = rows_of(j)
            fetch(j).wait()
            made[way, rows] = held[j].astype(BF16)
            store(j).start()
        for j in range(6):
            store(j).wait()

    def relay():
        for j in range(6):
            take(j).start()
        for j in range(6):
            take(j).wait()
            store(j).start()
        for j in range(6):
            store(j).wait()

    def below(way, inward):
        rows = pl.ds(size, passed[way] or sends[way].shape[0] - size)
        here = made.at[way, rows]
        if inward:
            return pltpu.make_async_copy(seen[way].at[rows], here, below_sem.at[way])
        return pltpu.make_async_copy(here, sends[way].at[rows], below_sem.at[way])

    for way in range(2):
        if passed[way]:
            below(way, True).start()
        if slabs[way]:
            tokens, features = both.shape[0], both.shape[1] // 2
            moves = column_pieces([part.shape[1] for part in parts], width)
            for part, begin, piece, to, run in moves:
                units = parts[part][:, begin : begin + run]
                made[way, pl.ds(size + piece * tokens, tokens), pl.ds(to, run)] = (
                    jnp.where(roles.lost, jnp.zeros_like(units), units)
                )
            row = size + (1 + moves[-1][2]) * tokens
            for far in range(slabs[way], 0, -1):
                target = roles.neighbour(far if way == 0 else n - far)
                slab = pl.ds(pl.multiple_of(features + target * width, 128), width)
                made[way, pl.ds(row, tokens)] = both[:, slab]
                row += tokens
            below(way, False).start()

    for way in range(2):
        if passed[way]:
            below(way, True).wait()
            below(way, False).start()

    if seen:
        pl.when(roles.me == roles.source)(convert)
        pl.when(roles.me != roles.source)(relay)
    else:
        convert()

    for way in range(2):
        if slabs[way] or passed[way]:
            below(way, False).wait()


def pack(failed, n, state, seen, parcel, after, places, chunk, slabs, passed):
    width = state[0].shape[2]
    extra = list(passed)
    if parcel:
        tokens = parcel[0].shape[0]
        pieces = -(-sum(part.shape[1] for part in parcel[1:]) // width)
        extra = [tokens * (pieces + count) if count else 0 for count in slabs]
    counts = (len(seen), max(len(parcel) - 1, 0), len(after))
    return pl.pallas_call(
        functools.partial(
            pack_body,
            n=n,
            places=places,
            chunk=chunk,
            slabs=slabs,
            passed=passed,
            counts=counts,
        ),
        in_specs=[SMEM] * bool(seen)
        + [ANY] * (3 + len(seen))
        + [WHOLE] * len(parcel)
        + [ANY] * len(after),
        out_specs=[ANY, ANY],
        out_shape=[
            jax.ShapeDtypeStruct((3 * chunk + more, width), BF16) for more in extra
        ],
        scratch_shapes=[
            pltpu.VMEM((6, chunk, width), F32),
            pltpu.VMEM((2, 3 * chunk + max(extra), width), BF16),
            pltpu.SemaphoreType.DMA((6,)),
            pltpu.SemaphoreType.DMA((6,)),
            pltpu.SemaphoreType.DMA((2,)),
        ],
        compiler_params=PARAMS,
        cost_estimate=cost(0, 2 * 3 * chunk * width * 6),
        name="pack",
    )(*([failed] if seen else []), *state, *seen, *parcel, *after)


def beside_body(*refs):
    tokens, d_out, out = refs[0], refs[1], refs[-1]
    width = tokens.shape[1]
    out[0, :, :width] = tokens[...]
    out[0, :, width:] = d_out[...]


def beside(tokens, d_out, after):
    rows, width = tokens.shape
    return pl.pallas_call(
        beside_body,
        in_specs=[WHOLE, WHOLE] + [ANY] * len(after),
        out_specs=WHOLE,
        out_shape=jax.ShapeDtypeStruct((1, rows, 2 * width), tokens.dtype),
        compiler_params=PARAMS,
        cost_estimate=cost(0, 4 * rows * width * 2),
        name="beside",
    )(tokens, d_out, *after)


def join_body(own, other, *refs, axis, apart, last):
    out = refs[-1]
    count, rows = own.shape[:2]
    second = lax.rem(lax.div(lax.axis_index(axis).astype(jnp.int32), apart), 2)
    if not last:
        out[pl.ds(second * count, count)] = own[...]
        out[pl.ds((1 - second) * count, count)] = other[...]
        return
    for i in range(2 * count):
        here, there = (own, other) if i < count else (other, own)
        value = jnp.where(second == 1, there[i % count], here[i % count])
        out[pl.ds(i * rows, rows)] = value


def join(own, other, after, axis, apart, last):
    count, rows, width = own.shape
    shape = (2 * count * rows, width) if last else (2 * count, rows, width)
    return pl.pallas_call(
        functools.partial(join_body, axis=axis, apart=apart, last=last),
        in_specs=[WHOLE, WHOLE] + [ANY] * len(after),
        out_specs=WHOLE,
        out_shape=jax.ShapeDtypeStruct(shape, own.dtype),
        compiler_params=PARAMS,
        cost_estimate=cost(0, 8 * count * rows * width),
        name="join",
    )(own, other, *after)


def by_rows(a, b):
    return lax.dot_general(a, b, (((1,), (1,)), ((), ())), preferred_element_type=F32)


def layer_body(both, *refs, resumed, tile, first, count):
    weights = refs[:3]
    hidden_ref, sum_ref = refs[-2:]
    features = weights[0].shape[0]
    rows = both.shape[0]
    joined = tile % 128 == 0
    sum_ref[...] = refs[3][...] if resumed else jnp.zeros_like(sum_ref)

    def step(gate_ref, up_ref, down_ref, hidden):
        x, dy = both[:, :features], both[:, features:]
        w_gate, w_up = gate_ref[...], up_ref[...]
        if joined:
            w_both = jnp.concatenate([w_gate, w_up], axis=1)
            gate_up = jnp.dot(x, w_both, preferred_element_type=F32)
            gate, up = gate_up[:, :tile], gate_up[:, tile:]
        else:
            gate = jnp.dot(x, w_gate, preferred_element_type=F32)
            up = jnp.dot(x, w_up, preferred_element_type=F32)
        d_hidden = by_rows(dy, down_ref[...])
        sig = 1.0 / (1.0 + jnp.exp(-gate))
        hidden[...] = (gate * sig * up).astype(BF16)
        d_gate = (d_hidden * up * sig * (1.0 + gate * (1.0 - sig))).astype(BF16)
        d_up = (d_hidden * gate * sig).astype(BF16)
        if joined:
            sum_ref[...] += by_rows(jnp.concatenate([d_gate, d_up], axis=1), w_both)
        else:
            sum_ref[...] += by_rows(d_gate, w_gate) + by_rows(d_up, w_up)

    deep = pl.Buffered(min(BUFFERS, count + 1))
    across = pl.BlockSpec((features, tile), lambda i: (0, first + i), pipeline_mode=deep)
    pltpu.emit_pipeline(
        step,
        grid=(count,),
        in_specs=[
            across,
            across,
            pl.BlockSpec((tile, features), lambda i: (first + i, 0), pipeline_mode=deep),
        ],
        out_specs=[pl.BlockSpec((rows, tile), lambda i: (0, i))],
    )(*weights, hidden_ref)


def layer(both, w_gate, w_up, w_down, partial_sum, after, tile, first, count):
    rows = both.shape[0]
    features = w_gate.shape[0]
    resumed = partial_sum is not None
    return pl.pallas_call(
        functools.partial(layer_body, resumed=resumed, tile=tile, first=first, count=count),
        in_specs=[WHOLE] + [ANY] * 3 + [WHOLE] * resumed + [ANY] * len(after),
        out_specs=[ANY, WHOLE],
        out_shape=[
            jax.ShapeDtypeStruct((rows, count * tile), BF16),
            jax.ShapeDtypeStruct((rows, features), F32),
        ],
        compiler_params=PARAMS,
        cost_estimate=cost(
            10 * rows * features * count * tile,
            3 * features * count * tile * 2,
            rows * count * tile,
        ),
        name="layer",
    )(both, w_gate, w_up, w_down, *([partial_sum] if resumed else []), *after)


def halve_body(bit, *refs, arrived, final):
    value = refs[0][...]
    if arrived:
        value = value + refs[1][...]
    if final:
        refs[-1][...] = value.astype(BF16)
        return
    kept, sent = refs[-2:]
    half = value.shape[0] // 2
    low, high = value[:half], value[half:]
    upper = bit[0] == 1
    kept[...] = jnp.where(upper, high, low)
    sent[...] = jnp.where(upper, low, high)


def halve(bit, value, arrived, after, final):
    rows, features = value.shape
    if final:
        out_shape = jax.ShapeDtypeStruct((rows, features), BF16)
    else:
        out_shape = [jax.ShapeDtypeStruct((rows // 2, features), F32)] * 2
    return pl.pallas_call(
        functools.partial(halve_body, arrived=bool(arrived), final=final),
        in_specs=[SMEM] + [WHOLE] * (1 + len(arrived)) + [ANY] * len(after),
        out_specs=WHOLE if final else [WHOLE, WHOLE],
        out_shape=out_shape,
        compiler_params=PARAMS,
        cost_estimate=cost(0, 3 * rows * features * 4),
        name="halve",
    )(bit, value, *arrived, *after)


class ScatteredSum:
    def __init__(self, value, axes):
        sizes = [lax.axis_size(axis) for axis in axes]
        self.value, self.arrived, self.levels = value, (), []
        self.done = any(size & (size - 1) for size in sizes)
        if self.done:
            summed = lax.psum_scatter(value, axes, scatter_dimension=0, tiled=True)
            self.value = summed.astype(BF16)
            return
        for axis, size in zip(axes, sizes):
            apart = size // 2
            while apart:
                self.levels.append((axis, size, apart))
                apart //= 2

    def advance(self, after):
        if self.done:
            return ()
        if self.levels:
            axis, size, apart = self.levels.pop(0)
            bit = ((lax.axis_index(axis) // apart) % 2).astype(jnp.int32)[None]
            self.value, sent = halve(bit, self.value, self.arrived, after, False)
            route = [(i, i ^ apart) for i in range(size)]
            self.arrived = (lax.ppermute(sent, axis, route),)
        else:
            bit = jnp.zeros((1,), jnp.int32)
            self.value = halve(bit, self.value, self.arrived, after, True)
            self.done = True
        return (self.value,)


def collect_body(failed, both, *refs, n, places, parts_count, size, pieces):
    roles = Roles(failed, n)
    parts = refs[:parts_count]
    blocks = refs[parts_count : parts_count + len(places)]
    hidden_t, outs, held, sem = refs[-4:]
    tokens, features = both.shape[0], both.shape[1] // 2
    width = outs.shape[1]

    def fetch(j, part):
        rows = pl.ds(size, pieces * tokens) if part == 0 else pl.ds(places[j], tokens)
        here = pl.ds(0, pieces * tokens) if part == 0 else pl.ds(pieces * tokens, tokens)
        return pltpu.make_async_copy(
            blocks[j].at[rows], held.at[j + 1, here], sem.at[j, part]
        )

    for j in range(len(places)):
        for part in range(2):
            fetch(j, part).start()
    for part, begin, piece, to, run in column_pieces([p.shape[1] for p in parts], width):
        units = parts[part][:, begin : begin + run]
        held[0, pl.ds(piece * tokens, tokens), pl.ds(to, run)] = jnp.where(
            roles.lost, jnp.zeros_like(units), units
        )
    slab = pl.ds(pl.multiple_of(features + roles.me * width, 128), width)
    held[0, pl.ds(pieces * tokens, tokens)] = both[:, slab]
    for j in range(len(places)):
        for part in range(2):
            fetch(j, part).wait()

    count = len(places) + 1
    for j in range(count):
        outs[pl.ds(j * tokens, tokens)] = held[j, pl.ds(pieces * tokens, tokens)]
    for piece in range(pieces):
        run = min(width, hidden_t.shape[0] - piece * width)
        rows = pl.ds(piece * tokens, tokens)
        hidden = jnp.concatenate([held[j, rows, :run] for j in range(count)], axis=0)
        hidden_t[pl.ds(piece * width, run)] = hidden.astype(F32).T.astype(BF16)


def collect(failed, n, both, parts, blocks, places, size, width, after):
    tokens = both.shape[0]
    units = sum(part.shape[1] for part in parts)
    pieces = -(-units // width)
    depth = tokens * (len(blocks) + 1)
    return pl.pallas_call(
        functools.partial(
            collect_body,
            n=n,
            places=places,
            parts_count=len(parts),
            size=size,
            pieces=pieces,
        ),
        in_specs=[SMEM]
        + [WHOLE] * (1 + len(parts))
        + [ANY] * (len(blocks) + len(after)),
        out_specs=[WHOLE, WHOLE],
        out_shape=[
            jax.ShapeDtypeStruct((units, depth), BF16),
            jax.ShapeDtypeStruct((depth, width), BF16),
        ],
        scratch_shapes=[
            pltpu.VMEM((len(blocks) + 1, (pieces + 1) * tokens, width), BF16),
            pltpu.SemaphoreType.DMA((len(blocks), 2)),
        ],
        compiler_params=PARAMS,
        cost_estimate=cost(0, 4 * depth * (units + width)),
        name="collect",
    )(failed, both, *parts, *blocks, *after)


def update_body(failed, hid_ref, out_ref, *refs, n, block, first, count, unread):
    state, news = refs[:3], refs[3 + unread : 6 + unread]
    total = refs[6 + unread]
    width = out_ref.shape[1]
    group = row_group(block)

    def step(hid, m_ref, a_ref, b_ref, m_new, a_new, b_new):
        total[...] = jnp.dot(hid[...], out_ref[...], preferred_element_type=F32)

        @pl.loop(0, block // group)
        def _(i):
            here = pl.ds(pl.multiple_of(i * group, group), group)
            m_new[here], a_new[here], b_new[here] = updated(
                m_ref[0, here], a_ref[0, here], b_ref[0, here], total[here], n - 1.0
            )

    deep = pl.Buffered(min(BUFFERS, count + 1))
    old = pl.BlockSpec(
        (1, block, width), lambda i: (0, first + i, 0), pipeline_mode=deep
    )
    new = pl.BlockSpec((block, width), lambda i: (first + i, 0))

    @pl.when(jnp.logical_not(Roles(failed, n).lost))
    def _():
        pltpu.emit_pipeline(
            step,
            grid=(count,),
            in_specs=[
                pl.BlockSpec((block, hid_ref.shape[1]), lambda i: (first + i, 0)),
                old,
                old,
                old,
            ],
            out_specs=[new] * 3,
        )(hid_ref, *state, *news)


def update(failed, n, hidden_t, outs, state, news, after, block, first, count):
    _, rows, width = state[0].shape
    depth = hidden_t.shape[1]
    shape = jax.ShapeDtypeStruct((rows, width), F32)
    unread = len(news) + len(after)
    return pl.pallas_call(
        functools.partial(
            update_body,
            n=n,
            block=block,
            first=first,
            count=count,
            unread=unread,
        ),
        in_specs=[SMEM, ANY, WHOLE] + [ANY] * (3 + unread),
        out_specs=[ANY] * 3,
        out_shape=[shape] * 3,
        scratch_shapes=[pltpu.VMEM((block, width), F32)],
        input_output_aliases={6 + k: k for k in range(len(news))},
        compiler_params=PARAMS,
        cost_estimate=cost(
            2 * count * block * width * depth,
            6 * count * block * width * 4,
            2 * count * block * width,
        ),
        name="update",
    )(failed, hidden_t, outs, *state, *news, *after)


def patch_body(failed, hid_ref, out_ref, *refs, arrivals, chunks, n, count_after):
    count = len(arrivals)
    got = refs[:count]
    rest = refs[count + 3 + count_after :]
    news = rest[:3]
    held, made, total, in_sem, out_sem = rest[3:]
    chunk = made.shape[2]
    group = row_group(chunk)
    roles = Roles(failed, n)
    ahead = roles.ahead()
    lag_of = {True: LAG * (ahead - 1), False: LAG * (n - ahead - 1)}

    def fetch(j):
        rows = got[j].at[pl.ds(0, 3 * chunk)]
        return pltpu.make_async_copy(rows, held.at[j % FETCHED], in_sem.at[j % FETCHED])

    def first_row(j):
        step, forward = arrivals[j]
        place = step - lag_of[forward]
        if not forward:
            place = chunks - 1 - place
        return pl.multiple_of(jnp.clip(place, 0, chunks - 1) * chunk, TILE)

    def store(j, k):
        return pltpu.make_async_copy(
            made.at[j % BUFFERS, k],
            news[k].at[pl.ds(first_row(j), chunk)],
            out_sem.at[j % BUFFERS, k],
        )

    def valid(j):
        step, forward = arrivals[j]
        return step >= lag_of[forward]

    def finish(j):
        @pl.when(valid(j))
        def _():
            for k in range(3):
                store(j, k).wait()

    @pl.when(roles.lost)
    def _():
        for j in range(min(FETCHED - 1, count)):
            fetch(j).start()
        for j in range(count):
            if j + FETCHED - 1 < count:
                fetch(j + FETCHED - 1).start()
            fetch(j).wait()
            if j >= BUFFERS:
                finish(j - BUFFERS)

            @pl.when(valid(j))
            def _(j=j, slot=j % FETCHED, out_slot=j % BUFFERS):
                first = first_row(j)

                units = hid_ref[pl.ds(first, chunk)]
                total[...] = jnp.dot(units, out_ref[...], preferred_element_type=F32)

                @pl.loop(0, chunk // group)
                def _(i):
                    base = pl.multiple_of(i * group, group)
                    old = [
                        held[slot, pl.ds(k * chunk + base, group)].astype(F32)
                        for k in range(3)
                    ]
                    new = updated(*old, total[pl.ds(base, group)], n - 1.0)
                    for k in range(3):
                        made[out_slot, k, pl.ds(base, group)] = new[k]

                for k in range(3):
                    store(j, k).start()

        for j in range(max(count - BUFFERS, 0), count):
            finish(j)


def patch(failed, n, hidden_t, outs, got, arrivals, news, after, chunks):
    rows, width = news[0].shape
    chunk = rows // chunks
    count = len(got)
    shape = jax.ShapeDtypeStruct((rows, width), F32)
    return pl.pallas_call(
        functools.partial(
            patch_body, arrivals=arrivals, chunks=chunks, n=n, count_after=len(after)
        ),
        in_specs=[SMEM, WHOLE, WHOLE] + [ANY] * (count + 3 + len(after)),
        out_specs=[ANY] * 3,
        out_shape=[shape] * 3,
        scratch_shapes=[
            pltpu.VMEM((FETCHED, 3 * chunk, width), BF16),
            pltpu.VMEM((BUFFERS, 3, chunk, width), F32),
            pltpu.VMEM((chunk, width), F32),
            pltpu.SemaphoreType.DMA((FETCHED,)),
            pltpu.SemaphoreType.DMA((BUFFERS, 3)),
        ],
        input_output_aliases={3 + count + k: k for k in range(3)},
        compiler_params=PARAMS,
        cost_estimate=cost(
            2 * count * chunk * width * hidden_t.shape[1],
            count * 3 * chunk * width * 6,
            2 * count * chunk * width,
        ),
        name="patch",
    )(failed, hidden_t, outs, *got, *news, *after)


def per_device(tokens, d_out, w_gate, w_up, w_down, failed, master, moment1, moment2):
    n = lax.axis_size("replica")
    _, rows, width = master.shape
    features, units = w_gate.shape

    order = ring_order(n)

    state = (master, moment1, moment2)
    chunks = largest(
        (c for c in range(2, MOST_CHUNKS + 1, 2) if rows % (TILE * c) == 0), 2
    )
    chunk = rows // chunks
    steps = (chunks + LAG * (n - 2)) // 2
    reach = (n // 2, (n - 1) // 2)
    forward = [(order[p], order[(p + 1) % n]) for p in range(n)]
    backward = [(b, a) for a, b in forward]
    sends, got = [], []
    parcel_from = None

    def send(*after, parcel=()):
        nonlocal parcel_from
        step = len(got)
        seen = got[step - LAG] if step >= LAG else ()
        here = min(step, chunks - 1)
        slabs, passed = (0, 0), (0, 0)
        if parcel:
            parcel_from, slabs = step, reach
        elif parcel_from is not None and (step - parcel_from) % LAG == 0:
            hop = (step - parcel_from) // LAG
            passed = tuple(
                seen[way].shape[0] - 3 * chunk - both.shape[0]
                if hop < reach[way]
                else 0
                for way in range(2)
            )
        sends.append(
            pack(
                failed,
                n,
                state,
                seen,
                parcel,
                after,
                (here, chunks - 1 - here),
                chunk,
                slabs,
                passed,
            )
        )
        got.append(
            (
                lax.ppermute(sends[-1][0], "replica", forward),
                lax.ppermute(sends[-1][1], "replica", backward),
            )
        )
        return (sends[-1][0],)

    sent = send()
    both = beside(tokens[0], d_out[0], sent)
    exchanges = []
    for axis in ("tensor", "fsdp"):
        size = lax.axis_size(axis)
        exchanges += [(axis, size, 1 << k) for k in range((size - 1).bit_length())]
    if all(size & (size - 1) == 0 for _, size, _ in exchanges):
        for level, (axis, size, apart) in enumerate(exchanges):
            last = level == len(exchanges) - 1
            other = lax.ppermute(both, axis, [(i, i ^ apart) for i in range(size)])
            after = ()
            if level == 0 or last:
                after = sent = send(both)
            both = join(both, other, after, axis, apart, last)
    else:
        sent = send(both)
        both = lax.all_gather(both[0], ("fsdp", "tensor"), axis=0, tiled=True)
        sent = send(both)

    tile = 128 if units % 128 == 0 else units
    hidden, d_rows = [], None
    pieces = shares(units // tile, 5)
    for first, count in pieces:
        part, d_rows = layer(both, w_gate, w_up, w_down, d_rows, sent, tile, first, count)
        hidden.append(part)
        last = len(hidden) == len(pieces)
        sent = send(d_rows, parcel=(both, *hidden) if last else ())
    cotangents = ScatteredSum(d_rows, ("fsdp", "tensor"))

    news = ()
    patched = 0
    hidden_t = outs = None

    def gathered(after):
        blocks, places = [], []
        for way in range(2):
            for hop in range(reach[way]):
                blocks.append(got[parcel_from + LAG * hop][way])
                places.append(blocks[-1].shape[0] - both.shape[0])
        return collect(
            failed, n, both, hidden, blocks, places, 3 * chunk, width, after
        )

    def update_part(first, count, after):
        return update(
            failed, n, hidden_t, outs, state, news, after, block, first, count
        )

    def patch_to(step, after):
        nonlocal patched
        arrivals = [(s, way) for s in range(patched, step) for way in (True, False)]
        if not arrivals:
            return news
        blocks = [b for s in range(patched, step) for b in got[s]]
        patched = step
        return patch(failed, n, hidden_t, outs, blocks, arrivals, news, after, chunks)

    block = largest((b for b in range(TILE, 193, TILE) if rows % b == 0), rows)
    blocks = rows // block
    early = blocks // 4
    ready = parcel_from + LAG * reach[0] + 1
    while len(got) < steps:
        sent = send(*cotangents.advance(sent), *news[:1])
        if len(got) == ready and early and len(got) < steps:
            hidden_t, outs = gathered(sent)
            news = update_part(0, early, (hidden_t,))
            news = patch_to(len(got) // 2, ())
    if hidden_t is None:
        hidden_t, outs = gathered(sent)
        early = 0
    news = update_part(early, blocks - early, sent)
    for step in (steps - 2, steps - 1, steps):
        news = patch_to(step, ())
    while not cotangents.done:
        cotangents.advance(sent)
    return (cotangents.value[None], *news)


def solution(mesh):
    placed = (
        P("replica", ("fsdp", "tensor"), None),
        P("replica", ("fsdp", "tensor"), None),
        P(None, ("fsdp", "tensor")),
        P(None, ("fsdp", "tensor")),
        P(("fsdp", "tensor"), None),
        P(("fsdp", "tensor")),
        P(None, ("fsdp", "tensor"), "replica"),
        P(None, ("fsdp", "tensor"), "replica"),
        P(None, ("fsdp", "tensor"), "replica"),
    )
    return jax.shard_map(
        per_device,
        mesh=mesh,
        in_specs=placed,
        out_specs=(
            P("replica", ("fsdp", "tensor"), None),
            P(("fsdp", "tensor"), "replica"),
            P(("fsdp", "tensor"), "replica"),
            P(("fsdp", "tensor"), "replica"),
        ),
        check_vma=False,
    )
```

profile of v0, /device:TPU:0, one launch (start us, length us, event | category | flops | bytes accessed | tf_op | source)
XLA Modules:
  0.0 176.4 jit_solution(9001870841738437464)
XLA Ops:
  0.7 2.5 %pack.14 = (bf16[240,1024]{1,0:T(8,128)(2,1)S(1)}, bf16[240,1024]{1,0:T(8,128)(2,1)S(1)}) custom-call(f32[2,1920,1024]{2,1,0:T(8,128)} %refs_0_.29, f32[2,1920,1024]{2,1,0:T(8,128)} %refs_1_.41, f32[2,1920,1024]{2,1,0:T(8,128)} %refs_2_.41), custom_call_target="tpu_custom_call" | custom-call | bytes 2949120 | tf_op jit(solution)/shard_map/pack/pallas_call | solution.py:198
  3.1 3.0 %collective-permute-start.4 = (bf16[240,1024]{1,0:T(8,128)(2,1)S(1)}, bf16[240,1024]{1,0:T(8,128)(2,1)S(1)}, u32[]{:S(2)}, u32[]{:S(2)}) collective-permute-start(bf16[240,1024]{1,0:T(8,128)(2,1)S(1)} %get-tuple-element.70), channel_id=1, source_target_pairs={{8,0},{24,8},{16,24},{0,16},{9,1},{25,9},{17,25},{1,17},{10,2},{26... | collective-permute-start | bytes 1474568 | tf_op jit(solution)/shard_map/ppermute | solution.py:703
  6.2 2.5 %pack.15 = (bf16[240,1024]{1,0:T(8,128)(2,1)S(1)}, bf16[240,1024]{1,0:T(8,128)(2,1)S(1)}) custom-call(f32[2,1920,1024]{2,1,0:T(8,128)} %refs_0_.29, f32[2,1920,1024]{2,1,0:T(8,128)} %refs_1_.41, f32[2,1920,1024]{2,1,0:T(8,128)} %refs_2_.41, bf16[1,2,8192]{2,1,0:T(2,128)(2,1)S(1)} %beside.1.refs_3_.own), custom_call_target="tpu_custom_call" | custom-call | bytes 2949120 | tf_op jit(solution)/shard_map/pack/pallas_call | solution.py:198
  8.7 2.0 %collective-permute-start.6 = (bf16[240,1024]{1,0:T(8,128)(2,1)S(1)}, bf16[240,1024]{1,0:T(8,128)(2,1)S(1)}, u32[]{:S(2)}, u32[]{:S(2)}) collective-permute-start(bf16[240,1024]{1,0:T(8,128)(2,1)S(1)} %get-tuple-element.73), channel_id=1, source_target_pairs={{8,0},{24,8},{16,24},{0,16},{9,1},{25,9},{17,25},{1,17},{10,2},{26... | collective-permute-start | bytes 1474568 | tf_op jit(solution)/shard_map/ppermute | solution.py:703
  12.0 2.1 %collective-permute-start.1 = (bf16[2,2,8192]{2,1,0:T(2,128)(2,1)S(1)}, bf16[2,2,8192]{2,1,0:T(2,128)(2,1)S(1)}, u32[]{:S(2)}, u32[]{:S(2)}) collective-permute-start(bf16[2,2,8192]{2,1,0:T(2,128)(2,1)S(1)} %join.3.own), channel_id=1, source_target_pairs={{0,2},{2,0},{4,6},{6,4},{1,3},{3,1},{5,7},{7,5},{8,10},{10,8},{12,... | collective-permute-start | bytes 196616 | tf_op jit(solution)/shard_map/ppermute | solution.py:717
  14.1 2.4 %collective-permute-done.1.other = bf16[2,2,8192]{2,1,0:T(2,128)(2,1)S(1)} collective-permute-done((bf16[2,2,8192]{2,1,0:T(2,128)(2,1)S(1)}, bf16[2,2,8192]{2,1,0:T(2,128)(2,1)S(1)}, u32[]{:S(2)}, u32[]{:S(2)}) %collective-permute-start.1) | collective-permute-done | bytes 65568 | tf_op jit(solution)/shard_map/ppermute | solution.py:717
  16.5 2.9 %collective-permute-start.2 = (bf16[4,2,8192]{2,1,0:T(2,128)(2,1)S(1)}, bf16[4,2,8192]{2,1,0:T(2,128)(2,1)S(1)}, u32[]{:S(2)}, u32[]{:S(2)}) collective-permute-start(bf16[4,2,8192]{2,1,0:T(2,128)(2,1)S(1)} %join.4.refs_6_.own), channel_id=1, source_target_pairs={{0,4},{2,6},{4,0},{6,2},{1,5},{3,7},{5,1},{7,3},{8,12},{10,14},{12... | collective-permute-start | bytes 393224 | tf_op jit(solution)/shard_map/ppermute | solution.py:717
  20.3 2.6 %pack.16 = (bf16[240,1024]{1,0:T(8,128)(2,1)S(1)}, bf16[240,1024]{1,0:T(8,128)(2,1)S(1)}) custom-call(s32[1]{0:T(128)S(6)} %copy.43.refs_0_.failed, f32[2,1920,1024]{2,1,0:T(8,128)} %refs_0_.29, f32[2,1920,1024]{2,1,0:T(8,128)} %refs_1_.41, f32[2,1920,1024]{2,1,0:T(8,128)} %refs_2_.41, bf16[240,1024]{1,0:T(8,128)(2,1)S(1)} %collective-permute-done.3.refs_4_.refs_0_, ...), custom_call_target="tpu_custom_call" | custom-call | bytes 2949120 | tf_op jit(solution)/shard_map/pack/pallas_call | solution.py:198
  23.0 1.5 collective-permute-start.8
  25.5 5.7 %layer.5 = (bf16[16,384]{1,0:T(8,128)(2,1)S(1)}, f32[16,4096]{1,0:T(8,128)S(1)}) custom-call(bf16[16,8192]{1,0:T(8,128)(2,1)S(1)} %join.5.both.refs_6_, bf16[4096,1920]{1,0:T(8,128)(2,1)} %refs_0_.27, bf16[4096,1920]{1,0:T(8,128)(2,1)} %refs_1_.32, bf16[1920,4096]{1,0:T(8,128)(2,1)} %refs_2_.32, bf16[240,1024]{1,0:T(8,128)(2,1)S(1)} %get-tuple-element.71.refs_0_.refs_3_), custom_call_target="tpu_custom_call" | custom-call | flops 251658240 | bytes 9437184 | tf_op jit(solution)/shard_map/layer/pallas_call | solution.py:327
  31.3 2.7 %pack.17 = (bf16[240,1024]{1,0:T(8,128)(2,1)S(1)}, bf16[240,1024]{1,0:T(8,128)(2,1)S(1)}) custom-call(s32[1]{0:T(128)S(6)} %copy.43.refs_0_.failed, f32[2,1920,1024]{2,1,0:T(8,128)} %refs_0_.29, f32[2,1920,1024]{2,1,0:T(8,128)} %refs_1_.41, f32[2,1920,1024]{2,1,0:T(8,128)} %refs_2_.41, bf16[240,1024]{1,0:T(8,128)(2,1)S(1)} %collective-permute-done.5.refs_4_.refs_2_, ...), custom_call_target="tpu_custom_call" | custom-call | bytes 2949120 | tf_op jit(solution)/shard_map/pack/pallas_call | solution.py:198
  34.0 1.5 collective-permute-start.10
  36.1 5.7 %layer.6 = (bf16[16,384]{1,0:T(8,128)(2,1)S(1)}, f32[16,4096]{1,0:T(8,128)S(1)}) custom-call(bf16[16,8192]{1,0:T(8,128)(2,1)S(1)} %join.5.both.refs_6_, bf16[4096,1920]{1,0:T(8,128)(2,1)} %refs_0_.27, bf16[4096,1920]{1,0:T(8,128)(2,1)} %refs_1_.32, bf16[1920,4096]{1,0:T(8,128)(2,1)} %refs_2_.32, f32[16,4096]{1,0:T(8,128)S(1)} %get-tuple-element.72.refs_6_.refs_3_, ...), custom_call_target="tpu_custom_call" | custom-call | flops 251658240 | bytes 9437184 | tf_op jit(solution)/shard_map/layer/pallas_call | solution.py:327
  41.8 2.7 %pack.18 = (bf16[240,1024]{1,0:T(8,128)(2,1)S(1)}, bf16[240,1024]{1,0:T(8,128)(2,1)S(1)}) custom-call(s32[1]{0:T(128)S(6)} %copy.43.refs_0_.failed, f32[2,1920,1024]{2,1,0:T(8,128)} %refs_0_.29, f32[2,1920,1024]{2,1,0:T(8,128)} %refs_1_.41, f32[2,1920,1024]{2,1,0:T(8,128)} %refs_2_.41, bf16[240,1024]{1,0:T(8,128)(2,1)S(1)} %collective-permute-done.7.refs_4_, ...), custom_call_target="tpu_custom_call" | custom-call | bytes 2949120 | tf_op jit(solution)/shard_map/pack/pallas_call | solution.py:198
  44.6 1.5 collective-permute-start.12
  46.6 5.7 %layer.7 = (bf16[16,384]{1,0:T(8,128)(2,1)S(1)}, f32[16,4096]{1,0:T(8,128)S(1)}) custom-call(bf16[16,8192]{1,0:T(8,128)(2,1)S(1)} %join.5.both.refs_6_, bf16[4096,1920]{1,0:T(8,128)(2,1)} %refs_0_.27, bf16[4096,1920]{1,0:T(8,128)(2,1)} %refs_1_.32, bf16[1920,4096]{1,0:T(8,128)(2,1)} %refs_2_.32, f32[16,4096]{1,0:T(8,128)S(1)} %get-tuple-element.75.refs_6_.refs_3_, ...), custom_call_target="tpu_custom_call" | custom-call | flops 251658240 | bytes 9437184 | tf_op jit(solution)/shard_map/layer/pallas_call | solution.py:327
  52.4 2.7 %pack.19 = (bf16[240,1024]{1,0:T(8,128)(2,1)S(1)}, bf16[240,1024]{1,0:T(8,128)(2,1)S(1)}) custom-call(s32[1]{0:T(128)S(6)} %copy.43.refs_0_.failed, f32[2,1920,1024]{2,1,0:T(8,128)} %refs_0_.29, f32[2,1920,1024]{2,1,0:T(8,128)} %refs_1_.41, f32[2,1920,1024]{2,1,0:T(8,128)} %refs_2_.41, bf16[240,1024]{1,0:T(8,128)(2,1)S(1)} %collective-permute-done.9.refs_4_.refs_6_, ...), custom_call_target="tpu_custom_call" | custom-call | bytes 2949120 | tf_op jit(solution)/shard_map/pack/pallas_call | solution.py:198
  55.1 1.5 collective-permute-start.14
  57.2 5.7 %layer.8 = (bf16[16,384]{1,0:T(8,128)(2,1)S(1)}, f32[16,4096]{1,0:T(8,128)S(1)}) custom-call(bf16[16,8192]{1,0:T(8,128)(2,1)S(1)} %join.5.both.refs_6_, bf16[4096,1920]{1,0:T(8,128)(2,1)} %refs_0_.27, bf16[4096,1920]{1,0:T(8,128)(2,1)} %refs_1_.32, bf16[1920,4096]{1,0:T(8,128)(2,1)} %refs_2_.32, f32[16,4096]{1,0:T(8,128)S(1)} %get-tuple-element.78.refs_6_.refs_3_, ...), custom_call_target="tpu_custom_call" | custom-call | flops 251658240 | bytes 9437184 | tf_op jit(solution)/shard_map/layer/pallas_call | solution.py:327
  62.9 2.4 %pack.20 = (bf16[240,1024]{1,0:T(8,128)(2,1)}, bf16[240,1024]{1,0:T(8,128)(2,1)}) custom-call(s32[1]{0:T(128)S(6)} %copy.43.refs_0_.failed, f32[2,1920,1024]{2,1,0:T(8,128)} %refs_0_.29, f32[2,1920,1024]{2,1,0:T(8,128)} %refs_1_.41, f32[2,1920,1024]{2,1,0:T(8,128)} %refs_2_.41, bf16[240,1024]{1,0:T(8,128)(2,1)S(1)} %collective-permute-done.11.refs_4_.refs_8_, ...), custom_call_target="tpu_custom_call" | custom-call | bytes 2949120 | tf_op jit(solution)/shard_map/pack/pallas_call | solution.py:198
  65.3 5.7 %layer.9 = (bf16[16,384]{1,0:T(8,128)(2,1)S(1)}, f32[16,4096]{1,0:T(8,128)S(1)}) custom-call(bf16[16,8192]{1,0:T(8,128)(2,1)S(1)} %join.5.both.refs_6_, bf16[4096,1920]{1,0:T(8,128)(2,1)} %refs_0_.27, bf16[4096,1920]{1,0:T(8,128)(2,1)} %refs_1_.32, bf16[1920,4096]{1,0:T(8,128)(2,1)} %refs_2_.32, f32[16,4096]{1,0:T(8,128)S(1)} %get-tuple-element.81.refs_6_.refs_3_, ...), custom_call_target="tpu_custom_call" | custom-call | flops 251658240 | bytes 9437184 | tf_op jit(solution)/shard_map/layer/pallas_call | solution.py:327
  71.5 2.4 %pack.21 = (bf16[304,1024]{1,0:T(8,128)(2,1)}, bf16[288,1024]{1,0:T(8,128)(2,1)}) custom-call(s32[1]{0:T(128)S(6)} %copy.43.refs_0_.failed, f32[2,1920,1024]{2,1,0:T(8,128)} %refs_0_.29, f32[2,1920,1024]{2,1,0:T(8,128)} %refs_1_.41, f32[2,1920,1024]{2,1,0:T(8,128)} %refs_2_.41, bf16[240,1024]{1,0:T(8,128)(2,1)S(1)} %collective-permute-done.13.refs_4_.refs_10_, ...), custom_call_target="tpu_custom_call" | custom-call | bytes 2949120 | tf_op jit(solution)/shard_map/pack/pallas_call | solution.py:198
  73.9 1.7 collective-permute-start.19
  76.0 1.5 collective-permute-start.17
  78.7 2.6 %collective-permute-start.15 = (f32[8,4096]{1,0:T(8,128)}, f32[8,4096]{1,0:T(8,128)S(1)}, u32[]{:S(2)}, u32[]{:S(2)}) collective-permute-start(f32[8,4096]{1,0:T(8,128)} %get-tuple-element.93), channel_id=1, source_target_pairs={{0,4},{2,6},{4,0},{6,2},{1,5},{3,7},{5,1},{7,3},{8,12},{10,14},{12... | collective-permute-start | bytes 393224 | tf_op jit(solution)/shard_map/ppermute | solution.py:400
  81.3 17.7 %collective-permute-done.17.refs_5_.refs_1_ = bf16[240,1024]{1,0:T(8,128)(2,1)S(1)} collective-permute-done((bf16[240,1024]{1,0:T(8,128)(2,1)}, bf16[240,1024]{1,0:T(8,128)(2,1)S(1)}, u32[]{:S(2)}, u32[]{:S(2)}) %collective-permute-start.17) | collective-permute-done | bytes 491552 | tf_op jit(solution)/shard_map/ppermute | solution.py:703
  99.3 2.3 %pack.22 = (bf16[240,1024]{1,0:T(8,128)(2,1)}, bf16[240,1024]{1,0:T(8,128)(2,1)}) custom-call(s32[1]{0:T(128)S(6)} %copy.43.refs_0_.failed, f32[2,1920,1024]{2,1,0:T(8,128)} %refs_0_.29, f32[2,1920,1024]{2,1,0:T(8,128)} %refs_1_.41, f32[2,1920,1024]{2,1,0:T(8,128)} %refs_2_.41, bf16[240,1024]{1,0:T(8,128)(2,1)S(1)} %collective-permute-done.16.refs_4_.refs_0_, ...), custom_call_target="tpu_custom_call" | custom-call | bytes 2949120 | tf_op jit(solution)/shard_map/pack/pallas_call | solution.py:198
  102.3 2.5 %pack.23 = (bf16[288,1024]{1,0:T(8,128)(2,1)}, bf16[240,1024]{1,0:T(8,128)(2,1)}) custom-call(s32[1]{0:T(128)S(6)} %copy.43.refs_0_.failed, f32[2,1920,1024]{2,1,0:T(8,128)} %refs_0_.29, f32[2,1920,1024]{2,1,0:T(8,128)} %refs_1_.41, f32[2,1920,1024]{2,1,0:T(8,128)} %refs_2_.41, bf16[304,1024]{1,0:T(8,128)(2,1)S(1)} %collective-permute-done.19.refs_4_.refs_5_.refs_2_, ...), custom_call_target="tpu_custom_call" | custom-call | bytes 2949120 | tf_op jit(solution)/shard_map/pack/pallas_call | solution.py:198
  104.8 1.8 collective-permute-start.24
  106.9 1.7 collective-permute-start.22
  108.9 1.8 %collective-permute-start.18 = (f32[4,4096]{1,0:T(4,128)}, f32[4,4096]{1,0:T(4,128)}, u32[]{:S(2)}, u32[]{:S(2)}) collective-permute-start(f32[4,4096]{1,0:T(4,128)} %get-tuple-element.97), channel_id=1, source_target_pairs={{0,2},{2,0},{4,6},{6,4},{1,3},{3,1},{5,7},{7,5},{8,10},{10,8},{12,... | collective-permute-start | bytes 196616 | tf_op jit(solution)/shard_map/ppermute | solution.py:400
  110.7 2.8 %collective-permute-done.18.refs_1_ = f32[4,4096]{1,0:T(4,128)} collective-permute-done((f32[4,4096]{1,0:T(4,128)}, f32[4,4096]{1,0:T(4,128)}, u32[]{:S(2)}, u32[]{:S(2)}) %collective-permute-start.18) | collective-permute-done | bytes 65568 | tf_op jit(solution)/shard_map/ppermute | solution.py:400
  115.2 5.8 %collective-permute-done.23.refs_5_ = bf16[240,1024]{1,0:T(8,128)(2,1)} collective-permute-done((bf16[240,1024]{1,0:T(8,128)(2,1)}, bf16[240,1024]{1,0:T(8,128)(2,1)}, u32[]{:S(2)}, u32[]{:S(2)}) %collective-permute-start.23) | collective-permute-done | bytes 491552 | tf_op jit(solution)/shard_map/ppermute | solution.py:703
  121.0 7.6 %collective-permute-done.22.refs_4_ = bf16[240,1024]{1,0:T(8,128)(2,1)} collective-permute-done((bf16[240,1024]{1,0:T(8,128)(2,1)}, bf16[240,1024]{1,0:T(8,128)(2,1)}, u32[]{:S(2)}, u32[]{:S(2)}) %collective-permute-start.22) | collective-permute-done | bytes 491552 | tf_op jit(solution)/shard_map/ppermute | solution.py:702
  128.6 2.3 %pack.24 = (bf16[240,1024]{1,0:T(8,128)(2,1)S(1)}, bf16[240,1024]{1,0:T(8,128)(2,1)S(1)}) custom-call(s32[1]{0:T(128)S(6)} %copy.43.refs_0_.failed, f32[2,1920,1024]{2,1,0:T(8,128)} %refs_0_.29, f32[2,1920,1024]{2,1,0:T(8,128)} %refs_1_.41, f32[2,1920,1024]{2,1,0:T(8,128)} %refs_2_.41, bf16[240,1024]{1,0:T(8,128)(2,1)} %collective-permute-done.22.refs_4_, ...), custom_call_target="tpu_custom_call" | custom-call | bytes 2949120 | tf_op jit(solution)/shard_map/pack/pallas_call | solution.py:198
  130.9 1.5 collective-permute-start.31
  134.4 2.3 %pack.25 = (bf16[240,1024]{1,0:T(8,128)(2,1)S(1)}, bf16[240,1024]{1,0:T(8,128)(2,1)S(1)}) custom-call(s32[1]{0:T(128)S(6)} %copy.43.refs_0_.failed, f32[2,1920,1024]{2,1,0:T(8,128)} %refs_0_.29, f32[2,1920,1024]{2,1,0:T(8,128)} %refs_1_.41, f32[2,1920,1024]{2,1,0:T(8,128)} %refs_2_.41, bf16[288,1024]{1,0:T(8,128)(2,1)S(1)} %collective-permute-done.24.refs_4_.refs_6_, ...), custom_call_target="tpu_custom_call" | custom-call | bytes 2949120 | tf_op jit(solution)/shard_map/pack/pallas_call | solution.py:198
  136.6 1.5 collective-permute-start.27
  141.2 7.9 %patch.4 = (f32[1920,1024]{1,0:T(8,128)}, f32[1920,1024]{1,0:T(8,128)}, f32[1920,1024]{1,0:T(8,128)}) custom-call(s32[1]{0:T(128)S(6)} %copy.43.refs_0_.failed, bf16[1920,64]{1,0:T(8,128)(2,1)S(1)} %get-tuple-element.106.hid_ref.refs_3_, ...), custom_call_target="tpu_custom_call", output_to_operand_aliasing={{0}: (15, {}), {1}: (16, {}), {2}: (17, {})} | custom-call | flops 125829120 | bytes 17694720 | tf_op jit(solution)/shard_map/patch/pallas_call | solution.py:626
  149.2 2.7 %pack.27 = (bf16[240,1024]{1,0:T(8,128)(2,1)S(1)}, bf16[240,1024]{1,0:T(8,128)(2,1)S(1)}) custom-call(s32[1]{0:T(128)S(6)} %copy.43.refs_0_.failed, f32[2,1920,1024]{2,1,0:T(8,128)} %refs_0_.29, f32[2,1920,1024]{2,1,0:T(8,128)} %refs_1_.41, f32[2,1920,1024]{2,1,0:T(8,128)} %refs_2_.41, bf16[240,1024]{1,0:T(8,128)(2,1)S(1)} %collective-permute-done.30.refs_4_.refs_8_, ...), custom_call_target="tpu_custom_call" | custom-call | bytes 2949120 | tf_op jit(solution)/shard_map/pack/pallas_call | solution.py:198
  151.9 2.0 %collective-permute-start.33 = (bf16[240,1024]{1,0:T(8,128)(2,1)S(1)}, bf16[240,1024]{1,0:T(8,128)(2,1)S(1)}, u32[]{:S(2)}, u32[]{:S(2)}) collective-permute-start(bf16[240,1024]{1,0:T(8,128)(2,1)S(1)} %get-tuple-element.117), channel_id=1, source_target_pairs={{8,0},{24,8},{16,24},{0,16},{9,1},{25,9},{17,25},{1,17},{10,2},{26... | collective-permute-start | bytes 1474568 | tf_op jit(solution)/shard_map/ppermute | solution.py:703
  153.9 1.7 collective-permute-done.27.refs_5_.refs_11_
  155.7 2.7 %pack.26 = (bf16[240,1024]{1,0:T(8,128)(2,1)S(1)}, bf16[240,1024]{1,0:T(8,128)(2,1)S(1)}) custom-call(s32[1]{0:T(128)S(6)} %copy.43.refs_0_.failed, f32[2,1920,1024]{2,1,0:T(8,128)} %refs_0_.29, f32[2,1920,1024]{2,1,0:T(8,128)} %refs_1_.41, f32[2,1920,1024]{2,1,0:T(8,128)} %refs_2_.41, bf16[240,1024]{1,0:T(8,128)(2,1)S(1)} %collective-permute-done.26.refs_4_.refs_10_, ...), custom_call_target="tpu_custom_call" | custom-call | bytes 2949120 | tf_op jit(solution)/shard_map/pack/pallas_call | solution.py:198
  158.9 1.6 collective-permute-start.28
  160.5 7.9 %patch.5 = (f32[1920,1024]{1,0:T(8,128)}, f32[1920,1024]{1,0:T(8,128)}, f32[1920,1024]{1,0:T(8,128)}) custom-call(s32[1]{0:T(128)S(6)} %copy.43.refs_0_.failed, bf16[1920,64]{1,0:T(8,128)(2,1)S(1)} %get-tuple-element.106.hid_ref.refs_3_, ...), custom_call_target="tpu_custom_call", output_to_operand_aliasing={{0}: (15, {}), {1}: (16, {}), {2}: (17, {})} | custom-call | flops 125829120 | bytes 17694720 | tf_op jit(solution)/shard_map/patch/pallas_call | solution.py:626
  168.4 2.6 %patch.6 = (f32[1920,1024]{1,0:T(8,128)}, f32[1920,1024]{1,0:T(8,128)}, f32[1920,1024]{1,0:T(8,128)}) custom-call(s32[1]{0:T(128)S(6)} %copy.43.refs_0_.failed, bf16[1920,64]{1,0:T(8,128)(2,1)S(1)} %get-tuple-element.106.hid_ref.refs_3_, bf16[64,1024]{1,0:T(8,128)(2,1)S(1)} %get-tuple-element.107.out_ref, ...), custom_call_target="tpu_custom_call", output_to_operand_aliasing={{0}: (5, {}), {1}: (6, {}), {2}: (7, {})} | custom-call | flops 20971520 | bytes 2949120 | tf_op jit(solution)/shard_map/patch/pallas_call | solution.py:626
  171.0 1.5 collective-permute-done.29.refs_1_
  173.7 2.5 %patch.7 = (f32[1920,1024]{1,0:T(8,128)}, f32[1920,1024]{1,0:T(8,128)}, f32[1920,1024]{1,0:T(8,128)}) custom-call(s32[1]{0:T(128)S(6)} %copy.43.refs_0_.failed, bf16[1920,64]{1,0:T(8,128)(2,1)S(1)} %get-tuple-element.106.hid_ref.refs_3_, bf16[64,1024]{1,0:T(8,128)(2,1)S(1)} %get-tuple-element.107.out_ref, ...), custom_call_target="tpu_custom_call", output_to_operand_aliasing={{0}: (5, {}), {1}: (6, {}), {2}: (7, {})} | custom-call | flops 20971520 | bytes 2949120 | tf_op jit(solution)/shard_map/patch/pallas_call | solution.py:626
  (124 shorter events, 16.4 us)
Async XLA Ops:
  0.6 5.6 %copy-start.34 = (bf16[1,2,4096]{2,1,0:T(2,128)(2,1)S(1)}, bf16[1,2,4096]{2,1,0:T(2,128)(2,1)}, u32[]{:S(2)}) copy-start(bf16[1,2,4096]{2,1,0:T(2,128)(2,1)} %param.10) | copy-start | bytes 49156
  0.6 5.6 %copy-start.33 = (bf16[1,2,4096]{2,1,0:T(2,128)(2,1)S(1)}, bf16[1,2,4096]{2,1,0:T(2,128)(2,1)}, u32[]{:S(2)}) copy-start(bf16[1,2,4096]{2,1,0:T(2,128)(2,1)} %param.9) | copy-start | bytes 49156
  3.1 17.0 %collective-permute-start.4 = (bf16[240,1024]{1,0:T(8,128)(2,1)S(1)}, bf16[240,1024]{1,0:T(8,128)(2,1)S(1)}, u32[]{:S(2)}, u32[]{:S(2)}) collective-permute-start(bf16[240,1024]{1,0:T(8,128)(2,1)S(1)} %get-tuple-element.70), channel_id=1, source_target_pairs={{8,0},{24,8},{16,24},{0,16},{9,1},{25,9},{17,25},{1,17},{10,2},{26... | collective-permute-start | bytes 1474568 | tf_op jit(solution)/shard_map/ppermute | solution.py:703
  6.2 14.1 %collective-permute-start.3 = (bf16[240,1024]{1,0:T(8,128)(2,1)S(1)}, bf16[240,1024]{1,0:T(8,128)(2,1)S(1)}, u32[]{:S(2)}, u32[]{:S(2)}) collective-permute-start(bf16[240,1024]{1,0:T(8,128)(2,1)S(1)} %get-tuple-element.68.refs_2_), channel_id=1, source_target_pairs={{0,8},{8,24},{24,16},{16,0},{1,9},{9,25},{25,17},{17,1},{2,10},{10... | collective-permute-start | bytes 1474568 | tf_op jit(solution)/shard_map/ppermute | solution.py:702
  8.7 22.5 %collective-permute-start.6 = (bf16[240,1024]{1,0:T(8,128)(2,1)S(1)}, bf16[240,1024]{1,0:T(8,128)(2,1)S(1)}, u32[]{:S(2)}, u32[]{:S(2)}) collective-permute-start(bf16[240,1024]{1,0:T(8,128)(2,1)S(1)} %get-tuple-element.73), channel_id=1, source_target_pairs={{8,0},{24,8},{16,24},{0,16},{9,1},{25,9},{17,25},{1,17},{10,2},{26... | collective-permute-start | bytes 1474568 | tf_op jit(solution)/shard_map/ppermute | solution.py:703
  10.7 20.5 %collective-permute-start.5 = (bf16[240,1024]{1,0:T(8,128)(2,1)S(1)}, bf16[240,1024]{1,0:T(8,128)(2,1)S(1)}, u32[]{:S(2)}, u32[]{:S(2)}) collective-permute-start(bf16[240,1024]{1,0:T(8,128)(2,1)S(1)} %get-tuple-element.69.refs_0_), channel_id=1, source_target_pairs={{0,8},{8,24},{24,16},{16,0},{1,9},{9,25},{25,17},{17,1},{2,10},{10... | collective-permute-start | bytes 1474568 | tf_op jit(solution)/shard_map/ppermute | solution.py:702
  10.8 1.2 collective-permute-start
  12.0 4.5 %collective-permute-start.1 = (bf16[2,2,8192]{2,1,0:T(2,128)(2,1)S(1)}, bf16[2,2,8192]{2,1,0:T(2,128)(2,1)S(1)}, u32[]{:S(2)}, u32[]{:S(2)}) collective-permute-start(bf16[2,2,8192]{2,1,0:T(2,128)(2,1)S(1)} %join.3.own), channel_id=1, source_target_pairs={{0,2},{2,0},{4,6},{6,4},{1,3},{3,1},{5,7},{7,5},{8,10},{10,8},{12,... | collective-permute-start | bytes 196616 | tf_op jit(solution)/shard_map/ppermute | solution.py:717
  16.5 8.8 %collective-permute-start.2 = (bf16[4,2,8192]{2,1,0:T(2,128)(2,1)S(1)}, bf16[4,2,8192]{2,1,0:T(2,128)(2,1)S(1)}, u32[]{:S(2)}, u32[]{:S(2)}) collective-permute-start(bf16[4,2,8192]{2,1,0:T(2,128)(2,1)S(1)} %join.4.refs_6_.own), channel_id=1, source_target_pairs={{0,4},{2,6},{4,0},{6,2},{1,5},{3,7},{5,1},{7,3},{8,12},{10,14},{12... | collective-permute-start | bytes 393224 | tf_op jit(solution)/shard_map/ppermute | solution.py:717
  23.0 18.8 %collective-permute-start.8 = (bf16[240,1024]{1,0:T(8,128)(2,1)S(1)}, bf16[240,1024]{1,0:T(8,128)(2,1)S(1)}, u32[]{:S(2)}, u32[]{:S(2)}) collective-permute-start(bf16[240,1024]{1,0:T(8,128)(2,1)S(1)} %get-tuple-element.76), channel_id=1, source_target_pairs={{8,0},{24,8},{16,24},{0,16},{9,1},{25,9},{17,25},{1,17},{10,2},{26... | collective-permute-start | bytes 1474568 | tf_op jit(solution)/shard_map/ppermute | solution.py:703
  24.5 17.3 %collective-permute-start.7 = (bf16[240,1024]{1,0:T(8,128)(2,1)S(1)}, bf16[240,1024]{1,0:T(8,128)(2,1)S(1)}, u32[]{:S(2)}, u32[]{:S(2)}) collective-permute-start(bf16[240,1024]{1,0:T(8,128)(2,1)S(1)} %get-tuple-element.71.refs_0_.refs_3_), channel_id=1, source_target_pairs={{0,8},{8,24},{24,16},{16,0},{1,9},{9,25},{25,17},{17,1},{2,10},{10... | collective-permute-start | bytes 1474568 | tf_op jit(solution)/shard_map/ppermute | solution.py:702
  34.0 18.4 %collective-permute-start.10 = (bf16[240,1024]{1,0:T(8,128)(2,1)S(1)}, bf16[240,1024]{1,0:T(8,128)(2,1)S(1)}, u32[]{:S(2)}, u32[]{:S(2)}) collective-permute-start(bf16[240,1024]{1,0:T(8,128)(2,1)S(1)} %get-tuple-element.79), channel_id=1, source_target_pairs={{8,0},{24,8},{16,24},{0,16},{9,1},{25,9},{17,25},{1,17},{10,2},{26... | collective-permute-start | bytes 1474568 | tf_op jit(solution)/shard_map/ppermute | solution.py:703
  35.5 16.9 %collective-permute-start.9 = (bf16[240,1024]{1,0:T(8,128)(2,1)S(1)}, bf16[240,1024]{1,0:T(8,128)(2,1)S(1)}, u32[]{:S(2)}, u32[]{:S(2)}) collective-permute-start(bf16[240,1024]{1,0:T(8,128)(2,1)S(1)} %get-tuple-element.74.refs_4_), channel_id=1, source_target_pairs={{0,8},{8,24},{24,16},{16,0},{1,9},{9,25},{25,17},{17,1},{2,10},{10... | collective-permute-start | bytes 1474568 | tf_op jit(solution)/shard_map/ppermute | solution.py:702
  41.8 29.7 %copy-start.25 = (bf16[16,384]{1,0:T(8,128)(2,1)}, bf16[16,384]{1,0:T(8,128)(2,1)S(1)}, u32[]{:S(2)}) copy-start(bf16[16,384]{1,0:T(8,128)(2,1)S(1)} %get-tuple-element.87.refs_8_.refs_1_) | copy-start | bytes 36868
  44.6 18.3 %collective-permute-start.12 = (bf16[240,1024]{1,0:T(8,128)(2,1)S(1)}, bf16[240,1024]{1,0:T(8,128)(2,1)S(1)}, u32[]{:S(2)}, u32[]{:S(2)}) collective-permute-start(bf16[240,1024]{1,0:T(8,128)(2,1)S(1)} %get-tuple-element.82), channel_id=1, source_target_pairs={{8,0},{24,8},{16,24},{0,16},{9,1},{25,9},{17,25},{1,17},{10,2},{26... | collective-permute-start | bytes 1474568 | tf_op jit(solution)/shard_map/ppermute | solution.py:703
  46.1 16.9 %collective-permute-start.11 = (bf16[240,1024]{1,0:T(8,128)(2,1)S(1)}, bf16[240,1024]{1,0:T(8,128)(2,1)S(1)}, u32[]{:S(2)}, u32[]{:S(2)}) collective-permute-start(bf16[240,1024]{1,0:T(8,128)(2,1)S(1)} %get-tuple-element.77.refs_4_), channel_id=1, source_target_pairs={{0,8},{8,24},{24,16},{16,0},{1,9},{9,25},{25,17},{17,1},{2,10},{10... | collective-permute-start | bytes 1474568 | tf_op jit(solution)/shard_map/ppermute | solution.py:702
  52.3 19.2 %copy-start.27 = (bf16[16,384]{1,0:T(8,128)(2,1)}, bf16[16,384]{1,0:T(8,128)(2,1)S(1)}, u32[]{:S(2)}) copy-start(bf16[16,384]{1,0:T(8,128)(2,1)S(1)} %get-tuple-element.88.refs_9_.refs_2_) | copy-start | bytes 36868
  55.1 15.9 %collective-permute-start.14 = (bf16[240,1024]{1,0:T(8,128)(2,1)S(1)}, bf16[240,1024]{1,0:T(8,128)(2,1)S(1)}, u32[]{:S(2)}, u32[]{:S(2)}) collective-permute-start(bf16[240,1024]{1,0:T(8,128)(2,1)S(1)} %get-tuple-element.85), channel_id=1, source_target_pairs={{8,0},{24,8},{16,24},{0,16},{9,1},{25,9},{17,25},{1,17},{10,2},{26... | collective-permute-start | bytes 1474568 | tf_op jit(solution)/shard_map/ppermute | solution.py:703
  56.6 14.9 %collective-permute-start.13 = (bf16[240,1024]{1,0:T(8,128)(2,1)S(1)}, bf16[240,1024]{1,0:T(8,128)(2,1)S(1)}, u32[]{:S(2)}, u32[]{:S(2)}) collective-permute-start(bf16[240,1024]{1,0:T(8,128)(2,1)S(1)} %get-tuple-element.80.refs_4_), channel_id=1, source_target_pairs={{0,8},{8,24},{24,16},{16,0},{1,9},{9,25},{25,17},{17,1},{2,10},{10... | collective-permute-start | bytes 1474568 | tf_op jit(solution)/shard_map/ppermute | solution.py:702
  62.9 8.6 %copy-start.29 = (bf16[16,384]{1,0:T(8,128)(2,1)}, bf16[16,384]{1,0:T(8,128)(2,1)S(1)}, u32[]{:S(2)}) copy-start(bf16[16,384]{1,0:T(8,128)(2,1)S(1)} %get-tuple-element.89.refs_10_.refs_3_) | copy-start | bytes 36868
  71.0 2.9 %copy-start.31 = (bf16[16,384]{1,0:T(8,128)(2,1)}, bf16[16,384]{1,0:T(8,128)(2,1)S(1)}, u32[]{:S(2)}) copy-start(bf16[16,384]{1,0:T(8,128)(2,1)S(1)} %get-tuple-element.90.refs_11_.refs_4_) | copy-start | bytes 36868
  71.1 2.9 %copy-start.18 = (bf16[240,1024]{1,0:T(8,128)(2,1)}, bf16[240,1024]{1,0:T(8,128)(2,1)S(1)}, u32[]{:S(2)}) copy-start(bf16[240,1024]{1,0:T(8,128)(2,1)S(1)} %collective-permute-done.14.refs_5_.refs_11_) | copy-start | bytes 1474564
  73.9 28.3 %collective-permute-start.19 = (bf16[304,1024]{1,0:T(8,128)(2,1)}, bf16[304,1024]{1,0:T(8,128)(2,1)S(1)}, u32[]{:S(2)}, u32[]{:S(2)}) collective-permute-start(bf16[304,1024]{1,0:T(8,128)(2,1)} %get-tuple-element.91.refs_1_), channel_id=1, source_target_pairs={{0,8},{8,24},{24,16},{16,0},{1,9},{9,25},{25,17},{17,1},{2,10},{10... | collective-permute-start | bytes 1867784 | tf_op jit(solution)/shard_map/ppermute | solution.py:702
  75.6 26.6 %collective-permute-start.20 = (bf16[288,1024]{1,0:T(8,128)(2,1)}, bf16[288,1024]{1,0:T(8,128)(2,1)S(1)}, u32[]{:S(2)}, u32[]{:S(2)}) collective-permute-start(bf16[288,1024]{1,0:T(8,128)(2,1)} %get-tuple-element.98), channel_id=1, source_target_pairs={{8,0},{24,8},{16,24},{0,16},{9,1},{25,9},{17,25},{1,17},{10,2},{26... | collective-permute-start | bytes 1769480 | tf_op jit(solution)/shard_map/ppermute | solution.py:703
  76.0 23.0 %collective-permute-start.17 = (bf16[240,1024]{1,0:T(8,128)(2,1)}, bf16[240,1024]{1,0:T(8,128)(2,1)S(1)}, u32[]{:S(2)}, u32[]{:S(2)}) collective-permute-start(bf16[240,1024]{1,0:T(8,128)(2,1)} %get-tuple-element.94), channel_id=1, source_target_pairs={{8,0},{24,8},{16,24},{0,16},{9,1},{25,9},{17,25},{1,17},{10,2},{26... | collective-permute-start | bytes 1474568 | tf_op jit(solution)/shard_map/ppermute | solution.py:703
  77.5 21.8 %collective-permute-start.16 = (bf16[240,1024]{1,0:T(8,128)(2,1)}, bf16[240,1024]{1,0:T(8,128)(2,1)S(1)}, u32[]{:S(2)}, u32[]{:S(2)}) collective-permute-start(bf16[240,1024]{1,0:T(8,128)(2,1)} %get-tuple-element.83.refs_4_), channel_id=1, source_target_pairs={{0,8},{8,24},{24,16},{16,0},{1,9},{9,25},{25,17},{17,1},{2,10},{10... | collective-permute-start | bytes 1474568 | tf_op jit(solution)/shard_map/ppermute | solution.py:702
  78.7 22.9 %collective-permute-start.15 = (f32[8,4096]{1,0:T(8,128)}, f32[8,4096]{1,0:T(8,128)S(1)}, u32[]{:S(2)}, u32[]{:S(2)}) collective-permute-start(f32[8,4096]{1,0:T(8,128)} %get-tuple-element.93), channel_id=1, source_target_pairs={{0,4},{2,6},{4,0},{6,2},{1,5},{3,7},{5,1},{7,3},{8,12},{10,14},{12... | collective-permute-start | bytes 393224 | tf_op jit(solution)/shard_map/ppermute | solution.py:400
  102.3 36.5 %copy-start.1 = (bf16[288,1024]{1,0:T(8,128)(2,1)}, bf16[288,1024]{1,0:T(8,128)(2,1)S(1)}, u32[]{:S(2)}) copy-start(bf16[288,1024]{1,0:T(8,128)(2,1)S(1)} %collective-permute-done.20.refs_5_.refs_7_.refs_3_) | copy-start | bytes 1769476
  102.3 36.5 %copy-start = (bf16[304,1024]{1,0:T(8,128)(2,1)}, bf16[304,1024]{1,0:T(8,128)(2,1)S(1)}, u32[]{:S(2)}) copy-start(bf16[304,1024]{1,0:T(8,128)(2,1)S(1)} %collective-permute-done.19.refs_4_.refs_5_.refs_2_) | copy-start | bytes 1867780
  104.8 28.9 %collective-permute-start.24 = (bf16[288,1024]{1,0:T(8,128)(2,1)}, bf16[288,1024]{1,0:T(8,128)(2,1)S(1)}, u32[]{:S(2)}, u32[]{:S(2)}) collective-permute-start(bf16[288,1024]{1,0:T(8,128)(2,1)} %get-tuple-element.99.refs_2_), channel_id=1, source_target_pairs={{0,8},{8,24},{24,16},{16,0},{1,9},{9,25},{25,17},{17,1},{2,10},{10... | collective-permute-start | bytes 1769480 | tf_op jit(solution)/shard_map/ppermute | solution.py:702
  106.5 14.5 %collective-permute-start.23 = (bf16[240,1024]{1,0:T(8,128)(2,1)}, bf16[240,1024]{1,0:T(8,128)(2,1)}, u32[]{:S(2)}, u32[]{:S(2)}) collective-permute-start(bf16[240,1024]{1,0:T(8,128)(2,1)} %get-tuple-element.102), channel_id=1, source_target_pairs={{8,0},{24,8},{16,24},{0,16},{9,1},{25,9},{17,25},{1,17},{10,2},{26... | collective-permute-start | bytes 1474568 | tf_op jit(solution)/shard_map/ppermute | solution.py:703
  106.9 21.8 %collective-permute-start.22 = (bf16[240,1024]{1,0:T(8,128)(2,1)}, bf16[240,1024]{1,0:T(8,128)(2,1)}, u32[]{:S(2)}, u32[]{:S(2)}) collective-permute-start(bf16[240,1024]{1,0:T(8,128)(2,1)} %get-tuple-element.95.refs_2_), channel_id=1, source_target_pairs={{0,8},{8,24},{24,16},{16,0},{1,9},{9,25},{25,17},{17,1},{2,10},{10... | collective-permute-start | bytes 1474568 | tf_op jit(solution)/shard_map/ppermute | solution.py:702
  108.6 25.1 %collective-permute-start.25 = (bf16[240,1024]{1,0:T(8,128)(2,1)}, bf16[240,1024]{1,0:T(8,128)(2,1)}, u32[]{:S(2)}, u32[]{:S(2)}) collective-permute-start(bf16[240,1024]{1,0:T(8,128)(2,1)} %get-tuple-element.104), channel_id=1, source_target_pairs={{8,0},{24,8},{16,24},{0,16},{9,1},{25,9},{17,25},{1,17},{10,2},{26... | collective-permute-start | bytes 1474568 | tf_op jit(solution)/shard_map/ppermute | solution.py:703
  108.9 4.6 %collective-permute-start.18 = (f32[4,4096]{1,0:T(4,128)}, f32[4,4096]{1,0:T(4,128)}, u32[]{:S(2)}, u32[]{:S(2)}) collective-permute-start(f32[4,4096]{1,0:T(4,128)} %get-tuple-element.97), channel_id=1, source_target_pairs={{0,2},{2,0},{4,6},{6,4},{1,3},{3,1},{5,7},{7,5},{8,10},{10,8},{12,... | collective-permute-start | bytes 196616 | tf_op jit(solution)/shard_map/ppermute | solution.py:400
  115.2 17.8 %collective-permute-start.21 = (f32[2,4096]{1,0:T(2,128)S(1)}, f32[2,4096]{1,0:T(2,128)S(1)}, u32[]{:S(2)}, u32[]{:S(2)}) collective-permute-start(f32[2,4096]{1,0:T(2,128)S(1)} %get-tuple-element.101), channel_id=1, source_target_pairs={{0,1},{1,0},{2,3},{3,2},{4,5},{5,4},{6,7},{7,6},{8,9},{9,8},{10,11... | collective-permute-start | bytes 98312 | tf_op jit(solution)/shard_map/ppermute | solution.py:400
  130.9 18.2 %collective-permute-start.31 = (bf16[240,1024]{1,0:T(8,128)(2,1)S(1)}, bf16[240,1024]{1,0:T(8,128)(2,1)S(1)}, u32[]{:S(2)}, u32[]{:S(2)}) collective-permute-start(bf16[240,1024]{1,0:T(8,128)(2,1)S(1)} %get-tuple-element.115), channel_id=1, source_target_pairs={{8,0},{24,8},{16,24},{0,16},{9,1},{25,9},{17,25},{1,17},{10,2},{26... | collective-permute-start | bytes 1474568 | tf_op jit(solution)/shard_map/ppermute | solution.py:703
  132.5 16.7 %collective-permute-start.30 = (bf16[240,1024]{1,0:T(8,128)(2,1)S(1)}, bf16[240,1024]{1,0:T(8,128)(2,1)S(1)}, u32[]{:S(2)}, u32[]{:S(2)}) collective-permute-start(bf16[240,1024]{1,0:T(8,128)(2,1)S(1)} %get-tuple-element.103.refs_2_), channel_id=1, source_target_pairs={{0,8},{8,24},{24,16},{16,0},{1,9},{9,25},{25,17},{17,1},{2,10},{10... | collective-permute-start | bytes 1474568 | tf_op jit(solution)/shard_map/ppermute | solution.py:702
  133.0 5.7 %copy-start.26 = (bf16[16,384]{1,0:T(8,128)(2,1)S(1)}, bf16[16,384]{1,0:T(8,128)(2,1)}, u32[]{:S(2)}) copy-start(bf16[16,384]{1,0:T(8,128)(2,1)} %copy-done.25) | copy-start | bytes 36868
  133.0 5.7 %copy-start.28 = (bf16[16,384]{1,0:T(8,128)(2,1)S(1)}, bf16[16,384]{1,0:T(8,128)(2,1)}, u32[]{:S(2)}) copy-start(bf16[16,384]{1,0:T(8,128)(2,1)} %copy-done.27) | copy-start | bytes 36868
  133.0 5.7 %copy-start.30 = (bf16[16,384]{1,0:T(8,128)(2,1)S(1)}, bf16[16,384]{1,0:T(8,128)(2,1)}, u32[]{:S(2)}) copy-start(bf16[16,384]{1,0:T(8,128)(2,1)} %copy-done.29) | copy-start | bytes 36868
  133.0 5.7 %copy-start.32 = (bf16[16,384]{1,0:T(8,128)(2,1)S(1)}, bf16[16,384]{1,0:T(8,128)(2,1)}, u32[]{:S(2)}) copy-start(bf16[16,384]{1,0:T(8,128)(2,1)} %copy-done.31) | copy-start | bytes 36868
  134.4 4.3 %copy-start.2 = (bf16[288,1024]{1,0:T(8,128)(2,1)}, bf16[288,1024]{1,0:T(8,128)(2,1)S(1)}, u32[]{:S(2)}) copy-start(bf16[288,1024]{1,0:T(8,128)(2,1)S(1)} %collective-permute-done.24.refs_4_.refs_6_) | copy-start | bytes 1769476
  136.6 19.0 %collective-permute-start.27 = (bf16[240,1024]{1,0:T(8,128)(2,1)S(1)}, bf16[240,1024]{1,0:T(8,128)(2,1)S(1)}, u32[]{:S(2)}, u32[]{:S(2)}) collective-permute-start(bf16[240,1024]{1,0:T(8,128)(2,1)S(1)} %get-tuple-element.108), channel_id=1, source_target_pairs={{8,0},{24,8},{16,24},{0,16},{9,1},{25,9},{17,25},{1,17},{10,2},{26... | collective-permute-start | bytes 1474568 | tf_op jit(solution)/shard_map/ppermute | solution.py:703
  138.2 17.5 %collective-permute-start.26 = (bf16[240,1024]{1,0:T(8,128)(2,1)S(1)}, bf16[240,1024]{1,0:T(8,128)(2,1)S(1)}, u32[]{:S(2)}, u32[]{:S(2)}) collective-permute-start(bf16[240,1024]{1,0:T(8,128)(2,1)S(1)} %get-tuple-element.105.refs_8_), channel_id=1, source_target_pairs={{0,8},{8,24},{24,16},{16,0},{1,9},{9,25},{25,17},{17,1},{2,10},{10... | collective-permute-start | bytes 1474568 | tf_op jit(solution)/shard_map/ppermute | solution.py:702
  151.9 16.5 %collective-permute-start.32 = (bf16[240,1024]{1,0:T(8,128)(2,1)S(1)}, bf16[240,1024]{1,0:T(8,128)(2,1)S(1)}, u32[]{:S(2)}, u32[]{:S(2)}) collective-permute-start(bf16[240,1024]{1,0:T(8,128)(2,1)S(1)} %get-tuple-element.116), channel_id=1, source_target_pairs={{0,8},{8,24},{24,16},{16,0},{1,9},{9,25},{25,17},{17,1},{2,10},{10... | collective-permute-start | bytes 1474568 | tf_op jit(solution)/shard_map/ppermute | solution.py:702
  151.9 16.5 %collective-permute-start.33 = (bf16[240,1024]{1,0:T(8,128)(2,1)S(1)}, bf16[240,1024]{1,0:T(8,128)(2,1)S(1)}, u32[]{:S(2)}, u32[]{:S(2)}) collective-permute-start(bf16[240,1024]{1,0:T(8,128)(2,1)S(1)} %get-tuple-element.117), channel_id=1, source_target_pairs={{8,0},{24,8},{16,24},{0,16},{9,1},{25,9},{17,25},{1,17},{10,2},{26... | collective-permute-start | bytes 1474568 | tf_op jit(solution)/shard_map/ppermute | solution.py:703
  158.4 14.1 %collective-permute-start.29 = (bf16[240,1024]{1,0:T(8,128)(2,1)S(1)}, bf16[240,1024]{1,0:T(8,128)(2,1)S(1)}, u32[]{:S(2)}, u32[]{:S(2)}) collective-permute-start(bf16[240,1024]{1,0:T(8,128)(2,1)S(1)} %get-tuple-element.114), channel_id=1, source_target_pairs={{8,0},{24,8},{16,24},{0,16},{9,1},{25,9},{17,25},{1,17},{10,2},{26... | collective-permute-start | bytes 1474568 | tf_op jit(solution)/shard_map/ppermute | solution.py:703
  158.9 14.8 %collective-permute-start.28 = (bf16[240,1024]{1,0:T(8,128)(2,1)S(1)}, bf16[240,1024]{1,0:T(8,128)(2,1)S(1)}, u32[]{:S(2)}, u32[]{:S(2)}) collective-permute-start(bf16[240,1024]{1,0:T(8,128)(2,1)S(1)} %get-tuple-element.113.refs_6_), channel_id=1, source_target_pairs={{0,8},{8,24},{24,16},{16,0},{1,9},{9,25},{25,17},{17,1},{2,10},{10... | collective-permute-start | bytes 1474568 | tf_op jit(solution)/shard_map/ppermute | solution.py:702
  (21 other events, 44.1 us)
where the time goes:
time: 177 us; the launch traced here: 176 us
  Pallas kernels  88.2 us (50%)
  waiting for transfers between devices  43.2 us (24%)
  starting transfers between devices  39.5 us (22%)
  local copies, waits for them, and re-layouts  3.36 us (2%)
  between operations  2.1 us (1%)
    pallas_call x14, Pallas kernels, pack(): pl.pallas_call(functools.partial(pack_body, n=n, places=places, chunk=chu...  35.1 us
    pallas_call x5, Pallas kernels, layer(): pl.pallas_call(functools.partial(layer_body, resumed=resumed, tile=tile,...  28.5 us
    ppermute x14, waiting for transfers between devices, send(): lax.ppermute(sends[-1][1], 'replica', backward)  26.8 us
    pallas_call x4, Pallas kernels, patch(): pl.pallas_call(functools.partial(patch_body, arrivals=arrivals, chunks=ch...  20.9 us
    ppermute x14, starting transfers between devices, send(): lax.ppermute(sends[-1][1], 'replica', backward)  19.3 us
    ppermute x14, starting transfers between devices, send(): lax.ppermute(sends[-1][0], 'replica', forward)  10.7 us
    ppermute x14, waiting for transfers between devices, send(): lax.ppermute(sends[-1][0], 'replica', forward)  9.76 us
    ppermute x3, starting transfers between devices, per_device(): other = lax.ppermute(both, axis, [(i, i ^ apart) for i in range(size)])  5.05 us
  transfers between devices with their start and end apart: 34, of which 13 were waited for; matrix products, arithmetic and copies ran while one was open for 0% of the time, Pallas kernels for 44%

commit v1 on v0

--- a/solution.py
+++ b/solution.py
@@ -8,6 +8,7 @@
 from jax.sharding import PartitionSpec as P
 
 BF16, F32 = jnp.bfloat16, jnp.float32
+SUM_AFTER = 1
 LAG = 2
 MOST_CHUNKS = 24
 TILE = 16
@@ -726,7 +727,7 @@
 
     tile = 128 if units % 128 == 0 else units
     hidden, d_rows = [], None
-    pieces = shares(units // tile, 5)
+    pieces = shares(units // tile, 4)
     for first, count in pieces:
         part, d_rows = layer(both, w_gate, w_up, w_down, d_rows, sent, tile, first, count)
         hidden.append(part)
@@ -767,7 +768,8 @@
     early = blocks // 4
     ready = parcel_from + LAG * reach[0] + 1
     while len(got) < steps:
-        sent = send(*cotangents.advance(sent), *news[:1])
+        ready_sum = len(got) > parcel_from + SUM_AFTER
+        sent = send(*(cotangents.advance(sent) if ready_sum else ()), *news[:1])
         if len(got) == ready and early and len(got) < steps:
             hidden_t, outs = gathered(sent)
             news = update_part(0, early, (hidden_t,))

time: 177 us -> 168 us (0.949)
  waiting for transfers between devices: 43.2 us -> 39.2 us
  starting transfers between devices: 39.5 us -> 36.4 us
    pallas_call x4, Pallas kernels: 20.9 us -> 0.51 us  [patch(): pl.pallas_call(functools.partial(patch_body, arrivals=arrivals, chunks=ch...]
    pallas_call x2, Pallas kernels: 0.02 us -> 18.6 us  [update(): pl.pallas_call(functools.partial(update_body, n=n, block=block, first=fir...]
    ppermute x14, waiting for transfers between devices: 26.8 us -> 14.8 us  [send(): lax.ppermute(sends[-1][1], 'replica', backward)]
    ppermute x3, waiting for transfers between devices: 3.91 us -> 7.65 us  [per_device(): other = lax.ppermute(both, axis, [(i, i ^ apart) for i in range(size)])]
    ppermute x3, starting transfers between devices: 4.49 us -> 1.5 us  [advance(): self.arrived = (lax.ppermute(sent, axis, route),)]
    ppermute x14, waiting for transfers between devices: 9.76 us -> 12.3 us  [send(): lax.ppermute(sends[-1][0], 'replica', forward)]
    ppermute x14, starting transfers between devices: 19.3 us -> 21.1 us  [send(): lax.ppermute(sends[-1][1], 'replica', backward)]
    pallas_call x5 -> x4, Pallas kernels: 28.5 us -> 26.7 us  [layer(): pl.pallas_call(functools.partial(layer_body, resumed=resumed, tile=tile,...]
  transfers between devices with their start and end apart: 34 -> 34, of which waited for: 13 -> 15; matrix products, arithmetic and copies ran while one was open for 0% -> 0% of each run, Pallas kernels for 44% -> 50%
where the time goes in v1:
time: 168 us; the launch traced here: 167 us
  Pallas kernels  86.5 us (51%)
  waiting for transfers between devices  39.2 us (23%)
  starting transfers between devices  36.4 us (22%)
  local copies, waits for them, and re-layouts  2.61 us (2%)
  between operations  2.1 us (1%)
    pallas_call x14, Pallas kernels, pack(): pl.pallas_call(functools.partial(pack_body, n=n, places=places, chunk=chu...  36.1 us
    pallas_call x4, Pallas kernels, layer(): pl.pallas_call(functools.partial(layer_body, resumed=resumed, tile=tile,...  26.7 us
    ppermute x14, starting transfers between devices, send(): lax.ppermute(sends[-1][1], 'replica', backward)  21.1 us
    pallas_call x2, Pallas kernels, update(): pl.pallas_call(functools.partial(update_body, n=n, block=block, first=fir...  18.6 us
    ppermute x14, waiting for transfers between devices, send(): lax.ppermute(sends[-1][1], 'replica', backward)  14.8 us
    ppermute x14, waiting for transfers between devices, send(): lax.ppermute(sends[-1][0], 'replica', forward)  12.3 us
    ppermute x14, starting transfers between devices, send(): lax.ppermute(sends[-1][0], 'replica', forward)  9.06 us
    ppermute x3, waiting for transfers between devices, per_device(): other = lax.ppermute(both, axis, [(i, i ^ apart) for i in range(size)])  7.65 us
  transfers between devices with their start and end apart: 34, of which 15 were waited for; matrix products, arithmetic and copies ran while one was open for 0% of the time, Pallas kernels for 50%

profile of v1, /device:TPU:0, one launch (start us, length us, event | category | flops | bytes accessed | tf_op | source)
XLA Modules:
  0.0 166.7 jit_solution(9493310718327675778)
XLA Ops:
  0.7 2.5 %pack.14 = (bf16[240,1024]{1,0:T(8,128)(2,1)S(1)}, bf16[240,1024]{1,0:T(8,128)(2,1)S(1)}) custom-call(f32[2,1920,1024]{2,1,0:T(8,128)} %refs_0_.27, f32[2,1920,1024]{2,1,0:T(8,128)} %refs_1_.39, f32[2,1920,1024]{2,1,0:T(8,128)} %refs_2_.39), custom_call_target="tpu_custom_call" | custom-call | bytes 2949120 | tf_op jit(solution)/shard_map/pack/pallas_call | solution.py:199
  3.1 3.0 %collective-permute-start.4 = (bf16[240,1024]{1,0:T(8,128)(2,1)S(1)}, bf16[240,1024]{1,0:T(8,128)(2,1)S(1)}, u32[]{:S(2)}, u32[]{:S(2)}) collective-permute-start(bf16[240,1024]{1,0:T(8,128)(2,1)S(1)} %get-tuple-element.68), channel_id=1, source_target_pairs={{8,0},{24,8},{16,24},{0,16},{9,1},{25,9},{17,25},{1,17},{10,2},{26... | collective-permute-start | bytes 1474568 | tf_op jit(solution)/shard_map/ppermute | solution.py:704
  6.2 2.5 %pack.15 = (bf16[240,1024]{1,0:T(8,128)(2,1)S(1)}, bf16[240,1024]{1,0:T(8,128)(2,1)S(1)}) custom-call(f32[2,1920,1024]{2,1,0:T(8,128)} %refs_0_.27, f32[2,1920,1024]{2,1,0:T(8,128)} %refs_1_.39, f32[2,1920,1024]{2,1,0:T(8,128)} %refs_2_.39, bf16[1,2,8192]{2,1,0:T(2,128)(2,1)S(1)} %beside.1.refs_3_.own), custom_call_target="tpu_custom_call" | custom-call | bytes 2949120 | tf_op jit(solution)/shard_map/pack/pallas_call | solution.py:199
  8.7 2.0 %collective-permute-start.6 = (bf16[240,1024]{1,0:T(8,128)(2,1)S(1)}, bf16[240,1024]{1,0:T(8,128)(2,1)S(1)}, u32[]{:S(2)}, u32[]{:S(2)}) collective-permute-start(bf16[240,1024]{1,0:T(8,128)(2,1)S(1)} %get-tuple-element.71), channel_id=1, source_target_pairs={{8,0},{24,8},{16,24},{0,16},{9,1},{25,9},{17,25},{1,17},{10,2},{26... | collective-permute-start | bytes 1474568 | tf_op jit(solution)/shard_map/ppermute | solution.py:704
  10.8 1.2 collective-permute-done.other
  12.0 2.1 %collective-permute-start.1 = (bf16[2,2,8192]{2,1,0:T(2,128)(2,1)S(1)}, bf16[2,2,8192]{2,1,0:T(2,128)(2,1)S(1)}, u32[]{:S(2)}, u32[]{:S(2)}) collective-permute-start(bf16[2,2,8192]{2,1,0:T(2,128)(2,1)S(1)} %join.3.own), channel_id=1, source_target_pairs={{0,2},{2,0},{4,6},{6,4},{1,3},{3,1},{5,7},{7,5},{8,10},{10,8},{12,... | collective-permute-start | bytes 196616 | tf_op jit(solution)/shard_map/ppermute | solution.py:718
  14.8 1.8 %collective-permute-done.1.other = bf16[2,2,8192]{2,1,0:T(2,128)(2,1)S(1)} collective-permute-done((bf16[2,2,8192]{2,1,0:T(2,128)(2,1)S(1)}, bf16[2,2,8192]{2,1,0:T(2,128)(2,1)S(1)}, u32[]{:S(2)}, u32[]{:S(2)}) %collective-permute-start.1) | collective-permute-done | bytes 65568 | tf_op jit(solution)/shard_map/ppermute | solution.py:718
  16.5 1.6 collective-permute-done.4.refs_5_.refs_1_
  18.2 2.1 %collective-permute-done.3.refs_4_.refs_0_ = bf16[240,1024]{1,0:T(8,128)(2,1)S(1)} collective-permute-done((bf16[240,1024]{1,0:T(8,128)(2,1)S(1)}, bf16[240,1024]{1,0:T(8,128)(2,1)S(1)}, u32[]{:S(2)}, u32[]{:S(2)}) %collective-permute-start.3) | collective-permute-done | bytes 491552 | tf_op jit(solution)/shard_map/ppermute | solution.py:703
  20.3 2.7 %pack.16 = (bf16[240,1024]{1,0:T(8,128)(2,1)S(1)}, bf16[240,1024]{1,0:T(8,128)(2,1)S(1)}) custom-call(s32[1]{0:T(128)S(6)} %copy.43.refs_0_.failed, f32[2,1920,1024]{2,1,0:T(8,128)} %refs_0_.27, f32[2,1920,1024]{2,1,0:T(8,128)} %refs_1_.39, f32[2,1920,1024]{2,1,0:T(8,128)} %refs_2_.39, bf16[240,1024]{1,0:T(8,128)(2,1)S(1)} %collective-permute-done.3.refs_4_.refs_0_, ...), custom_call_target="tpu_custom_call" | custom-call | bytes 2949120 | tf_op jit(solution)/shard_map/pack/pallas_call | solution.py:199
  23.0 1.5 collective-permute-start.8
  25.1 2.6 %collective-permute-start.2 = (bf16[4,2,8192]{2,1,0:T(2,128)(2,1)S(1)}, bf16[4,2,8192]{2,1,0:T(2,128)(2,1)S(1)}, u32[]{:S(2)}, u32[]{:S(2)}) collective-permute-start(bf16[4,2,8192]{2,1,0:T(2,128)(2,1)S(1)} %join.4.refs_6_.own), channel_id=1, source_target_pairs={{0,4},{2,6},{4,0},{6,2},{1,5},{3,7},{5,1},{7,3},{8,12},{10,14},{12... | collective-permute-start | bytes 393224 | tf_op jit(solution)/shard_map/ppermute | solution.py:718
  27.7 4.7 %collective-permute-done.2.other = bf16[4,2,8192]{2,1,0:T(2,128)(2,1)S(1)} collective-permute-done((bf16[4,2,8192]{2,1,0:T(2,128)(2,1)S(1)}, bf16[4,2,8192]{2,1,0:T(2,128)(2,1)S(1)}, u32[]{:S(2)}, u32[]{:S(2)}) %collective-permute-start.2) | collective-permute-done | bytes 131104 | tf_op jit(solution)/shard_map/ppermute | solution.py:718
  32.5 5.7 %layer.4 = (bf16[16,384]{1,0:T(8,128)(2,1)S(1)}, f32[16,4096]{1,0:T(8,128)S(1)}) custom-call(bf16[16,8192]{1,0:T(8,128)(2,1)S(1)} %join.5.both.refs_6_, bf16[4096,1920]{1,0:T(8,128)(2,1)} %refs_0_.25, bf16[4096,1920]{1,0:T(8,128)(2,1)} %refs_1_.29, bf16[1920,4096]{1,0:T(8,128)(2,1)} %refs_2_.29, bf16[240,1024]{1,0:T(8,128)(2,1)S(1)} %get-tuple-element.69.refs_0_.refs_3_), custom_call_target="tpu_custom_call" | custom-call | flops 251658240 | bytes 9437184 | tf_op jit(solution)/shard_map/layer/pallas_call | solution.py:328
  38.3 2.7 %pack.17 = (bf16[240,1024]{1,0:T(8,128)(2,1)S(1)}, bf16[240,1024]{1,0:T(8,128)(2,1)S(1)}) custom-call(s32[1]{0:T(128)S(6)} %copy.43.refs_0_.failed, f32[2,1920,1024]{2,1,0:T(8,128)} %refs_0_.27, f32[2,1920,1024]{2,1,0:T(8,128)} %refs_1_.39, f32[2,1920,1024]{2,1,0:T(8,128)} %refs_2_.39, bf16[240,1024]{1,0:T(8,128)(2,1)S(1)} %collective-permute-done.5.refs_4_.refs_2_, ...), custom_call_target="tpu_custom_call" | custom-call | bytes 2949120 | tf_op jit(solution)/shard_map/pack/pallas_call | solution.py:199
  41.0 1.5 collective-permute-start.10
  43.1 7.0 %layer.5 = (bf16[16,512]{1,0:T(8,128)(2,1)S(1)}, f32[16,4096]{1,0:T(8,128)S(1)}) custom-call(bf16[16,8192]{1,0:T(8,128)(2,1)S(1)} %join.5.both.refs_6_, bf16[4096,1920]{1,0:T(8,128)(2,1)} %refs_0_.25, bf16[4096,1920]{1,0:T(8,128)(2,1)} %refs_1_.29, bf16[1920,4096]{1,0:T(8,128)(2,1)} %refs_2_.29, f32[16,4096]{1,0:T(8,128)S(1)} %get-tuple-element.70.refs_6_.refs_3_, ...), custom_call_target="tpu_custom_call" | custom-call | flops 335544320 | bytes 12582912 | tf_op jit(solution)/shard_map/layer/pallas_call | solution.py:328
  50.1 2.7 %pack.18 = (bf16[240,1024]{1,0:T(8,128)(2,1)S(1)}, bf16[240,1024]{1,0:T(8,128)(2,1)S(1)}) custom-call(s32[1]{0:T(128)S(6)} %copy.43.refs_0_.failed, f32[2,1920,1024]{2,1,0:T(8,128)} %refs_0_.27, f32[2,1920,1024]{2,1,0:T(8,128)} %refs_1_.39, f32[2,1920,1024]{2,1,0:T(8,128)} %refs_2_.39, bf16[240,1024]{1,0:T(8,128)(2,1)S(1)} %collective-permute-done.7.refs_4_, ...), custom_call_target="tpu_custom_call" | custom-call | bytes 2949120 | tf_op jit(solution)/shard_map/pack/pallas_call | solution.py:199
  52.8 1.5 collective-permute-start.15
  54.9 7.0 %layer.6 = (bf16[16,512]{1,0:T(8,128)(2,1)S(1)}, f32[16,4096]{1,0:T(8,128)S(1)}) custom-call(bf16[16,8192]{1,0:T(8,128)(2,1)S(1)} %join.5.both.refs_6_, bf16[4096,1920]{1,0:T(8,128)(2,1)} %refs_0_.25, bf16[4096,1920]{1,0:T(8,128)(2,1)} %refs_1_.29, bf16[1920,4096]{1,0:T(8,128)(2,1)} %refs_2_.29, f32[16,4096]{1,0:T(8,128)S(1)} %get-tuple-element.73.refs_6_.refs_3_, ...), custom_call_target="tpu_custom_call" | custom-call | flops 335544320 | bytes 12582912 | tf_op jit(solution)/shard_map/layer/pallas_call | solution.py:328
  61.9 2.7 %pack.19 = (bf16[240,1024]{1,0:T(8,128)(2,1)S(1)}, bf16[240,1024]{1,0:T(8,128)(2,1)S(1)}) custom-call(s32[1]{0:T(128)S(6)} %copy.43.refs_0_.failed, f32[2,1920,1024]{2,1,0:T(8,128)} %refs_0_.27, f32[2,1920,1024]{2,1,0:T(8,128)} %refs_1_.39, f32[2,1920,1024]{2,1,0:T(8,128)} %refs_2_.39, bf16[240,1024]{1,0:T(8,128)(2,1)S(1)} %collective-permute-done.9.refs_4_.refs_6_, ...), custom_call_target="tpu_custom_call" | custom-call | bytes 2949120 | tf_op jit(solution)/shard_map/pack/pallas_call | solution.py:199
  64.7 1.5 collective-permute-start.12
  66.8 7.0 %layer.7 = (bf16[16,512]{1,0:T(8,128)(2,1)S(1)}, f32[16,4096]{1,0:T(8,128)S(1)}) custom-call(bf16[16,8192]{1,0:T(8,128)(2,1)S(1)} %join.5.both.refs_6_, bf16[4096,1920]{1,0:T(8,128)(2,1)} %refs_0_.25, bf16[4096,1920]{1,0:T(8,128)(2,1)} %refs_1_.29, bf16[1920,4096]{1,0:T(8,128)(2,1)} %refs_2_.29, f32[16,4096]{1,0:T(8,128)S(1)} %get-tuple-element.76.refs_6_.refs_3_, ...), custom_call_target="tpu_custom_call" | custom-call | flops 335544320 | bytes 12582912 | tf_op jit(solution)/shard_map/layer/pallas_call | solution.py:328
  73.9 2.8 %pack.21 = (bf16[304,1024]{1,0:T(8,128)(2,1)}, bf16[288,1024]{1,0:T(8,128)(2,1)}) custom-call(s32[1]{0:T(128)S(6)} %copy.43.refs_0_.failed, f32[2,1920,1024]{2,1,0:T(8,128)} %refs_0_.27, f32[2,1920,1024]{2,1,0:T(8,128)} %refs_1_.39, f32[2,1920,1024]{2,1,0:T(8,128)} %refs_2_.39, bf16[240,1024]{1,0:T(8,128)(2,1)S(1)} %collective-permute-done.14.refs_4_.refs_8_, ...), custom_call_target="tpu_custom_call" | custom-call | bytes 2949120 | tf_op jit(solution)/shard_map/pack/pallas_call | solution.py:199
  76.7 2.0 %collective-permute-start.17 = (bf16[288,1024]{1,0:T(8,128)(2,1)}, bf16[288,1024]{1,0:T(8,128)(2,1)S(1)}, u32[]{:S(2)}, u32[]{:S(2)}) collective-permute-start(bf16[288,1024]{1,0:T(8,128)(2,1)} %get-tuple-element.90), channel_id=1, source_target_pairs={{8,0},{24,8},{16,24},{0,16},{9,1},{25,9},{17,25},{1,17},{10,2},{26... | collective-permute-start | bytes 1769480 | tf_op jit(solution)/shard_map/ppermute | solution.py:704
  78.7 2.3 %pack.20 = (bf16[240,1024]{1,0:T(8,128)(2,1)}, bf16[240,1024]{1,0:T(8,128)(2,1)}) custom-call(s32[1]{0:T(128)S(6)} %copy.43.refs_0_.failed, f32[2,1920,1024]{2,1,0:T(8,128)} %refs_0_.27, f32[2,1920,1024]{2,1,0:T(8,128)} %refs_1_.39, f32[2,1920,1024]{2,1,0:T(8,128)} %refs_2_.39, bf16[240,1024]{1,0:T(8,128)(2,1)S(1)} %collective-permute-done.11.refs_4_.refs_0_, ...), custom_call_target="tpu_custom_call" | custom-call | bytes 2949120 | tf_op jit(solution)/shard_map/pack/pallas_call | solution.py:199
  83.8 1.3 collective-permute-start.13
  85.1 8.2 %collective-permute-done.17.refs_5_.refs_6_.refs_3_ = bf16[288,1024]{1,0:T(8,128)(2,1)S(1)} collective-permute-done((bf16[288,1024]{1,0:T(8,128)(2,1)}, bf16[288,1024]{1,0:T(8,128)(2,1)S(1)}, u32[]{:S(2)}, u32[]{:S(2)}) %collective-permute-start.17) | collective-permute-done | bytes 589856 | tf_op jit(solution)/shard_map/ppermute | solution.py:704
  93.9 2.5 %pack.22 = (bf16[288,1024]{1,0:T(8,128)(2,1)}, bf16[240,1024]{1,0:T(8,128)(2,1)}) custom-call(s32[1]{0:T(128)S(6)} %copy.43.refs_0_.failed, f32[2,1920,1024]{2,1,0:T(8,128)} %refs_0_.27, f32[2,1920,1024]{2,1,0:T(8,128)} %refs_1_.39, f32[2,1920,1024]{2,1,0:T(8,128)} %refs_2_.39, bf16[304,1024]{1,0:T(8,128)(2,1)S(1)} %collective-permute-done.16.refs_4_.refs_2_, ...), custom_call_target="tpu_custom_call" | custom-call | bytes 2949120 | tf_op jit(solution)/shard_map/pack/pallas_call | solution.py:199
  97.3 1.2 collective-permute-start.23
  99.4 1.5 halve.5
  101.0 2.9 %collective-permute-done.20.refs_5_ = bf16[240,1024]{1,0:T(8,128)(2,1)} collective-permute-done((bf16[240,1024]{1,0:T(8,128)(2,1)}, bf16[240,1024]{1,0:T(8,128)(2,1)}, u32[]{:S(2)}, u32[]{:S(2)}) %collective-permute-start.20) | collective-permute-done | bytes 491552 | tf_op jit(solution)/shard_map/ppermute | solution.py:704
  104.5 2.3 %pack.23 = (bf16[240,1024]{1,0:T(8,128)(2,1)}, bf16[240,1024]{1,0:T(8,128)(2,1)}) custom-call(s32[1]{0:T(128)S(6)} %copy.43.refs_0_.failed, f32[2,1920,1024]{2,1,0:T(8,128)} %refs_0_.27, f32[2,1920,1024]{2,1,0:T(8,128)} %refs_1_.39, f32[2,1920,1024]{2,1,0:T(8,128)} %refs_2_.39, bf16[240,1024]{1,0:T(8,128)(2,1)} %collective-permute-done.19.refs_4_, ...), custom_call_target="tpu_custom_call" | custom-call | bytes 2949120 | tf_op jit(solution)/shard_map/pack/pallas_call | solution.py:199
  106.8 1.2 collective-permute-start.25
  109.0 4.4 %collective-permute-done.18.refs_1_ = f32[4,4096]{1,0:T(4,128)} collective-permute-done((f32[4,4096]{1,0:T(4,128)}, f32[4,4096]{1,0:T(4,128)}, u32[]{:S(2)}, u32[]{:S(2)}) %collective-permute-start.18) | collective-permute-done | bytes 65568 | tf_op jit(solution)/shard_map/ppermute | solution.py:401
  115.3 1.5 collective-permute-done.22.refs_4_.refs_5_.refs_6_
  116.8 2.7 %pack.24 = (bf16[240,1024]{1,0:T(8,128)(2,1)S(1)}, bf16[240,1024]{1,0:T(8,128)(2,1)S(1)}) custom-call(s32[1]{0:T(128)S(6)} %copy.43.refs_0_.failed, f32[2,1920,1024]{2,1,0:T(8,128)} %refs_0_.27, f32[2,1920,1024]{2,1,0:T(8,128)} %refs_1_.39, f32[2,1920,1024]{2,1,0:T(8,128)} %refs_2_.39, bf16[288,1024]{1,0:T(8,128)(2,1)S(1)} %collective-permute-done.22.refs_4_.refs_5_.refs_6_, ...), custom_call_target="tpu_custom_call" | custom-call | bytes 2949120 | tf_op jit(solution)/shard_map/pack/pallas_call | solution.py:199
  119.7 1.9 %collective-permute-start.30 = (bf16[240,1024]{1,0:T(8,128)(2,1)S(1)}, bf16[240,1024]{1,0:T(8,128)(2,1)S(1)}, u32[]{:S(2)}, u32[]{:S(2)}) collective-permute-start(bf16[240,1024]{1,0:T(8,128)(2,1)S(1)} %get-tuple-element.99.refs_2_.refs_7_), channel_id=1, source_target_pairs={{0,8},{8,24},{24,16},{16,0},{1,9},{9,25},{25,17},{17,1},{2,10},{10... | collective-permute-start | bytes 1474568 | tf_op jit(solution)/shard_map/ppermute | solution.py:703
  122.4 4.7 %update.2 = (f32[1920,1024]{1,0:T(8,128)}, f32[1920,1024]{1,0:T(8,128)}, f32[1920,1024]{1,0:T(8,128)}) custom-call(s32[1]{0:T(128)S(6)} %copy.43.refs_0_.failed, bf16[1920,64]{1,0:T(8,128)(2,1)S(1)} %get-tuple-element.100.hid_ref.refs_3_, bf16[64,1024]{1,0:T(8,128)(2,1)S(1)} %get-tuple-element.101.out_ref, f32[2,1920,1024]{2,1,0:T(8,128)} %refs_0_.27, ...), custom_call_target="tpu_custom_call" | custom-call | flops 50331648 | bytes 9437184 | tf_op jit(solution)/shard_map/update/pallas_call | solution.py:522
  128.6 2.5 %pack.25 = (bf16[240,1024]{1,0:T(8,128)(2,1)S(1)}, bf16[240,1024]{1,0:T(8,128)(2,1)S(1)}) custom-call(s32[1]{0:T(128)S(6)} %copy.43.refs_0_.failed, f32[2,1920,1024]{2,1,0:T(8,128)} %refs_0_.27, f32[2,1920,1024]{2,1,0:T(8,128)} %refs_1_.39, f32[2,1920,1024]{2,1,0:T(8,128)} %refs_2_.39, bf16[240,1024]{1,0:T(8,128)(2,1)} %collective-permute-done.24.refs_4_.refs_8_, ...), custom_call_target="tpu_custom_call" | custom-call | bytes 2949120 | tf_op jit(solution)/shard_map/pack/pallas_call | solution.py:199
  131.2 2.0 %collective-permute-start.27 = (bf16[240,1024]{1,0:T(8,128)(2,1)S(1)}, bf16[240,1024]{1,0:T(8,128)(2,1)S(1)}, u32[]{:S(2)}, u32[]{:S(2)}) collective-permute-start(bf16[240,1024]{1,0:T(8,128)(2,1)S(1)} %get-tuple-element.108), channel_id=1, source_target_pairs={{8,0},{24,8},{16,24},{0,16},{9,1},{25,9},{17,25},{1,17},{10,2},{26... | collective-permute-start | bytes 1474568 | tf_op jit(solution)/shard_map/ppermute | solution.py:704
  133.5 2.7 %pack.27 = (bf16[240,1024]{1,0:T(8,128)(2,1)S(1)}, bf16[240,1024]{1,0:T(8,128)(2,1)S(1)}) custom-call(s32[1]{0:T(128)S(6)} %copy.43.refs_0_.failed, f32[2,1920,1024]{2,1,0:T(8,128)} %refs_0_.27, f32[2,1920,1024]{2,1,0:T(8,128)} %refs_1_.39, f32[2,1920,1024]{2,1,0:T(8,128)} %refs_2_.39, bf16[240,1024]{1,0:T(8,128)(2,1)S(1)} %collective-permute-done.30.refs_4_.refs_10_, ...), custom_call_target="tpu_custom_call" | custom-call | bytes 2949120 | tf_op jit(solution)/shard_map/pack/pallas_call | solution.py:199
  137.1 1.1 collective-permute-start.33
  138.3 7.0 %collective-permute-done.26.refs_4_.refs_12_ = bf16[240,1024]{1,0:T(8,128)(2,1)S(1)} collective-permute-done((bf16[240,1024]{1,0:T(8,128)(2,1)S(1)}, bf16[240,1024]{1,0:T(8,128)(2,1)S(1)}, u32[]{:S(2)}, u32[]{:S(2)}) %collective-permute-start.26) | collective-permute-done | bytes 491552 | tf_op jit(solution)/shard_map/ppermute | solution.py:703
  146.2 2.7 %pack.26 = (bf16[240,1024]{1,0:T(8,128)(2,1)S(1)}, bf16[240,1024]{1,0:T(8,128)(2,1)S(1)}) custom-call(s32[1]{0:T(128)S(6)} %copy.43.refs_0_.failed, f32[2,1920,1024]{2,1,0:T(8,128)} %refs_0_.27, f32[2,1920,1024]{2,1,0:T(8,128)} %refs_1_.39, f32[2,1920,1024]{2,1,0:T(8,128)} %refs_2_.39, bf16[240,1024]{1,0:T(8,128)(2,1)S(1)} %collective-permute-done.26.refs_4_.refs_12_, ...), custom_call_target="tpu_custom_call" | custom-call | bytes 2949120 | tf_op jit(solution)/shard_map/pack/pallas_call | solution.py:199
  148.9 1.2 collective-permute-start.29
  151.1 13.9 %update.3 = (f32[1920,1024]{1,0:T(8,128)}, f32[1920,1024]{1,0:T(8,128)}, f32[1920,1024]{1,0:T(8,128)}) custom-call(s32[1]{0:T(128)S(6)} %copy.43.refs_0_.failed, bf16[1920,64]{1,0:T(8,128)(2,1)S(1)} %get-tuple-element.100.hid_ref.refs_3_, ...), custom_call_target="tpu_custom_call", output_to_operand_aliasing={{0}: (6, {}), {1}: (7, {}), {2}: (8, {})} | custom-call | flops 201326592 | bytes 37748736 | tf_op jit(solution)/shard_map/update/pallas_call | solution.py:522
  165.3 1.2 collective-permute-done.29.refs_1_
  (127 shorter events, 17.3 us)
Async XLA Ops:
  0.6 5.6 %copy-start.36 = (bf16[1,2,4096]{2,1,0:T(2,128)(2,1)S(1)}, bf16[1,2,4096]{2,1,0:T(2,128)(2,1)}, u32[]{:S(2)}) copy-start(bf16[1,2,4096]{2,1,0:T(2,128)(2,1)} %param.10) | copy-start | bytes 49156
  0.6 5.6 %copy-start.35 = (bf16[1,2,4096]{2,1,0:T(2,128)(2,1)S(1)}, bf16[1,2,4096]{2,1,0:T(2,128)(2,1)}, u32[]{:S(2)}) copy-start(bf16[1,2,4096]{2,1,0:T(2,128)(2,1)} %param.9) | copy-start | bytes 49156
  3.1 15.0 %collective-permute-start.4 = (bf16[240,1024]{1,0:T(8,128)(2,1)S(1)}, bf16[240,1024]{1,0:T(8,128)(2,1)S(1)}, u32[]{:S(2)}, u32[]{:S(2)}) collective-permute-start(bf16[240,1024]{1,0:T(8,128)(2,1)S(1)} %get-tuple-element.68), channel_id=1, source_target_pairs={{8,0},{24,8},{16,24},{0,16},{9,1},{25,9},{17,25},{1,17},{10,2},{26... | collective-permute-start | bytes 1474568 | tf_op jit(solution)/shard_map/ppermute | solution.py:704
  6.2 14.1 %collective-permute-start.3 = (bf16[240,1024]{1,0:T(8,128)(2,1)S(1)}, bf16[240,1024]{1,0:T(8,128)(2,1)S(1)}, u32[]{:S(2)}, u32[]{:S(2)}) collective-permute-start(bf16[240,1024]{1,0:T(8,128)(2,1)S(1)} %get-tuple-element.66.refs_2_), channel_id=1, source_target_pairs={{0,8},{8,24},{24,16},{16,0},{1,9},{9,25},{25,17},{17,1},{2,10},{10... | collective-permute-start | bytes 1474568 | tf_op jit(solution)/shard_map/ppermute | solution.py:703
  8.7 29.5 %collective-permute-start.6 = (bf16[240,1024]{1,0:T(8,128)(2,1)S(1)}, bf16[240,1024]{1,0:T(8,128)(2,1)S(1)}, u32[]{:S(2)}, u32[]{:S(2)}) collective-permute-start(bf16[240,1024]{1,0:T(8,128)(2,1)S(1)} %get-tuple-element.71), channel_id=1, source_target_pairs={{8,0},{24,8},{16,24},{0,16},{9,1},{25,9},{17,25},{1,17},{10,2},{26... | collective-permute-start | bytes 1474568 | tf_op jit(solution)/shard_map/ppermute | solution.py:704
  10.7 27.5 %collective-permute-start.5 = (bf16[240,1024]{1,0:T(8,128)(2,1)S(1)}, bf16[240,1024]{1,0:T(8,128)(2,1)S(1)}, u32[]{:S(2)}, u32[]{:S(2)}) collective-permute-start(bf16[240,1024]{1,0:T(8,128)(2,1)S(1)} %get-tuple-element.67.refs_0_), channel_id=1, source_target_pairs={{0,8},{8,24},{24,16},{16,0},{1,9},{9,25},{25,17},{17,1},{2,10},{10... | collective-permute-start | bytes 1474568 | tf_op jit(solution)/shard_map/ppermute | solution.py:703
  10.8 1.2 collective-permute-start
  12.0 4.5 %collective-permute-start.1 = (bf16[2,2,8192]{2,1,0:T(2,128)(2,1)S(1)}, bf16[2,2,8192]{2,1,0:T(2,128)(2,1)S(1)}, u32[]{:S(2)}, u32[]{:S(2)}) collective-permute-start(bf16[2,2,8192]{2,1,0:T(2,128)(2,1)S(1)} %join.3.own), channel_id=1, source_target_pairs={{0,2},{2,0},{4,6},{6,4},{1,3},{3,1},{5,7},{7,5},{8,10},{10,8},{12,... | collective-permute-start | bytes 196616 | tf_op jit(solution)/shard_map/ppermute | solution.py:718
  18.2 4.8 %copy-start.3 = (bf16[240,1024]{1,0:T(8,128)(2,1)}, bf16[240,1024]{1,0:T(8,128)(2,1)S(1)}, u32[]{:S(2)}) copy-start(bf16[240,1024]{1,0:T(8,128)(2,1)S(1)} %collective-permute-done.4.refs_5_.refs_1_) | copy-start | bytes 1474564
  23.0 27.1 %collective-permute-start.8 = (bf16[240,1024]{1,0:T(8,128)(2,1)S(1)}, bf16[240,1024]{1,0:T(8,128)(2,1)S(1)}, u32[]{:S(2)}, u32[]{:S(2)}) collective-permute-start(bf16[240,1024]{1,0:T(8,128)(2,1)S(1)} %get-tuple-element.74), channel_id=1, source_target_pairs={{8,0},{24,8},{16,24},{0,16},{9,1},{25,9},{17,25},{1,17},{10,2},{26... | collective-permute-start | bytes 1474568 | tf_op jit(solution)/shard_map/ppermute | solution.py:704
  24.5 25.6 %collective-permute-start.7 = (bf16[240,1024]{1,0:T(8,128)(2,1)S(1)}, bf16[240,1024]{1,0:T(8,128)(2,1)S(1)}, u32[]{:S(2)}, u32[]{:S(2)}) collective-permute-start(bf16[240,1024]{1,0:T(8,128)(2,1)S(1)} %get-tuple-element.69.refs_0_.refs_3_), channel_id=1, source_target_pairs={{0,8},{8,24},{24,16},{16,0},{1,9},{9,25},{25,17},{17,1},{2,10},{10... | collective-permute-start | bytes 1474568 | tf_op jit(solution)/shard_map/ppermute | solution.py:703
  25.1 7.3 %collective-permute-start.2 = (bf16[4,2,8192]{2,1,0:T(2,128)(2,1)S(1)}, bf16[4,2,8192]{2,1,0:T(2,128)(2,1)S(1)}, u32[]{:S(2)}, u32[]{:S(2)}) collective-permute-start(bf16[4,2,8192]{2,1,0:T(2,128)(2,1)S(1)} %join.4.refs_6_.own), channel_id=1, source_target_pairs={{0,4},{2,6},{4,0},{6,2},{1,5},{3,7},{5,1},{7,3},{8,12},{10,14},{12... | collective-permute-start | bytes 393224 | tf_op jit(solution)/shard_map/ppermute | solution.py:718
  38.2 35.6 %copy-start.33 = (bf16[16,384]{1,0:T(8,128)(2,1)}, bf16[16,384]{1,0:T(8,128)(2,1)S(1)}, u32[]{:S(2)}) copy-start(bf16[16,384]{1,0:T(8,128)(2,1)S(1)} %get-tuple-element.85.refs_7_.refs_0_) | copy-start | bytes 36868
  41.0 20.9 %collective-permute-start.10 = (bf16[240,1024]{1,0:T(8,128)(2,1)S(1)}, bf16[240,1024]{1,0:T(8,128)(2,1)S(1)}, u32[]{:S(2)}, u32[]{:S(2)}) collective-permute-start(bf16[240,1024]{1,0:T(8,128)(2,1)S(1)} %get-tuple-element.77), channel_id=1, source_target_pairs={{8,0},{24,8},{16,24},{0,16},{9,1},{25,9},{17,25},{1,17},{10,2},{26... | collective-permute-start | bytes 1474568 | tf_op jit(solution)/shard_map/ppermute | solution.py:704
  42.5 19.4 %collective-permute-start.9 = (bf16[240,1024]{1,0:T(8,128)(2,1)S(1)}, bf16[240,1024]{1,0:T(8,128)(2,1)S(1)}, u32[]{:S(2)}, u32[]{:S(2)}) collective-permute-start(bf16[240,1024]{1,0:T(8,128)(2,1)S(1)} %get-tuple-element.72.refs_4_), channel_id=1, source_target_pairs={{0,8},{8,24},{24,16},{16,0},{1,9},{9,25},{25,17},{17,1},{2,10},{10... | collective-permute-start | bytes 1474568 | tf_op jit(solution)/shard_map/ppermute | solution.py:703
  52.8 21.0 %collective-permute-start.15 = (bf16[240,1024]{1,0:T(8,128)(2,1)S(1)}, bf16[240,1024]{1,0:T(8,128)(2,1)S(1)}, u32[]{:S(2)}, u32[]{:S(2)}) collective-permute-start(bf16[240,1024]{1,0:T(8,128)(2,1)S(1)} %get-tuple-element.84), channel_id=1, source_target_pairs={{8,0},{24,8},{16,24},{0,16},{9,1},{25,9},{17,25},{1,17},{10,2},{26... | collective-permute-start | bytes 1474568 | tf_op jit(solution)/shard_map/ppermute | solution.py:704
  54.3 19.5 %collective-permute-start.14 = (bf16[240,1024]{1,0:T(8,128)(2,1)S(1)}, bf16[240,1024]{1,0:T(8,128)(2,1)S(1)}, u32[]{:S(2)}, u32[]{:S(2)}) collective-permute-start(bf16[240,1024]{1,0:T(8,128)(2,1)S(1)} %get-tuple-element.75.refs_4_), channel_id=1, source_target_pairs={{0,8},{8,24},{24,16},{16,0},{1,9},{9,25},{25,17},{17,1},{2,10},{10... | collective-permute-start | bytes 1474568 | tf_op jit(solution)/shard_map/ppermute | solution.py:703
  61.9 12.0 %copy-start.28 = (bf16[16,512]{1,0:T(8,128)(2,1)}, bf16[16,512]{1,0:T(8,128)(2,1)S(1)}, u32[]{:S(2)}) copy-start(bf16[16,512]{1,0:T(8,128)(2,1)S(1)} %get-tuple-element.87.refs_9_.refs_2_) | copy-start | bytes 49156
  64.7 14.0 %collective-permute-start.12 = (bf16[240,1024]{1,0:T(8,128)(2,1)S(1)}, bf16[240,1024]{1,0:T(8,128)(2,1)S(1)}, u32[]{:S(2)}, u32[]{:S(2)}) collective-permute-start(bf16[240,1024]{1,0:T(8,128)(2,1)S(1)} %get-tuple-element.80), channel_id=1, source_target_pairs={{8,0},{24,8},{16,24},{0,16},{9,1},{25,9},{17,25},{1,17},{10,2},{26... | collective-permute-start | bytes 1474568 | tf_op jit(solution)/shard_map/ppermute | solution.py:704
  66.2 12.6 %collective-permute-start.11 = (bf16[240,1024]{1,0:T(8,128)(2,1)S(1)}, bf16[240,1024]{1,0:T(8,128)(2,1)S(1)}, u32[]{:S(2)}, u32[]{:S(2)}) collective-permute-start(bf16[240,1024]{1,0:T(8,128)(2,1)S(1)} %get-tuple-element.78.refs_4_), channel_id=1, source_target_pairs={{0,8},{8,24},{24,16},{16,0},{1,9},{9,25},{25,17},{17,1},{2,10},{10... | collective-permute-start | bytes 1474568 | tf_op jit(solution)/shard_map/ppermute | solution.py:703
  76.7 17.2 %collective-permute-start.16 = (bf16[304,1024]{1,0:T(8,128)(2,1)}, bf16[304,1024]{1,0:T(8,128)(2,1)S(1)}, u32[]{:S(2)}, u32[]{:S(2)}) collective-permute-start(bf16[304,1024]{1,0:T(8,128)(2,1)} %get-tuple-element.89), channel_id=1, source_target_pairs={{0,8},{8,24},{24,16},{16,0},{1,9},{9,25},{25,17},{17,1},{2,10},{10... | collective-permute-start | bytes 1867784 | tf_op jit(solution)/shard_map/ppermute | solution.py:703
  76.7 6.4 %copy-start.23 = (f32[16,4096]{1,0:T(8,128)S(1)}, f32[16,4096]{1,0:T(8,128)}, u32[]{:S(2)}) copy-start(f32[16,4096]{1,0:T(8,128)} %copy-done.22) | copy-start | bytes 786436
  76.7 16.5 %collective-permute-start.17 = (bf16[288,1024]{1,0:T(8,128)(2,1)}, bf16[288,1024]{1,0:T(8,128)(2,1)S(1)}, u32[]{:S(2)}, u32[]{:S(2)}) collective-permute-start(bf16[288,1024]{1,0:T(8,128)(2,1)} %get-tuple-element.90), channel_id=1, source_target_pairs={{8,0},{24,8},{16,24},{0,16},{9,1},{25,9},{17,25},{1,17},{10,2},{26... | collective-permute-start | bytes 1769480 | tf_op jit(solution)/shard_map/ppermute | solution.py:704
  81.0 22.9 %collective-permute-start.20 = (bf16[240,1024]{1,0:T(8,128)(2,1)}, bf16[240,1024]{1,0:T(8,128)(2,1)}, u32[]{:S(2)}, u32[]{:S(2)}) collective-permute-start(bf16[240,1024]{1,0:T(8,128)(2,1)} %get-tuple-element.94), channel_id=1, source_target_pairs={{8,0},{24,8},{16,24},{0,16},{9,1},{25,9},{17,25},{1,17},{10,2},{26... | collective-permute-start | bytes 1474568 | tf_op jit(solution)/shard_map/ppermute | solution.py:704
  82.2 22.4 %collective-permute-start.19 = (bf16[240,1024]{1,0:T(8,128)(2,1)}, bf16[240,1024]{1,0:T(8,128)(2,1)}, u32[]{:S(2)}, u32[]{:S(2)}) collective-permute-start(bf16[240,1024]{1,0:T(8,128)(2,1)} %get-tuple-element.81.refs_1_), channel_id=1, source_target_pairs={{0,8},{8,24},{24,16},{16,0},{1,9},{9,25},{25,17},{17,1},{2,10},{10... | collective-permute-start | bytes 1474568 | tf_op jit(solution)/shard_map/ppermute | solution.py:703
  83.8 12.6 %copy-start.24 = (f32[8,4096]{1,0:T(8,128)}, f32[8,4096]{1,0:T(8,128)S(1)}, u32[]{:S(2)}) copy-start(f32[8,4096]{1,0:T(8,128)S(1)} %get-tuple-element.82.refs_6_.refs_0_) | copy-start | bytes 393220
  83.8 14.7 %collective-permute-start.13 = (f32[8,4096]{1,0:T(8,128)}, f32[8,4096]{1,0:T(8,128)}, u32[]{:S(2)}, u32[]{:S(2)}) collective-permute-start(f32[8,4096]{1,0:T(8,128)} %get-tuple-element.83), channel_id=1, source_target_pairs={{0,4},{2,6},{4,0},{6,2},{1,5},{3,7},{5,1},{7,3},{8,12},{10,14},{12... | collective-permute-start | bytes 393224 | tf_op jit(solution)/shard_map/ppermute | solution.py:401
  93.3 28.4 %copy-start.1 = (bf16[288,1024]{1,0:T(8,128)(2,1)}, bf16[288,1024]{1,0:T(8,128)(2,1)S(1)}, u32[]{:S(2)}) copy-start(bf16[288,1024]{1,0:T(8,128)(2,1)S(1)} %collective-permute-done.17.refs_5_.refs_6_.refs_3_) | copy-start | bytes 1769476
  93.9 27.7 %copy-start = (bf16[304,1024]{1,0:T(8,128)(2,1)}, bf16[304,1024]{1,0:T(8,128)(2,1)S(1)}, u32[]{:S(2)}) copy-start(bf16[304,1024]{1,0:T(8,128)(2,1)S(1)} %collective-permute-done.16.refs_4_.refs_2_) | copy-start | bytes 1867780
  96.5 20.3 %collective-permute-start.22 = (bf16[288,1024]{1,0:T(8,128)(2,1)}, bf16[288,1024]{1,0:T(8,128)(2,1)S(1)}, u32[]{:S(2)}, u32[]{:S(2)}) collective-permute-start(bf16[288,1024]{1,0:T(8,128)(2,1)} %get-tuple-element.91.refs_2_), channel_id=1, source_target_pairs={{0,8},{8,24},{24,16},{16,0},{1,9},{9,25},{25,17},{17,1},{2,10},{10... | collective-permute-start | bytes 1769480 | tf_op jit(solution)/shard_map/ppermute | solution.py:703
  97.3 18.0 %collective-permute-start.23 = (bf16[240,1024]{1,0:T(8,128)(2,1)}, bf16[240,1024]{1,0:T(8,128)(2,1)}, u32[]{:S(2)}, u32[]{:S(2)}) collective-permute-start(bf16[240,1024]{1,0:T(8,128)(2,1)} %get-tuple-element.98), channel_id=1, source_target_pairs={{8,0},{24,8},{16,24},{0,16},{9,1},{25,9},{17,25},{1,17},{10,2},{26... | collective-permute-start | bytes 1474568 | tf_op jit(solution)/shard_map/ppermute | solution.py:704
  101.0 5.8 %copy-start.26 = (f32[4,4096]{1,0:T(4,128)}, f32[4,4096]{1,0:T(4,128)S(1)}, u32[]{:S(2)}) copy-start(f32[4,4096]{1,0:T(4,128)S(1)} %get-tuple-element.92.refs_6_.refs_0_) | copy-start | bytes 196612
  106.8 21.1 %collective-permute-start.25 = (bf16[240,1024]{1,0:T(8,128)(2,1)}, bf16[240,1024]{1,0:T(8,128)(2,1)}, u32[]{:S(2)}, u32[]{:S(2)}) collective-permute-start(bf16[240,1024]{1,0:T(8,128)(2,1)} %get-tuple-element.102), channel_id=1, source_target_pairs={{8,0},{24,8},{16,24},{0,16},{9,1},{25,9},{17,25},{1,17},{10,2},{26... | collective-permute-start | bytes 1474568 | tf_op jit(solution)/shard_map/ppermute | solution.py:704
  108.0 19.9 %collective-permute-start.24 = (bf16[240,1024]{1,0:T(8,128)(2,1)}, bf16[240,1024]{1,0:T(8,128)(2,1)}, u32[]{:S(2)}, u32[]{:S(2)}) collective-permute-start(bf16[240,1024]{1,0:T(8,128)(2,1)} %get-tuple-element.95.refs_2_), channel_id=1, source_target_pairs={{0,8},{8,24},{24,16},{16,0},{1,9},{9,25},{25,17},{17,1},{2,10},{10... | collective-permute-start | bytes 1474568 | tf_op jit(solution)/shard_map/ppermute | solution.py:703
  108.9 4.6 %collective-permute-start.18 = (f32[4,4096]{1,0:T(4,128)}, f32[4,4096]{1,0:T(4,128)}, u32[]{:S(2)}, u32[]{:S(2)}) collective-permute-start(f32[4,4096]{1,0:T(4,128)} %get-tuple-element.93), channel_id=1, source_target_pairs={{0,2},{2,0},{4,6},{6,4},{1,3},{3,1},{5,7},{7,5},{8,10},{10,8},{12,... | collective-permute-start | bytes 196616 | tf_op jit(solution)/shard_map/ppermute | solution.py:401
  115.2 12.1 %collective-permute-start.21 = (f32[2,4096]{1,0:T(2,128)S(1)}, f32[2,4096]{1,0:T(2,128)S(1)}, u32[]{:S(2)}, u32[]{:S(2)}) collective-permute-start(f32[2,4096]{1,0:T(2,128)S(1)} %get-tuple-element.97), channel_id=1, source_target_pairs={{0,1},{1,0},{2,3},{3,2},{4,5},{5,4},{6,7},{7,6},{8,9},{9,8},{10,11... | collective-permute-start | bytes 98312 | tf_op jit(solution)/shard_map/ppermute | solution.py:401
  116.8 4.8 %copy-start.2 = (bf16[288,1024]{1,0:T(8,128)(2,1)}, bf16[288,1024]{1,0:T(8,128)(2,1)S(1)}, u32[]{:S(2)}) copy-start(bf16[288,1024]{1,0:T(8,128)(2,1)S(1)} %collective-permute-done.22.refs_4_.refs_5_.refs_6_) | copy-start | bytes 1769476
  116.8 4.8 %copy-start.29 = (bf16[16,512]{1,0:T(8,128)(2,1)S(1)}, bf16[16,512]{1,0:T(8,128)(2,1)}, u32[]{:S(2)}) copy-start(bf16[16,512]{1,0:T(8,128)(2,1)} %copy-done.28) | copy-start | bytes 49156
  116.8 4.8 %copy-start.31 = (bf16[16,512]{1,0:T(8,128)(2,1)S(1)}, bf16[16,512]{1,0:T(8,128)(2,1)}, u32[]{:S(2)}) copy-start(bf16[16,512]{1,0:T(8,128)(2,1)} %copy-done.30) | copy-start | bytes 49156
  116.8 4.8 %copy-start.34 = (bf16[16,384]{1,0:T(8,128)(2,1)S(1)}, bf16[16,384]{1,0:T(8,128)(2,1)}, u32[]{:S(2)}) copy-start(bf16[16,384]{1,0:T(8,128)(2,1)} %copy-done.33) | copy-start | bytes 36868
  119.5 13.7 %collective-permute-start.31 = (bf16[240,1024]{1,0:T(8,128)(2,1)S(1)}, bf16[240,1024]{1,0:T(8,128)(2,1)S(1)}, u32[]{:S(2)}, u32[]{:S(2)}) collective-permute-start(bf16[240,1024]{1,0:T(8,128)(2,1)S(1)} %get-tuple-element.111), channel_id=1, source_target_pairs={{8,0},{24,8},{16,24},{0,16},{9,1},{25,9},{17,25},{1,17},{10,2},{26... | collective-permute-start | bytes 1474568 | tf_op jit(solution)/shard_map/ppermute | solution.py:704
  119.7 13.8 %collective-permute-start.30 = (bf16[240,1024]{1,0:T(8,128)(2,1)S(1)}, bf16[240,1024]{1,0:T(8,128)(2,1)S(1)}, u32[]{:S(2)}, u32[]{:S(2)}) collective-permute-start(bf16[240,1024]{1,0:T(8,128)(2,1)S(1)} %get-tuple-element.99.refs_2_.refs_7_), channel_id=1, source_target_pairs={{0,8},{8,24},{24,16},{16,0},{1,9},{9,25},{25,17},{17,1},{2,10},{10... | collective-permute-start | bytes 1474568 | tf_op jit(solution)/shard_map/ppermute | solution.py:703
  131.1 14.2 %collective-permute-start.26 = (bf16[240,1024]{1,0:T(8,128)(2,1)S(1)}, bf16[240,1024]{1,0:T(8,128)(2,1)S(1)}, u32[]{:S(2)}, u32[]{:S(2)}) collective-permute-start(bf16[240,1024]{1,0:T(8,128)(2,1)S(1)} %get-tuple-element.107), channel_id=1, source_target_pairs={{0,8},{8,24},{24,16},{16,0},{1,9},{9,25},{25,17},{17,1},{2,10},{10... | collective-permute-start | bytes 1474568 | tf_op jit(solution)/shard_map/ppermute | solution.py:703
  131.2 15.0 %collective-permute-start.27 = (bf16[240,1024]{1,0:T(8,128)(2,1)S(1)}, bf16[240,1024]{1,0:T(8,128)(2,1)S(1)}, u32[]{:S(2)}, u32[]{:S(2)}) collective-permute-start(bf16[240,1024]{1,0:T(8,128)(2,1)S(1)} %get-tuple-element.108), channel_id=1, source_target_pairs={{8,0},{24,8},{16,24},{0,16},{9,1},{25,9},{17,25},{1,17},{10,2},{26... | collective-permute-start | bytes 1474568 | tf_op jit(solution)/shard_map/ppermute | solution.py:704
  136.2 29.0 %collective-permute-start.32 = (bf16[240,1024]{1,0:T(8,128)(2,1)S(1)}, bf16[240,1024]{1,0:T(8,128)(2,1)S(1)}, u32[]{:S(2)}, u32[]{:S(2)}) collective-permute-start(bf16[240,1024]{1,0:T(8,128)(2,1)S(1)} %get-tuple-element.112), channel_id=1, source_target_pairs={{0,8},{8,24},{24,16},{16,0},{1,9},{9,25},{25,17},{17,1},{2,10},{10... | collective-permute-start | bytes 1474568 | tf_op jit(solution)/shard_map/ppermute | solution.py:703
  137.1 28.0 %collective-permute-start.33 = (bf16[240,1024]{1,0:T(8,128)(2,1)S(1)}, bf16[240,1024]{1,0:T(8,128)(2,1)S(1)}, u32[]{:S(2)}, u32[]{:S(2)}) collective-permute-start(bf16[240,1024]{1,0:T(8,128)(2,1)S(1)} %get-tuple-element.113), channel_id=1, source_target_pairs={{8,0},{24,8},{16,24},{0,16},{9,1},{25,9},{17,25},{1,17},{10,2},{26... | collective-permute-start | bytes 1474568 | tf_op jit(solution)/shard_map/ppermute | solution.py:704
  148.9 17.6 %collective-permute-start.29 = (bf16[240,1024]{1,0:T(8,128)(2,1)S(1)}, bf16[240,1024]{1,0:T(8,128)(2,1)S(1)}, u32[]{:S(2)}, u32[]{:S(2)}) collective-permute-start(bf16[240,1024]{1,0:T(8,128)(2,1)S(1)} %get-tuple-element.110), channel_id=1, source_target_pairs={{8,0},{24,8},{16,24},{0,16},{9,1},{25,9},{17,25},{1,17},{10,2},{26... | collective-permute-start | bytes 1474568 | tf_op jit(solution)/shard_map/ppermute | solution.py:704
  150.1 16.4 %collective-permute-start.28 = (bf16[240,1024]{1,0:T(8,128)(2,1)S(1)}, bf16[240,1024]{1,0:T(8,128)(2,1)S(1)}, u32[]{:S(2)}, u32[]{:S(2)}) collective-permute-start(bf16[240,1024]{1,0:T(8,128)(2,1)S(1)} %get-tuple-element.109.refs_6_), channel_id=1, source_target_pairs={{0,8},{8,24},{24,16},{16,0},{1,9},{9,25},{25,17},{17,1},{2,10},{10... | collective-permute-start | bytes 1474568 | tf_op jit(solution)/shard_map/ppermute | solution.py:703
  (23 other events, 70.6 us)

commit v2 on v1

--- a/solution.py
+++ b/solution.py
@@ -13,6 +13,7 @@
 MOST_CHUNKS = 24
 TILE = 16
 BUFFERS = 3
+PIECES = 4
 FETCHED = 4
 VMEM = 50 << 20
 
@@ -93,138 +94,151 @@
     return moves
 
 
-def pack_body(*refs, n, places, chunk, slabs, passed, counts):
-    count_seen, count_parts, count_after = counts
-    if count_seen:
-        roles, refs = Roles(refs[0], n), refs[1:]
-    state = refs[0:3]
-    seen = refs[3 : 3 + count_seen]
-    rest = refs[3 + count_seen :]
-    if count_parts:
-        both, parts, rest = rest[0], rest[1 : 1 + count_parts], rest[1 + count_parts :]
-    sends = rest[count_after : count_after + 2]
-    held, made, sem, out_sem, below_sem = rest[count_after + 2 :]
-    width = held.shape[2]
-    size = 3 * chunk
-
-    def rows_of(j):
+class Packing:
+    def __init__(self, failed, n, state, seen, sends, scratch, plan):
+        self.state, self.seen, self.sends, self.n = state, seen, sends, n
+        self.held, self.made, self.sem, self.out_sem, self.below_sem = scratch
+        self.places, self.chunk, self.slabs, self.passed = plan
+        self.size = 3 * self.chunk
+        self.roles = Roles(failed, n) if seen else None
+
+    def rows_of(self, j):
         way, k = divmod(j, 3)
-        return way, pl.ds(k * chunk, chunk)
-
-    def fetch(j):
+        return way, pl.ds(k * self.chunk, self.chunk)
+
+    def fetch(self, j):
         way, k = divmod(j, 3)
-        rows = pl.ds(places[way] * chunk, chunk)
-        return pltpu.make_async_copy(state[k].at[1, rows], held.at[j], sem.at[j])
-
-    def take(j):
-        way, rows = rows_of(j)
-        return pltpu.make_async_copy(seen[way].at[rows], made.at[way, rows], sem.at[j])
-
-    def store(j):
-        way, rows = rows_of(j)
+        rows = pl.ds(self.places[way] * self.chunk, self.chunk)
         return pltpu.make_async_copy(
-            made.at[way, rows], sends[way].at[rows], out_sem.at[j]
+            self.state[k].at[1, rows], self.held.at[j], self.sem.at[j]
         )
 
-    def convert():
-        for j in range(6):
-            fetch(j).start()
-        for j in range(6):
-            way, rows = rows_of(j)
-            fetch(j).wait()
-            made[way, rows] = held[j].astype(BF16)
-            store(j).start()
-        for j in range(6):
-            store(j).wait()
-
-    def relay():
-        for j in range(6):
-            take(j).start()
-        for j in range(6):
-            take(j).wait()
-            store(j).start()
-        for j in range(6):
-            store(j).wait()
-
-    def below(way, inward):
-        rows = pl.ds(size, passed[way] or sends[way].shape[0] - size)
-        here = made.at[way, rows]
+    def take(self, j):
+        way, rows = self.rows_of(j)
+        return pltpu.make_async_copy(
+            self.seen[way].at[rows], self.made.at[way, rows], self.sem.at[j]
+        )
+
+    def store(self, j):
+        way, rows = self.rows_of(j)
+        return pltpu.make_async_copy(
+            self.made.at[way, rows], self.sends[way].at[rows], self.out_sem.at[j]
+        )
+
+    def below(self, way, inward):
+        count = self.passed[way] or self.sends[way].shape[0] - self.size
+        rows = pl.ds(self.size, count)
+        here, sem = self.made.at[way, rows], self.below_sem.at[way]
         if inward:
-            return pltpu.make_async_copy(seen[way].at[rows], here, below_sem.at[way])
-        return pltpu.make_async_copy(here, sends[way].at[rows], below_sem.at[way])
-
-    for way in range(2):
-        if passed[way]:
-            below(way, True).start()
-        if slabs[way]:
-            tokens, features = both.shape[0], both.shape[1] // 2
-            moves = column_pieces([part.shape[1] for part in parts], width)
+            return pltpu.make_async_copy(self.seen[way].at[rows], here, sem)
+        return pltpu.make_async_copy(here, self.sends[way].at[rows], sem)
+
+    def by_role(self, on_source, elsewhere):
+        if not self.seen:
+            on_source()
+            return
+        pl.when(self.roles.me == self.roles.source)(on_source)
+        pl.when(self.roles.me != self.roles.source)(elsewhere)
+
+    def start(self):
+        def fetch_all():
+            for j in range(6):
+                self.fetch(j).start()
+
+        def take_all():
+            for j in range(6):
+                self.take(j).start()
+
+        self.by_role(fetch_all, take_all)
+        for way in range(2):
+            if self.passed[way]:
+                self.below(way, True).start()
+
+    def turn_round(self):
+        def convert():
+            for j in range(6):
+                way, rows = self.rows_of(j)
+                self.fetch(j).wait()
+                self.made[way, rows] = self.held[j].astype(BF16)
+                self.store(j).start()
+
+        def relay():
+            for j in range(6):
+                self.take(j).wait()
+                self.store(j).start()
+
+        self.by_role(convert, relay)
+        for way in range(2):
+            if self.passed[way]:
+                self.below(way, True).wait()
+                self.below(way, False).start()
+
+    def add_parcels(self, both, parts):
+        tokens, features = both.shape[0], both.shape[1] // 2
+        width = self.held.shape[2]
+        moves = column_pieces([part.shape[1] for part in parts], width)
+        for way in range(2):
+            if not self.slabs[way]:
+                continue
             for part, begin, piece, to, run in moves:
                 units = parts[part][:, begin : begin + run]
-                made[way, pl.ds(size + piece * tokens, tokens), pl.ds(to, run)] = (
-                    jnp.where(roles.lost, jnp.zeros_like(units), units)
+                rows = pl.ds(self.size + piece * tokens, tokens)
+                self.made[way, rows, pl.ds(to, run)] = jnp.where(
+                    self.roles.lost, jnp.zeros_like(units), units
                 )
-            row = size + (1 + moves[-1][2]) * tokens
-            for far in range(slabs[way], 0, -1):
-                target = roles.neighbour(far if way == 0 else n - far)
+            row = self.size + (1 + moves[-1][2]) * tokens
+            for far in range(self.slabs[way], 0, -1):
+                target = self.roles.neighbour(far if way == 0 else self.n - far)
                 slab = pl.ds(pl.multiple_of(features + target * width, 128), width)
-                made[way, pl.ds(row, tokens)] = both[:, slab]
+                self.made[way, pl.ds(row, tokens)] = both[:, slab]
                 row += tokens
-            below(way, False).start()
-
-    for way in range(2):
-        if passed[way]:
-            below(way, True).wait()
-            below(way, False).start()
-
-    if seen:
-        pl.when(roles.me == roles.source)(convert)
-        pl.when(roles.me != roles.source)(relay)
-    else:
-        convert()
-
-    for way in range(2):
-        if slabs[way] or passed[way]:
-            below(way, False).wait()
-
-
-def pack(failed, n, state, seen, parcel, after, places, chunk, slabs, passed):
-    width = state[0].shape[2]
-    extra = list(passed)
-    if parcel:
-        tokens = parcel[0].shape[0]
-        pieces = -(-sum(part.shape[1] for part in parcel[1:]) // width)
-        extra = [tokens * (pieces + count) if count else 0 for count in slabs]
-    counts = (len(seen), max(len(parcel) - 1, 0), len(after))
+            self.below(way, False).start()
+
+    def finish(self):
+        for j in range(6):
+            self.store(j).wait()
+        for way in range(2):
+            if self.slabs[way] or self.passed[way]:
+                self.below(way, False).wait()
+
+
+def packed_shapes(extra, chunk, width):
+    shapes = [jax.ShapeDtypeStruct((3 * chunk + more, width), BF16) for more in extra]
+    scratch = [
+        pltpu.VMEM((6, chunk, width), F32),
+        pltpu.VMEM((2, 3 * chunk + max(extra), width), BF16),
+        pltpu.SemaphoreType.DMA((6,)),
+        pltpu.SemaphoreType.DMA((6,)),
+        pltpu.SemaphoreType.DMA((2,)),
+    ]
+    return shapes, scratch
+
+
+def pack_body(*refs, n, plan, count_seen, count_after):
+    failed, refs = (refs[0], refs[1:]) if count_seen else (None, refs)
+    state, seen = refs[0:3], refs[3 : 3 + count_seen]
+    rest = refs[3 + count_seen + count_after :]
+    packing = Packing(failed, n, state, seen, rest[:2], rest[2:], plan)
+    packing.start()
+    packing.turn_round()
+    packing.finish()
+
+
+def pack(failed, n, state, seen, after, extra, plan):
+    chunk, width = plan[1], state[0].shape[2]
+    shapes, scratch = packed_shapes(extra, chunk, width)
     return pl.pallas_call(
         functools.partial(
-            pack_body,
-            n=n,
-            places=places,
-            chunk=chunk,
-            slabs=slabs,
-            passed=passed,
-            counts=counts,
+            pack_body, n=n, plan=plan, count_seen=len(seen), count_after=len(after)
         ),
-        in_specs=[SMEM] * bool(seen)
-        + [ANY] * (3 + len(seen))
-        + [WHOLE] * len(parcel)
-        + [ANY] * len(after),
+        in_specs=[SMEM] * bool(seen) + [ANY] * (3 + len(seen) + len(after)),
         out_specs=[ANY, ANY],
-        out_shape=[
-            jax.ShapeDtypeStruct((3 * chunk + more, width), BF16) for more in extra
-        ],
-        scratch_shapes=[
-            pltpu.VMEM((6, chunk, width), F32),
-            pltpu.VMEM((2, 3 * chunk + max(extra), width), BF16),
-            pltpu.SemaphoreType.DMA((6,)),
-            pltpu.SemaphoreType.DMA((6,)),
-            pltpu.SemaphoreType.DMA((2,)),
-        ],
+        out_shape=shapes,
+        scratch_shapes=scratch,
         compiler_params=PARAMS,
         cost_estimate=cost(0, 2 * 3 * chunk * width * 6),
         name="pack",
-    )(*([failed] if seen else []), *state, *seen, *parcel, *after)
+    )(*([failed] if seen else []), *state, *seen, *after)
 
 
 def beside_body(*refs):
@@ -279,15 +293,25 @@
     return lax.dot_general(a, b, (((1,), (1,)), ((), ())), preferred_element_type=F32)
 
 
-def layer_body(both, *refs, resumed, tile, first, count):
-    weights = refs[:3]
-    hidden_ref, sum_ref = refs[-2:]
+def layer_body(failed, both, *refs, n, tile, first, count, plan, counts):
+    count_sums, count_parts, count_seen, count_after = counts
+    weights, refs = refs[:3], refs[3:]
+    sums, refs = refs[:count_sums], refs[count_sums:]
+    parts, refs = refs[:count_parts], refs[count_parts:]
+    state, seen = refs[:3], refs[3 : 3 + count_seen]
+    hidden_ref, sum_ref, *rest = refs[3 + count_seen + count_after :]
+    done = rest[-1]
+    packing = Packing(failed, n, state, seen, rest[:2], rest[2:-1], plan)
     features = weights[0].shape[0]
-    rows = both.shape[0]
     joined = tile % 128 == 0
-    sum_ref[...] = refs[3][...] if resumed else jnp.zeros_like(sum_ref)
-
-    def step(gate_ref, up_ref, down_ref, hidden):
+
+    packing.start()
+    done[0] = 0
+    sum_ref[...] = sums[0][...] if sums else jnp.zeros_like(sum_ref)
+
+    def step(gate_ref, up_ref, down_ref):
+        at = done[0]
+        pl.when(at == min(1, count - 1))(packing.turn_round)
         x, dy = both[:, :features], both[:, features:]
         w_gate, w_up = gate_ref[...], up_ref[...]
         if joined:
@@ -299,13 +323,18 @@
             up = jnp.dot(x, w_up, preferred_element_type=F32)
         d_hidden = by_rows(dy, down_ref[...])
         sig = 1.0 / (1.0 + jnp.exp(-gate))
-        hidden[...] = (gate * sig * up).astype(BF16)
+        hidden = (gate * sig * up).astype(BF16)
+        if count == 1:
+            hidden_ref[...] = hidden
+        else:
+            hidden_ref[:, pl.ds(pl.multiple_of(at * tile, 128), tile)] = hidden
         d_gate = (d_hidden * up * sig * (1.0 + gate * (1.0 - sig))).astype(BF16)
         d_up = (d_hidden * gate * sig).astype(BF16)
         if joined:
             sum_ref[...] += by_rows(jnp.concatenate([d_gate, d_up], axis=1), w_both)
         else:
             sum_ref[...] += by_rows(d_gate, w_gate) + by_rows(d_up, w_up)
+        done[0] = at + 1
 
     deep = pl.Buffered(min(BUFFERS, count + 1))
     across = pl.BlockSpec((features, tile), lambda i: (0, first + i), pipeline_mode=deep)
@@ -317,22 +346,36 @@
             across,
             pl.BlockSpec((tile, features), lambda i: (first + i, 0), pipeline_mode=deep),
         ],
-        out_specs=[pl.BlockSpec((rows, tile), lambda i: (0, i))],
-    )(*weights, hidden_ref)
-
-
-def layer(both, w_gate, w_up, w_down, partial_sum, after, tile, first, count):
-    rows = both.shape[0]
-    features = w_gate.shape[0]
-    resumed = partial_sum is not None
+    )(*weights)
+    if any(packing.slabs):
+        packing.add_parcels(both, [*parts, hidden_ref])
+    packing.finish()
+
+
+def layer(
+    failed, n, both, weights, partial_sum, parts, state, seen, after, extra, plan, share, tile
+):
+    first, count = share
+    rows, features = both.shape[0], weights[0].shape[0]
+    chunk, width = plan[1], state[0].shape[2]
+    sums = [] if partial_sum is None else [partial_sum]
+    shapes, scratch = packed_shapes(extra, chunk, width)
+    counts = (len(sums), len(parts), len(seen), len(after))
     return pl.pallas_call(
-        functools.partial(layer_body, resumed=resumed, tile=tile, first=first, count=count),
-        in_specs=[WHOLE] + [ANY] * 3 + [WHOLE] * resumed + [ANY] * len(after),
-        out_specs=[ANY, WHOLE],
+        functools.partial(
+            layer_body, n=n, tile=tile, first=first, count=count, plan=plan, counts=counts
+        ),
+        in_specs=[SMEM, WHOLE]
+        + [ANY] * 3
+        + [WHOLE] * (len(sums) + len(parts))
+        + [ANY] * (3 + len(seen) + len(after)),
+        out_specs=[WHOLE, WHOLE, ANY, ANY],
         out_shape=[
             jax.ShapeDtypeStruct((rows, count * tile), BF16),
             jax.ShapeDtypeStruct((rows, features), F32),
+            *shapes,
         ],
+        scratch_shapes=[*scratch, pltpu.SMEM((1,), jnp.int32)],
         compiler_params=PARAMS,
         cost_estimate=cost(
             10 * rows * features * count * tile,
@@ -340,7 +383,7 @@
             rows * count * tile,
         ),
         name="layer",
-    )(both, w_gate, w_up, w_down, *([partial_sum] if resumed else []), *after)
+    )(failed, both, *weights, *sums, *parts, *state, *seen, *after)
 
 
 def halve_body(bit, *refs, arrived, final):
@@ -665,74 +708,76 @@
     reach = (n // 2, (n - 1) // 2)
     forward = [(order[p], order[(p + 1) % n]) for p in range(n)]
     backward = [(b, a) for a, b in forward]
-    sends, got = [], []
-    parcel_from = None
-
-    def send(*after, parcel=()):
-        nonlocal parcel_from
+    got = []
+    parcel_from = d_rows = None
+    tile = 128 if units % 128 == 0 else units
+    hidden = []
+
+    def send(*after, share=None):
+        nonlocal d_rows, parcel_from
         step = len(got)
         seen = got[step - LAG] if step >= LAG else ()
         here = min(step, chunks - 1)
-        slabs, passed = (0, 0), (0, 0)
-        if parcel:
+        slabs, passed, extra = (0, 0), (0, 0), (0, 0)
+        if share is not None and sum(share) == units // tile:
             parcel_from, slabs = step, reach
+            pieces = -(-units // width)
+            extra = [both.shape[0] * (pieces + count) if count else 0 for count in slabs]
         elif parcel_from is not None and (step - parcel_from) % LAG == 0:
             hop = (step - parcel_from) // LAG
-            passed = tuple(
-                seen[way].shape[0] - 3 * chunk - both.shape[0]
-                if hop < reach[way]
-                else 0
+            passed = extra = tuple(
+                seen[way].shape[0] - 3 * chunk - both.shape[0] if hop < reach[way] else 0
                 for way in range(2)
             )
-        sends.append(
-            pack(
+        plan = ((here, chunks - 1 - here), chunk, slabs, passed)
+        if share is None:
+            packed = pack(failed, n, state, seen, after, extra, plan)
+        else:
+            parts = hidden if any(slabs) else []
+            part, d_rows, *packed = layer(
                 failed,
                 n,
+                both,
+                (w_gate, w_up, w_down),
+                d_rows,
+                parts,
                 state,
                 seen,
-                parcel,
                 after,
-                (here, chunks - 1 - here),
-                chunk,
-                slabs,
-                passed,
+                extra,
+                plan,
+                share,
+                tile,
+            )
+            hidden.append(part)
+        got.append(
+            (
+                lax.ppermute(packed[0], "replica", forward),
+                lax.ppermute(packed[1], "replica", backward),
             )
         )
-        got.append(
-            (
-                lax.ppermute(sends[-1][0], "replica", forward),
-                lax.ppermute(sends[-1][1], "replica", backward),
-            )
-        )
-        return (sends[-1][0],)
+        return (packed[0],)
 
     sent = send()
     both = beside(tokens[0], d_out[0], sent)
+    sent = send(both)
     exchanges = []
     for axis in ("tensor", "fsdp"):
         size = lax.axis_size(axis)
         exchanges += [(axis, size, 1 << k) for k in range((size - 1).bit_length())]
     if all(size & (size - 1) == 0 for _, size, _ in exchanges):
+        after = sent
         for level, (axis, size, apart) in enumerate(exchanges):
+            other = lax.ppermute(both, axis, [(i, i ^ apart) for i in range(size)])
             last = level == len(exchanges) - 1
-            other = lax.ppermute(both, axis, [(i, i ^ apart) for i in range(size)])
+            both = join(both, other, after, axis, apart, last)
             after = ()
-            if level == 0 or last:
-                after = sent = send(both)
-            both = join(both, other, after, axis, apart, last)
     else:
-        sent = send(both)
         both = lax.all_gather(both[0], ("fsdp", "tensor"), axis=0, tiled=True)
-        sent = send(both)
-
-    tile = 128 if units % 128 == 0 else units
-    hidden, d_rows = [], None
-    pieces = shares(units // tile, 4)
-    for first, count in pieces:
-        part, d_rows = layer(both, w_gate, w_up, w_down, d_rows, sent, tile, first, count)
-        hidden.append(part)
-        last = len(hidden) == len(pieces)
-        sent = send(d_rows, parcel=(both, *hidden) if last else ())
+    sent = send(both)
+
+    for share in shares(units // tile, PIECES):
+        sent = send(*sent, share=share)
     cotangents = ScatteredSum(d_rows, ("fsdp", "tensor"))
 
     news = ()

time: 168 us -> 168 us (level)
  waiting for transfers between devices: 39.2 us -> 36 us
  starting transfers between devices: 36.4 us -> 38.9 us
    ppermute x28, waiting for transfers between devices: 27.1 us -> 23.8 us  [the longest x14 13 us: send(): lax.ppermute(packed[1], 'replica', backward)]
    pallas_call x18 -> x14, Pallas kernels: 62.8 us -> 62.1 us  [the longest x4 37.5 us: layer(): pl.pallas_call(functools.partial(layer_body, n=n, tile=tile, first=first,...]
  transfers between devices with their start and end apart: 34 -> 34, of which waited for: 15 -> 13; matrix products, arithmetic and copies ran while one was open for 0% -> 0% of each run, Pallas kernels for 50% -> 50%
where the time goes in v2:
time: 168 us; the launch traced here: 166 us
  Pallas kernels  85.9 us (51%)
  starting transfers between devices  38.9 us (23%)
  waiting for transfers between devices  36 us (21%)
  local copies, waits for them, and re-layouts  3.54 us (2%)
  between operations  2.05 us (1%)
    pallas_call x4, Pallas kernels, layer(): pl.pallas_call(functools.partial(layer_body, n=n, tile=tile, first=first,...  37.5 us
    pallas_call x10, Pallas kernels, pack(): pl.pallas_call(functools.partial(pack_body, n=n, plan=plan, count_seen=le...  24.6 us
    pallas_call x2, Pallas kernels, update(): pl.pallas_call(functools.partial(update_body, n=n, block=block, first=fir...  18.7 us
    ppermute x14, starting transfers between devices, send(): lax.ppermute(packed[0], 'replica', forward)  16.5 us
    ppermute x14, starting transfers between devices, send(): lax.ppermute(packed[1], 'replica', backward)  14.6 us
    ppermute x14, waiting for transfers between devices, send(): lax.ppermute(packed[1], 'replica', backward)  13 us
    ppermute x14, waiting for transfers between devices, send(): lax.ppermute(packed[0], 'replica', forward)  10.9 us
    ppermute x3, waiting for transfers between devices, per_device(): other = lax.ppermute(both, axis, [(i, i ^ apart) for i in range(size)])  8.85 us
  transfers between devices with their start and end apart: 34, of which 13 were waited for; matrix products, arithmetic and copies ran while one was open for 0% of the time, Pallas kernels for 50%

profile of v2, /device:TPU:0, one launch (start us, length us, event | category | flops | bytes accessed | tf_op | source)
XLA Modules:
  0.0 166.3 jit_solution(8239498618470208119)
XLA Ops:
  0.7 2.5 %pack.10 = (bf16[240,1024]{1,0:T(8,128)(2,1)S(1)}, bf16[240,1024]{1,0:T(8,128)(2,1)S(1)}) custom-call(f32[2,1920,1024]{2,1,0:T(8,128)} %refs_0_.23, f32[2,1920,1024]{2,1,0:T(8,128)} %refs_1_.31, f32[2,1920,1024]{2,1,0:T(8,128)} %refs_2_.31), custom_call_target="tpu_custom_call" | custom-call | bytes 2949120 | tf_op jit(solution)/shard_map/pack/pallas_call | solution.py:230
  3.1 3.0 %collective-permute-start.6 = (bf16[240,1024]{1,0:T(8,128)(2,1)S(1)}, bf16[240,1024]{1,0:T(8,128)(2,1)S(1)}, u32[]{:S(2)}, u32[]{:S(2)}) collective-permute-start(bf16[240,1024]{1,0:T(8,128)(2,1)S(1)} %get-tuple-element.69), channel_id=1, source_target_pairs={{8,0},{24,8},{16,24},{0,16},{9,1},{25,9},{17,25},{1,17},{10,2},{26... | collective-permute-start | bytes 1474568 | tf_op jit(solution)/shard_map/ppermute | solution.py:756
  6.2 2.5 %pack.11 = (bf16[240,1024]{1,0:T(8,128)(2,1)S(1)}, bf16[240,1024]{1,0:T(8,128)(2,1)S(1)}) custom-call(f32[2,1920,1024]{2,1,0:T(8,128)} %refs_0_.23, f32[2,1920,1024]{2,1,0:T(8,128)} %refs_1_.31, f32[2,1920,1024]{2,1,0:T(8,128)} %refs_2_.31, bf16[1,2,8192]{2,1,0:T(2,128)(2,1)S(1)} %beside.1.refs_3_.own), custom_call_target="tpu_custom_call" | custom-call | bytes 2949120 | tf_op jit(solution)/shard_map/pack/pallas_call | solution.py:230
  8.7 2.0 %collective-permute-start.4 = (bf16[240,1024]{1,0:T(8,128)(2,1)S(1)}, bf16[240,1024]{1,0:T(8,128)(2,1)S(1)}, u32[]{:S(2)}, u32[]{:S(2)}) collective-permute-start(bf16[240,1024]{1,0:T(8,128)(2,1)S(1)} %get-tuple-element.68), channel_id=1, source_target_pairs={{8,0},{24,8},{16,24},{0,16},{9,1},{25,9},{17,25},{1,17},{10,2},{26... | collective-permute-start | bytes 1474568 | tf_op jit(solution)/shard_map/ppermute | solution.py:756
  10.8 1.2 collective-permute-done.other
  12.0 2.1 %collective-permute-start.1 = (bf16[2,2,8192]{2,1,0:T(2,128)(2,1)S(1)}, bf16[2,2,8192]{2,1,0:T(2,128)(2,1)S(1)}, u32[]{:S(2)}, u32[]{:S(2)}) collective-permute-start(bf16[2,2,8192]{2,1,0:T(2,128)(2,1)S(1)} %join.3.own), channel_id=1, source_target_pairs={{0,2},{2,0},{4,6},{6,4},{1,3},{3,1},{5,7},{7,5},{8,10},{10,8},{12,... | collective-permute-start | bytes 196616 | tf_op jit(solution)/shard_map/ppermute | solution.py:771
  14.1 2.4 %collective-permute-done.1.other = bf16[2,2,8192]{2,1,0:T(2,128)(2,1)S(1)} collective-permute-done((bf16[2,2,8192]{2,1,0:T(2,128)(2,1)S(1)}, bf16[2,2,8192]{2,1,0:T(2,128)(2,1)S(1)}, u32[]{:S(2)}, u32[]{:S(2)}) %collective-permute-start.1) | collective-permute-done | bytes 65568 | tf_op jit(solution)/shard_map/ppermute | solution.py:771
  16.5 2.9 %collective-permute-start.2 = (bf16[4,2,8192]{2,1,0:T(2,128)(2,1)S(1)}, bf16[4,2,8192]{2,1,0:T(2,128)(2,1)S(1)}, u32[]{:S(2)}, u32[]{:S(2)}) collective-permute-start(bf16[4,2,8192]{2,1,0:T(2,128)(2,1)S(1)} %join.4.own), channel_id=1, source_target_pairs={{0,4},{2,6},{4,0},{6,2},{1,5},{3,7},{5,1},{7,3},{8,12},{10,14},{12... | collective-permute-start | bytes 393224 | tf_op jit(solution)/shard_map/ppermute | solution.py:771
  20.1 5.2 %collective-permute-done.2.other = bf16[4,2,8192]{2,1,0:T(2,128)(2,1)S(1)} collective-permute-done((bf16[4,2,8192]{2,1,0:T(2,128)(2,1)S(1)}, bf16[4,2,8192]{2,1,0:T(2,128)(2,1)S(1)}, u32[]{:S(2)}, u32[]{:S(2)}) %collective-permute-start.2) | collective-permute-done | bytes 131104 | tf_op jit(solution)/shard_map/ppermute | solution.py:771
  25.5 2.7 %pack.12 = (bf16[240,1024]{1,0:T(8,128)(2,1)S(1)}, bf16[240,1024]{1,0:T(8,128)(2,1)S(1)}) custom-call(s32[1]{0:T(128)S(6)} %copy.43.refs_0_.failed, f32[2,1920,1024]{2,1,0:T(8,128)} %refs_0_.23, f32[2,1920,1024]{2,1,0:T(8,128)} %refs_1_.31, f32[2,1920,1024]{2,1,0:T(8,128)} %refs_2_.31, bf16[240,1024]{1,0:T(8,128)(2,1)S(1)} %collective-permute-done.5.refs_4_.refs_0_, ...), custom_call_target="tpu_custom_call" | custom-call | bytes 2949120 | tf_op jit(solution)/shard_map/pack/pallas_call | solution.py:230
  28.3 1.6 collective-permute-start.8
  30.4 8.5 %layer.4 = (bf16[16,384]{1,0:T(8,128)(2,1)S(1)}, f32[16,4096]{1,0:T(8,128)S(1)}, bf16[240,1024]{1,0:T(8,128)(2,1)S(1)}, bf16[240,1024]{1,0:T(8,128)(2,1)S(1)}) custom-call(s32[1]{0:T(128)S(6)} %copy.43.refs_0_.failed, bf16[16,8192]{1,0:T(8,128)(2,1)S(1)} %join.5.refs_6_.both, bf16[4096,1920]{1,0:T(8,128)(2,1)} %refs_0_.21, bf16[4096,1920]{1,0:T(8,128)(2,1)} %refs_1_.22, ...), custom_call_target="tpu_custom_call" | custom-call | flops 251658240 | bytes 9437184 | tf_op jit(solution)/shard_map/layer/pallas_call | solution.py:364
  38.9 1.0 collective-permute-start.10
  39.9 1.1 collective-permute-start.9
  41.0 1.4 collective-permute-done.7.refs_7_.refs_4_
  42.3 9.9 %layer.5 = (bf16[16,512]{1,0:T(8,128)(2,1)S(1)}, f32[16,4096]{1,0:T(8,128)S(1)}, bf16[240,1024]{1,0:T(8,128)(2,1)S(1)}, bf16[240,1024]{1,0:T(8,128)(2,1)S(1)}) custom-call(s32[1]{0:T(128)S(6)} %copy.43.refs_0_.failed, bf16[16,8192]{1,0:T(8,128)(2,1)S(1)} %join.5.refs_6_.both, bf16[4096,1920]{1,0:T(8,128)(2,1)} %refs_0_.21, bf16[4096,1920]{1,0:T(8,128)(2,1)} %refs_1_.22, ...), custom_call_target="tpu_custom_call" | custom-call | flops 335544320 | bytes 12582912 | tf_op jit(solution)/shard_map/layer/pallas_call | solution.py:364
  53.0 1.3 collective-permute-start.11
  54.4 9.9 %layer.6 = (bf16[16,512]{1,0:T(8,128)(2,1)S(1)}, f32[16,4096]{1,0:T(8,128)S(1)}, bf16[240,1024]{1,0:T(8,128)(2,1)S(1)}, bf16[240,1024]{1,0:T(8,128)(2,1)S(1)}) custom-call(s32[1]{0:T(128)S(6)} %copy.43.refs_0_.failed, bf16[16,8192]{1,0:T(8,128)(2,1)S(1)} %join.5.refs_6_.both, bf16[4096,1920]{1,0:T(8,128)(2,1)} %refs_0_.21, bf16[4096,1920]{1,0:T(8,128)(2,1)} %refs_1_.22, ...), custom_call_target="tpu_custom_call" | custom-call | flops 335544320 | bytes 12582912 | tf_op jit(solution)/shard_map/layer/pallas_call | solution.py:364
  64.9 1.6 collective-permute-start.13
  66.5 9.1 %layer.7 = (bf16[16,512]{1,0:T(8,128)(2,1)S(1)}, f32[16,4096]{1,0:T(8,128)S(1)}, bf16[304,1024]{1,0:T(8,128)(2,1)}, bf16[288,1024]{1,0:T(8,128)(2,1)}) custom-call(s32[1]{0:T(128)S(6)} %copy.43.refs_0_.failed, bf16[16,8192]{1,0:T(8,128)(2,1)S(1)} %join.5.refs_6_.both, bf16[4096,1920]{1,0:T(8,128)(2,1)} %refs_0_.21, bf16[4096,1920]{1,0:T(8,128)(2,1)} %refs_1_.22, ...), custom_call_target="tpu_custom_call" | custom-call | flops 335544320 | bytes 12582912 | tf_op jit(solution)/shard_map/layer/pallas_call | solution.py:364
  76.0 1.7 %collective-permute-start.17 = (bf16[288,1024]{1,0:T(8,128)(2,1)}, bf16[288,1024]{1,0:T(8,128)(2,1)S(1)}, u32[]{:S(2)}, u32[]{:S(2)}) collective-permute-start(bf16[288,1024]{1,0:T(8,128)(2,1)} %get-tuple-element.89), channel_id=1, source_target_pairs={{8,0},{24,8},{16,24},{0,16},{9,1},{25,9},{17,25},{1,17},{10,2},{26... | collective-permute-start | bytes 1769480 | tf_op jit(solution)/shard_map/ppermute | solution.py:756
  77.7 2.3 %pack.13 = (bf16[240,1024]{1,0:T(8,128)(2,1)}, bf16[240,1024]{1,0:T(8,128)(2,1)}) custom-call(s32[1]{0:T(128)S(6)} %copy.43.refs_0_.failed, f32[2,1920,1024]{2,1,0:T(8,128)} %refs_0_.23, f32[2,1920,1024]{2,1,0:T(8,128)} %refs_1_.31, f32[2,1920,1024]{2,1,0:T(8,128)} %refs_2_.31, bf16[240,1024]{1,0:T(8,128)(2,1)S(1)} %collective-permute-done.13.refs_4_.refs_0_, ...), custom_call_target="tpu_custom_call" | custom-call | bytes 2949120 | tf_op jit(solution)/shard_map/pack/pallas_call | solution.py:230
  80.5 1.7 %collective-permute-start.19 = (bf16[240,1024]{1,0:T(8,128)(2,1)}, bf16[240,1024]{1,0:T(8,128)(2,1)}, u32[]{:S(2)}, u32[]{:S(2)}) collective-permute-start(bf16[240,1024]{1,0:T(8,128)(2,1)} %get-tuple-element.85.refs_1_), channel_id=1, source_target_pairs={{0,8},{8,24},{24,16},{16,0},{1,9},{9,25},{25,17},{17,1},{2,10},{10... | collective-permute-start | bytes 1474568 | tf_op jit(solution)/shard_map/ppermute | solution.py:755
  82.2 0.9 copy-done.27
  83.8 1.4 collective-permute-start.15
  85.2 7.2 %collective-permute-done.17.refs_5_.refs_6_.refs_3_ = bf16[288,1024]{1,0:T(8,128)(2,1)S(1)} collective-permute-done((bf16[288,1024]{1,0:T(8,128)(2,1)}, bf16[288,1024]{1,0:T(8,128)(2,1)S(1)}, u32[]{:S(2)}, u32[]{:S(2)}) %collective-permute-start.17) | collective-permute-done | bytes 589856 | tf_op jit(solution)/shard_map/ppermute | solution.py:756
  92.9 2.5 %pack.14 = (bf16[288,1024]{1,0:T(8,128)(2,1)}, bf16[240,1024]{1,0:T(8,128)(2,1)}) custom-call(s32[1]{0:T(128)S(6)} %copy.43.refs_0_.failed, f32[2,1920,1024]{2,1,0:T(8,128)} %refs_0_.23, f32[2,1920,1024]{2,1,0:T(8,128)} %refs_1_.31, f32[2,1920,1024]{2,1,0:T(8,128)} %refs_2_.31, bf16[304,1024]{1,0:T(8,128)(2,1)S(1)} %collective-permute-done.16.refs_4_.refs_2_, ...), custom_call_target="tpu_custom_call" | custom-call | bytes 2949120 | tf_op jit(solution)/shard_map/pack/pallas_call | solution.py:230
  95.3 1.0 collective-permute-start.22
  96.4 1.0 collective-permute-start.23
  98.3 1.6 halve.5
  99.9 3.2 %collective-permute-done.20.refs_5_ = bf16[240,1024]{1,0:T(8,128)(2,1)} collective-permute-done((bf16[240,1024]{1,0:T(8,128)(2,1)}, bf16[240,1024]{1,0:T(8,128)(2,1)}, u32[]{:S(2)}, u32[]{:S(2)}) %collective-permute-start.20) | collective-permute-done | bytes 491552 | tf_op jit(solution)/shard_map/ppermute | solution.py:756
  103.5 2.1 %pack.15 = (bf16[240,1024]{1,0:T(8,128)(2,1)}, bf16[240,1024]{1,0:T(8,128)(2,1)}) custom-call(s32[1]{0:T(128)S(6)} %copy.43.refs_0_.failed, f32[2,1920,1024]{2,1,0:T(8,128)} %refs_0_.23, f32[2,1920,1024]{2,1,0:T(8,128)} %refs_1_.31, f32[2,1920,1024]{2,1,0:T(8,128)} %refs_2_.31, bf16[240,1024]{1,0:T(8,128)(2,1)} %collective-permute-done.19.refs_4_, ...), custom_call_target="tpu_custom_call" | custom-call | bytes 2949120 | tf_op jit(solution)/shard_map/pack/pallas_call | solution.py:230
  105.6 1.6 collective-permute-start.25
  107.7 1.3 collective-permute-start.18
  109.0 3.3 %collective-permute-done.18.refs_1_ = f32[4,4096]{1,0:T(4,128)} collective-permute-done((f32[4,4096]{1,0:T(4,128)}, f32[4,4096]{1,0:T(4,128)}, u32[]{:S(2)}, u32[]{:S(2)}) %collective-permute-start.18) | collective-permute-done | bytes 65568 | tf_op jit(solution)/shard_map/ppermute | solution.py:444
  114.1 2.0 %collective-permute-done.22.refs_4_.refs_5_.refs_6_ = bf16[288,1024]{1,0:T(8,128)(2,1)S(1)} collective-permute-done((bf16[288,1024]{1,0:T(8,128)(2,1)}, bf16[288,1024]{1,0:T(8,128)(2,1)S(1)}, u32[]{:S(2)}, u32[]{:S(2)}) %collective-permute-start.22) | collective-permute-done | bytes 589856 | tf_op jit(solution)/shard_map/ppermute | solution.py:755
  116.1 2.3 %pack.16 = (bf16[240,1024]{1,0:T(8,128)(2,1)S(1)}, bf16[240,1024]{1,0:T(8,128)(2,1)S(1)}) custom-call(s32[1]{0:T(128)S(6)} %copy.43.refs_0_.failed, f32[2,1920,1024]{2,1,0:T(8,128)} %refs_0_.23, f32[2,1920,1024]{2,1,0:T(8,128)} %refs_1_.31, f32[2,1920,1024]{2,1,0:T(8,128)} %refs_2_.31, bf16[288,1024]{1,0:T(8,128)(2,1)S(1)} %collective-permute-done.22.refs_4_.refs_5_.refs_6_, ...), custom_call_target="tpu_custom_call" | custom-call | bytes 2949120 | tf_op jit(solution)/shard_map/pack/pallas_call | solution.py:230
  119.0 1.4 collective-permute-start.30
  121.2 4.7 %update.2 = (f32[1920,1024]{1,0:T(8,128)}, f32[1920,1024]{1,0:T(8,128)}, f32[1920,1024]{1,0:T(8,128)}) custom-call(s32[1]{0:T(128)S(6)} %copy.43.refs_0_.failed, bf16[1920,64]{1,0:T(8,128)(2,1)S(1)} %get-tuple-element.100.hid_ref.refs_3_, bf16[64,1024]{1,0:T(8,128)(2,1)S(1)} %get-tuple-element.101.out_ref, f32[2,1920,1024]{2,1,0:T(8,128)} %refs_0_.23, ...), custom_call_target="tpu_custom_call" | custom-call | flops 50331648 | bytes 9437184 | tf_op jit(solution)/shard_map/update/pallas_call | solution.py:565
  127.4 2.3 %pack.17 = (bf16[240,1024]{1,0:T(8,128)(2,1)S(1)}, bf16[240,1024]{1,0:T(8,128)(2,1)S(1)}) custom-call(s32[1]{0:T(128)S(6)} %copy.43.refs_0_.failed, f32[2,1920,1024]{2,1,0:T(8,128)} %refs_0_.23, f32[2,1920,1024]{2,1,0:T(8,128)} %refs_1_.31, f32[2,1920,1024]{2,1,0:T(8,128)} %refs_2_.31, bf16[240,1024]{1,0:T(8,128)(2,1)} %collective-permute-done.24.refs_4_.refs_8_, ...), custom_call_target="tpu_custom_call" | custom-call | bytes 2949120 | tf_op jit(solution)/shard_map/pack/pallas_call | solution.py:230
  129.7 3.1 %collective-permute-start.26 = (bf16[240,1024]{1,0:T(8,128)(2,1)S(1)}, bf16[240,1024]{1,0:T(8,128)(2,1)S(1)}, u32[]{:S(2)}, u32[]{:S(2)}) collective-permute-start(bf16[240,1024]{1,0:T(8,128)(2,1)S(1)} %get-tuple-element.107), channel_id=1, source_target_pairs={{0,8},{8,24},{24,16},{16,0},{1,9},{9,25},{25,17},{17,1},{2,10},{10... | collective-permute-start | bytes 1474568 | tf_op jit(solution)/shard_map/ppermute | solution.py:755
  133.2 2.8 %pack.19 = (bf16[240,1024]{1,0:T(8,128)(2,1)S(1)}, bf16[240,1024]{1,0:T(8,128)(2,1)S(1)}) custom-call(s32[1]{0:T(128)S(6)} %copy.43.refs_0_.failed, f32[2,1920,1024]{2,1,0:T(8,128)} %refs_0_.23, f32[2,1920,1024]{2,1,0:T(8,128)} %refs_1_.31, f32[2,1920,1024]{2,1,0:T(8,128)} %refs_2_.31, bf16[240,1024]{1,0:T(8,128)(2,1)S(1)} %collective-permute-done.30.refs_4_.refs_10_, ...), custom_call_target="tpu_custom_call" | custom-call | bytes 2949120 | tf_op jit(solution)/shard_map/pack/pallas_call | solution.py:230
  136.0 1.8 %collective-permute-start.32 = (bf16[240,1024]{1,0:T(8,128)(2,1)S(1)}, bf16[240,1024]{1,0:T(8,128)(2,1)S(1)}, u32[]{:S(2)}, u32[]{:S(2)}) collective-permute-start(bf16[240,1024]{1,0:T(8,128)(2,1)S(1)} %get-tuple-element.112), channel_id=1, source_target_pairs={{0,8},{8,24},{24,16},{16,0},{1,9},{9,25},{25,17},{17,1},{2,10},{10... | collective-permute-start | bytes 1474568 | tf_op jit(solution)/shard_map/ppermute | solution.py:755
  138.1 6.4 %collective-permute-done.26.refs_4_.refs_12_ = bf16[240,1024]{1,0:T(8,128)(2,1)S(1)} collective-permute-done((bf16[240,1024]{1,0:T(8,128)(2,1)S(1)}, bf16[240,1024]{1,0:T(8,128)(2,1)S(1)}, u32[]{:S(2)}, u32[]{:S(2)}) %collective-permute-start.26) | collective-permute-done | bytes 491552 | tf_op jit(solution)/shard_map/ppermute | solution.py:755
  144.5 2.5 %collective-permute-done.27.refs_5_.refs_13_ = bf16[240,1024]{1,0:T(8,128)(2,1)S(1)} collective-permute-done((bf16[240,1024]{1,0:T(8,128)(2,1)S(1)}, bf16[240,1024]{1,0:T(8,128)(2,1)S(1)}, u32[]{:S(2)}, u32[]{:S(2)}) %collective-permute-start.27) | collective-permute-done | bytes 491552 | tf_op jit(solution)/shard_map/ppermute | solution.py:756
  147.0 2.7 %pack.18 = (bf16[240,1024]{1,0:T(8,128)(2,1)S(1)}, bf16[240,1024]{1,0:T(8,128)(2,1)S(1)}) custom-call(s32[1]{0:T(128)S(6)} %copy.43.refs_0_.failed, f32[2,1920,1024]{2,1,0:T(8,128)} %refs_0_.23, f32[2,1920,1024]{2,1,0:T(8,128)} %refs_1_.31, f32[2,1920,1024]{2,1,0:T(8,128)} %refs_2_.31, bf16[240,1024]{1,0:T(8,128)(2,1)S(1)} %collective-permute-done.26.refs_4_.refs_12_, ...), custom_call_target="tpu_custom_call" | custom-call | bytes 2949120 | tf_op jit(solution)/shard_map/pack/pallas_call | solution.py:230
  149.8 2.0 %collective-permute-start.28 = (bf16[240,1024]{1,0:T(8,128)(2,1)S(1)}, bf16[240,1024]{1,0:T(8,128)(2,1)S(1)}, u32[]{:S(2)}, u32[]{:S(2)}) collective-permute-start(bf16[240,1024]{1,0:T(8,128)(2,1)S(1)} %get-tuple-element.109.refs_6_), channel_id=1, source_target_pairs={{0,8},{8,24},{24,16},{16,0},{1,9},{9,25},{25,17},{17,1},{2,10},{10... | collective-permute-start | bytes 1474568 | tf_op jit(solution)/shard_map/ppermute | solution.py:755
  151.8 14.0 %update.3 = (f32[1920,1024]{1,0:T(8,128)}, f32[1920,1024]{1,0:T(8,128)}, f32[1920,1024]{1,0:T(8,128)}) custom-call(s32[1]{0:T(128)S(6)} %copy.43.refs_0_.failed, bf16[1920,64]{1,0:T(8,128)(2,1)S(1)} %get-tuple-element.100.hid_ref.refs_3_, ...), custom_call_target="tpu_custom_call", output_to_operand_aliasing={{0}: (6, {}), {1}: (7, {}), {2}: (8, {})} | custom-call | flops 201326592 | bytes 37748736 | tf_op jit(solution)/shard_map/update/pallas_call | solution.py:565
  (123 shorter events, 11.5 us)
Async XLA Ops:
  0.6 5.6 %copy-start.36 = (bf16[1,2,4096]{2,1,0:T(2,128)(2,1)S(1)}, bf16[1,2,4096]{2,1,0:T(2,128)(2,1)}, u32[]{:S(2)}) copy-start(bf16[1,2,4096]{2,1,0:T(2,128)(2,1)} %param.10) | copy-start | bytes 49156
  3.1 22.4 %collective-permute-start.6 = (bf16[240,1024]{1,0:T(8,128)(2,1)S(1)}, bf16[240,1024]{1,0:T(8,128)(2,1)S(1)}, u32[]{:S(2)}, u32[]{:S(2)}) collective-permute-start(bf16[240,1024]{1,0:T(8,128)(2,1)S(1)} %get-tuple-element.69), channel_id=1, source_target_pairs={{8,0},{24,8},{16,24},{0,16},{9,1},{25,9},{17,25},{1,17},{10,2},{26... | collective-permute-start | bytes 1474568 | tf_op jit(solution)/shard_map/ppermute | solution.py:756
  6.2 19.4 %collective-permute-start.5 = (bf16[240,1024]{1,0:T(8,128)(2,1)S(1)}, bf16[240,1024]{1,0:T(8,128)(2,1)S(1)}, u32[]{:S(2)}, u32[]{:S(2)}) collective-permute-start(bf16[240,1024]{1,0:T(8,128)(2,1)S(1)} %get-tuple-element.66.refs_2_), channel_id=1, source_target_pairs={{0,8},{8,24},{24,16},{16,0},{1,9},{9,25},{25,17},{17,1},{2,10},{10... | collective-permute-start | bytes 1474568 | tf_op jit(solution)/shard_map/ppermute | solution.py:755
  8.7 21.7 %collective-permute-start.4 = (bf16[240,1024]{1,0:T(8,128)(2,1)S(1)}, bf16[240,1024]{1,0:T(8,128)(2,1)S(1)}, u32[]{:S(2)}, u32[]{:S(2)}) collective-permute-start(bf16[240,1024]{1,0:T(8,128)(2,1)S(1)} %get-tuple-element.68), channel_id=1, source_target_pairs={{8,0},{24,8},{16,24},{0,16},{9,1},{25,9},{17,25},{1,17},{10,2},{26... | collective-permute-start | bytes 1474568 | tf_op jit(solution)/shard_map/ppermute | solution.py:756
  10.7 19.6 %collective-permute-start.3 = (bf16[240,1024]{1,0:T(8,128)(2,1)S(1)}, bf16[240,1024]{1,0:T(8,128)(2,1)S(1)}, u32[]{:S(2)}, u32[]{:S(2)}) collective-permute-start(bf16[240,1024]{1,0:T(8,128)(2,1)S(1)} %get-tuple-element.67.refs_0_), channel_id=1, source_target_pairs={{0,8},{8,24},{24,16},{16,0},{1,9},{9,25},{25,17},{17,1},{2,10},{10... | collective-permute-start | bytes 1474568 | tf_op jit(solution)/shard_map/ppermute | solution.py:755
  10.8 1.2 collective-permute-start
  12.0 4.5 %collective-permute-start.1 = (bf16[2,2,8192]{2,1,0:T(2,128)(2,1)S(1)}, bf16[2,2,8192]{2,1,0:T(2,128)(2,1)S(1)}, u32[]{:S(2)}, u32[]{:S(2)}) collective-permute-start(bf16[2,2,8192]{2,1,0:T(2,128)(2,1)S(1)} %join.3.own), channel_id=1, source_target_pairs={{0,2},{2,0},{4,6},{6,4},{1,3},{3,1},{5,7},{7,5},{8,10},{10,8},{12,... | collective-permute-start | bytes 196616 | tf_op jit(solution)/shard_map/ppermute | solution.py:771
  16.5 8.8 %collective-permute-start.2 = (bf16[4,2,8192]{2,1,0:T(2,128)(2,1)S(1)}, bf16[4,2,8192]{2,1,0:T(2,128)(2,1)S(1)}, u32[]{:S(2)}, u32[]{:S(2)}) collective-permute-start(bf16[4,2,8192]{2,1,0:T(2,128)(2,1)S(1)} %join.4.own), channel_id=1, source_target_pairs={{0,4},{2,6},{4,0},{6,2},{1,5},{3,7},{5,1},{7,3},{8,12},{10,14},{12... | collective-permute-start | bytes 393224 | tf_op jit(solution)/shard_map/ppermute | solution.py:771
  28.3 12.7 %collective-permute-start.8 = (bf16[240,1024]{1,0:T(8,128)(2,1)S(1)}, bf16[240,1024]{1,0:T(8,128)(2,1)S(1)}, u32[]{:S(2)}, u32[]{:S(2)}) collective-permute-start(bf16[240,1024]{1,0:T(8,128)(2,1)S(1)} %get-tuple-element.72), channel_id=1, source_target_pairs={{8,0},{24,8},{16,24},{0,16},{9,1},{25,9},{17,25},{1,17},{10,2},{26... | collective-permute-start | bytes 1474568 | tf_op jit(solution)/shard_map/ppermute | solution.py:756
  29.8 12.5 %collective-permute-start.7 = (bf16[240,1024]{1,0:T(8,128)(2,1)S(1)}, bf16[240,1024]{1,0:T(8,128)(2,1)S(1)}, u32[]{:S(2)}, u32[]{:S(2)}) collective-permute-start(bf16[240,1024]{1,0:T(8,128)(2,1)S(1)} %get-tuple-element.70.refs_8_), channel_id=1, source_target_pairs={{0,8},{8,24},{24,16},{16,0},{1,9},{9,25},{25,17},{17,1},{2,10},{10... | collective-permute-start | bytes 1474568 | tf_op jit(solution)/shard_map/ppermute | solution.py:755
  38.9 27.6 %copy-start.31 = (bf16[16,384]{1,0:T(8,128)(2,1)}, bf16[16,384]{1,0:T(8,128)(2,1)S(1)}, u32[]{:S(2)}) copy-start(bf16[16,384]{1,0:T(8,128)(2,1)S(1)} %get-tuple-element.78.refs_4_.refs_0_) | copy-start | bytes 36868
  38.9 15.5 %collective-permute-start.10 = (bf16[240,1024]{1,0:T(8,128)(2,1)S(1)}, bf16[240,1024]{1,0:T(8,128)(2,1)S(1)}, u32[]{:S(2)}, u32[]{:S(2)}) collective-permute-start(bf16[240,1024]{1,0:T(8,128)(2,1)S(1)} %get-tuple-element.75), channel_id=1, source_target_pairs={{8,0},{24,8},{16,24},{0,16},{9,1},{25,9},{17,25},{1,17},{10,2},{26... | collective-permute-start | bytes 1474568 | tf_op jit(solution)/shard_map/ppermute | solution.py:756
  39.9 14.5 %collective-permute-start.9 = (bf16[240,1024]{1,0:T(8,128)(2,1)S(1)}, bf16[240,1024]{1,0:T(8,128)(2,1)S(1)}, u32[]{:S(2)}, u32[]{:S(2)}) collective-permute-start(bf16[240,1024]{1,0:T(8,128)(2,1)S(1)} %get-tuple-element.73.refs_9_), channel_id=1, source_target_pairs={{0,8},{8,24},{24,16},{16,0},{1,9},{9,25},{25,17},{17,1},{2,10},{10... | collective-permute-start | bytes 1474568 | tf_op jit(solution)/shard_map/ppermute | solution.py:755
  41.0 11.3 %copy-start.9 = (bf16[240,1024]{1,0:T(8,128)(2,1)}, bf16[240,1024]{1,0:T(8,128)(2,1)S(1)}, u32[]{:S(2)}) copy-start(bf16[240,1024]{1,0:T(8,128)(2,1)S(1)} %collective-permute-done.8.refs_8_.refs_5_) | copy-start | bytes 1474564
  42.3 9.9 %copy-start.11 = (bf16[240,1024]{1,0:T(8,128)(2,1)}, bf16[240,1024]{1,0:T(8,128)(2,1)S(1)}, u32[]{:S(2)}) copy-start(bf16[240,1024]{1,0:T(8,128)(2,1)S(1)} %collective-permute-done.7.refs_7_.refs_4_) | copy-start | bytes 1474564
  52.3 14.2 %collective-permute-start.12 = (bf16[240,1024]{1,0:T(8,128)(2,1)S(1)}, bf16[240,1024]{1,0:T(8,128)(2,1)S(1)}, u32[]{:S(2)}, u32[]{:S(2)}) collective-permute-start(bf16[240,1024]{1,0:T(8,128)(2,1)S(1)} %get-tuple-element.81), channel_id=1, source_target_pairs={{8,0},{24,8},{16,24},{0,16},{9,1},{25,9},{17,25},{1,17},{10,2},{26... | collective-permute-start | bytes 1474568 | tf_op jit(solution)/shard_map/ppermute | solution.py:756
  53.0 13.4 %collective-permute-start.11 = (bf16[240,1024]{1,0:T(8,128)(2,1)S(1)}, bf16[240,1024]{1,0:T(8,128)(2,1)S(1)}, u32[]{:S(2)}, u32[]{:S(2)}) collective-permute-start(bf16[240,1024]{1,0:T(8,128)(2,1)S(1)} %get-tuple-element.76.refs_9_), channel_id=1, source_target_pairs={{0,8},{8,24},{24,16},{16,0},{1,9},{9,25},{25,17},{17,1},{2,10},{10... | collective-permute-start | bytes 1474568 | tf_op jit(solution)/shard_map/ppermute | solution.py:755
  54.3 10.0 %copy-start.13 = (bf16[240,1024]{1,0:T(8,128)(2,1)}, bf16[240,1024]{1,0:T(8,128)(2,1)S(1)}, u32[]{:S(2)}) copy-start(bf16[240,1024]{1,0:T(8,128)(2,1)S(1)} %collective-permute-done.10.refs_8_.refs_7_) | copy-start | bytes 1474564
  54.4 10.0 %copy-start.14 = (bf16[240,1024]{1,0:T(8,128)(2,1)}, bf16[240,1024]{1,0:T(8,128)(2,1)S(1)}, u32[]{:S(2)}) copy-start(bf16[240,1024]{1,0:T(8,128)(2,1)S(1)} %collective-permute-done.9.refs_7_.refs_6_) | copy-start | bytes 1474564
  64.3 11.2 %copy-start.28 = (bf16[16,512]{1,0:T(8,128)(2,1)}, bf16[16,512]{1,0:T(8,128)(2,1)S(1)}, u32[]{:S(2)}) copy-start(bf16[16,512]{1,0:T(8,128)(2,1)S(1)} %get-tuple-element.80.refs_6_.refs_2_) | copy-start | bytes 49156
  64.4 13.4 %collective-permute-start.14 = (bf16[240,1024]{1,0:T(8,128)(2,1)S(1)}, bf16[240,1024]{1,0:T(8,128)(2,1)S(1)}, u32[]{:S(2)}, u32[]{:S(2)}) collective-permute-start(bf16[240,1024]{1,0:T(8,128)(2,1)S(1)} %get-tuple-element.84), channel_id=1, source_target_pairs={{8,0},{24,8},{16,24},{0,16},{9,1},{25,9},{17,25},{1,17},{10,2},{26... | collective-permute-start | bytes 1474568 | tf_op jit(solution)/shard_map/ppermute | solution.py:756
  64.9 12.9 %collective-permute-start.13 = (bf16[240,1024]{1,0:T(8,128)(2,1)S(1)}, bf16[240,1024]{1,0:T(8,128)(2,1)S(1)}, u32[]{:S(2)}, u32[]{:S(2)}) collective-permute-start(bf16[240,1024]{1,0:T(8,128)(2,1)S(1)} %get-tuple-element.82.refs_12_), channel_id=1, source_target_pairs={{0,8},{8,24},{24,16},{16,0},{1,9},{9,25},{25,17},{17,1},{2,10},{10... | collective-permute-start | bytes 1474568 | tf_op jit(solution)/shard_map/ppermute | solution.py:755
  66.4 9.2 %copy-start.16 = (bf16[240,1024]{1,0:T(8,128)(2,1)}, bf16[240,1024]{1,0:T(8,128)(2,1)S(1)}, u32[]{:S(2)}) copy-start(bf16[240,1024]{1,0:T(8,128)(2,1)S(1)} %collective-permute-done.12.refs_11_.refs_9_) | copy-start | bytes 1474564
  66.4 9.2 %copy-start.17 = (bf16[240,1024]{1,0:T(8,128)(2,1)}, bf16[240,1024]{1,0:T(8,128)(2,1)S(1)}, u32[]{:S(2)}) copy-start(bf16[240,1024]{1,0:T(8,128)(2,1)S(1)} %collective-permute-done.11.refs_10_.refs_8_) | copy-start | bytes 1474564
  75.6 17.2 %collective-permute-start.16 = (bf16[304,1024]{1,0:T(8,128)(2,1)}, bf16[304,1024]{1,0:T(8,128)(2,1)S(1)}, u32[]{:S(2)}, u32[]{:S(2)}) collective-permute-start(bf16[304,1024]{1,0:T(8,128)(2,1)} %get-tuple-element.88), channel_id=1, source_target_pairs={{0,8},{8,24},{24,16},{16,0},{1,9},{9,25},{25,17},{17,1},{2,10},{10... | collective-permute-start | bytes 1867784 | tf_op jit(solution)/shard_map/ppermute | solution.py:755
  76.0 16.5 %collective-permute-start.17 = (bf16[288,1024]{1,0:T(8,128)(2,1)}, bf16[288,1024]{1,0:T(8,128)(2,1)S(1)}, u32[]{:S(2)}, u32[]{:S(2)}) collective-permute-start(bf16[288,1024]{1,0:T(8,128)(2,1)} %get-tuple-element.89), channel_id=1, source_target_pairs={{8,0},{24,8},{16,24},{0,16},{9,1},{25,9},{17,25},{1,17},{10,2},{26... | collective-permute-start | bytes 1769480 | tf_op jit(solution)/shard_map/ppermute | solution.py:756
  80.1 23.0 %collective-permute-start.20 = (bf16[240,1024]{1,0:T(8,128)(2,1)}, bf16[240,1024]{1,0:T(8,128)(2,1)}, u32[]{:S(2)}, u32[]{:S(2)}) collective-permute-start(bf16[240,1024]{1,0:T(8,128)(2,1)} %get-tuple-element.93), channel_id=1, source_target_pairs={{8,0},{24,8},{16,24},{0,16},{9,1},{25,9},{17,25},{1,17},{10,2},{26... | collective-permute-start | bytes 1474568 | tf_op jit(solution)/shard_map/ppermute | solution.py:756
  80.5 23.0 %collective-permute-start.19 = (bf16[240,1024]{1,0:T(8,128)(2,1)}, bf16[240,1024]{1,0:T(8,128)(2,1)}, u32[]{:S(2)}, u32[]{:S(2)}) collective-permute-start(bf16[240,1024]{1,0:T(8,128)(2,1)} %get-tuple-element.85.refs_1_), channel_id=1, source_target_pairs={{0,8},{8,24},{24,16},{16,0},{1,9},{9,25},{25,17},{17,1},{2,10},{10... | collective-permute-start | bytes 1474568 | tf_op jit(solution)/shard_map/ppermute | solution.py:755
  83.8 11.5 %copy-start.22 = (f32[8,4096]{1,0:T(8,128)}, f32[8,4096]{1,0:T(8,128)S(1)}, u32[]{:S(2)}) copy-start(f32[8,4096]{1,0:T(8,128)S(1)} %get-tuple-element.86.refs_6_.refs_0_) | copy-start | bytes 393220
  83.8 13.6 %collective-permute-start.15 = (f32[8,4096]{1,0:T(8,128)}, f32[8,4096]{1,0:T(8,128)}, u32[]{:S(2)}, u32[]{:S(2)}) collective-permute-start(f32[8,4096]{1,0:T(8,128)} %get-tuple-element.87), channel_id=1, source_target_pairs={{0,4},{2,6},{4,0},{6,2},{1,5},{3,7},{5,1},{7,3},{8,12},{10,14},{12... | collective-permute-start | bytes 393224 | tf_op jit(solution)/shard_map/ppermute | solution.py:444
  92.5 28.0 %copy-start.1 = (bf16[288,1024]{1,0:T(8,128)(2,1)}, bf16[288,1024]{1,0:T(8,128)(2,1)S(1)}, u32[]{:S(2)}) copy-start(bf16[288,1024]{1,0:T(8,128)(2,1)S(1)} %collective-permute-done.17.refs_5_.refs_6_.refs_3_) | copy-start | bytes 1769476
  92.9 27.6 %copy-start = (bf16[304,1024]{1,0:T(8,128)(2,1)}, bf16[304,1024]{1,0:T(8,128)(2,1)S(1)}, u32[]{:S(2)}) copy-start(bf16[304,1024]{1,0:T(8,128)(2,1)S(1)} %collective-permute-done.16.refs_4_.refs_2_) | copy-start | bytes 1867780
  95.3 20.7 %collective-permute-start.22 = (bf16[288,1024]{1,0:T(8,128)(2,1)}, bf16[288,1024]{1,0:T(8,128)(2,1)S(1)}, u32[]{:S(2)}, u32[]{:S(2)}) collective-permute-start(bf16[288,1024]{1,0:T(8,128)(2,1)} %get-tuple-element.90.refs_2_), channel_id=1, source_target_pairs={{0,8},{8,24},{24,16},{16,0},{1,9},{9,25},{25,17},{17,1},{2,10},{10... | collective-permute-start | bytes 1769480 | tf_op jit(solution)/shard_map/ppermute | solution.py:755
  96.4 17.7 %collective-permute-start.23 = (bf16[240,1024]{1,0:T(8,128)(2,1)}, bf16[240,1024]{1,0:T(8,128)(2,1)}, u32[]{:S(2)}, u32[]{:S(2)}) collective-permute-start(bf16[240,1024]{1,0:T(8,128)(2,1)} %get-tuple-element.97), channel_id=1, source_target_pairs={{8,0},{24,8},{16,24},{0,16},{9,1},{25,9},{17,25},{1,17},{10,2},{26... | collective-permute-start | bytes 1474568 | tf_op jit(solution)/shard_map/ppermute | solution.py:756
  99.9 5.7 %copy-start.24 = (f32[4,4096]{1,0:T(4,128)}, f32[4,4096]{1,0:T(4,128)S(1)}, u32[]{:S(2)}) copy-start(f32[4,4096]{1,0:T(4,128)S(1)} %get-tuple-element.91.refs_6_.refs_0_) | copy-start | bytes 196612
  105.6 21.1 %collective-permute-start.25 = (bf16[240,1024]{1,0:T(8,128)(2,1)}, bf16[240,1024]{1,0:T(8,128)(2,1)}, u32[]{:S(2)}, u32[]{:S(2)}) collective-permute-start(bf16[240,1024]{1,0:T(8,128)(2,1)} %get-tuple-element.102), channel_id=1, source_target_pairs={{8,0},{24,8},{16,24},{0,16},{9,1},{25,9},{17,25},{1,17},{10,2},{26... | collective-permute-start | bytes 1474568 | tf_op jit(solution)/shard_map/ppermute | solution.py:756
  107.2 19.5 %collective-permute-start.24 = (bf16[240,1024]{1,0:T(8,128)(2,1)}, bf16[240,1024]{1,0:T(8,128)(2,1)}, u32[]{:S(2)}, u32[]{:S(2)}) collective-permute-start(bf16[240,1024]{1,0:T(8,128)(2,1)} %get-tuple-element.94.refs_2_), channel_id=1, source_target_pairs={{0,8},{8,24},{24,16},{16,0},{1,9},{9,25},{25,17},{17,1},{2,10},{10... | collective-permute-start | bytes 1474568 | tf_op jit(solution)/shard_map/ppermute | solution.py:755
  107.7 4.6 %collective-permute-start.18 = (f32[4,4096]{1,0:T(4,128)}, f32[4,4096]{1,0:T(4,128)}, u32[]{:S(2)}, u32[]{:S(2)}) collective-permute-start(f32[4,4096]{1,0:T(4,128)} %get-tuple-element.92), channel_id=1, source_target_pairs={{0,2},{2,0},{4,6},{6,4},{1,3},{3,1},{5,7},{7,5},{8,10},{10,8},{12,... | collective-permute-start | bytes 196616 | tf_op jit(solution)/shard_map/ppermute | solution.py:444
  114.0 12.1 %collective-permute-start.21 = (f32[2,4096]{1,0:T(2,128)S(1)}, f32[2,4096]{1,0:T(2,128)S(1)}, u32[]{:S(2)}, u32[]{:S(2)}) collective-permute-start(f32[2,4096]{1,0:T(2,128)S(1)} %get-tuple-element.96), channel_id=1, source_target_pairs={{0,1},{1,0},{2,3},{3,2},{4,5},{5,4},{6,7},{7,6},{8,9},{9,8},{10,11... | collective-permute-start | bytes 98312 | tf_op jit(solution)/shard_map/ppermute | solution.py:444
  118.4 14.5 %collective-permute-start.31 = (bf16[240,1024]{1,0:T(8,128)(2,1)S(1)}, bf16[240,1024]{1,0:T(8,128)(2,1)S(1)}, u32[]{:S(2)}, u32[]{:S(2)}) collective-permute-start(bf16[240,1024]{1,0:T(8,128)(2,1)S(1)} %get-tuple-element.111), channel_id=1, source_target_pairs={{8,0},{24,8},{16,24},{0,16},{9,1},{25,9},{17,25},{1,17},{10,2},{26... | collective-permute-start | bytes 1474568 | tf_op jit(solution)/shard_map/ppermute | solution.py:756
  119.0 14.2 %collective-permute-start.30 = (bf16[240,1024]{1,0:T(8,128)(2,1)S(1)}, bf16[240,1024]{1,0:T(8,128)(2,1)S(1)}, u32[]{:S(2)}, u32[]{:S(2)}) collective-permute-start(bf16[240,1024]{1,0:T(8,128)(2,1)S(1)} %get-tuple-element.98.refs_2_.refs_7_), channel_id=1, source_target_pairs={{0,8},{8,24},{24,16},{16,0},{1,9},{9,25},{25,17},{17,1},{2,10},{10... | collective-permute-start | bytes 1474568 | tf_op jit(solution)/shard_map/ppermute | solution.py:755
  129.7 14.8 %collective-permute-start.26 = (bf16[240,1024]{1,0:T(8,128)(2,1)S(1)}, bf16[240,1024]{1,0:T(8,128)(2,1)S(1)}, u32[]{:S(2)}, u32[]{:S(2)}) collective-permute-start(bf16[240,1024]{1,0:T(8,128)(2,1)S(1)} %get-tuple-element.107), channel_id=1, source_target_pairs={{0,8},{8,24},{24,16},{16,0},{1,9},{9,25},{25,17},{17,1},{2,10},{10... | collective-permute-start | bytes 1474568 | tf_op jit(solution)/shard_map/ppermute | solution.py:755
  132.8 14.2 %collective-permute-start.27 = (bf16[240,1024]{1,0:T(8,128)(2,1)S(1)}, bf16[240,1024]{1,0:T(8,128)(2,1)S(1)}, u32[]{:S(2)}, u32[]{:S(2)}) collective-permute-start(bf16[240,1024]{1,0:T(8,128)(2,1)S(1)} %get-tuple-element.108), channel_id=1, source_target_pairs={{8,0},{24,8},{16,24},{0,16},{9,1},{25,9},{17,25},{1,17},{10,2},{26... | collective-permute-start | bytes 1474568 | tf_op jit(solution)/shard_map/ppermute | solution.py:756
  136.0 29.8 %collective-permute-start.32 = (bf16[240,1024]{1,0:T(8,128)(2,1)S(1)}, bf16[240,1024]{1,0:T(8,128)(2,1)S(1)}, u32[]{:S(2)}, u32[]{:S(2)}) collective-permute-start(bf16[240,1024]{1,0:T(8,128)(2,1)S(1)} %get-tuple-element.112), channel_id=1, source_target_pairs={{0,8},{8,24},{24,16},{16,0},{1,9},{9,25},{25,17},{17,1},{2,10},{10... | collective-permute-start | bytes 1474568 | tf_op jit(solution)/shard_map/ppermute | solution.py:755
  137.9 28.0 %collective-permute-start.33 = (bf16[240,1024]{1,0:T(8,128)(2,1)S(1)}, bf16[240,1024]{1,0:T(8,128)(2,1)S(1)}, u32[]{:S(2)}, u32[]{:S(2)}) collective-permute-start(bf16[240,1024]{1,0:T(8,128)(2,1)S(1)} %get-tuple-element.113), channel_id=1, source_target_pairs={{8,0},{24,8},{16,24},{0,16},{9,1},{25,9},{17,25},{1,17},{10,2},{26... | collective-permute-start | bytes 1474568 | tf_op jit(solution)/shard_map/ppermute | solution.py:756
  149.7 16.3 %collective-permute-start.29 = (bf16[240,1024]{1,0:T(8,128)(2,1)S(1)}, bf16[240,1024]{1,0:T(8,128)(2,1)S(1)}, u32[]{:S(2)}, u32[]{:S(2)}) collective-permute-start(bf16[240,1024]{1,0:T(8,128)(2,1)S(1)} %get-tuple-element.110), channel_id=1, source_target_pairs={{8,0},{24,8},{16,24},{0,16},{9,1},{25,9},{17,25},{1,17},{10,2},{26... | collective-permute-start | bytes 1474568 | tf_op jit(solution)/shard_map/ppermute | solution.py:756
  149.8 16.3 %collective-permute-start.28 = (bf16[240,1024]{1,0:T(8,128)(2,1)S(1)}, bf16[240,1024]{1,0:T(8,128)(2,1)S(1)}, u32[]{:S(2)}, u32[]{:S(2)}) collective-permute-start(bf16[240,1024]{1,0:T(8,128)(2,1)S(1)} %get-tuple-element.109.refs_6_), channel_id=1, source_target_pairs={{0,8},{8,24},{24,16},{16,0},{1,9},{9,25},{25,17},{17,1},{2,10},{10... | collective-permute-start | bytes 1474568 | tf_op jit(solution)/shard_map/ppermute | solution.py:755
  151.8 14.0 %copy-start.8 = (bf16[240,1024]{1,0:T(8,128)(2,1)S(1)}, bf16[240,1024]{1,0:T(8,128)(2,1)}, u32[]{:S(2)}) copy-start(bf16[240,1024]{1,0:T(8,128)(2,1)} %copy-done.7) | copy-start | bytes 1474564
  (23 other events, 80.9 us)

commit v3 on v1

--- a/solution.py
+++ b/solution.py
@@ -13,6 +13,7 @@
 MOST_CHUNKS = 24
 TILE = 16
 BUFFERS = 3
+PIECES = 6
 FETCHED = 4
 VMEM = 50 << 20
 
@@ -708,26 +709,25 @@
 
     sent = send()
     both = beside(tokens[0], d_out[0], sent)
+    sent = send(both)
     exchanges = []
     for axis in ("tensor", "fsdp"):
         size = lax.axis_size(axis)
         exchanges += [(axis, size, 1 << k) for k in range((size - 1).bit_length())]
     if all(size & (size - 1) == 0 for _, size, _ in exchanges):
+        after = sent
         for level, (axis, size, apart) in enumerate(exchanges):
+            other = lax.ppermute(both, axis, [(i, i ^ apart) for i in range(size)])
             last = level == len(exchanges) - 1
-            other = lax.ppermute(both, axis, [(i, i ^ apart) for i in range(size)])
+            both = join(both, other, after, axis, apart, last)
             after = ()
-            if level == 0 or last:
-                after = sent = send(both)
-            both = join(both, other, after, axis, apart, last)
     else:
-        sent = send(both)
         both = lax.all_gather(both[0], ("fsdp", "tensor"), axis=0, tiled=True)
-        sent = send(both)
+    sent = send(both)
 
     tile = 128 if units % 128 == 0 else units
     hidden, d_rows = [], None
-    pieces = shares(units // tile, 4)
+    pieces = shares(units // tile, PIECES)
     for first, count in pieces:
         part, d_rows = layer(both, w_gate, w_up, w_down, d_rows, sent, tile, first, count)
         hidden.append(part)

time: 168 us -> 167 us (level)
  waiting for transfers between devices: 39.2 us -> 30.6 us
  starting transfers between devices: 36.4 us -> 40.2 us
  Pallas kernels: 86.5 us -> 89.2 us
    ppermute x14, waiting for transfers between devices: 12.3 us -> 7.05 us  [send(): lax.ppermute(sends[-1][0], 'replica', forward)]
    pallas_call x4 -> x6, Pallas kernels: 26.7 us -> 30.4 us  [layer(): pl.pallas_call(functools.partial(layer_body, resumed=resumed, tile=tile,...]
    ppermute x14, starting transfers between devices: 21.1 us -> 24.8 us  [send(): lax.ppermute(sends[-1][1], 'replica', backward)]
    ppermute x14, waiting for transfers between devices: 14.8 us -> 11.6 us  [send(): lax.ppermute(sends[-1][1], 'replica', backward)]
    unnamed x74 -> x86, local copies, waits for them, and re-layouts: 2.61 us -> 3.58 us
  transfers between devices with their start and end apart: 34 -> 34, of which waited for: 15 -> 12; matrix products, arithmetic and copies ran while one was open for 0% -> 0% of each run, Pallas kernels for 50% -> 52%
where the time goes in v3:
time: 167 us; the launch traced here: 166 us
  Pallas kernels  89.2 us (53%)
  starting transfers between devices  40.2 us (24%)
  waiting for transfers between devices  30.6 us (18%)
  local copies, waits for them, and re-layouts  3.58 us (2%)
  between operations  2.19 us (1%)
    pallas_call x14, Pallas kernels, pack(): pl.pallas_call(functools.partial(pack_body, n=n, places=places, chunk=chu...  35 us
    pallas_call x6, Pallas kernels, layer(): pl.pallas_call(functools.partial(layer_body, resumed=resumed, tile=tile,...  30.4 us
    ppermute x14, starting transfers between devices, send(): lax.ppermute(sends[-1][1], 'replica', backward)  24.8 us
    pallas_call x2, Pallas kernels, update(): pl.pallas_call(functools.partial(update_body, n=n, block=block, first=fir...  18.7 us
    ppermute x14, waiting for transfers between devices, send(): lax.ppermute(sends[-1][1], 'replica', backward)  11.6 us
    ppermute x3, waiting for transfers between devices, per_device(): other = lax.ppermute(both, axis, [(i, i ^ apart) for i in range(size)])  8.85 us
    ppermute x14, starting transfers between devices, send(): lax.ppermute(sends[-1][0], 'replica', forward)  8.15 us
    ppermute x14, waiting for transfers between devices, send(): lax.ppermute(sends[-1][0], 'replica', forward)  7.05 us
  transfers between devices with their start and end apart: 34, of which 12 were waited for; matrix products, arithmetic and copies ran while one was open for 0% of the time, Pallas kernels for 52%

profile of v3, /device:TPU:0, one launch (start us, length us, event | category | flops | bytes accessed | tf_op | source)
XLA Modules:
  0.0 165.8 jit_solution(974876880399706227)
XLA Ops:
  0.7 2.5 %pack.14 = (bf16[240,1024]{1,0:T(8,128)(2,1)S(1)}, bf16[240,1024]{1,0:T(8,128)(2,1)S(1)}) custom-call(f32[2,1920,1024]{2,1,0:T(8,128)} %refs_0_.31, f32[2,1920,1024]{2,1,0:T(8,128)} %refs_1_.43, f32[2,1920,1024]{2,1,0:T(8,128)} %refs_2_.43), custom_call_target="tpu_custom_call" | custom-call | bytes 2949120 | tf_op jit(solution)/shard_map/pack/pallas_call | solution.py:200
  3.1 3.0 %collective-permute-start.4 = (bf16[240,1024]{1,0:T(8,128)(2,1)S(1)}, bf16[240,1024]{1,0:T(8,128)(2,1)S(1)}, u32[]{:S(2)}, u32[]{:S(2)}) collective-permute-start(bf16[240,1024]{1,0:T(8,128)(2,1)S(1)} %get-tuple-element.72), channel_id=1, source_target_pairs={{8,0},{24,8},{16,24},{0,16},{9,1},{25,9},{17,25},{1,17},{10,2},{26... | collective-permute-start | bytes 1474568 | tf_op jit(solution)/shard_map/ppermute | solution.py:705
  6.2 2.5 %pack.15 = (bf16[240,1024]{1,0:T(8,128)(2,1)S(1)}, bf16[240,1024]{1,0:T(8,128)(2,1)S(1)}) custom-call(f32[2,1920,1024]{2,1,0:T(8,128)} %refs_0_.31, f32[2,1920,1024]{2,1,0:T(8,128)} %refs_1_.43, f32[2,1920,1024]{2,1,0:T(8,128)} %refs_2_.43, bf16[1,2,8192]{2,1,0:T(2,128)(2,1)S(1)} %beside.1.refs_3_.own), custom_call_target="tpu_custom_call" | custom-call | bytes 2949120 | tf_op jit(solution)/shard_map/pack/pallas_call | solution.py:200
  8.7 2.0 %collective-permute-start.6 = (bf16[240,1024]{1,0:T(8,128)(2,1)S(1)}, bf16[240,1024]{1,0:T(8,128)(2,1)S(1)}, u32[]{:S(2)}, u32[]{:S(2)}) collective-permute-start(bf16[240,1024]{1,0:T(8,128)(2,1)S(1)} %get-tuple-element.75), channel_id=1, source_target_pairs={{8,0},{24,8},{16,24},{0,16},{9,1},{25,9},{17,25},{1,17},{10,2},{26... | collective-permute-start | bytes 1474568 | tf_op jit(solution)/shard_map/ppermute | solution.py:705
  12.0 2.1 %collective-permute-start.1 = (bf16[2,2,8192]{2,1,0:T(2,128)(2,1)S(1)}, bf16[2,2,8192]{2,1,0:T(2,128)(2,1)S(1)}, u32[]{:S(2)}, u32[]{:S(2)}) collective-permute-start(bf16[2,2,8192]{2,1,0:T(2,128)(2,1)S(1)} %join.3.own), channel_id=1, source_target_pairs={{0,2},{2,0},{4,6},{6,4},{1,3},{3,1},{5,7},{7,5},{8,10},{10,8},{12,... | collective-permute-start | bytes 196616 | tf_op jit(solution)/shard_map/ppermute | solution.py:720
  14.1 2.4 %collective-permute-done.1.other = bf16[2,2,8192]{2,1,0:T(2,128)(2,1)S(1)} collective-permute-done((bf16[2,2,8192]{2,1,0:T(2,128)(2,1)S(1)}, bf16[2,2,8192]{2,1,0:T(2,128)(2,1)S(1)}, u32[]{:S(2)}, u32[]{:S(2)}) %collective-permute-start.1) | collective-permute-done | bytes 65568 | tf_op jit(solution)/shard_map/ppermute | solution.py:720
  16.5 2.9 %collective-permute-start.2 = (bf16[4,2,8192]{2,1,0:T(2,128)(2,1)S(1)}, bf16[4,2,8192]{2,1,0:T(2,128)(2,1)S(1)}, u32[]{:S(2)}, u32[]{:S(2)}) collective-permute-start(bf16[4,2,8192]{2,1,0:T(2,128)(2,1)S(1)} %join.4.own), channel_id=1, source_target_pairs={{0,4},{2,6},{4,0},{6,2},{1,5},{3,7},{5,1},{7,3},{8,12},{10,14},{12... | collective-permute-start | bytes 393224 | tf_op jit(solution)/shard_map/ppermute | solution.py:720
  20.1 5.2 %collective-permute-done.2.other = bf16[4,2,8192]{2,1,0:T(2,128)(2,1)S(1)} collective-permute-done((bf16[4,2,8192]{2,1,0:T(2,128)(2,1)S(1)}, bf16[4,2,8192]{2,1,0:T(2,128)(2,1)S(1)}, u32[]{:S(2)}, u32[]{:S(2)}) %collective-permute-start.2) | collective-permute-done | bytes 131104 | tf_op jit(solution)/shard_map/ppermute | solution.py:720
  25.5 2.7 %pack.16 = (bf16[240,1024]{1,0:T(8,128)(2,1)S(1)}, bf16[240,1024]{1,0:T(8,128)(2,1)S(1)}) custom-call(s32[1]{0:T(128)S(6)} %copy.43.refs_0_.failed, f32[2,1920,1024]{2,1,0:T(8,128)} %refs_0_.31, f32[2,1920,1024]{2,1,0:T(8,128)} %refs_1_.43, f32[2,1920,1024]{2,1,0:T(8,128)} %refs_2_.43, bf16[240,1024]{1,0:T(8,128)(2,1)S(1)} %collective-permute-done.3.refs_4_.refs_0_, ...), custom_call_target="tpu_custom_call" | custom-call | bytes 2949120 | tf_op jit(solution)/shard_map/pack/pallas_call | solution.py:200
  28.3 1.6 collective-permute-start.8
  30.3 4.4 %layer.6 = (bf16[16,256]{1,0:T(8,128)(2,1)S(1)}, f32[16,4096]{1,0:T(8,128)S(1)}) custom-call(bf16[16,8192]{1,0:T(8,128)(2,1)S(1)} %join.5.refs_6_.both, bf16[4096,1920]{1,0:T(8,128)(2,1)} %refs_0_.29, bf16[4096,1920]{1,0:T(8,128)(2,1)} %refs_1_.35, bf16[1920,4096]{1,0:T(8,128)(2,1)} %refs_2_.35, bf16[240,1024]{1,0:T(8,128)(2,1)S(1)} %get-tuple-element.73.refs_3_), custom_call_target="tpu_custom_call" | custom-call | flops 167772160 | bytes 6291456 | tf_op jit(solution)/shard_map/layer/pallas_call | solution.py:329
  34.8 2.7 %pack.17 = (bf16[240,1024]{1,0:T(8,128)(2,1)S(1)}, bf16[240,1024]{1,0:T(8,128)(2,1)S(1)}) custom-call(s32[1]{0:T(128)S(6)} %copy.43.refs_0_.failed, f32[2,1920,1024]{2,1,0:T(8,128)} %refs_0_.31, f32[2,1920,1024]{2,1,0:T(8,128)} %refs_1_.43, f32[2,1920,1024]{2,1,0:T(8,128)} %refs_2_.43, bf16[240,1024]{1,0:T(8,128)(2,1)S(1)} %collective-permute-done.5.refs_4_.refs_2_, ...), custom_call_target="tpu_custom_call" | custom-call | bytes 2949120 | tf_op jit(solution)/shard_map/pack/pallas_call | solution.py:200
  37.6 1.6 collective-permute-start.10
  39.6 5.7 %layer.7 = (bf16[16,384]{1,0:T(8,128)(2,1)S(1)}, f32[16,4096]{1,0:T(8,128)S(1)}) custom-call(bf16[16,8192]{1,0:T(8,128)(2,1)S(1)} %join.5.refs_6_.both, bf16[4096,1920]{1,0:T(8,128)(2,1)} %refs_0_.29, bf16[4096,1920]{1,0:T(8,128)(2,1)} %refs_1_.35, bf16[1920,4096]{1,0:T(8,128)(2,1)} %refs_2_.35, f32[16,4096]{1,0:T(8,128)S(1)} %get-tuple-element.74.refs_6_.refs_3_, ...), custom_call_target="tpu_custom_call" | custom-call | flops 251658240 | bytes 9437184 | tf_op jit(solution)/shard_map/layer/pallas_call | solution.py:329
  45.4 2.7 %pack.18 = (bf16[240,1024]{1,0:T(8,128)(2,1)S(1)}, bf16[240,1024]{1,0:T(8,128)(2,1)S(1)}) custom-call(s32[1]{0:T(128)S(6)} %copy.43.refs_0_.failed, f32[2,1920,1024]{2,1,0:T(8,128)} %refs_0_.31, f32[2,1920,1024]{2,1,0:T(8,128)} %refs_1_.43, f32[2,1920,1024]{2,1,0:T(8,128)} %refs_2_.43, bf16[240,1024]{1,0:T(8,128)(2,1)S(1)} %collective-permute-done.7.refs_4_, ...), custom_call_target="tpu_custom_call" | custom-call | bytes 2949120 | tf_op jit(solution)/shard_map/pack/pallas_call | solution.py:200
  48.1 1.7 %collective-permute-start.12 = (bf16[240,1024]{1,0:T(8,128)(2,1)S(1)}, bf16[240,1024]{1,0:T(8,128)(2,1)S(1)}, u32[]{:S(2)}, u32[]{:S(2)}) collective-permute-start(bf16[240,1024]{1,0:T(8,128)(2,1)S(1)} %get-tuple-element.84), channel_id=1, source_target_pairs={{8,0},{24,8},{16,24},{0,16},{9,1},{25,9},{17,25},{1,17},{10,2},{26... | collective-permute-start | bytes 1474568 | tf_op jit(solution)/shard_map/ppermute | solution.py:705
  50.2 4.4 %layer.8 = (bf16[16,256]{1,0:T(8,128)(2,1)S(1)}, f32[16,4096]{1,0:T(8,128)S(1)}) custom-call(bf16[16,8192]{1,0:T(8,128)(2,1)S(1)} %join.5.refs_6_.both, bf16[4096,1920]{1,0:T(8,128)(2,1)} %refs_0_.29, bf16[4096,1920]{1,0:T(8,128)(2,1)} %refs_1_.35, bf16[1920,4096]{1,0:T(8,128)(2,1)} %refs_2_.35, f32[16,4096]{1,0:T(8,128)S(1)} %get-tuple-element.77.refs_6_.refs_3_, ...), custom_call_target="tpu_custom_call" | custom-call | flops 167772160 | bytes 6291456 | tf_op jit(solution)/shard_map/layer/pallas_call | solution.py:329
  54.7 2.7 %pack.19 = (bf16[240,1024]{1,0:T(8,128)(2,1)S(1)}, bf16[240,1024]{1,0:T(8,128)(2,1)S(1)}) custom-call(s32[1]{0:T(128)S(6)} %copy.43.refs_0_.failed, f32[2,1920,1024]{2,1,0:T(8,128)} %refs_0_.31, f32[2,1920,1024]{2,1,0:T(8,128)} %refs_1_.43, f32[2,1920,1024]{2,1,0:T(8,128)} %refs_2_.43, bf16[240,1024]{1,0:T(8,128)(2,1)S(1)} %collective-permute-done.9.refs_4_.refs_6_, ...), custom_call_target="tpu_custom_call" | custom-call | bytes 2949120 | tf_op jit(solution)/shard_map/pack/pallas_call | solution.py:200
  57.4 1.7 %collective-permute-start.14 = (bf16[240,1024]{1,0:T(8,128)(2,1)S(1)}, bf16[240,1024]{1,0:T(8,128)(2,1)S(1)}, u32[]{:S(2)}, u32[]{:S(2)}) collective-permute-start(bf16[240,1024]{1,0:T(8,128)(2,1)S(1)} %get-tuple-element.87), channel_id=1, source_target_pairs={{8,0},{24,8},{16,24},{0,16},{9,1},{25,9},{17,25},{1,17},{10,2},{26... | collective-permute-start | bytes 1474568 | tf_op jit(solution)/shard_map/ppermute | solution.py:705
  59.5 5.7 %layer.9 = (bf16[16,384]{1,0:T(8,128)(2,1)S(1)}, f32[16,4096]{1,0:T(8,128)S(1)}) custom-call(bf16[16,8192]{1,0:T(8,128)(2,1)S(1)} %join.5.refs_6_.both, bf16[4096,1920]{1,0:T(8,128)(2,1)} %refs_0_.29, bf16[4096,1920]{1,0:T(8,128)(2,1)} %refs_1_.35, bf16[1920,4096]{1,0:T(8,128)(2,1)} %refs_2_.35, f32[16,4096]{1,0:T(8,128)S(1)} %get-tuple-element.80.refs_6_.refs_3_, ...), custom_call_target="tpu_custom_call" | custom-call | flops 251658240 | bytes 9437184 | tf_op jit(solution)/shard_map/layer/pallas_call | solution.py:329
  65.2 2.7 %pack.20 = (bf16[240,1024]{1,0:T(8,128)(2,1)S(1)}, bf16[240,1024]{1,0:T(8,128)(2,1)S(1)}) custom-call(s32[1]{0:T(128)S(6)} %copy.43.refs_0_.failed, f32[2,1920,1024]{2,1,0:T(8,128)} %refs_0_.31, f32[2,1920,1024]{2,1,0:T(8,128)} %refs_1_.43, f32[2,1920,1024]{2,1,0:T(8,128)} %refs_2_.43, bf16[240,1024]{1,0:T(8,128)(2,1)S(1)} %collective-permute-done.11.refs_4_.refs_8_, ...), custom_call_target="tpu_custom_call" | custom-call | bytes 2949120 | tf_op jit(solution)/shard_map/pack/pallas_call | solution.py:200
  68.0 1.8 %collective-permute-start.19 = (bf16[240,1024]{1,0:T(8,128)(2,1)S(1)}, bf16[240,1024]{1,0:T(8,128)(2,1)S(1)}, u32[]{:S(2)}, u32[]{:S(2)}) collective-permute-start(bf16[240,1024]{1,0:T(8,128)(2,1)S(1)} %get-tuple-element.94), channel_id=1, source_target_pairs={{8,0},{24,8},{16,24},{0,16},{9,1},{25,9},{17,25},{1,17},{10,2},{26... | collective-permute-start | bytes 1474568 | tf_op jit(solution)/shard_map/ppermute | solution.py:705
  70.0 4.4 %layer.10 = (bf16[16,256]{1,0:T(8,128)(2,1)S(1)}, f32[16,4096]{1,0:T(8,128)S(1)}) custom-call(bf16[16,8192]{1,0:T(8,128)(2,1)S(1)} %join.5.refs_6_.both, bf16[4096,1920]{1,0:T(8,128)(2,1)} %refs_0_.29, bf16[4096,1920]{1,0:T(8,128)(2,1)} %refs_1_.35, bf16[1920,4096]{1,0:T(8,128)(2,1)} %refs_2_.35, f32[16,4096]{1,0:T(8,128)S(1)} %get-tuple-element.83.refs_6_.refs_3_, ...), custom_call_target="tpu_custom_call" | custom-call | flops 167772160 | bytes 6291456 | tf_op jit(solution)/shard_map/layer/pallas_call | solution.py:329
  74.9 2.6 %pack.21 = (bf16[240,1024]{1,0:T(8,128)(2,1)S(1)}, bf16[240,1024]{1,0:T(8,128)(2,1)S(1)}) custom-call(s32[1]{0:T(128)S(6)} %copy.43.refs_0_.failed, f32[2,1920,1024]{2,1,0:T(8,128)} %refs_0_.31, f32[2,1920,1024]{2,1,0:T(8,128)} %refs_1_.43, f32[2,1920,1024]{2,1,0:T(8,128)} %refs_2_.43, bf16[240,1024]{1,0:T(8,128)(2,1)S(1)} %collective-permute-done.13.refs_4_.refs_10_, ...), custom_call_target="tpu_custom_call" | custom-call | bytes 2949120 | tf_op jit(solution)/shard_map/pack/pallas_call | solution.py:200
  77.6 1.6 collective-permute-start.16
  79.6 5.7 %layer.11 = (bf16[16,384]{1,0:T(8,128)(2,1)S(1)}, f32[16,4096]{1,0:T(8,128)S(1)}) custom-call(bf16[16,8192]{1,0:T(8,128)(2,1)S(1)} %join.5.refs_6_.both, bf16[4096,1920]{1,0:T(8,128)(2,1)} %refs_0_.29, bf16[4096,1920]{1,0:T(8,128)(2,1)} %refs_1_.35, bf16[1920,4096]{1,0:T(8,128)(2,1)} %refs_2_.35, f32[16,4096]{1,0:T(8,128)S(1)} %get-tuple-element.86.refs_6_.refs_3_, ...), custom_call_target="tpu_custom_call" | custom-call | flops 251658240 | bytes 9437184 | tf_op jit(solution)/shard_map/layer/pallas_call | solution.py:329
  85.4 2.5 %pack.23 = (bf16[304,1024]{1,0:T(8,128)(2,1)}, bf16[288,1024]{1,0:T(8,128)(2,1)}) custom-call(s32[1]{0:T(128)S(6)} %copy.43.refs_0_.failed, f32[2,1920,1024]{2,1,0:T(8,128)} %refs_0_.31, f32[2,1920,1024]{2,1,0:T(8,128)} %refs_1_.43, f32[2,1920,1024]{2,1,0:T(8,128)} %refs_2_.43, bf16[240,1024]{1,0:T(8,128)(2,1)S(1)} %collective-permute-done.18.refs_4_.refs_0_, ...), custom_call_target="tpu_custom_call" | custom-call | bytes 2949120 | tf_op jit(solution)/shard_map/pack/pallas_call | solution.py:200
  90.1 4.8 %collective-permute-done.16.refs_5_.refs_3_ = bf16[240,1024]{1,0:T(8,128)(2,1)S(1)} collective-permute-done((bf16[240,1024]{1,0:T(8,128)(2,1)S(1)}, bf16[240,1024]{1,0:T(8,128)(2,1)S(1)}, u32[]{:S(2)}, u32[]{:S(2)}) %collective-permute-start.16) | collective-permute-done | bytes 491552 | tf_op jit(solution)/shard_map/ppermute | solution.py:705
  96.0 2.3 %pack.22 = (bf16[240,1024]{1,0:T(8,128)(2,1)}, bf16[240,1024]{1,0:T(8,128)(2,1)}) custom-call(s32[1]{0:T(128)S(6)} %copy.43.refs_0_.failed, f32[2,1920,1024]{2,1,0:T(8,128)} %refs_0_.31, f32[2,1920,1024]{2,1,0:T(8,128)} %refs_1_.43, f32[2,1920,1024]{2,1,0:T(8,128)} %refs_2_.43, bf16[240,1024]{1,0:T(8,128)(2,1)S(1)} %collective-permute-done.15.refs_4_.refs_2_, ...), custom_call_target="tpu_custom_call" | custom-call | bytes 2949120 | tf_op jit(solution)/shard_map/pack/pallas_call | solution.py:200
  98.3 1.7 %collective-permute-start.24 = (bf16[240,1024]{1,0:T(8,128)(2,1)}, bf16[240,1024]{1,0:T(8,128)(2,1)}, u32[]{:S(2)}, u32[]{:S(2)}) collective-permute-start(bf16[240,1024]{1,0:T(8,128)(2,1)} %get-tuple-element.106), channel_id=1, source_target_pairs={{8,0},{24,8},{16,24},{0,16},{9,1},{25,9},{17,25},{1,17},{10,2},{26... | collective-permute-start | bytes 1474568 | tf_op jit(solution)/shard_map/ppermute | solution.py:705
  102.6 4.9 %collective-permute-done.21.refs_5_.refs_8_ = bf16[288,1024]{1,0:T(8,128)(2,1)S(1)} collective-permute-done((bf16[288,1024]{1,0:T(8,128)(2,1)}, bf16[288,1024]{1,0:T(8,128)(2,1)S(1)}, u32[]{:S(2)}, u32[]{:S(2)}) %collective-permute-start.21) | collective-permute-done | bytes 589856 | tf_op jit(solution)/shard_map/ppermute | solution.py:705
  107.5 1.8 %collective-permute-done.20.refs_4_.refs_6_ = bf16[304,1024]{1,0:T(8,128)(2,1)S(1)} collective-permute-done((bf16[304,1024]{1,0:T(8,128)(2,1)}, bf16[304,1024]{1,0:T(8,128)(2,1)S(1)}, u32[]{:S(2)}, u32[]{:S(2)}) %collective-permute-start.20) | collective-permute-done | bytes 622624 | tf_op jit(solution)/shard_map/ppermute | solution.py:704
  109.3 2.4 %pack.24 = (bf16[288,1024]{1,0:T(8,128)(2,1)}, bf16[240,1024]{1,0:T(8,128)(2,1)}) custom-call(s32[1]{0:T(128)S(6)} %copy.43.refs_0_.failed, f32[2,1920,1024]{2,1,0:T(8,128)} %refs_0_.31, f32[2,1920,1024]{2,1,0:T(8,128)} %refs_1_.43, f32[2,1920,1024]{2,1,0:T(8,128)} %refs_2_.43, bf16[304,1024]{1,0:T(8,128)(2,1)S(1)} %collective-permute-done.20.refs_4_.refs_6_, ...), custom_call_target="tpu_custom_call" | custom-call | bytes 2949120 | tf_op jit(solution)/shard_map/pack/pallas_call | solution.py:200
  114.7 1.6 halve.5
  116.3 1.8 %collective-permute-done.24.refs_5_.refs_7_ = bf16[240,1024]{1,0:T(8,128)(2,1)} collective-permute-done((bf16[240,1024]{1,0:T(8,128)(2,1)}, bf16[240,1024]{1,0:T(8,128)(2,1)}, u32[]{:S(2)}, u32[]{:S(2)}) %collective-permute-start.24) | collective-permute-done | bytes 491552 | tf_op jit(solution)/shard_map/ppermute | solution.py:705
  118.1 1.8 %collective-permute-done.23.refs_4_.refs_6_ = bf16[240,1024]{1,0:T(8,128)(2,1)} collective-permute-done((bf16[240,1024]{1,0:T(8,128)(2,1)}, bf16[240,1024]{1,0:T(8,128)(2,1)}, u32[]{:S(2)}, u32[]{:S(2)}) %collective-permute-start.23) | collective-permute-done | bytes 491552 | tf_op jit(solution)/shard_map/ppermute | solution.py:704
  119.9 2.1 %pack.25 = (bf16[240,1024]{1,0:T(8,128)(2,1)}, bf16[240,1024]{1,0:T(8,128)(2,1)}) custom-call(s32[1]{0:T(128)S(6)} %copy.43.refs_0_.failed, f32[2,1920,1024]{2,1,0:T(8,128)} %refs_0_.31, f32[2,1920,1024]{2,1,0:T(8,128)} %refs_1_.43, f32[2,1920,1024]{2,1,0:T(8,128)} %refs_2_.43, bf16[240,1024]{1,0:T(8,128)(2,1)} %collective-permute-done.23.refs_4_.refs_6_, ...), custom_call_target="tpu_custom_call" | custom-call | bytes 2949120 | tf_op jit(solution)/shard_map/pack/pallas_call | solution.py:200
  122.1 1.7 %collective-permute-start.29 = (bf16[240,1024]{1,0:T(8,128)(2,1)}, bf16[240,1024]{1,0:T(8,128)(2,1)}, u32[]{:S(2)}, u32[]{:S(2)}) collective-permute-start(bf16[240,1024]{1,0:T(8,128)(2,1)} %get-tuple-element.114), channel_id=1, source_target_pairs={{8,0},{24,8},{16,24},{0,16},{9,1},{25,9},{17,25},{1,17},{10,2},{26... | collective-permute-start | bytes 1474568 | tf_op jit(solution)/shard_map/ppermute | solution.py:705
  124.1 1.5 collective-permute-start.22
  125.6 3.1 %collective-permute-done.22.refs_1_ = f32[4,4096]{1,0:T(4,128)} collective-permute-done((f32[4,4096]{1,0:T(4,128)}, f32[4,4096]{1,0:T(4,128)}, u32[]{:S(2)}, u32[]{:S(2)}) %collective-permute-start.22) | collective-permute-done | bytes 65568 | tf_op jit(solution)/shard_map/ppermute | solution.py:402
  130.5 2.0 %collective-permute-done.26.refs_4_.refs_7_.refs_8_ = bf16[288,1024]{1,0:T(8,128)(2,1)S(1)} collective-permute-done((bf16[288,1024]{1,0:T(8,128)(2,1)}, bf16[288,1024]{1,0:T(8,128)(2,1)S(1)}, u32[]{:S(2)}, u32[]{:S(2)}) %collective-permute-start.26) | collective-permute-done | bytes 589856 | tf_op jit(solution)/shard_map/ppermute | solution.py:704
  132.5 2.3 %pack.26 = (bf16[240,1024]{1,0:T(8,128)(2,1)S(1)}, bf16[240,1024]{1,0:T(8,128)(2,1)S(1)}) custom-call(s32[1]{0:T(128)S(6)} %copy.43.refs_0_.failed, f32[2,1920,1024]{2,1,0:T(8,128)} %refs_0_.31, f32[2,1920,1024]{2,1,0:T(8,128)} %refs_1_.43, f32[2,1920,1024]{2,1,0:T(8,128)} %refs_2_.43, bf16[288,1024]{1,0:T(8,128)(2,1)S(1)} %collective-permute-done.26.refs_4_.refs_7_.refs_8_, ...), custom_call_target="tpu_custom_call" | custom-call | bytes 2949120 | tf_op jit(solution)/shard_map/pack/pallas_call | solution.py:200
  134.8 2.0 %collective-permute-start.33 = (bf16[240,1024]{1,0:T(8,128)(2,1)S(1)}, bf16[240,1024]{1,0:T(8,128)(2,1)S(1)}, u32[]{:S(2)}, u32[]{:S(2)}) collective-permute-start(bf16[240,1024]{1,0:T(8,128)(2,1)S(1)} %get-tuple-element.121), channel_id=1, source_target_pairs={{8,0},{24,8},{16,24},{0,16},{9,1},{25,9},{17,25},{1,17},{10,2},{26... | collective-permute-start | bytes 1474568 | tf_op jit(solution)/shard_map/ppermute | solution.py:705
  137.7 4.7 %update.2 = (f32[1920,1024]{1,0:T(8,128)}, f32[1920,1024]{1,0:T(8,128)}, f32[1920,1024]{1,0:T(8,128)}) custom-call(s32[1]{0:T(128)S(6)} %copy.43.refs_0_.failed, bf16[1920,64]{1,0:T(8,128)(2,1)S(1)} %get-tuple-element.112.hid_ref.refs_3_, bf16[64,1024]{1,0:T(8,128)(2,1)S(1)} %get-tuple-element.113.out_ref, f32[2,1920,1024]{2,1,0:T(8,128)} %refs_0_.31, ...), custom_call_target="tpu_custom_call" | custom-call | flops 50331648 | bytes 9437184 | tf_op jit(solution)/shard_map/update/pallas_call | solution.py:523
  144.0 2.3 %pack.27 = (bf16[240,1024]{1,0:T(8,128)(2,1)S(1)}, bf16[240,1024]{1,0:T(8,128)(2,1)S(1)}) custom-call(s32[1]{0:T(128)S(6)} %copy.43.refs_0_.failed, f32[2,1920,1024]{2,1,0:T(8,128)} %refs_0_.31, f32[2,1920,1024]{2,1,0:T(8,128)} %refs_1_.43, f32[2,1920,1024]{2,1,0:T(8,128)} %refs_2_.43, bf16[240,1024]{1,0:T(8,128)(2,1)} %collective-permute-done.28.refs_4_.refs_10_, ...), custom_call_target="tpu_custom_call" | custom-call | bytes 2949120 | tf_op jit(solution)/shard_map/pack/pallas_call | solution.py:200
  146.2 2.2 %collective-permute-start.31 = (bf16[240,1024]{1,0:T(8,128)(2,1)S(1)}, bf16[240,1024]{1,0:T(8,128)(2,1)S(1)}, u32[]{:S(2)}, u32[]{:S(2)}) collective-permute-start(bf16[240,1024]{1,0:T(8,128)(2,1)S(1)} %get-tuple-element.120), channel_id=1, source_target_pairs={{8,0},{24,8},{16,24},{0,16},{9,1},{25,9},{17,25},{1,17},{10,2},{26... | collective-permute-start | bytes 1474568 | tf_op jit(solution)/shard_map/ppermute | solution.py:705
  148.4 2.8 %collective-permute-start.30 = (bf16[240,1024]{1,0:T(8,128)(2,1)S(1)}, bf16[240,1024]{1,0:T(8,128)(2,1)S(1)}, u32[]{:S(2)}, u32[]{:S(2)}) collective-permute-start(bf16[240,1024]{1,0:T(8,128)(2,1)S(1)} %get-tuple-element.119.refs_6_), channel_id=1, source_target_pairs={{0,8},{8,24},{24,16},{16,0},{1,9},{9,25},{25,17},{17,1},{2,10},{10... | collective-permute-start | bytes 1474568 | tf_op jit(solution)/shard_map/ppermute | solution.py:704
  151.2 14.0 %update.3 = (f32[1920,1024]{1,0:T(8,128)}, f32[1920,1024]{1,0:T(8,128)}, f32[1920,1024]{1,0:T(8,128)}) custom-call(s32[1]{0:T(128)S(6)} %copy.43.refs_0_.failed, bf16[1920,64]{1,0:T(8,128)(2,1)S(1)} %get-tuple-element.112.hid_ref.refs_3_, ...), custom_call_target="tpu_custom_call", output_to_operand_aliasing={{0}: (6, {}), {1}: (7, {}), {2}: (8, {})} | custom-call | flops 201326592 | bytes 37748736 | tf_op jit(solution)/shard_map/update/pallas_call | solution.py:523
  (141 shorter events, 18.3 us)
Async XLA Ops:
  0.6 5.6 %copy-start.42 = (bf16[1,2,4096]{2,1,0:T(2,128)(2,1)S(1)}, bf16[1,2,4096]{2,1,0:T(2,128)(2,1)}, u32[]{:S(2)}) copy-start(bf16[1,2,4096]{2,1,0:T(2,128)(2,1)} %param.10) | copy-start | bytes 49156
  0.6 5.6 %copy-start.41 = (bf16[1,2,4096]{2,1,0:T(2,128)(2,1)S(1)}, bf16[1,2,4096]{2,1,0:T(2,128)(2,1)}, u32[]{:S(2)}) copy-start(bf16[1,2,4096]{2,1,0:T(2,128)(2,1)} %param.9) | copy-start | bytes 49156
  3.1 22.4 %collective-permute-start.4 = (bf16[240,1024]{1,0:T(8,128)(2,1)S(1)}, bf16[240,1024]{1,0:T(8,128)(2,1)S(1)}, u32[]{:S(2)}, u32[]{:S(2)}) collective-permute-start(bf16[240,1024]{1,0:T(8,128)(2,1)S(1)} %get-tuple-element.72), channel_id=1, source_target_pairs={{8,0},{24,8},{16,24},{0,16},{9,1},{25,9},{17,25},{1,17},{10,2},{26... | collective-permute-start | bytes 1474568 | tf_op jit(solution)/shard_map/ppermute | solution.py:705
  6.2 19.4 %collective-permute-start.3 = (bf16[240,1024]{1,0:T(8,128)(2,1)S(1)}, bf16[240,1024]{1,0:T(8,128)(2,1)S(1)}, u32[]{:S(2)}, u32[]{:S(2)}) collective-permute-start(bf16[240,1024]{1,0:T(8,128)(2,1)S(1)} %get-tuple-element.70.refs_2_), channel_id=1, source_target_pairs={{0,8},{8,24},{24,16},{16,0},{1,9},{9,25},{25,17},{17,1},{2,10},{10... | collective-permute-start | bytes 1474568 | tf_op jit(solution)/shard_map/ppermute | solution.py:704
  8.7 26.1 %collective-permute-start.6 = (bf16[240,1024]{1,0:T(8,128)(2,1)S(1)}, bf16[240,1024]{1,0:T(8,128)(2,1)S(1)}, u32[]{:S(2)}, u32[]{:S(2)}) collective-permute-start(bf16[240,1024]{1,0:T(8,128)(2,1)S(1)} %get-tuple-element.75), channel_id=1, source_target_pairs={{8,0},{24,8},{16,24},{0,16},{9,1},{25,9},{17,25},{1,17},{10,2},{26... | collective-permute-start | bytes 1474568 | tf_op jit(solution)/shard_map/ppermute | solution.py:705
  10.7 24.1 %collective-permute-start.5 = (bf16[240,1024]{1,0:T(8,128)(2,1)S(1)}, bf16[240,1024]{1,0:T(8,128)(2,1)S(1)}, u32[]{:S(2)}, u32[]{:S(2)}) collective-permute-start(bf16[240,1024]{1,0:T(8,128)(2,1)S(1)} %get-tuple-element.71.refs_0_), channel_id=1, source_target_pairs={{0,8},{8,24},{24,16},{16,0},{1,9},{9,25},{25,17},{17,1},{2,10},{10... | collective-permute-start | bytes 1474568 | tf_op jit(solution)/shard_map/ppermute | solution.py:704
  10.8 1.2 collective-permute-start
  12.0 4.5 %collective-permute-start.1 = (bf16[2,2,8192]{2,1,0:T(2,128)(2,1)S(1)}, bf16[2,2,8192]{2,1,0:T(2,128)(2,1)S(1)}, u32[]{:S(2)}, u32[]{:S(2)}) collective-permute-start(bf16[2,2,8192]{2,1,0:T(2,128)(2,1)S(1)} %join.3.own), channel_id=1, source_target_pairs={{0,2},{2,0},{4,6},{6,4},{1,3},{3,1},{5,7},{7,5},{8,10},{10,8},{12,... | collective-permute-start | bytes 196616 | tf_op jit(solution)/shard_map/ppermute | solution.py:720
  16.5 8.8 %collective-permute-start.2 = (bf16[4,2,8192]{2,1,0:T(2,128)(2,1)S(1)}, bf16[4,2,8192]{2,1,0:T(2,128)(2,1)S(1)}, u32[]{:S(2)}, u32[]{:S(2)}) collective-permute-start(bf16[4,2,8192]{2,1,0:T(2,128)(2,1)S(1)} %join.4.own), channel_id=1, source_target_pairs={{0,4},{2,6},{4,0},{6,2},{1,5},{3,7},{5,1},{7,3},{8,12},{10,14},{12... | collective-permute-start | bytes 393224 | tf_op jit(solution)/shard_map/ppermute | solution.py:720
  28.3 17.1 %collective-permute-start.8 = (bf16[240,1024]{1,0:T(8,128)(2,1)S(1)}, bf16[240,1024]{1,0:T(8,128)(2,1)S(1)}, u32[]{:S(2)}, u32[]{:S(2)}) collective-permute-start(bf16[240,1024]{1,0:T(8,128)(2,1)S(1)} %get-tuple-element.78), channel_id=1, source_target_pairs={{8,0},{24,8},{16,24},{0,16},{9,1},{25,9},{17,25},{1,17},{10,2},{26... | collective-permute-start | bytes 1474568 | tf_op jit(solution)/shard_map/ppermute | solution.py:705
  29.8 15.5 %collective-permute-start.7 = (bf16[240,1024]{1,0:T(8,128)(2,1)S(1)}, bf16[240,1024]{1,0:T(8,128)(2,1)S(1)}, u32[]{:S(2)}, u32[]{:S(2)}) collective-permute-start(bf16[240,1024]{1,0:T(8,128)(2,1)S(1)} %get-tuple-element.73.refs_3_), channel_id=1, source_target_pairs={{0,8},{8,24},{24,16},{16,0},{1,9},{9,25},{25,17},{17,1},{2,10},{10... | collective-permute-start | bytes 1474568 | tf_op jit(solution)/shard_map/ppermute | solution.py:704
  34.8 50.6 %copy-start.35 = (bf16[16,256]{1,0:T(8,128)(2,1)}, bf16[16,256]{1,0:T(8,128)(2,1)S(1)}, u32[]{:S(2)}) copy-start(bf16[16,256]{1,0:T(8,128)(2,1)S(1)} %get-tuple-element.95.refs_7_.refs_0_) | copy-start | bytes 24580
  37.6 17.1 %collective-permute-start.10 = (bf16[240,1024]{1,0:T(8,128)(2,1)S(1)}, bf16[240,1024]{1,0:T(8,128)(2,1)S(1)}, u32[]{:S(2)}, u32[]{:S(2)}) collective-permute-start(bf16[240,1024]{1,0:T(8,128)(2,1)S(1)} %get-tuple-element.81), channel_id=1, source_target_pairs={{8,0},{24,8},{16,24},{0,16},{9,1},{25,9},{17,25},{1,17},{10,2},{26... | collective-permute-start | bytes 1474568 | tf_op jit(solution)/shard_map/ppermute | solution.py:705
  39.2 15.5 %collective-permute-start.9 = (bf16[240,1024]{1,0:T(8,128)(2,1)S(1)}, bf16[240,1024]{1,0:T(8,128)(2,1)S(1)}, u32[]{:S(2)}, u32[]{:S(2)}) collective-permute-start(bf16[240,1024]{1,0:T(8,128)(2,1)S(1)} %get-tuple-element.76.refs_4_), channel_id=1, source_target_pairs={{0,8},{8,24},{24,16},{16,0},{1,9},{9,25},{25,17},{17,1},{2,10},{10... | collective-permute-start | bytes 1474568 | tf_op jit(solution)/shard_map/ppermute | solution.py:704
  48.1 17.1 %collective-permute-start.12 = (bf16[240,1024]{1,0:T(8,128)(2,1)S(1)}, bf16[240,1024]{1,0:T(8,128)(2,1)S(1)}, u32[]{:S(2)}, u32[]{:S(2)}) collective-permute-start(bf16[240,1024]{1,0:T(8,128)(2,1)S(1)} %get-tuple-element.84), channel_id=1, source_target_pairs={{8,0},{24,8},{16,24},{0,16},{9,1},{25,9},{17,25},{1,17},{10,2},{26... | collective-permute-start | bytes 1474568 | tf_op jit(solution)/shard_map/ppermute | solution.py:705
  49.8 15.4 %collective-permute-start.11 = (bf16[240,1024]{1,0:T(8,128)(2,1)S(1)}, bf16[240,1024]{1,0:T(8,128)(2,1)S(1)}, u32[]{:S(2)}, u32[]{:S(2)}) collective-permute-start(bf16[240,1024]{1,0:T(8,128)(2,1)S(1)} %get-tuple-element.79.refs_4_), channel_id=1, source_target_pairs={{0,8},{8,24},{24,16},{16,0},{1,9},{9,25},{25,17},{17,1},{2,10},{10... | collective-permute-start | bytes 1474568 | tf_op jit(solution)/shard_map/ppermute | solution.py:704
  54.6 30.8 %copy-start.37 = (bf16[16,256]{1,0:T(8,128)(2,1)}, bf16[16,256]{1,0:T(8,128)(2,1)S(1)}, u32[]{:S(2)}) copy-start(bf16[16,256]{1,0:T(8,128)(2,1)S(1)} %get-tuple-element.97.refs_9_.refs_2_) | copy-start | bytes 24580
  57.4 17.1 %collective-permute-start.14 = (bf16[240,1024]{1,0:T(8,128)(2,1)S(1)}, bf16[240,1024]{1,0:T(8,128)(2,1)S(1)}, u32[]{:S(2)}, u32[]{:S(2)}) collective-permute-start(bf16[240,1024]{1,0:T(8,128)(2,1)S(1)} %get-tuple-element.87), channel_id=1, source_target_pairs={{8,0},{24,8},{16,24},{0,16},{9,1},{25,9},{17,25},{1,17},{10,2},{26... | collective-permute-start | bytes 1474568 | tf_op jit(solution)/shard_map/ppermute | solution.py:705
  59.1 15.8 %collective-permute-start.13 = (bf16[240,1024]{1,0:T(8,128)(2,1)S(1)}, bf16[240,1024]{1,0:T(8,128)(2,1)S(1)}, u32[]{:S(2)}, u32[]{:S(2)}) collective-permute-start(bf16[240,1024]{1,0:T(8,128)(2,1)S(1)} %get-tuple-element.82.refs_4_), channel_id=1, source_target_pairs={{0,8},{8,24},{24,16},{16,0},{1,9},{9,25},{25,17},{17,1},{2,10},{10... | collective-permute-start | bytes 1474568 | tf_op jit(solution)/shard_map/ppermute | solution.py:704
  65.2 20.2 %copy-start.31 = (bf16[16,384]{1,0:T(8,128)(2,1)}, bf16[16,384]{1,0:T(8,128)(2,1)S(1)}, u32[]{:S(2)}) copy-start(bf16[16,384]{1,0:T(8,128)(2,1)S(1)} %get-tuple-element.98.refs_10_.refs_3_) | copy-start | bytes 36868
  68.0 17.4 %collective-permute-start.19 = (bf16[240,1024]{1,0:T(8,128)(2,1)S(1)}, bf16[240,1024]{1,0:T(8,128)(2,1)S(1)}, u32[]{:S(2)}, u32[]{:S(2)}) collective-permute-start(bf16[240,1024]{1,0:T(8,128)(2,1)S(1)} %get-tuple-element.94), channel_id=1, source_target_pairs={{8,0},{24,8},{16,24},{0,16},{9,1},{25,9},{17,25},{1,17},{10,2},{26... | collective-permute-start | bytes 1474568 | tf_op jit(solution)/shard_map/ppermute | solution.py:705
  69.7 15.7 %collective-permute-start.18 = (bf16[240,1024]{1,0:T(8,128)(2,1)S(1)}, bf16[240,1024]{1,0:T(8,128)(2,1)S(1)}, u32[]{:S(2)}, u32[]{:S(2)}) collective-permute-start(bf16[240,1024]{1,0:T(8,128)(2,1)S(1)} %get-tuple-element.85.refs_4_), channel_id=1, source_target_pairs={{0,8},{8,24},{24,16},{16,0},{1,9},{9,25},{25,17},{17,1},{2,10},{10... | collective-permute-start | bytes 1474568 | tf_op jit(solution)/shard_map/ppermute | solution.py:704
  74.5 11.0 %copy-start.39 = (bf16[16,256]{1,0:T(8,128)(2,1)}, bf16[16,256]{1,0:T(8,128)(2,1)S(1)}, u32[]{:S(2)}) copy-start(bf16[16,256]{1,0:T(8,128)(2,1)S(1)} %get-tuple-element.99.refs_11_.refs_4_) | copy-start | bytes 24580
  77.6 17.3 %collective-permute-start.16 = (bf16[240,1024]{1,0:T(8,128)(2,1)S(1)}, bf16[240,1024]{1,0:T(8,128)(2,1)S(1)}, u32[]{:S(2)}, u32[]{:S(2)}) collective-permute-start(bf16[240,1024]{1,0:T(8,128)(2,1)S(1)} %get-tuple-element.90), channel_id=1, source_target_pairs={{8,0},{24,8},{16,24},{0,16},{9,1},{25,9},{17,25},{1,17},{10,2},{26... | collective-permute-start | bytes 1474568 | tf_op jit(solution)/shard_map/ppermute | solution.py:705
  79.1 16.8 %collective-permute-start.15 = (bf16[240,1024]{1,0:T(8,128)(2,1)S(1)}, bf16[240,1024]{1,0:T(8,128)(2,1)S(1)}, u32[]{:S(2)}, u32[]{:S(2)}) collective-permute-start(bf16[240,1024]{1,0:T(8,128)(2,1)S(1)} %get-tuple-element.88.refs_4_), channel_id=1, source_target_pairs={{0,8},{8,24},{24,16},{16,0},{1,9},{9,25},{25,17},{17,1},{2,10},{10... | collective-permute-start | bytes 1474568 | tf_op jit(solution)/shard_map/ppermute | solution.py:704
  88.0 21.3 %collective-permute-start.20 = (bf16[304,1024]{1,0:T(8,128)(2,1)}, bf16[304,1024]{1,0:T(8,128)(2,1)S(1)}, u32[]{:S(2)}, u32[]{:S(2)}) collective-permute-start(bf16[304,1024]{1,0:T(8,128)(2,1)} %get-tuple-element.101), channel_id=1, source_target_pairs={{0,8},{8,24},{24,16},{16,0},{1,9},{9,25},{25,17},{17,1},{2,10},{10... | collective-permute-start | bytes 1867784 | tf_op jit(solution)/shard_map/ppermute | solution.py:704
  89.1 18.4 %collective-permute-start.21 = (bf16[288,1024]{1,0:T(8,128)(2,1)}, bf16[288,1024]{1,0:T(8,128)(2,1)S(1)}, u32[]{:S(2)}, u32[]{:S(2)}) collective-permute-start(bf16[288,1024]{1,0:T(8,128)(2,1)} %get-tuple-element.102), channel_id=1, source_target_pairs={{8,0},{24,8},{16,24},{0,16},{9,1},{25,9},{17,25},{1,17},{10,2},{26... | collective-permute-start | bytes 1769480 | tf_op jit(solution)/shard_map/ppermute | solution.py:705
  98.3 19.9 %collective-permute-start.24 = (bf16[240,1024]{1,0:T(8,128)(2,1)}, bf16[240,1024]{1,0:T(8,128)(2,1)}, u32[]{:S(2)}, u32[]{:S(2)}) collective-permute-start(bf16[240,1024]{1,0:T(8,128)(2,1)} %get-tuple-element.106), channel_id=1, source_target_pairs={{8,0},{24,8},{16,24},{0,16},{9,1},{25,9},{17,25},{1,17},{10,2},{26... | collective-permute-start | bytes 1474568 | tf_op jit(solution)/shard_map/ppermute | solution.py:705
  100.0 20.0 %collective-permute-start.23 = (bf16[240,1024]{1,0:T(8,128)(2,1)}, bf16[240,1024]{1,0:T(8,128)(2,1)}, u32[]{:S(2)}, u32[]{:S(2)}) collective-permute-start(bf16[240,1024]{1,0:T(8,128)(2,1)} %get-tuple-element.91.refs_1_), channel_id=1, source_target_pairs={{0,8},{8,24},{24,16},{16,0},{1,9},{9,25},{25,17},{17,1},{2,10},{10... | collective-permute-start | bytes 1474568 | tf_op jit(solution)/shard_map/ppermute | solution.py:704
  102.0 9.8 %copy-start.26 = (f32[8,4096]{1,0:T(8,128)}, f32[8,4096]{1,0:T(8,128)S(1)}, u32[]{:S(2)}) copy-start(f32[8,4096]{1,0:T(8,128)S(1)} %get-tuple-element.92.refs_6_.refs_0_) | copy-start | bytes 393220
  102.0 11.9 %collective-permute-start.17 = (f32[8,4096]{1,0:T(8,128)}, f32[8,4096]{1,0:T(8,128)}, u32[]{:S(2)}, u32[]{:S(2)}) collective-permute-start(f32[8,4096]{1,0:T(8,128)} %get-tuple-element.93), channel_id=1, source_target_pairs={{0,4},{2,6},{4,0},{6,2},{1,5},{3,7},{5,1},{7,3},{8,12},{10,14},{12... | collective-permute-start | bytes 393224 | tf_op jit(solution)/shard_map/ppermute | solution.py:402
  107.5 29.4 %copy-start.1 = (bf16[288,1024]{1,0:T(8,128)(2,1)}, bf16[288,1024]{1,0:T(8,128)(2,1)S(1)}, u32[]{:S(2)}) copy-start(bf16[288,1024]{1,0:T(8,128)(2,1)S(1)} %collective-permute-done.21.refs_5_.refs_8_) | copy-start | bytes 1769476
  109.3 27.6 %copy-start = (bf16[304,1024]{1,0:T(8,128)(2,1)}, bf16[304,1024]{1,0:T(8,128)(2,1)S(1)}, u32[]{:S(2)}) copy-start(bf16[304,1024]{1,0:T(8,128)(2,1)S(1)} %collective-permute-done.20.refs_4_.refs_6_) | copy-start | bytes 1867780
  111.8 20.7 %collective-permute-start.26 = (bf16[288,1024]{1,0:T(8,128)(2,1)}, bf16[288,1024]{1,0:T(8,128)(2,1)S(1)}, u32[]{:S(2)}, u32[]{:S(2)}) collective-permute-start(bf16[288,1024]{1,0:T(8,128)(2,1)} %get-tuple-element.103.refs_2_), channel_id=1, source_target_pairs={{0,8},{8,24},{24,16},{16,0},{1,9},{9,25},{25,17},{17,1},{2,10},{10... | collective-permute-start | bytes 1769480 | tf_op jit(solution)/shard_map/ppermute | solution.py:704
  112.5 18.0 %collective-permute-start.27 = (bf16[240,1024]{1,0:T(8,128)(2,1)}, bf16[240,1024]{1,0:T(8,128)(2,1)}, u32[]{:S(2)}, u32[]{:S(2)}) collective-permute-start(bf16[240,1024]{1,0:T(8,128)(2,1)} %get-tuple-element.110), channel_id=1, source_target_pairs={{8,0},{24,8},{16,24},{0,16},{9,1},{25,9},{17,25},{1,17},{10,2},{26... | collective-permute-start | bytes 1474568 | tf_op jit(solution)/shard_map/ppermute | solution.py:705
  116.3 5.7 %copy-start.28 = (f32[4,4096]{1,0:T(4,128)}, f32[4,4096]{1,0:T(4,128)S(1)}, u32[]{:S(2)}) copy-start(f32[4,4096]{1,0:T(4,128)S(1)} %get-tuple-element.104.refs_6_.refs_0_) | copy-start | bytes 196612
  122.1 21.2 %collective-permute-start.29 = (bf16[240,1024]{1,0:T(8,128)(2,1)}, bf16[240,1024]{1,0:T(8,128)(2,1)}, u32[]{:S(2)}, u32[]{:S(2)}) collective-permute-start(bf16[240,1024]{1,0:T(8,128)(2,1)} %get-tuple-element.114), channel_id=1, source_target_pairs={{8,0},{24,8},{16,24},{0,16},{9,1},{25,9},{17,25},{1,17},{10,2},{26... | collective-permute-start | bytes 1474568 | tf_op jit(solution)/shard_map/ppermute | solution.py:705
  123.8 19.5 %collective-permute-start.28 = (bf16[240,1024]{1,0:T(8,128)(2,1)}, bf16[240,1024]{1,0:T(8,128)(2,1)}, u32[]{:S(2)}, u32[]{:S(2)}) collective-permute-start(bf16[240,1024]{1,0:T(8,128)(2,1)} %get-tuple-element.107.refs_2_), channel_id=1, source_target_pairs={{0,8},{8,24},{24,16},{16,0},{1,9},{9,25},{25,17},{17,1},{2,10},{10... | collective-permute-start | bytes 1474568 | tf_op jit(solution)/shard_map/ppermute | solution.py:704
  124.1 4.6 %collective-permute-start.22 = (f32[4,4096]{1,0:T(4,128)}, f32[4,4096]{1,0:T(4,128)}, u32[]{:S(2)}, u32[]{:S(2)}) collective-permute-start(f32[4,4096]{1,0:T(4,128)} %get-tuple-element.105), channel_id=1, source_target_pairs={{0,2},{2,0},{4,6},{6,4},{1,3},{3,1},{5,7},{7,5},{8,10},{10,8},{12,... | collective-permute-start | bytes 196616 | tf_op jit(solution)/shard_map/ppermute | solution.py:402
  130.4 12.2 %collective-permute-start.25 = (f32[2,4096]{1,0:T(2,128)S(1)}, f32[2,4096]{1,0:T(2,128)S(1)}, u32[]{:S(2)}, u32[]{:S(2)}) collective-permute-start(f32[2,4096]{1,0:T(2,128)S(1)} %get-tuple-element.109), channel_id=1, source_target_pairs={{0,1},{1,0},{2,3},{3,2},{4,5},{5,4},{6,7},{7,6},{8,9},{9,8},{10,11... | collective-permute-start | bytes 98312 | tf_op jit(solution)/shard_map/ppermute | solution.py:402
  134.8 30.5 %collective-permute-start.33 = (bf16[240,1024]{1,0:T(8,128)(2,1)S(1)}, bf16[240,1024]{1,0:T(8,128)(2,1)S(1)}, u32[]{:S(2)}, u32[]{:S(2)}) collective-permute-start(bf16[240,1024]{1,0:T(8,128)(2,1)S(1)} %get-tuple-element.121), channel_id=1, source_target_pairs={{8,0},{24,8},{16,24},{0,16},{9,1},{25,9},{17,25},{1,17},{10,2},{26... | collective-permute-start | bytes 1474568 | tf_op jit(solution)/shard_map/ppermute | solution.py:705
  136.8 28.5 %collective-permute-start.32 = (bf16[240,1024]{1,0:T(8,128)(2,1)S(1)}, bf16[240,1024]{1,0:T(8,128)(2,1)S(1)}, u32[]{:S(2)}, u32[]{:S(2)}) collective-permute-start(bf16[240,1024]{1,0:T(8,128)(2,1)S(1)} %get-tuple-element.111.refs_2_.refs_9_), channel_id=1, source_target_pairs={{0,8},{8,24},{24,16},{16,0},{1,9},{9,25},{25,17},{17,1},{2,10},{10... | collective-permute-start | bytes 1474568 | tf_op jit(solution)/shard_map/ppermute | solution.py:704
  137.6 4.8 %copy-start.4 = (bf16[240,1024]{1,0:T(8,128)(2,1)S(1)}, bf16[240,1024]{1,0:T(8,128)(2,1)}, u32[]{:S(2)}) copy-start(bf16[240,1024]{1,0:T(8,128)(2,1)} %copy-done.3) | copy-start | bytes 1474564
  137.6 4.8 %copy-start.6 = (bf16[240,1024]{1,0:T(8,128)(2,1)S(1)}, bf16[240,1024]{1,0:T(8,128)(2,1)}, u32[]{:S(2)}) copy-start(bf16[240,1024]{1,0:T(8,128)(2,1)} %copy-done.5) | copy-start | bytes 1474564
  137.7 4.7 %copy-start.8 = (bf16[240,1024]{1,0:T(8,128)(2,1)S(1)}, bf16[240,1024]{1,0:T(8,128)(2,1)}, u32[]{:S(2)}) copy-start(bf16[240,1024]{1,0:T(8,128)(2,1)} %copy-done.7) | copy-start | bytes 1474564
  146.2 19.2 %collective-permute-start.31 = (bf16[240,1024]{1,0:T(8,128)(2,1)S(1)}, bf16[240,1024]{1,0:T(8,128)(2,1)S(1)}, u32[]{:S(2)}, u32[]{:S(2)}) collective-permute-start(bf16[240,1024]{1,0:T(8,128)(2,1)S(1)} %get-tuple-element.120), channel_id=1, source_target_pairs={{8,0},{24,8},{16,24},{0,16},{9,1},{25,9},{17,25},{1,17},{10,2},{26... | collective-permute-start | bytes 1474568 | tf_op jit(solution)/shard_map/ppermute | solution.py:705
  148.4 17.1 %collective-permute-start.30 = (bf16[240,1024]{1,0:T(8,128)(2,1)S(1)}, bf16[240,1024]{1,0:T(8,128)(2,1)S(1)}, u32[]{:S(2)}, u32[]{:S(2)}) collective-permute-start(bf16[240,1024]{1,0:T(8,128)(2,1)S(1)} %get-tuple-element.119.refs_6_), channel_id=1, source_target_pairs={{0,8},{8,24},{24,16},{16,0},{1,9},{9,25},{25,17},{17,1},{2,10},{10... | collective-permute-start | bytes 1474568 | tf_op jit(solution)/shard_map/ppermute | solution.py:704
  151.2 14.0 %copy-start.23 = (bf16[240,1024]{1,0:T(8,128)(2,1)S(1)}, bf16[240,1024]{1,0:T(8,128)(2,1)}, u32[]{:S(2)}) copy-start(bf16[240,1024]{1,0:T(8,128)(2,1)} %copy-done.22) | copy-start | bytes 1474564
  (29 other events, 89.5 us)

commit v4 on v3

--- a/solution.py
+++ b/solution.py
@@ -10,10 +10,10 @@
 BF16, F32 = jnp.bfloat16, jnp.float32
 SUM_AFTER = 1
 LAG = 2
-MOST_CHUNKS = 24
+MOST_CHUNKS = 20
 TILE = 16
 BUFFERS = 3
-PIECES = 6
+PIECES = 4
 FETCHED = 4
 VMEM = 50 << 20
 

time: 167 us -> 167 us (level)
  waiting for transfers between devices: 30.6 us -> 38.7 us
  starting transfers between devices: 40.2 us -> 35.2 us
  Pallas kernels: 89.2 us -> 85.9 us
    ppermute x14 -> x12, waiting for transfers between devices: 7.05 us -> 15.7 us  [send(): lax.ppermute(sends[-1][0], 'replica', forward)]
    ppermute x14 -> x12, starting transfers between devices: 24.8 us -> 20.7 us  [send(): lax.ppermute(sends[-1][1], 'replica', backward)]
    pallas_call x6 -> x4, Pallas kernels: 30.4 us -> 26.7 us  [layer(): pl.pallas_call(functools.partial(layer_body, resumed=resumed, tile=tile,...]
    ppermute x14 -> x12, starting transfers between devices: 8.15 us -> 5.18 us  [send(): lax.ppermute(sends[-1][0], 'replica', forward)]
    ppermute x3, starting transfers between devices: 2.22 us -> 4.24 us  [advance(): self.arrived = (lax.ppermute(sent, axis, route),)]
    ppermute x14 -> x12, waiting for transfers between devices: 11.6 us -> 11.1 us  [send(): lax.ppermute(sends[-1][1], 'replica', backward)]
    pallas_call x14 -> x12, Pallas kernels: 35 us -> 34.6 us  [pack(): pl.pallas_call(functools.partial(pack_body, n=n, places=places, chunk=chu...]
  transfers between devices with their start and end apart: 34 -> 30, of which waited for: 12 -> 13; matrix products, arithmetic and copies ran while one was open for 0% -> 0% of each run, Pallas kernels for 52% -> 50%
where the time goes in v4:
time: 167 us; the launch traced here: 165 us
  Pallas kernels  85.9 us (51%)
  waiting for transfers between devices  38.7 us (23%)
  starting transfers between devices  35.2 us (21%)
  local copies, waits for them, and re-layouts  3.58 us (2%)
  between operations  2.11 us (1%)
    pallas_call x12, Pallas kernels, pack(): pl.pallas_call(functools.partial(pack_body, n=n, places=places, chunk=chu...  34.6 us
    pallas_call x4, Pallas kernels, layer(): pl.pallas_call(functools.partial(layer_body, resumed=resumed, tile=tile,...  26.7 us
    ppermute x12, starting transfers between devices, send(): lax.ppermute(sends[-1][1], 'replica', backward)  20.7 us
    pallas_call x2, Pallas kernels, update(): pl.pallas_call(functools.partial(update_body, n=n, block=block, first=fir...  19.3 us
    ppermute x12, waiting for transfers between devices, send(): lax.ppermute(sends[-1][0], 'replica', forward)  15.7 us
    ppermute x12, waiting for transfers between devices, send(): lax.ppermute(sends[-1][1], 'replica', backward)  11.1 us
    ppermute x3, waiting for transfers between devices, per_device(): other = lax.ppermute(both, axis, [(i, i ^ apart) for i in range(size)])  8.85 us
    ppermute x12, starting transfers between devices, send(): lax.ppermute(sends[-1][0], 'replica', forward)  5.18 us
  transfers between devices with their start and end apart: 30, of which 13 were waited for; matrix products, arithmetic and copies ran while one was open for 0% of the time, Pallas kernels for 50%

profile of v4, /device:TPU:0, one launch (start us, length us, event | category | flops | bytes accessed | tf_op | source)
XLA Modules:
  0.0 165.5 jit_solution(17167793463187661171)
XLA Ops:
  0.7 2.8 %pack.12 = (bf16[288,1024]{1,0:T(8,128)(2,1)S(1)}, bf16[288,1024]{1,0:T(8,128)(2,1)S(1)}) custom-call(f32[2,1920,1024]{2,1,0:T(8,128)} %refs_0_.25, f32[2,1920,1024]{2,1,0:T(8,128)} %refs_1_.35, f32[2,1920,1024]{2,1,0:T(8,128)} %refs_2_.35), custom_call_target="tpu_custom_call" | custom-call | bytes 3538944 | tf_op jit(solution)/shard_map/pack/pallas_call | solution.py:200
  3.4 3.0 %collective-permute-start.4 = (bf16[288,1024]{1,0:T(8,128)(2,1)S(1)}, bf16[288,1024]{1,0:T(8,128)(2,1)S(1)}, u32[]{:S(2)}, u32[]{:S(2)}) collective-permute-start(bf16[288,1024]{1,0:T(8,128)(2,1)S(1)} %get-tuple-element.64), channel_id=1, source_target_pairs={{8,0},{24,8},{16,24},{0,16},{9,1},{25,9},{17,25},{1,17},{10,2},{26... | collective-permute-start | bytes 1769480 | tf_op jit(solution)/shard_map/ppermute | solution.py:705
  6.5 2.8 %pack.13 = (bf16[288,1024]{1,0:T(8,128)(2,1)S(1)}, bf16[288,1024]{1,0:T(8,128)(2,1)S(1)}) custom-call(f32[2,1920,1024]{2,1,0:T(8,128)} %refs_0_.25, f32[2,1920,1024]{2,1,0:T(8,128)} %refs_1_.35, f32[2,1920,1024]{2,1,0:T(8,128)} %refs_2_.35, bf16[1,2,8192]{2,1,0:T(2,128)(2,1)S(1)} %beside.1.refs_3_.own), custom_call_target="tpu_custom_call" | custom-call | bytes 3538944 | tf_op jit(solution)/shard_map/pack/pallas_call | solution.py:200
  9.3 2.0 %collective-permute-start.6 = (bf16[288,1024]{1,0:T(8,128)(2,1)S(1)}, bf16[288,1024]{1,0:T(8,128)(2,1)S(1)}, u32[]{:S(2)}, u32[]{:S(2)}) collective-permute-start(bf16[288,1024]{1,0:T(8,128)(2,1)S(1)} %get-tuple-element.67), channel_id=1, source_target_pairs={{8,0},{24,8},{16,24},{0,16},{9,1},{25,9},{17,25},{1,17},{10,2},{26... | collective-permute-start | bytes 1769480 | tf_op jit(solution)/shard_map/ppermute | solution.py:705
  11.4 1.2 collective-permute-done.other
  12.6 2.1 %collective-permute-start.1 = (bf16[2,2,8192]{2,1,0:T(2,128)(2,1)S(1)}, bf16[2,2,8192]{2,1,0:T(2,128)(2,1)S(1)}, u32[]{:S(2)}, u32[]{:S(2)}) collective-permute-start(bf16[2,2,8192]{2,1,0:T(2,128)(2,1)S(1)} %join.3.own), channel_id=1, source_target_pairs={{0,2},{2,0},{4,6},{6,4},{1,3},{3,1},{5,7},{7,5},{8,10},{10,8},{12,... | collective-permute-start | bytes 196616 | tf_op jit(solution)/shard_map/ppermute | solution.py:720
  14.7 2.4 %collective-permute-done.1.other = bf16[2,2,8192]{2,1,0:T(2,128)(2,1)S(1)} collective-permute-done((bf16[2,2,8192]{2,1,0:T(2,128)(2,1)S(1)}, bf16[2,2,8192]{2,1,0:T(2,128)(2,1)S(1)}, u32[]{:S(2)}, u32[]{:S(2)}) %collective-permute-start.1) | collective-permute-done | bytes 65568 | tf_op jit(solution)/shard_map/ppermute | solution.py:720
  17.1 2.9 %collective-permute-start.2 = (bf16[4,2,8192]{2,1,0:T(2,128)(2,1)S(1)}, bf16[4,2,8192]{2,1,0:T(2,128)(2,1)S(1)}, u32[]{:S(2)}, u32[]{:S(2)}) collective-permute-start(bf16[4,2,8192]{2,1,0:T(2,128)(2,1)S(1)} %join.4.own), channel_id=1, source_target_pairs={{0,4},{2,6},{4,0},{6,2},{1,5},{3,7},{5,1},{7,3},{8,12},{10,14},{12... | collective-permute-start | bytes 393224 | tf_op jit(solution)/shard_map/ppermute | solution.py:720
  20.7 5.2 %collective-permute-done.2.other = bf16[4,2,8192]{2,1,0:T(2,128)(2,1)S(1)} collective-permute-done((bf16[4,2,8192]{2,1,0:T(2,128)(2,1)S(1)}, bf16[4,2,8192]{2,1,0:T(2,128)(2,1)S(1)}, u32[]{:S(2)}, u32[]{:S(2)}) %collective-permute-start.2) | collective-permute-done | bytes 131104 | tf_op jit(solution)/shard_map/ppermute | solution.py:720
  26.1 3.1 %pack.14 = (bf16[288,1024]{1,0:T(8,128)(2,1)S(1)}, bf16[288,1024]{1,0:T(8,128)(2,1)S(1)}) custom-call(s32[1]{0:T(128)S(6)} %copy.43.refs_0_.failed, f32[2,1920,1024]{2,1,0:T(8,128)} %refs_0_.25, f32[2,1920,1024]{2,1,0:T(8,128)} %refs_1_.35, f32[2,1920,1024]{2,1,0:T(8,128)} %refs_2_.35, bf16[288,1024]{1,0:T(8,128)(2,1)S(1)} %collective-permute-done.3.refs_4_.refs_0_, ...), custom_call_target="tpu_custom_call" | custom-call | bytes 3538944 | tf_op jit(solution)/shard_map/pack/pallas_call | solution.py:200
  29.3 1.6 collective-permute-start.8
  31.3 5.7 %layer.4 = (bf16[16,384]{1,0:T(8,128)(2,1)S(1)}, f32[16,4096]{1,0:T(8,128)S(1)}) custom-call(bf16[16,8192]{1,0:T(8,128)(2,1)S(1)} %join.5.refs_6_.both, bf16[4096,1920]{1,0:T(8,128)(2,1)} %refs_0_.23, bf16[4096,1920]{1,0:T(8,128)(2,1)} %refs_1_.27, bf16[1920,4096]{1,0:T(8,128)(2,1)} %refs_2_.27, bf16[288,1024]{1,0:T(8,128)(2,1)S(1)} %get-tuple-element.65.refs_3_), custom_call_target="tpu_custom_call" | custom-call | flops 251658240 | bytes 9437184 | tf_op jit(solution)/shard_map/layer/pallas_call | solution.py:329
  37.1 3.1 %pack.15 = (bf16[288,1024]{1,0:T(8,128)(2,1)S(1)}, bf16[288,1024]{1,0:T(8,128)(2,1)S(1)}) custom-call(s32[1]{0:T(128)S(6)} %copy.43.refs_0_.failed, f32[2,1920,1024]{2,1,0:T(8,128)} %refs_0_.25, f32[2,1920,1024]{2,1,0:T(8,128)} %refs_1_.35, f32[2,1920,1024]{2,1,0:T(8,128)} %refs_2_.35, bf16[288,1024]{1,0:T(8,128)(2,1)S(1)} %collective-permute-done.5.refs_4_.refs_2_, ...), custom_call_target="tpu_custom_call" | custom-call | bytes 3538944 | tf_op jit(solution)/shard_map/pack/pallas_call | solution.py:200
  40.2 1.7 %collective-permute-start.10 = (bf16[288,1024]{1,0:T(8,128)(2,1)S(1)}, bf16[288,1024]{1,0:T(8,128)(2,1)S(1)}, u32[]{:S(2)}, u32[]{:S(2)}) collective-permute-start(bf16[288,1024]{1,0:T(8,128)(2,1)S(1)} %get-tuple-element.73), channel_id=1, source_target_pairs={{8,0},{24,8},{16,24},{0,16},{9,1},{25,9},{17,25},{1,17},{10,2},{26... | collective-permute-start | bytes 1769480 | tf_op jit(solution)/shard_map/ppermute | solution.py:705
  42.3 7.0 %layer.5 = (bf16[16,512]{1,0:T(8,128)(2,1)S(1)}, f32[16,4096]{1,0:T(8,128)S(1)}) custom-call(bf16[16,8192]{1,0:T(8,128)(2,1)S(1)} %join.5.refs_6_.both, bf16[4096,1920]{1,0:T(8,128)(2,1)} %refs_0_.23, bf16[4096,1920]{1,0:T(8,128)(2,1)} %refs_1_.27, bf16[1920,4096]{1,0:T(8,128)(2,1)} %refs_2_.27, f32[16,4096]{1,0:T(8,128)S(1)} %get-tuple-element.66.refs_6_.refs_3_, ...), custom_call_target="tpu_custom_call" | custom-call | flops 335544320 | bytes 12582912 | tf_op jit(solution)/shard_map/layer/pallas_call | solution.py:329
  49.3 3.1 %pack.16 = (bf16[288,1024]{1,0:T(8,128)(2,1)S(1)}, bf16[288,1024]{1,0:T(8,128)(2,1)S(1)}) custom-call(s32[1]{0:T(128)S(6)} %copy.43.refs_0_.failed, f32[2,1920,1024]{2,1,0:T(8,128)} %refs_0_.25, f32[2,1920,1024]{2,1,0:T(8,128)} %refs_1_.35, f32[2,1920,1024]{2,1,0:T(8,128)} %refs_2_.35, bf16[288,1024]{1,0:T(8,128)(2,1)S(1)} %collective-permute-done.7.refs_4_, ...), custom_call_target="tpu_custom_call" | custom-call | bytes 3538944 | tf_op jit(solution)/shard_map/pack/pallas_call | solution.py:200
  52.4 1.8 %collective-permute-start.15 = (bf16[288,1024]{1,0:T(8,128)(2,1)S(1)}, bf16[288,1024]{1,0:T(8,128)(2,1)S(1)}, u32[]{:S(2)}, u32[]{:S(2)}) collective-permute-start(bf16[288,1024]{1,0:T(8,128)(2,1)S(1)} %get-tuple-element.80), channel_id=1, source_target_pairs={{8,0},{24,8},{16,24},{0,16},{9,1},{25,9},{17,25},{1,17},{10,2},{26... | collective-permute-start | bytes 1769480 | tf_op jit(solution)/shard_map/ppermute | solution.py:705
  54.5 7.0 %layer.6 = (bf16[16,512]{1,0:T(8,128)(2,1)S(1)}, f32[16,4096]{1,0:T(8,128)S(1)}) custom-call(bf16[16,8192]{1,0:T(8,128)(2,1)S(1)} %join.5.refs_6_.both, bf16[4096,1920]{1,0:T(8,128)(2,1)} %refs_0_.23, bf16[4096,1920]{1,0:T(8,128)(2,1)} %refs_1_.27, bf16[1920,4096]{1,0:T(8,128)(2,1)} %refs_2_.27, f32[16,4096]{1,0:T(8,128)S(1)} %get-tuple-element.69.refs_6_.refs_3_, ...), custom_call_target="tpu_custom_call" | custom-call | flops 335544320 | bytes 12582912 | tf_op jit(solution)/shard_map/layer/pallas_call | solution.py:329
  61.6 3.1 %pack.17 = (bf16[288,1024]{1,0:T(8,128)(2,1)S(1)}, bf16[288,1024]{1,0:T(8,128)(2,1)S(1)}) custom-call(s32[1]{0:T(128)S(6)} %copy.43.refs_0_.failed, f32[2,1920,1024]{2,1,0:T(8,128)} %refs_0_.25, f32[2,1920,1024]{2,1,0:T(8,128)} %refs_1_.35, f32[2,1920,1024]{2,1,0:T(8,128)} %refs_2_.35, bf16[288,1024]{1,0:T(8,128)(2,1)S(1)} %collective-permute-done.9.refs_4_.refs_6_, ...), custom_call_target="tpu_custom_call" | custom-call | bytes 3538944 | tf_op jit(solution)/shard_map/pack/pallas_call | solution.py:200
  64.7 2.0 %collective-permute-start.12 = (bf16[288,1024]{1,0:T(8,128)(2,1)S(1)}, bf16[288,1024]{1,0:T(8,128)(2,1)S(1)}, u32[]{:S(2)}, u32[]{:S(2)}) collective-permute-start(bf16[288,1024]{1,0:T(8,128)(2,1)S(1)} %get-tuple-element.76), channel_id=1, source_target_pairs={{8,0},{24,8},{16,24},{0,16},{9,1},{25,9},{17,25},{1,17},{10,2},{26... | collective-permute-start | bytes 1769480 | tf_op jit(solution)/shard_map/ppermute | solution.py:705
  66.8 7.0 %layer.7 = (bf16[16,512]{1,0:T(8,128)(2,1)S(1)}, f32[16,4096]{1,0:T(8,128)S(1)}) custom-call(bf16[16,8192]{1,0:T(8,128)(2,1)S(1)} %join.5.refs_6_.both, bf16[4096,1920]{1,0:T(8,128)(2,1)} %refs_0_.23, bf16[4096,1920]{1,0:T(8,128)(2,1)} %refs_1_.27, bf16[1920,4096]{1,0:T(8,128)(2,1)} %refs_2_.27, f32[16,4096]{1,0:T(8,128)S(1)} %get-tuple-element.72.refs_6_.refs_3_, ...), custom_call_target="tpu_custom_call" | custom-call | flops 335544320 | bytes 12582912 | tf_op jit(solution)/shard_map/layer/pallas_call | solution.py:329
  73.8 3.0 %pack.19 = (bf16[352,1024]{1,0:T(8,128)(2,1)}, bf16[336,1024]{1,0:T(8,128)(2,1)}) custom-call(s32[1]{0:T(128)S(6)} %copy.43.refs_0_.failed, f32[2,1920,1024]{2,1,0:T(8,128)} %refs_0_.25, f32[2,1920,1024]{2,1,0:T(8,128)} %refs_1_.35, f32[2,1920,1024]{2,1,0:T(8,128)} %refs_2_.35, bf16[288,1024]{1,0:T(8,128)(2,1)S(1)} %collective-permute-done.14.refs_4_.refs_8_, ...), custom_call_target="tpu_custom_call" | custom-call | bytes 3538944 | tf_op jit(solution)/shard_map/pack/pallas_call | solution.py:200
  76.8 1.6 collective-permute-start.16
  78.9 4.9 %collective-permute-done.12.refs_5_.refs_1_ = bf16[288,1024]{1,0:T(8,128)(2,1)S(1)} collective-permute-done((bf16[288,1024]{1,0:T(8,128)(2,1)S(1)}, bf16[288,1024]{1,0:T(8,128)(2,1)S(1)}, u32[]{:S(2)}, u32[]{:S(2)}) %collective-permute-start.12) | collective-permute-done | bytes 589856 | tf_op jit(solution)/shard_map/ppermute | solution.py:705
  83.8 2.1 %collective-permute-done.11.refs_4_.refs_0_ = bf16[288,1024]{1,0:T(8,128)(2,1)S(1)} collective-permute-done((bf16[288,1024]{1,0:T(8,128)(2,1)S(1)}, bf16[288,1024]{1,0:T(8,128)(2,1)S(1)}, u32[]{:S(2)}, u32[]{:S(2)}) %collective-permute-start.11) | collective-permute-done | bytes 589856 | tf_op jit(solution)/shard_map/ppermute | solution.py:704
  85.9 2.6 %pack.18 = (bf16[288,1024]{1,0:T(8,128)(2,1)}, bf16[288,1024]{1,0:T(8,128)(2,1)}) custom-call(s32[1]{0:T(128)S(6)} %copy.43.refs_0_.failed, f32[2,1920,1024]{2,1,0:T(8,128)} %refs_0_.25, f32[2,1920,1024]{2,1,0:T(8,128)} %refs_1_.35, f32[2,1920,1024]{2,1,0:T(8,128)} %refs_2_.35, bf16[288,1024]{1,0:T(8,128)(2,1)S(1)} %collective-permute-done.11.refs_4_.refs_0_, ...), custom_call_target="tpu_custom_call" | custom-call | bytes 3538944 | tf_op jit(solution)/shard_map/pack/pallas_call | solution.py:200
  88.6 1.5 collective-permute-start.20
  92.3 2.6 %collective-permute-start.13 = (f32[8,4096]{1,0:T(8,128)}, f32[8,4096]{1,0:T(8,128)}, u32[]{:S(2)}, u32[]{:S(2)}) collective-permute-start(f32[8,4096]{1,0:T(8,128)} %get-tuple-element.79), channel_id=1, source_target_pairs={{0,4},{2,6},{4,0},{6,2},{1,5},{3,7},{5,1},{7,3},{8,12},{10,14},{12... | collective-permute-start | bytes 393224 | tf_op jit(solution)/shard_map/ppermute | solution.py:402
  94.9 3.7 %collective-permute-done.17.refs_5_.refs_6_.refs_3_ = bf16[336,1024]{1,0:T(8,128)(2,1)S(1)} collective-permute-done((bf16[336,1024]{1,0:T(8,128)(2,1)}, bf16[336,1024]{1,0:T(8,128)(2,1)S(1)}, u32[]{:S(2)}, u32[]{:S(2)}) %collective-permute-start.17) | collective-permute-done | bytes 688160 | tf_op jit(solution)/shard_map/ppermute | solution.py:705
  98.5 2.8 %collective-permute-done.16.refs_4_.refs_2_ = bf16[352,1024]{1,0:T(8,128)(2,1)S(1)} collective-permute-done((bf16[352,1024]{1,0:T(8,128)(2,1)}, bf16[352,1024]{1,0:T(8,128)(2,1)S(1)}, u32[]{:S(2)}, u32[]{:S(2)}) %collective-permute-start.16) | collective-permute-done | bytes 720928 | tf_op jit(solution)/shard_map/ppermute | solution.py:704
  101.4 2.7 %pack.20 = (bf16[336,1024]{1,0:T(8,128)(2,1)}, bf16[288,1024]{1,0:T(8,128)(2,1)}) custom-call(s32[1]{0:T(128)S(6)} %copy.43.refs_0_.failed, f32[2,1920,1024]{2,1,0:T(8,128)} %refs_0_.25, f32[2,1920,1024]{2,1,0:T(8,128)} %refs_1_.35, f32[2,1920,1024]{2,1,0:T(8,128)} %refs_2_.35, bf16[352,1024]{1,0:T(8,128)(2,1)S(1)} %collective-permute-done.16.refs_4_.refs_2_, ...), custom_call_target="tpu_custom_call" | custom-call | bytes 3538944 | tf_op jit(solution)/shard_map/pack/pallas_call | solution.py:200
  104.2 2.0 %collective-permute-start.23 = (bf16[288,1024]{1,0:T(8,128)(2,1)}, bf16[288,1024]{1,0:T(8,128)(2,1)}, u32[]{:S(2)}, u32[]{:S(2)}) collective-permute-start(bf16[288,1024]{1,0:T(8,128)(2,1)} %get-tuple-element.94), channel_id=1, source_target_pairs={{8,0},{24,8},{16,24},{0,16},{9,1},{25,9},{17,25},{1,17},{10,2},{26... | collective-permute-start | bytes 1769480 | tf_op jit(solution)/shard_map/ppermute | solution.py:705
  107.1 1.6 halve.5
  108.6 2.5 %collective-permute-done.20.refs_5_ = bf16[288,1024]{1,0:T(8,128)(2,1)S(1)} collective-permute-done((bf16[288,1024]{1,0:T(8,128)(2,1)}, bf16[288,1024]{1,0:T(8,128)(2,1)S(1)}, u32[]{:S(2)}, u32[]{:S(2)}) %collective-permute-start.20) | collective-permute-done | bytes 589856 | tf_op jit(solution)/shard_map/ppermute | solution.py:705
  111.2 2.8 %collective-permute-done.19.refs_4_ = bf16[288,1024]{1,0:T(8,128)(2,1)S(1)} collective-permute-done((bf16[288,1024]{1,0:T(8,128)(2,1)}, bf16[288,1024]{1,0:T(8,128)(2,1)S(1)}, u32[]{:S(2)}, u32[]{:S(2)}) %collective-permute-start.19) | collective-permute-done | bytes 589856 | tf_op jit(solution)/shard_map/ppermute | solution.py:704
  114.0 2.6 %pack.21 = (bf16[288,1024]{1,0:T(8,128)(2,1)}, bf16[288,1024]{1,0:T(8,128)(2,1)}) custom-call(s32[1]{0:T(128)S(6)} %copy.43.refs_0_.failed, f32[2,1920,1024]{2,1,0:T(8,128)} %refs_0_.25, f32[2,1920,1024]{2,1,0:T(8,128)} %refs_1_.35, f32[2,1920,1024]{2,1,0:T(8,128)} %refs_2_.35, bf16[288,1024]{1,0:T(8,128)(2,1)S(1)} %collective-permute-done.19.refs_4_, ...), custom_call_target="tpu_custom_call" | custom-call | bytes 3538944 | tf_op jit(solution)/shard_map/pack/pallas_call | solution.py:200
  116.7 1.6 collective-permute-start.25
  118.7 1.6 collective-permute-start.18
  120.3 3.0 %collective-permute-done.18.refs_1_ = f32[4,4096]{1,0:T(4,128)} collective-permute-done((f32[4,4096]{1,0:T(4,128)}, f32[4,4096]{1,0:T(4,128)}, u32[]{:S(2)}, u32[]{:S(2)}) %collective-permute-start.18) | collective-permute-done | bytes 65568 | tf_op jit(solution)/shard_map/ppermute | solution.py:402
  125.1 3.6 %collective-permute-done.22.refs_4_.refs_5_.refs_6_ = bf16[336,1024]{1,0:T(8,128)(2,1)S(1)} collective-permute-done((bf16[336,1024]{1,0:T(8,128)(2,1)}, bf16[336,1024]{1,0:T(8,128)(2,1)S(1)}, u32[]{:S(2)}, u32[]{:S(2)}) %collective-permute-start.22) | collective-permute-done | bytes 688160 | tf_op jit(solution)/shard_map/ppermute | solution.py:704
  128.8 3.1 %pack.22 = (bf16[288,1024]{1,0:T(8,128)(2,1)S(1)}, bf16[288,1024]{1,0:T(8,128)(2,1)S(1)}) custom-call(s32[1]{0:T(128)S(6)} %copy.43.refs_0_.failed, f32[2,1920,1024]{2,1,0:T(8,128)} %refs_0_.25, f32[2,1920,1024]{2,1,0:T(8,128)} %refs_1_.35, f32[2,1920,1024]{2,1,0:T(8,128)} %refs_2_.35, bf16[336,1024]{1,0:T(8,128)(2,1)S(1)} %collective-permute-done.22.refs_4_.refs_5_.refs_6_, ...), custom_call_target="tpu_custom_call" | custom-call | bytes 3538944 | tf_op jit(solution)/shard_map/pack/pallas_call | solution.py:200
  131.8 1.1 collective-permute-start.29
  132.9 1.0 collective-permute-start.28
  134.7 4.7 %update.2 = (f32[1920,1024]{1,0:T(8,128)}, f32[1920,1024]{1,0:T(8,128)}, f32[1920,1024]{1,0:T(8,128)}) custom-call(s32[1]{0:T(128)S(6)} %copy.43.refs_0_.failed, bf16[1920,64]{1,0:T(8,128)(2,1)S(1)} %get-tuple-element.96.hid_ref.refs_3_, bf16[64,1024]{1,0:T(8,128)(2,1)S(1)} %get-tuple-element.97.out_ref, f32[2,1920,1024]{2,1,0:T(8,128)} %refs_0_.25, ...), custom_call_target="tpu_custom_call" | custom-call | flops 50331648 | bytes 9437184 | tf_op jit(solution)/shard_map/update/pallas_call | solution.py:523
  142.1 2.8 %pack.23 = (bf16[288,1024]{1,0:T(8,128)(2,1)S(1)}, bf16[288,1024]{1,0:T(8,128)(2,1)S(1)}) custom-call(s32[1]{0:T(128)S(6)} %copy.43.refs_0_.failed, f32[2,1920,1024]{2,1,0:T(8,128)} %refs_0_.25, f32[2,1920,1024]{2,1,0:T(8,128)} %refs_1_.35, f32[2,1920,1024]{2,1,0:T(8,128)} %refs_2_.35, bf16[288,1024]{1,0:T(8,128)(2,1)S(1)} %collective-permute-done.24.refs_4_.refs_8_, ...), custom_call_target="tpu_custom_call" | custom-call | bytes 3538944 | tf_op jit(solution)/shard_map/pack/pallas_call | solution.py:200
  144.9 1.9 %collective-permute-start.27 = (bf16[288,1024]{1,0:T(8,128)(2,1)S(1)}, bf16[288,1024]{1,0:T(8,128)(2,1)S(1)}, u32[]{:S(2)}, u32[]{:S(2)}) collective-permute-start(bf16[288,1024]{1,0:T(8,128)(2,1)S(1)} %get-tuple-element.104), channel_id=1, source_target_pairs={{8,0},{24,8},{16,24},{0,16},{9,1},{25,9},{17,25},{1,17},{10,2},{26... | collective-permute-start | bytes 1769480 | tf_op jit(solution)/shard_map/ppermute | solution.py:705
  147.0 14.6 %update.3 = (f32[1920,1024]{1,0:T(8,128)}, f32[1920,1024]{1,0:T(8,128)}, f32[1920,1024]{1,0:T(8,128)}) custom-call(s32[1]{0:T(128)S(6)} %copy.43.refs_0_.failed, bf16[1920,64]{1,0:T(8,128)(2,1)S(1)} %get-tuple-element.96.hid_ref.refs_3_, bf16[64,1024]{1,0:T(8,128)(2,1)S(1)} %get-tuple-element.97.out_ref, ...), custom_call_target="tpu_custom_call", output_to_operand_aliasing={{0}: (6, {}), {1}: (7, {}), {2}: (8, {})} | custom-call | flops 201326592 | bytes 37748736 | tf_op jit(solution)/shard_map/update/pallas_call | solution.py:523
  161.9 3.3 %collective-permute-done.26.refs_0_ = bf16[288,1024]{1,0:T(8,128)(2,1)S(1)} collective-permute-done((bf16[288,1024]{1,0:T(8,128)(2,1)S(1)}, bf16[288,1024]{1,0:T(8,128)(2,1)S(1)}, u32[]{:S(2)}, u32[]{:S(2)}) %collective-permute-start.26) | collective-permute-done | bytes 589856 | tf_op jit(solution)/shard_map/ppermute | solution.py:704
  (129 shorter events, 11.4 us)
Async XLA Ops:
  0.6 5.9 %copy-start.42 = (bf16[1,2,4096]{2,1,0:T(2,128)(2,1)S(1)}, bf16[1,2,4096]{2,1,0:T(2,128)(2,1)}, u32[]{:S(2)}) copy-start(bf16[1,2,4096]{2,1,0:T(2,128)(2,1)} %param.10) | copy-start | bytes 49156
  0.6 5.9 %copy-start.41 = (bf16[1,2,4096]{2,1,0:T(2,128)(2,1)S(1)}, bf16[1,2,4096]{2,1,0:T(2,128)(2,1)}, u32[]{:S(2)}) copy-start(bf16[1,2,4096]{2,1,0:T(2,128)(2,1)} %param.9) | copy-start | bytes 49156
  3.4 22.7 %collective-permute-start.4 = (bf16[288,1024]{1,0:T(8,128)(2,1)S(1)}, bf16[288,1024]{1,0:T(8,128)(2,1)S(1)}, u32[]{:S(2)}, u32[]{:S(2)}) collective-permute-start(bf16[288,1024]{1,0:T(8,128)(2,1)S(1)} %get-tuple-element.64), channel_id=1, source_target_pairs={{8,0},{24,8},{16,24},{0,16},{9,1},{25,9},{17,25},{1,17},{10,2},{26... | collective-permute-start | bytes 1769480 | tf_op jit(solution)/shard_map/ppermute | solution.py:705
  6.5 19.7 %collective-permute-start.3 = (bf16[288,1024]{1,0:T(8,128)(2,1)S(1)}, bf16[288,1024]{1,0:T(8,128)(2,1)S(1)}, u32[]{:S(2)}, u32[]{:S(2)}) collective-permute-start(bf16[288,1024]{1,0:T(8,128)(2,1)S(1)} %get-tuple-element.62.refs_2_), channel_id=1, source_target_pairs={{0,8},{8,24},{24,16},{16,0},{1,9},{9,25},{25,17},{17,1},{2,10},{10... | collective-permute-start | bytes 1769480 | tf_op jit(solution)/shard_map/ppermute | solution.py:704
  9.3 27.8 %collective-permute-start.6 = (bf16[288,1024]{1,0:T(8,128)(2,1)S(1)}, bf16[288,1024]{1,0:T(8,128)(2,1)S(1)}, u32[]{:S(2)}, u32[]{:S(2)}) collective-permute-start(bf16[288,1024]{1,0:T(8,128)(2,1)S(1)} %get-tuple-element.67), channel_id=1, source_target_pairs={{8,0},{24,8},{16,24},{0,16},{9,1},{25,9},{17,25},{1,17},{10,2},{26... | collective-permute-start | bytes 1769480 | tf_op jit(solution)/shard_map/ppermute | solution.py:705
  11.3 25.7 %collective-permute-start.5 = (bf16[288,1024]{1,0:T(8,128)(2,1)S(1)}, bf16[288,1024]{1,0:T(8,128)(2,1)S(1)}, u32[]{:S(2)}, u32[]{:S(2)}) collective-permute-start(bf16[288,1024]{1,0:T(8,128)(2,1)S(1)} %get-tuple-element.63.refs_0_), channel_id=1, source_target_pairs={{0,8},{8,24},{24,16},{16,0},{1,9},{9,25},{25,17},{17,1},{2,10},{10... | collective-permute-start | bytes 1769480 | tf_op jit(solution)/shard_map/ppermute | solution.py:704
  11.4 1.2 collective-permute-start
  12.6 4.5 %collective-permute-start.1 = (bf16[2,2,8192]{2,1,0:T(2,128)(2,1)S(1)}, bf16[2,2,8192]{2,1,0:T(2,128)(2,1)S(1)}, u32[]{:S(2)}, u32[]{:S(2)}) collective-permute-start(bf16[2,2,8192]{2,1,0:T(2,128)(2,1)S(1)} %join.3.own), channel_id=1, source_target_pairs={{0,2},{2,0},{4,6},{6,4},{1,3},{3,1},{5,7},{7,5},{8,10},{10,8},{12,... | collective-permute-start | bytes 196616 | tf_op jit(solution)/shard_map/ppermute | solution.py:720
  17.1 8.8 %collective-permute-start.2 = (bf16[4,2,8192]{2,1,0:T(2,128)(2,1)S(1)}, bf16[4,2,8192]{2,1,0:T(2,128)(2,1)S(1)}, u32[]{:S(2)}, u32[]{:S(2)}) collective-permute-start(bf16[4,2,8192]{2,1,0:T(2,128)(2,1)S(1)} %join.4.own), channel_id=1, source_target_pairs={{0,4},{2,6},{4,0},{6,2},{1,5},{3,7},{5,1},{7,3},{8,12},{10,14},{12... | collective-permute-start | bytes 393224 | tf_op jit(solution)/shard_map/ppermute | solution.py:720
  29.3 20.0 %collective-permute-start.8 = (bf16[288,1024]{1,0:T(8,128)(2,1)S(1)}, bf16[288,1024]{1,0:T(8,128)(2,1)S(1)}, u32[]{:S(2)}, u32[]{:S(2)}) collective-permute-start(bf16[288,1024]{1,0:T(8,128)(2,1)S(1)} %get-tuple-element.70), channel_id=1, source_target_pairs={{8,0},{24,8},{16,24},{0,16},{9,1},{25,9},{17,25},{1,17},{10,2},{26... | collective-permute-start | bytes 1769480 | tf_op jit(solution)/shard_map/ppermute | solution.py:705
  30.9 18.4 %collective-permute-start.7 = (bf16[288,1024]{1,0:T(8,128)(2,1)S(1)}, bf16[288,1024]{1,0:T(8,128)(2,1)S(1)}, u32[]{:S(2)}, u32[]{:S(2)}) collective-permute-start(bf16[288,1024]{1,0:T(8,128)(2,1)S(1)} %get-tuple-element.65.refs_3_), channel_id=1, source_target_pairs={{0,8},{8,24},{24,16},{16,0},{1,9},{9,25},{25,17},{17,1},{2,10},{10... | collective-permute-start | bytes 1769480 | tf_op jit(solution)/shard_map/ppermute | solution.py:704
  37.0 36.8 %copy-start.39 = (bf16[16,384]{1,0:T(8,128)(2,1)}, bf16[16,384]{1,0:T(8,128)(2,1)S(1)}, u32[]{:S(2)}) copy-start(bf16[16,384]{1,0:T(8,128)(2,1)S(1)} %get-tuple-element.81.refs_7_.refs_0_) | copy-start | bytes 36868
  40.2 21.3 %collective-permute-start.10 = (bf16[288,1024]{1,0:T(8,128)(2,1)S(1)}, bf16[288,1024]{1,0:T(8,128)(2,1)S(1)}, u32[]{:S(2)}, u32[]{:S(2)}) collective-permute-start(bf16[288,1024]{1,0:T(8,128)(2,1)S(1)} %get-tuple-element.73), channel_id=1, source_target_pairs={{8,0},{24,8},{16,24},{0,16},{9,1},{25,9},{17,25},{1,17},{10,2},{26... | collective-permute-start | bytes 1769480 | tf_op jit(solution)/shard_map/ppermute | solution.py:705
  41.9 19.6 %collective-permute-start.9 = (bf16[288,1024]{1,0:T(8,128)(2,1)S(1)}, bf16[288,1024]{1,0:T(8,128)(2,1)S(1)}, u32[]{:S(2)}, u32[]{:S(2)}) collective-permute-start(bf16[288,1024]{1,0:T(8,128)(2,1)S(1)} %get-tuple-element.68.refs_4_), channel_id=1, source_target_pairs={{0,8},{8,24},{24,16},{16,0},{1,9},{9,25},{25,17},{17,1},{2,10},{10... | collective-permute-start | bytes 1769480 | tf_op jit(solution)/shard_map/ppermute | solution.py:704
  52.4 21.3 %collective-permute-start.15 = (bf16[288,1024]{1,0:T(8,128)(2,1)S(1)}, bf16[288,1024]{1,0:T(8,128)(2,1)S(1)}, u32[]{:S(2)}, u32[]{:S(2)}) collective-permute-start(bf16[288,1024]{1,0:T(8,128)(2,1)S(1)} %get-tuple-element.80), channel_id=1, source_target_pairs={{8,0},{24,8},{16,24},{0,16},{9,1},{25,9},{17,25},{1,17},{10,2},{26... | collective-permute-start | bytes 1769480 | tf_op jit(solution)/shard_map/ppermute | solution.py:705
  54.3 19.5 %collective-permute-start.14 = (bf16[288,1024]{1,0:T(8,128)(2,1)S(1)}, bf16[288,1024]{1,0:T(8,128)(2,1)S(1)}, u32[]{:S(2)}, u32[]{:S(2)}) collective-permute-start(bf16[288,1024]{1,0:T(8,128)(2,1)S(1)} %get-tuple-element.71.refs_4_), channel_id=1, source_target_pairs={{0,8},{8,24},{24,16},{16,0},{1,9},{9,25},{25,17},{17,1},{2,10},{10... | collective-permute-start | bytes 1769480 | tf_op jit(solution)/shard_map/ppermute | solution.py:704
  61.5 12.3 %copy-start.35 = (bf16[16,512]{1,0:T(8,128)(2,1)}, bf16[16,512]{1,0:T(8,128)(2,1)S(1)}, u32[]{:S(2)}) copy-start(bf16[16,512]{1,0:T(8,128)(2,1)S(1)} %get-tuple-element.83.refs_9_.refs_2_) | copy-start | bytes 49156
  64.7 19.1 %collective-permute-start.12 = (bf16[288,1024]{1,0:T(8,128)(2,1)S(1)}, bf16[288,1024]{1,0:T(8,128)(2,1)S(1)}, u32[]{:S(2)}, u32[]{:S(2)}) collective-permute-start(bf16[288,1024]{1,0:T(8,128)(2,1)S(1)} %get-tuple-element.76), channel_id=1, source_target_pairs={{8,0},{24,8},{16,24},{0,16},{9,1},{25,9},{17,25},{1,17},{10,2},{26... | collective-permute-start | bytes 1769480 | tf_op jit(solution)/shard_map/ppermute | solution.py:705
  66.6 19.3 %collective-permute-start.11 = (bf16[288,1024]{1,0:T(8,128)(2,1)S(1)}, bf16[288,1024]{1,0:T(8,128)(2,1)S(1)}, u32[]{:S(2)}, u32[]{:S(2)}) collective-permute-start(bf16[288,1024]{1,0:T(8,128)(2,1)S(1)} %get-tuple-element.74.refs_4_), channel_id=1, source_target_pairs={{0,8},{8,24},{24,16},{16,0},{1,9},{9,25},{25,17},{17,1},{2,10},{10... | collective-permute-start | bytes 1769480 | tf_op jit(solution)/shard_map/ppermute | solution.py:704
  76.8 24.5 %collective-permute-start.16 = (bf16[352,1024]{1,0:T(8,128)(2,1)}, bf16[352,1024]{1,0:T(8,128)(2,1)S(1)}, u32[]{:S(2)}, u32[]{:S(2)}) collective-permute-start(bf16[352,1024]{1,0:T(8,128)(2,1)} %get-tuple-element.85), channel_id=1, source_target_pairs={{0,8},{8,24},{24,16},{16,0},{1,9},{9,25},{25,17},{17,1},{2,10},{10... | collective-permute-start | bytes 2162696 | tf_op jit(solution)/shard_map/ppermute | solution.py:704
  78.5 20.1 %collective-permute-start.17 = (bf16[336,1024]{1,0:T(8,128)(2,1)}, bf16[336,1024]{1,0:T(8,128)(2,1)S(1)}, u32[]{:S(2)}, u32[]{:S(2)}) collective-permute-start(bf16[336,1024]{1,0:T(8,128)(2,1)} %get-tuple-element.86), channel_id=1, source_target_pairs={{8,0},{24,8},{16,24},{0,16},{9,1},{25,9},{17,25},{1,17},{10,2},{26... | collective-permute-start | bytes 2064392 | tf_op jit(solution)/shard_map/ppermute | solution.py:705
  83.8 4.8 %copy-start.17 = (bf16[288,1024]{1,0:T(8,128)(2,1)}, bf16[288,1024]{1,0:T(8,128)(2,1)S(1)}, u32[]{:S(2)}) copy-start(bf16[288,1024]{1,0:T(8,128)(2,1)S(1)} %collective-permute-done.12.refs_5_.refs_1_) | copy-start | bytes 1769476
  88.6 22.6 %collective-permute-start.20 = (bf16[288,1024]{1,0:T(8,128)(2,1)}, bf16[288,1024]{1,0:T(8,128)(2,1)S(1)}, u32[]{:S(2)}, u32[]{:S(2)}) collective-permute-start(bf16[288,1024]{1,0:T(8,128)(2,1)} %get-tuple-element.90), channel_id=1, source_target_pairs={{8,0},{24,8},{16,24},{0,16},{9,1},{25,9},{17,25},{1,17},{10,2},{26... | collective-permute-start | bytes 1769480 | tf_op jit(solution)/shard_map/ppermute | solution.py:705
  90.1 23.9 %collective-permute-start.19 = (bf16[288,1024]{1,0:T(8,128)(2,1)}, bf16[288,1024]{1,0:T(8,128)(2,1)S(1)}, u32[]{:S(2)}, u32[]{:S(2)}) collective-permute-start(bf16[288,1024]{1,0:T(8,128)(2,1)} %get-tuple-element.77.refs_1_), channel_id=1, source_target_pairs={{0,8},{8,24},{24,16},{16,0},{1,9},{9,25},{25,17},{17,1},{2,10},{10... | collective-permute-start | bytes 1769480 | tf_op jit(solution)/shard_map/ppermute | solution.py:704
  92.3 11.8 %copy-start.30 = (f32[8,4096]{1,0:T(8,128)}, f32[8,4096]{1,0:T(8,128)S(1)}, u32[]{:S(2)}) copy-start(f32[8,4096]{1,0:T(8,128)S(1)} %get-tuple-element.78.refs_6_.refs_0_) | copy-start | bytes 393220
  92.3 13.9 %collective-permute-start.13 = (f32[8,4096]{1,0:T(8,128)}, f32[8,4096]{1,0:T(8,128)}, u32[]{:S(2)}, u32[]{:S(2)}) collective-permute-start(f32[8,4096]{1,0:T(8,128)} %get-tuple-element.79), channel_id=1, source_target_pairs={{0,4},{2,6},{4,0},{6,2},{1,5},{3,7},{5,1},{7,3},{8,12},{10,14},{12... | collective-permute-start | bytes 393224 | tf_op jit(solution)/shard_map/ppermute | solution.py:402
  98.5 35.4 %copy-start.2 = (bf16[336,1024]{1,0:T(8,128)(2,1)}, bf16[336,1024]{1,0:T(8,128)(2,1)S(1)}, u32[]{:S(2)}) copy-start(bf16[336,1024]{1,0:T(8,128)(2,1)S(1)} %collective-permute-done.17.refs_5_.refs_6_.refs_3_) | copy-start | bytes 2064388
  101.4 32.5 %copy-start = (bf16[352,1024]{1,0:T(8,128)(2,1)}, bf16[352,1024]{1,0:T(8,128)(2,1)S(1)}, u32[]{:S(2)}) copy-start(bf16[352,1024]{1,0:T(8,128)(2,1)S(1)} %collective-permute-done.16.refs_4_.refs_2_) | copy-start | bytes 2162692
  104.1 24.7 %collective-permute-start.22 = (bf16[336,1024]{1,0:T(8,128)(2,1)}, bf16[336,1024]{1,0:T(8,128)(2,1)S(1)}, u32[]{:S(2)}, u32[]{:S(2)}) collective-permute-start(bf16[336,1024]{1,0:T(8,128)(2,1)} %get-tuple-element.87.refs_2_), channel_id=1, source_target_pairs={{0,8},{8,24},{24,16},{16,0},{1,9},{9,25},{25,17},{17,1},{2,10},{10... | collective-permute-start | bytes 2064392 | tf_op jit(solution)/shard_map/ppermute | solution.py:704
  104.2 20.9 %collective-permute-start.23 = (bf16[288,1024]{1,0:T(8,128)(2,1)}, bf16[288,1024]{1,0:T(8,128)(2,1)}, u32[]{:S(2)}, u32[]{:S(2)}) collective-permute-start(bf16[288,1024]{1,0:T(8,128)(2,1)} %get-tuple-element.94), channel_id=1, source_target_pairs={{8,0},{24,8},{16,24},{0,16},{9,1},{25,9},{17,25},{1,17},{10,2},{26... | collective-permute-start | bytes 1769480 | tf_op jit(solution)/shard_map/ppermute | solution.py:705
  108.6 8.0 %copy-start.32 = (f32[4,4096]{1,0:T(4,128)}, f32[4,4096]{1,0:T(4,128)S(1)}, u32[]{:S(2)}) copy-start(f32[4,4096]{1,0:T(4,128)S(1)} %get-tuple-element.88.refs_6_.refs_0_) | copy-start | bytes 196612
  111.2 5.5 %copy-start.24 = (bf16[288,1024]{1,0:T(8,128)(2,1)}, bf16[288,1024]{1,0:T(8,128)(2,1)S(1)}, u32[]{:S(2)}) copy-start(bf16[288,1024]{1,0:T(8,128)(2,1)S(1)} %collective-permute-done.20.refs_5_) | copy-start | bytes 1769476
  116.7 23.7 %collective-permute-start.25 = (bf16[288,1024]{1,0:T(8,128)(2,1)}, bf16[288,1024]{1,0:T(8,128)(2,1)S(1)}, u32[]{:S(2)}, u32[]{:S(2)}) collective-permute-start(bf16[288,1024]{1,0:T(8,128)(2,1)} %get-tuple-element.98), channel_id=1, source_target_pairs={{8,0},{24,8},{16,24},{0,16},{9,1},{25,9},{17,25},{1,17},{10,2},{26... | collective-permute-start | bytes 1769480 | tf_op jit(solution)/shard_map/ppermute | solution.py:705
  118.3 23.1 %collective-permute-start.24 = (bf16[288,1024]{1,0:T(8,128)(2,1)}, bf16[288,1024]{1,0:T(8,128)(2,1)S(1)}, u32[]{:S(2)}, u32[]{:S(2)}) collective-permute-start(bf16[288,1024]{1,0:T(8,128)(2,1)} %get-tuple-element.91.refs_2_), channel_id=1, source_target_pairs={{0,8},{8,24},{24,16},{16,0},{1,9},{9,25},{25,17},{17,1},{2,10},{10... | collective-permute-start | bytes 1769480 | tf_op jit(solution)/shard_map/ppermute | solution.py:704
  118.7 4.6 %collective-permute-start.18 = (f32[4,4096]{1,0:T(4,128)}, f32[4,4096]{1,0:T(4,128)}, u32[]{:S(2)}, u32[]{:S(2)}) collective-permute-start(f32[4,4096]{1,0:T(4,128)} %get-tuple-element.89), channel_id=1, source_target_pairs={{0,2},{2,0},{4,6},{6,4},{1,3},{3,1},{5,7},{7,5},{8,10},{10,8},{12,... | collective-permute-start | bytes 196616 | tf_op jit(solution)/shard_map/ppermute | solution.py:402
  125.0 14.7 %collective-permute-start.21 = (f32[2,4096]{1,0:T(2,128)S(1)}, f32[2,4096]{1,0:T(2,128)S(1)}, u32[]{:S(2)}, u32[]{:S(2)}) collective-permute-start(f32[2,4096]{1,0:T(2,128)S(1)} %get-tuple-element.93), channel_id=1, source_target_pairs={{0,1},{1,0},{2,3},{3,2},{4,5},{5,4},{6,7},{7,6},{8,9},{9,8},{10,11... | collective-permute-start | bytes 98312 | tf_op jit(solution)/shard_map/ppermute | solution.py:402
  128.7 5.2 %copy-start.1 = (bf16[336,1024]{1,0:T(8,128)(2,1)}, bf16[336,1024]{1,0:T(8,128)(2,1)S(1)}, u32[]{:S(2)}) copy-start(bf16[336,1024]{1,0:T(8,128)(2,1)S(1)} %collective-permute-done.22.refs_4_.refs_5_.refs_6_) | copy-start | bytes 2064388
  128.7 5.2 %copy-start.36 = (bf16[16,512]{1,0:T(8,128)(2,1)S(1)}, bf16[16,512]{1,0:T(8,128)(2,1)}, u32[]{:S(2)}) copy-start(bf16[16,512]{1,0:T(8,128)(2,1)} %copy-done.35) | copy-start | bytes 49156
  128.7 5.2 %copy-start.38 = (bf16[16,512]{1,0:T(8,128)(2,1)S(1)}, bf16[16,512]{1,0:T(8,128)(2,1)}, u32[]{:S(2)}) copy-start(bf16[16,512]{1,0:T(8,128)(2,1)} %copy-done.37) | copy-start | bytes 49156
  128.8 5.2 %copy-start.40 = (bf16[16,384]{1,0:T(8,128)(2,1)S(1)}, bf16[16,384]{1,0:T(8,128)(2,1)}, u32[]{:S(2)}) copy-start(bf16[16,384]{1,0:T(8,128)(2,1)} %copy-done.39) | copy-start | bytes 36868
  131.8 29.9 %collective-permute-start.29 = (bf16[288,1024]{1,0:T(8,128)(2,1)S(1)}, bf16[288,1024]{1,0:T(8,128)(2,1)S(1)}, u32[]{:S(2)}, u32[]{:S(2)}) collective-permute-start(bf16[288,1024]{1,0:T(8,128)(2,1)S(1)} %get-tuple-element.105), channel_id=1, source_target_pairs={{8,0},{24,8},{16,24},{0,16},{9,1},{25,9},{17,25},{1,17},{10,2},{26... | collective-permute-start | bytes 1769480 | tf_op jit(solution)/shard_map/ppermute | solution.py:705
  132.9 28.9 %collective-permute-start.28 = (bf16[288,1024]{1,0:T(8,128)(2,1)S(1)}, bf16[288,1024]{1,0:T(8,128)(2,1)S(1)}, u32[]{:S(2)}, u32[]{:S(2)}) collective-permute-start(bf16[288,1024]{1,0:T(8,128)(2,1)S(1)} %get-tuple-element.95.refs_2_.refs_7_), channel_id=1, source_target_pairs={{0,8},{8,24},{24,16},{16,0},{1,9},{9,25},{25,17},{17,1},{2,10},{10... | collective-permute-start | bytes 1769480 | tf_op jit(solution)/shard_map/ppermute | solution.py:704
  144.9 17.0 %collective-permute-start.27 = (bf16[288,1024]{1,0:T(8,128)(2,1)S(1)}, bf16[288,1024]{1,0:T(8,128)(2,1)S(1)}, u32[]{:S(2)}, u32[]{:S(2)}) collective-permute-start(bf16[288,1024]{1,0:T(8,128)(2,1)S(1)} %get-tuple-element.104), channel_id=1, source_target_pairs={{8,0},{24,8},{16,24},{0,16},{9,1},{25,9},{17,25},{1,17},{10,2},{26... | collective-permute-start | bytes 1769480 | tf_op jit(solution)/shard_map/ppermute | solution.py:705
  146.8 18.4 %collective-permute-start.26 = (bf16[288,1024]{1,0:T(8,128)(2,1)S(1)}, bf16[288,1024]{1,0:T(8,128)(2,1)S(1)}, u32[]{:S(2)}, u32[]{:S(2)}) collective-permute-start(bf16[288,1024]{1,0:T(8,128)(2,1)S(1)} %get-tuple-element.103.refs_6_), channel_id=1, source_target_pairs={{0,8},{8,24},{24,16},{16,0},{1,9},{9,25},{25,17},{17,1},{2,10},{10... | collective-permute-start | bytes 1769480 | tf_op jit(solution)/shard_map/ppermute | solution.py:704
  147.0 14.6 %copy-start.18 = (bf16[288,1024]{1,0:T(8,128)(2,1)S(1)}, bf16[288,1024]{1,0:T(8,128)(2,1)}, u32[]{:S(2)}) copy-start(bf16[288,1024]{1,0:T(8,128)(2,1)} %copy-done.17) | copy-start | bytes 1769476
  147.0 14.6 %copy-start.21 = (bf16[288,1024]{1,0:T(8,128)(2,1)S(1)}, bf16[288,1024]{1,0:T(8,128)(2,1)}, u32[]{:S(2)}) copy-start(bf16[288,1024]{1,0:T(8,128)(2,1)} %copy-done.20) | copy-start | bytes 1769476
  147.0 14.6 %copy-start.25 = (bf16[288,1024]{1,0:T(8,128)(2,1)S(1)}, bf16[288,1024]{1,0:T(8,128)(2,1)}, u32[]{:S(2)}) copy-start(bf16[288,1024]{1,0:T(8,128)(2,1)} %copy-done.24) | copy-start | bytes 1769476
  147.0 14.6 %copy-start.27 = (bf16[288,1024]{1,0:T(8,128)(2,1)S(1)}, bf16[288,1024]{1,0:T(8,128)(2,1)}, u32[]{:S(2)}) copy-start(bf16[288,1024]{1,0:T(8,128)(2,1)} %copy-done.26) | copy-start | bytes 1769476
  (25 other events, 77.5 us)

commit v5 on v3

--- a/solution.py
+++ b/solution.py
@@ -765,7 +765,7 @@
 
     block = largest((b for b in range(TILE, 193, TILE) if rows % b == 0), rows)
     blocks = rows // block
-    early = blocks // 4
+    early = blocks // 3
     ready = parcel_from + LAG * reach[0] + 1
     while len(got) < steps:
         ready_sum = len(got) > parcel_from + SUM_AFTER
@@ -773,7 +773,7 @@
         if len(got) == ready and early and len(got) < steps:
             hidden_t, outs = gathered(sent)
             news = update_part(0, early, (hidden_t,))
-            news = patch_to(len(got) // 2, ())
+            news = patch_to(len(got) // 3, ())
     if hidden_t is None:
         hidden_t, outs = gathered(sent)
         early = 0

time: 167 us -> 170 us (1.018)
  local copies, waits for them, and re-layouts: 3.58 us -> 6.83 us
  starting transfers between devices: 40.2 us -> 37.2 us
  Pallas kernels: 89.2 us -> 92 us
    pallas_call x4, Pallas kernels: 0.54 us -> 22 us  [patch(): pl.pallas_call(functools.partial(patch_body, arrivals=arrivals, chunks=ch...]
    pallas_call x2, Pallas kernels: 18.7 us -> 0.04 us  [update(): pl.pallas_call(functools.partial(update_body, n=n, block=block, first=fir...]
    ppermute x14, starting transfers between devices: 24.8 us -> 20.9 us  [send(): lax.ppermute(sends[-1][1], 'replica', backward)]
    unnamed x86 -> x92, local copies, waits for them, and re-layouts: 3.58 us -> 6.83 us
  transfers between devices with their start and end apart: 34 -> 34, of which waited for: 12 -> 13; matrix products, arithmetic and copies ran while one was open for 0% -> 0% of each run, Pallas kernels for 52% -> 51%
where the time goes in v5:
time: 170 us; the launch traced here: 169 us
  Pallas kernels  92 us (54%)
  starting transfers between devices  37.2 us (22%)
  waiting for transfers between devices  30.8 us (18%)
  local copies, waits for them, and re-layouts  6.83 us (4%)
  between operations  2.19 us (1%)
    pallas_call x14, Pallas kernels, pack(): pl.pallas_call(functools.partial(pack_body, n=n, places=places, chunk=chu...  35 us
    pallas_call x6, Pallas kernels, layer(): pl.pallas_call(functools.partial(layer_body, resumed=resumed, tile=tile,...  30.4 us
    pallas_call x4, Pallas kernels, patch(): pl.pallas_call(functools.partial(patch_body, arrivals=arrivals, chunks=ch...  22 us
    ppermute x14, starting transfers between devices, send(): lax.ppermute(sends[-1][1], 'replica', backward)  20.9 us
    ppermute x14, waiting for transfers between devices, send(): lax.ppermute(sends[-1][1], 'replica', backward)  11.6 us
    ppermute x14, starting transfers between devices, send(): lax.ppermute(sends[-1][0], 'replica', forward)  9.16 us
    ppermute x3, waiting for transfers between devices, per_device(): other = lax.ppermute(both, axis, [(i, i ^ apart) for i in range(size)])  8.85 us
    ppermute x14, waiting for transfers between devices, send(): lax.ppermute(sends[-1][0], 'replica', forward)  7.07 us
  transfers between devices with their start and end apart: 34, of which 13 were waited for; matrix products, arithmetic and copies ran while one was open for 0% of the time, Pallas kernels for 51%

profile of v5, /device:TPU:0, one launch (start us, length us, event | category | flops | bytes accessed | tf_op | source)
XLA Modules:
  0.0 169.0 jit_solution(7193995445614085225)
XLA Ops:
  0.7 2.5 %pack.14 = (bf16[240,1024]{1,0:T(8,128)(2,1)S(1)}, bf16[240,1024]{1,0:T(8,128)(2,1)S(1)}) custom-call(f32[2,1920,1024]{2,1,0:T(8,128)} %refs_0_.31, f32[2,1920,1024]{2,1,0:T(8,128)} %refs_1_.43, f32[2,1920,1024]{2,1,0:T(8,128)} %refs_2_.43), custom_call_target="tpu_custom_call" | custom-call | bytes 2949120 | tf_op jit(solution)/shard_map/pack/pallas_call | solution.py:200
  3.1 3.0 %collective-permute-start.4 = (bf16[240,1024]{1,0:T(8,128)(2,1)S(1)}, bf16[240,1024]{1,0:T(8,128)(2,1)S(1)}, u32[]{:S(2)}, u32[]{:S(2)}) collective-permute-start(bf16[240,1024]{1,0:T(8,128)(2,1)S(1)} %get-tuple-element.72), channel_id=1, source_target_pairs={{8,0},{24,8},{16,24},{0,16},{9,1},{25,9},{17,25},{1,17},{10,2},{26... | collective-permute-start | bytes 1474568 | tf_op jit(solution)/shard_map/ppermute | solution.py:705
  6.2 2.5 %pack.15 = (bf16[240,1024]{1,0:T(8,128)(2,1)S(1)}, bf16[240,1024]{1,0:T(8,128)(2,1)S(1)}) custom-call(f32[2,1920,1024]{2,1,0:T(8,128)} %refs_0_.31, f32[2,1920,1024]{2,1,0:T(8,128)} %refs_1_.43, f32[2,1920,1024]{2,1,0:T(8,128)} %refs_2_.43, bf16[1,2,8192]{2,1,0:T(2,128)(2,1)S(1)} %beside.1.refs_3_.own), custom_call_target="tpu_custom_call" | custom-call | bytes 2949120 | tf_op jit(solution)/shard_map/pack/pallas_call | solution.py:200
  8.7 2.0 %collective-permute-start.6 = (bf16[240,1024]{1,0:T(8,128)(2,1)S(1)}, bf16[240,1024]{1,0:T(8,128)(2,1)S(1)}, u32[]{:S(2)}, u32[]{:S(2)}) collective-permute-start(bf16[240,1024]{1,0:T(8,128)(2,1)S(1)} %get-tuple-element.75), channel_id=1, source_target_pairs={{8,0},{24,8},{16,24},{0,16},{9,1},{25,9},{17,25},{1,17},{10,2},{26... | collective-permute-start | bytes 1474568 | tf_op jit(solution)/shard_map/ppermute | solution.py:705
  12.0 2.1 %collective-permute-start.1 = (bf16[2,2,8192]{2,1,0:T(2,128)(2,1)S(1)}, bf16[2,2,8192]{2,1,0:T(2,128)(2,1)S(1)}, u32[]{:S(2)}, u32[]{:S(2)}) collective-permute-start(bf16[2,2,8192]{2,1,0:T(2,128)(2,1)S(1)} %join.3.own), channel_id=1, source_target_pairs={{0,2},{2,0},{4,6},{6,4},{1,3},{3,1},{5,7},{7,5},{8,10},{10,8},{12,... | collective-permute-start | bytes 196616 | tf_op jit(solution)/shard_map/ppermute | solution.py:720
  14.1 2.4 %collective-permute-done.1.other = bf16[2,2,8192]{2,1,0:T(2,128)(2,1)S(1)} collective-permute-done((bf16[2,2,8192]{2,1,0:T(2,128)(2,1)S(1)}, bf16[2,2,8192]{2,1,0:T(2,128)(2,1)S(1)}, u32[]{:S(2)}, u32[]{:S(2)}) %collective-permute-start.1) | collective-permute-done | bytes 65568 | tf_op jit(solution)/shard_map/ppermute | solution.py:720
  16.5 2.9 %collective-permute-start.2 = (bf16[4,2,8192]{2,1,0:T(2,128)(2,1)S(1)}, bf16[4,2,8192]{2,1,0:T(2,128)(2,1)S(1)}, u32[]{:S(2)}, u32[]{:S(2)}) collective-permute-start(bf16[4,2,8192]{2,1,0:T(2,128)(2,1)S(1)} %join.4.own), channel_id=1, source_target_pairs={{0,4},{2,6},{4,0},{6,2},{1,5},{3,7},{5,1},{7,3},{8,12},{10,14},{12... | collective-permute-start | bytes 393224 | tf_op jit(solution)/shard_map/ppermute | solution.py:720
  20.1 5.2 %collective-permute-done.2.other = bf16[4,2,8192]{2,1,0:T(2,128)(2,1)S(1)} collective-permute-done((bf16[4,2,8192]{2,1,0:T(2,128)(2,1)S(1)}, bf16[4,2,8192]{2,1,0:T(2,128)(2,1)S(1)}, u32[]{:S(2)}, u32[]{:S(2)}) %collective-permute-start.2) | collective-permute-done | bytes 131104 | tf_op jit(solution)/shard_map/ppermute | solution.py:720
  25.5 2.7 %pack.16 = (bf16[240,1024]{1,0:T(8,128)(2,1)S(1)}, bf16[240,1024]{1,0:T(8,128)(2,1)S(1)}) custom-call(s32[1]{0:T(128)S(6)} %copy.43.refs_0_.failed, f32[2,1920,1024]{2,1,0:T(8,128)} %refs_0_.31, f32[2,1920,1024]{2,1,0:T(8,128)} %refs_1_.43, f32[2,1920,1024]{2,1,0:T(8,128)} %refs_2_.43, bf16[240,1024]{1,0:T(8,128)(2,1)S(1)} %collective-permute-done.3.refs_4_.refs_0_, ...), custom_call_target="tpu_custom_call" | custom-call | bytes 2949120 | tf_op jit(solution)/shard_map/pack/pallas_call | solution.py:200
  28.3 1.5 collective-permute-start.8
  30.3 4.4 %layer.6 = (bf16[16,256]{1,0:T(8,128)(2,1)S(1)}, f32[16,4096]{1,0:T(8,128)S(1)}) custom-call(bf16[16,8192]{1,0:T(8,128)(2,1)S(1)} %join.5.refs_6_.both, bf16[4096,1920]{1,0:T(8,128)(2,1)} %refs_0_.29, bf16[4096,1920]{1,0:T(8,128)(2,1)} %refs_1_.35, bf16[1920,4096]{1,0:T(8,128)(2,1)} %refs_2_.35, bf16[240,1024]{1,0:T(8,128)(2,1)S(1)} %get-tuple-element.73.refs_3_), custom_call_target="tpu_custom_call" | custom-call | flops 167772160 | bytes 6291456 | tf_op jit(solution)/shard_map/layer/pallas_call | solution.py:329
  34.8 2.7 %pack.17 = (bf16[240,1024]{1,0:T(8,128)(2,1)S(1)}, bf16[240,1024]{1,0:T(8,128)(2,1)S(1)}) custom-call(s32[1]{0:T(128)S(6)} %copy.43.refs_0_.failed, f32[2,1920,1024]{2,1,0:T(8,128)} %refs_0_.31, f32[2,1920,1024]{2,1,0:T(8,128)} %refs_1_.43, f32[2,1920,1024]{2,1,0:T(8,128)} %refs_2_.43, bf16[240,1024]{1,0:T(8,128)(2,1)S(1)} %collective-permute-done.5.refs_4_.refs_2_, ...), custom_call_target="tpu_custom_call" | custom-call | bytes 2949120 | tf_op jit(solution)/shard_map/pack/pallas_call | solution.py:200
  37.6 1.5 collective-permute-start.10
  39.6 5.7 %layer.7 = (bf16[16,384]{1,0:T(8,128)(2,1)S(1)}, f32[16,4096]{1,0:T(8,128)S(1)}) custom-call(bf16[16,8192]{1,0:T(8,128)(2,1)S(1)} %join.5.refs_6_.both, bf16[4096,1920]{1,0:T(8,128)(2,1)} %refs_0_.29, bf16[4096,1920]{1,0:T(8,128)(2,1)} %refs_1_.35, bf16[1920,4096]{1,0:T(8,128)(2,1)} %refs_2_.35, f32[16,4096]{1,0:T(8,128)S(1)} %get-tuple-element.74.refs_6_.refs_3_, ...), custom_call_target="tpu_custom_call" | custom-call | flops 251658240 | bytes 9437184 | tf_op jit(solution)/shard_map/layer/pallas_call | solution.py:329
  45.4 2.7 %pack.18 = (bf16[240,1024]{1,0:T(8,128)(2,1)S(1)}, bf16[240,1024]{1,0:T(8,128)(2,1)S(1)}) custom-call(s32[1]{0:T(128)S(6)} %copy.43.refs_0_.failed, f32[2,1920,1024]{2,1,0:T(8,128)} %refs_0_.31, f32[2,1920,1024]{2,1,0:T(8,128)} %refs_1_.43, f32[2,1920,1024]{2,1,0:T(8,128)} %refs_2_.43, bf16[240,1024]{1,0:T(8,128)(2,1)S(1)} %collective-permute-done.7.refs_4_, ...), custom_call_target="tpu_custom_call" | custom-call | bytes 2949120 | tf_op jit(solution)/shard_map/pack/pallas_call | solution.py:200
  48.1 1.5 collective-permute-start.12
  50.2 4.4 %layer.8 = (bf16[16,256]{1,0:T(8,128)(2,1)S(1)}, f32[16,4096]{1,0:T(8,128)S(1)}) custom-call(bf16[16,8192]{1,0:T(8,128)(2,1)S(1)} %join.5.refs_6_.both, bf16[4096,1920]{1,0:T(8,128)(2,1)} %refs_0_.29, bf16[4096,1920]{1,0:T(8,128)(2,1)} %refs_1_.35, bf16[1920,4096]{1,0:T(8,128)(2,1)} %refs_2_.35, f32[16,4096]{1,0:T(8,128)S(1)} %get-tuple-element.77.refs_6_.refs_3_, ...), custom_call_target="tpu_custom_call" | custom-call | flops 167772160 | bytes 6291456 | tf_op jit(solution)/shard_map/layer/pallas_call | solution.py:329
  54.7 2.7 %pack.19 = (bf16[240,1024]{1,0:T(8,128)(2,1)S(1)}, bf16[240,1024]{1,0:T(8,128)(2,1)S(1)}) custom-call(s32[1]{0:T(128)S(6)} %copy.43.refs_0_.failed, f32[2,1920,1024]{2,1,0:T(8,128)} %refs_0_.31, f32[2,1920,1024]{2,1,0:T(8,128)} %refs_1_.43, f32[2,1920,1024]{2,1,0:T(8,128)} %refs_2_.43, bf16[240,1024]{1,0:T(8,128)(2,1)S(1)} %collective-permute-done.9.refs_4_.refs_6_, ...), custom_call_target="tpu_custom_call" | custom-call | bytes 2949120 | tf_op jit(solution)/shard_map/pack/pallas_call | solution.py:200
  57.4 1.5 collective-permute-start.14
  59.5 5.7 %layer.9 = (bf16[16,384]{1,0:T(8,128)(2,1)S(1)}, f32[16,4096]{1,0:T(8,128)S(1)}) custom-call(bf16[16,8192]{1,0:T(8,128)(2,1)S(1)} %join.5.refs_6_.both, bf16[4096,1920]{1,0:T(8,128)(2,1)} %refs_0_.29, bf16[4096,1920]{1,0:T(8,128)(2,1)} %refs_1_.35, bf16[1920,4096]{1,0:T(8,128)(2,1)} %refs_2_.35, f32[16,4096]{1,0:T(8,128)S(1)} %get-tuple-element.80.refs_6_.refs_3_, ...), custom_call_target="tpu_custom_call" | custom-call | flops 251658240 | bytes 9437184 | tf_op jit(solution)/shard_map/layer/pallas_call | solution.py:329
  65.2 2.7 %pack.20 = (bf16[240,1024]{1,0:T(8,128)(2,1)S(1)}, bf16[240,1024]{1,0:T(8,128)(2,1)S(1)}) custom-call(s32[1]{0:T(128)S(6)} %copy.43.refs_0_.failed, f32[2,1920,1024]{2,1,0:T(8,128)} %refs_0_.31, f32[2,1920,1024]{2,1,0:T(8,128)} %refs_1_.43, f32[2,1920,1024]{2,1,0:T(8,128)} %refs_2_.43, bf16[240,1024]{1,0:T(8,128)(2,1)S(1)} %collective-permute-done.11.refs_4_.refs_0_, ...), custom_call_target="tpu_custom_call" | custom-call | bytes 2949120 | tf_op jit(solution)/shard_map/pack/pallas_call | solution.py:200
  68.0 1.5 collective-permute-start.19
  70.0 4.4 %layer.10 = (bf16[16,256]{1,0:T(8,128)(2,1)S(1)}, f32[16,4096]{1,0:T(8,128)S(1)}) custom-call(bf16[16,8192]{1,0:T(8,128)(2,1)S(1)} %join.5.refs_6_.both, bf16[4096,1920]{1,0:T(8,128)(2,1)} %refs_0_.29, bf16[4096,1920]{1,0:T(8,128)(2,1)} %refs_1_.35, bf16[1920,4096]{1,0:T(8,128)(2,1)} %refs_2_.35, f32[16,4096]{1,0:T(8,128)S(1)} %get-tuple-element.83.refs_6_.refs_3_, ...), custom_call_target="tpu_custom_call" | custom-call | flops 167772160 | bytes 6291456 | tf_op jit(solution)/shard_map/layer/pallas_call | solution.py:329
  74.9 2.6 %pack.21 = (bf16[240,1024]{1,0:T(8,128)(2,1)S(1)}, bf16[240,1024]{1,0:T(8,128)(2,1)S(1)}) custom-call(s32[1]{0:T(128)S(6)} %copy.43.refs_0_.failed, f32[2,1920,1024]{2,1,0:T(8,128)} %refs_0_.31, f32[2,1920,1024]{2,1,0:T(8,128)} %refs_1_.43, f32[2,1920,1024]{2,1,0:T(8,128)} %refs_2_.43, bf16[240,1024]{1,0:T(8,128)(2,1)S(1)} %collective-permute-done.13.refs_4_.refs_2_, ...), custom_call_target="tpu_custom_call" | custom-call | bytes 2949120 | tf_op jit(solution)/shard_map/pack/pallas_call | solution.py:200
  77.5 1.5 collective-permute-start.16
  79.6 5.7 %layer.11 = (bf16[16,384]{1,0:T(8,128)(2,1)S(1)}, f32[16,4096]{1,0:T(8,128)S(1)}) custom-call(bf16[16,8192]{1,0:T(8,128)(2,1)S(1)} %join.5.refs_6_.both, bf16[4096,1920]{1,0:T(8,128)(2,1)} %refs_0_.29, bf16[4096,1920]{1,0:T(8,128)(2,1)} %refs_1_.35, bf16[1920,4096]{1,0:T(8,128)(2,1)} %refs_2_.35, f32[16,4096]{1,0:T(8,128)S(1)} %get-tuple-element.86.refs_6_.refs_3_, ...), custom_call_target="tpu_custom_call" | custom-call | flops 251658240 | bytes 9437184 | tf_op jit(solution)/shard_map/layer/pallas_call | solution.py:329
  85.4 2.5 %pack.23 = (bf16[304,1024]{1,0:T(8,128)(2,1)}, bf16[288,1024]{1,0:T(8,128)(2,1)}) custom-call(s32[1]{0:T(128)S(6)} %copy.43.refs_0_.failed, f32[2,1920,1024]{2,1,0:T(8,128)} %refs_0_.31, f32[2,1920,1024]{2,1,0:T(8,128)} %refs_1_.43, f32[2,1920,1024]{2,1,0:T(8,128)} %refs_2_.43, bf16[240,1024]{1,0:T(8,128)(2,1)S(1)} %collective-permute-done.18.refs_4_, ...), custom_call_target="tpu_custom_call" | custom-call | bytes 2949120 | tf_op jit(solution)/shard_map/pack/pallas_call | solution.py:200
  90.1 4.8 %collective-permute-done.16.refs_5_.refs_7_ = bf16[240,1024]{1,0:T(8,128)(2,1)S(1)} collective-permute-done((bf16[240,1024]{1,0:T(8,128)(2,1)S(1)}, bf16[240,1024]{1,0:T(8,128)(2,1)S(1)}, u32[]{:S(2)}, u32[]{:S(2)}) %collective-permute-start.16) | collective-permute-done | bytes 491552 | tf_op jit(solution)/shard_map/ppermute | solution.py:705
  96.0 2.3 %pack.22 = (bf16[240,1024]{1,0:T(8,128)(2,1)}, bf16[240,1024]{1,0:T(8,128)(2,1)}) custom-call(s32[1]{0:T(128)S(6)} %copy.43.refs_0_.failed, f32[2,1920,1024]{2,1,0:T(8,128)} %refs_0_.31, f32[2,1920,1024]{2,1,0:T(8,128)} %refs_1_.43, f32[2,1920,1024]{2,1,0:T(8,128)} %refs_2_.43, bf16[240,1024]{1,0:T(8,128)(2,1)S(1)} %collective-permute-done.15.refs_4_.refs_6_, ...), custom_call_target="tpu_custom_call" | custom-call | bytes 2949120 | tf_op jit(solution)/shard_map/pack/pallas_call | solution.py:200
  98.3 1.5 collective-permute-start.24
  102.6 4.9 %collective-permute-done.21.refs_5_.refs_8_.refs_9_ = bf16[288,1024]{1,0:T(8,128)(2,1)S(1)} collective-permute-done((bf16[288,1024]{1,0:T(8,128)(2,1)}, bf16[288,1024]{1,0:T(8,128)(2,1)S(1)}, u32[]{:S(2)}, u32[]{:S(2)}) %collective-permute-start.21) | collective-permute-done | bytes 589856 | tf_op jit(solution)/shard_map/ppermute | solution.py:705
  107.5 1.8 %collective-permute-done.20.refs_4_.refs_6_.refs_8_ = bf16[304,1024]{1,0:T(8,128)(2,1)S(1)} collective-permute-done((bf16[304,1024]{1,0:T(8,128)(2,1)}, bf16[304,1024]{1,0:T(8,128)(2,1)S(1)}, u32[]{:S(2)}, u32[]{:S(2)}) %collective-permute-start.20) | collective-permute-done | bytes 622624 | tf_op jit(solution)/shard_map/ppermute | solution.py:704
  109.3 2.4 %pack.24 = (bf16[288,1024]{1,0:T(8,128)(2,1)}, bf16[240,1024]{1,0:T(8,128)(2,1)}) custom-call(s32[1]{0:T(128)S(6)} %copy.43.refs_0_.failed, f32[2,1920,1024]{2,1,0:T(8,128)} %refs_0_.31, f32[2,1920,1024]{2,1,0:T(8,128)} %refs_1_.43, f32[2,1920,1024]{2,1,0:T(8,128)} %refs_2_.43, bf16[304,1024]{1,0:T(8,128)(2,1)S(1)} %collective-permute-done.20.refs_4_.refs_6_.refs_8_, ...), custom_call_target="tpu_custom_call" | custom-call | bytes 2949120 | tf_op jit(solution)/shard_map/pack/pallas_call | solution.py:200
  114.7 1.5 halve.5
  116.3 1.9 %collective-permute-done.24.refs_5_.refs_11_ = bf16[240,1024]{1,0:T(8,128)(2,1)} collective-permute-done((bf16[240,1024]{1,0:T(8,128)(2,1)}, bf16[240,1024]{1,0:T(8,128)(2,1)}, u32[]{:S(2)}, u32[]{:S(2)}) %collective-permute-start.24) | collective-permute-done | bytes 491552 | tf_op jit(solution)/shard_map/ppermute | solution.py:705
  118.1 1.8 %collective-permute-done.23.refs_4_.refs_10_ = bf16[240,1024]{1,0:T(8,128)(2,1)} collective-permute-done((bf16[240,1024]{1,0:T(8,128)(2,1)}, bf16[240,1024]{1,0:T(8,128)(2,1)}, u32[]{:S(2)}, u32[]{:S(2)}) %collective-permute-start.23) | collective-permute-done | bytes 491552 | tf_op jit(solution)/shard_map/ppermute | solution.py:704
  119.9 2.1 %pack.25 = (bf16[240,1024]{1,0:T(8,128)(2,1)}, bf16[240,1024]{1,0:T(8,128)(2,1)}) custom-call(s32[1]{0:T(128)S(6)} %copy.43.refs_0_.failed, f32[2,1920,1024]{2,1,0:T(8,128)} %refs_0_.31, f32[2,1920,1024]{2,1,0:T(8,128)} %refs_1_.43, f32[2,1920,1024]{2,1,0:T(8,128)} %refs_2_.43, bf16[240,1024]{1,0:T(8,128)(2,1)} %collective-permute-done.23.refs_4_.refs_10_, ...), custom_call_target="tpu_custom_call" | custom-call | bytes 2949120 | tf_op jit(solution)/shard_map/pack/pallas_call | solution.py:200
  122.1 1.5 collective-permute-start.29
  125.5 3.2 %collective-permute-done.22.refs_1_ = f32[4,4096]{1,0:T(4,128)} collective-permute-done((f32[4,4096]{1,0:T(4,128)}, f32[4,4096]{1,0:T(4,128)}, u32[]{:S(2)}, u32[]{:S(2)}) %collective-permute-start.22) | collective-permute-done | bytes 65568 | tf_op jit(solution)/shard_map/ppermute | solution.py:402
  130.5 1.9 %collective-permute-done.26.refs_4_.refs_7_.refs_12_ = bf16[288,1024]{1,0:T(8,128)(2,1)S(1)} collective-permute-done((bf16[288,1024]{1,0:T(8,128)(2,1)}, bf16[288,1024]{1,0:T(8,128)(2,1)S(1)}, u32[]{:S(2)}, u32[]{:S(2)}) %collective-permute-start.26) | collective-permute-done | bytes 589856 | tf_op jit(solution)/shard_map/ppermute | solution.py:704
  132.5 2.3 %pack.26 = (bf16[240,1024]{1,0:T(8,128)(2,1)S(1)}, bf16[240,1024]{1,0:T(8,128)(2,1)S(1)}) custom-call(s32[1]{0:T(128)S(6)} %copy.43.refs_0_.failed, f32[2,1920,1024]{2,1,0:T(8,128)} %refs_0_.31, f32[2,1920,1024]{2,1,0:T(8,128)} %refs_1_.43, f32[2,1920,1024]{2,1,0:T(8,128)} %refs_2_.43, ...), custom_call_target="tpu_custom_call" | custom-call | bytes 2949120 | tf_op jit(solution)/shard_map/pack/pallas_call | solution.py:200
  134.8 1.5 collective-permute-start.33
  139.6 5.9 %patch.4 = (f32[1920,1024]{1,0:T(8,128)}, f32[1920,1024]{1,0:T(8,128)}, f32[1920,1024]{1,0:T(8,128)}) custom-call(s32[1]{0:T(128)S(6)} %copy.43.refs_0_.failed, bf16[1920,64]{1,0:T(8,128)(2,1)S(1)} %get-tuple-element.112.hid_ref.refs_3_, ...), custom_call_target="tpu_custom_call", output_to_operand_aliasing={{0}: (11, {}), {1}: (12, {}), {2}: (13, {})} | custom-call | flops 83886080 | bytes 11796480 | tf_op jit(solution)/shard_map/patch/pallas_call | solution.py:628
  146.8 2.3 %pack.27 = (bf16[240,1024]{1,0:T(8,128)(2,1)S(1)}, bf16[240,1024]{1,0:T(8,128)(2,1)S(1)}) custom-call(s32[1]{0:T(128)S(6)} %copy.43.refs_0_.failed, f32[2,1920,1024]{2,1,0:T(8,128)} %refs_0_.31, f32[2,1920,1024]{2,1,0:T(8,128)} %refs_1_.43, f32[2,1920,1024]{2,1,0:T(8,128)} %refs_2_.43, bf16[240,1024]{1,0:T(8,128)(2,1)} %collective-permute-done.28.refs_4_.refs_14_, ...), custom_call_target="tpu_custom_call" | custom-call | bytes 2949120 | tf_op jit(solution)/shard_map/pack/pallas_call | solution.py:200
  149.2 2.0 %collective-permute-start.30 = (bf16[240,1024]{1,0:T(8,128)(2,1)S(1)}, bf16[240,1024]{1,0:T(8,128)(2,1)S(1)}, u32[]{:S(2)}, u32[]{:S(2)}) collective-permute-start(bf16[240,1024]{1,0:T(8,128)(2,1)S(1)} %get-tuple-element.119.refs_6_), channel_id=1, source_target_pairs={{0,8},{8,24},{24,16},{16,0},{1,9},{9,25},{25,17},{17,1},{2,10},{10... | collective-permute-start | bytes 1474568 | tf_op jit(solution)/shard_map/ppermute | solution.py:704
  152.7 11.0 %patch.5 = (f32[1920,1024]{1,0:T(8,128)}, f32[1920,1024]{1,0:T(8,128)}, f32[1920,1024]{1,0:T(8,128)}) custom-call(s32[1]{0:T(128)S(6)} %copy.43.refs_0_.failed, bf16[1920,64]{1,0:T(8,128)(2,1)S(1)} %get-tuple-element.112.hid_ref.refs_3_, ...), custom_call_target="tpu_custom_call", output_to_operand_aliasing={{0}: (19, {}), {1}: (20, {}), {2}: (21, {})} | custom-call | flops 167772160 | bytes 23592960 | tf_op jit(solution)/shard_map/patch/pallas_call | solution.py:628
  163.7 2.6 %patch.6 = (f32[1920,1024]{1,0:T(8,128)}, f32[1920,1024]{1,0:T(8,128)}, f32[1920,1024]{1,0:T(8,128)}) custom-call(s32[1]{0:T(128)S(6)} %copy.43.refs_0_.failed, bf16[1920,64]{1,0:T(8,128)(2,1)S(1)} %get-tuple-element.112.hid_ref.refs_3_, bf16[64,1024]{1,0:T(8,128)(2,1)S(1)} %get-tuple-element.113.out_ref, ...), custom_call_target="tpu_custom_call", output_to_operand_aliasing={{0}: (5, {}), {1}: (6, {}), {2}: (7, {})} | custom-call | flops 20971520 | bytes 2949120 | tf_op jit(solution)/shard_map/patch/pallas_call | solution.py:628
  166.3 2.6 %patch.7 = (f32[1920,1024]{1,0:T(8,128)}, f32[1920,1024]{1,0:T(8,128)}, f32[1920,1024]{1,0:T(8,128)}) custom-call(s32[1]{0:T(128)S(6)} %copy.43.refs_0_.failed, bf16[1920,64]{1,0:T(8,128)(2,1)S(1)} %get-tuple-element.112.hid_ref.refs_3_, bf16[64,1024]{1,0:T(8,128)(2,1)S(1)} %get-tuple-element.113.out_ref, ...), custom_call_target="tpu_custom_call", output_to_operand_aliasing={{0}: (5, {}), {1}: (6, {}), {2}: (7, {})} | custom-call | flops 20971520 | bytes 2949120 | tf_op jit(solution)/shard_map/patch/pallas_call | solution.py:628
  (147 shorter events, 24.1 us)
Async XLA Ops:
  0.6 5.6 %copy-start.45 = (bf16[1,2,4096]{2,1,0:T(2,128)(2,1)S(1)}, bf16[1,2,4096]{2,1,0:T(2,128)(2,1)}, u32[]{:S(2)}) copy-start(bf16[1,2,4096]{2,1,0:T(2,128)(2,1)} %param.10) | copy-start | bytes 49156
  0.6 5.6 %copy-start.44 = (bf16[1,2,4096]{2,1,0:T(2,128)(2,1)S(1)}, bf16[1,2,4096]{2,1,0:T(2,128)(2,1)}, u32[]{:S(2)}) copy-start(bf16[1,2,4096]{2,1,0:T(2,128)(2,1)} %param.9) | copy-start | bytes 49156
  3.1 22.4 %collective-permute-start.4 = (bf16[240,1024]{1,0:T(8,128)(2,1)S(1)}, bf16[240,1024]{1,0:T(8,128)(2,1)S(1)}, u32[]{:S(2)}, u32[]{:S(2)}) collective-permute-start(bf16[240,1024]{1,0:T(8,128)(2,1)S(1)} %get-tuple-element.72), channel_id=1, source_target_pairs={{8,0},{24,8},{16,24},{0,16},{9,1},{25,9},{17,25},{1,17},{10,2},{26... | collective-permute-start | bytes 1474568 | tf_op jit(solution)/shard_map/ppermute | solution.py:705
  6.2 19.4 %collective-permute-start.3 = (bf16[240,1024]{1,0:T(8,128)(2,1)S(1)}, bf16[240,1024]{1,0:T(8,128)(2,1)S(1)}, u32[]{:S(2)}, u32[]{:S(2)}) collective-permute-start(bf16[240,1024]{1,0:T(8,128)(2,1)S(1)} %get-tuple-element.70.refs_2_), channel_id=1, source_target_pairs={{0,8},{8,24},{24,16},{16,0},{1,9},{9,25},{25,17},{17,1},{2,10},{10... | collective-permute-start | bytes 1474568 | tf_op jit(solution)/shard_map/ppermute | solution.py:704
  8.7 26.1 %collective-permute-start.6 = (bf16[240,1024]{1,0:T(8,128)(2,1)S(1)}, bf16[240,1024]{1,0:T(8,128)(2,1)S(1)}, u32[]{:S(2)}, u32[]{:S(2)}) collective-permute-start(bf16[240,1024]{1,0:T(8,128)(2,1)S(1)} %get-tuple-element.75), channel_id=1, source_target_pairs={{8,0},{24,8},{16,24},{0,16},{9,1},{25,9},{17,25},{1,17},{10,2},{26... | collective-permute-start | bytes 1474568 | tf_op jit(solution)/shard_map/ppermute | solution.py:705
  10.7 24.1 %collective-permute-start.5 = (bf16[240,1024]{1,0:T(8,128)(2,1)S(1)}, bf16[240,1024]{1,0:T(8,128)(2,1)S(1)}, u32[]{:S(2)}, u32[]{:S(2)}) collective-permute-start(bf16[240,1024]{1,0:T(8,128)(2,1)S(1)} %get-tuple-element.71.refs_0_), channel_id=1, source_target_pairs={{0,8},{8,24},{24,16},{16,0},{1,9},{9,25},{25,17},{17,1},{2,10},{10... | collective-permute-start | bytes 1474568 | tf_op jit(solution)/shard_map/ppermute | solution.py:704
  10.8 1.2 collective-permute-start
  12.0 4.5 %collective-permute-start.1 = (bf16[2,2,8192]{2,1,0:T(2,128)(2,1)S(1)}, bf16[2,2,8192]{2,1,0:T(2,128)(2,1)S(1)}, u32[]{:S(2)}, u32[]{:S(2)}) collective-permute-start(bf16[2,2,8192]{2,1,0:T(2,128)(2,1)S(1)} %join.3.own), channel_id=1, source_target_pairs={{0,2},{2,0},{4,6},{6,4},{1,3},{3,1},{5,7},{7,5},{8,10},{10,8},{12,... | collective-permute-start | bytes 196616 | tf_op jit(solution)/shard_map/ppermute | solution.py:720
  16.5 8.8 %collective-permute-start.2 = (bf16[4,2,8192]{2,1,0:T(2,128)(2,1)S(1)}, bf16[4,2,8192]{2,1,0:T(2,128)(2,1)S(1)}, u32[]{:S(2)}, u32[]{:S(2)}) collective-permute-start(bf16[4,2,8192]{2,1,0:T(2,128)(2,1)S(1)} %join.4.own), channel_id=1, source_target_pairs={{0,4},{2,6},{4,0},{6,2},{1,5},{3,7},{5,1},{7,3},{8,12},{10,14},{12... | collective-permute-start | bytes 393224 | tf_op jit(solution)/shard_map/ppermute | solution.py:720
  28.3 17.1 %collective-permute-start.8 = (bf16[240,1024]{1,0:T(8,128)(2,1)S(1)}, bf16[240,1024]{1,0:T(8,128)(2,1)S(1)}, u32[]{:S(2)}, u32[]{:S(2)}) collective-permute-start(bf16[240,1024]{1,0:T(8,128)(2,1)S(1)} %get-tuple-element.78), channel_id=1, source_target_pairs={{8,0},{24,8},{16,24},{0,16},{9,1},{25,9},{17,25},{1,17},{10,2},{26... | collective-permute-start | bytes 1474568 | tf_op jit(solution)/shard_map/ppermute | solution.py:705
  29.8 15.6 %collective-permute-start.7 = (bf16[240,1024]{1,0:T(8,128)(2,1)S(1)}, bf16[240,1024]{1,0:T(8,128)(2,1)S(1)}, u32[]{:S(2)}, u32[]{:S(2)}) collective-permute-start(bf16[240,1024]{1,0:T(8,128)(2,1)S(1)} %get-tuple-element.73.refs_3_), channel_id=1, source_target_pairs={{0,8},{8,24},{24,16},{16,0},{1,9},{9,25},{25,17},{17,1},{2,10},{10... | collective-permute-start | bytes 1474568 | tf_op jit(solution)/shard_map/ppermute | solution.py:704
  34.8 50.6 %copy-start.38 = (bf16[16,256]{1,0:T(8,128)(2,1)}, bf16[16,256]{1,0:T(8,128)(2,1)S(1)}, u32[]{:S(2)}) copy-start(bf16[16,256]{1,0:T(8,128)(2,1)S(1)} %get-tuple-element.95.refs_7_.refs_0_) | copy-start | bytes 24580
  37.6 17.1 %collective-permute-start.10 = (bf16[240,1024]{1,0:T(8,128)(2,1)S(1)}, bf16[240,1024]{1,0:T(8,128)(2,1)S(1)}, u32[]{:S(2)}, u32[]{:S(2)}) collective-permute-start(bf16[240,1024]{1,0:T(8,128)(2,1)S(1)} %get-tuple-element.81), channel_id=1, source_target_pairs={{8,0},{24,8},{16,24},{0,16},{9,1},{25,9},{17,25},{1,17},{10,2},{26... | collective-permute-start | bytes 1474568 | tf_op jit(solution)/shard_map/ppermute | solution.py:705
  39.1 15.6 %collective-permute-start.9 = (bf16[240,1024]{1,0:T(8,128)(2,1)S(1)}, bf16[240,1024]{1,0:T(8,128)(2,1)S(1)}, u32[]{:S(2)}, u32[]{:S(2)}) collective-permute-start(bf16[240,1024]{1,0:T(8,128)(2,1)S(1)} %get-tuple-element.76.refs_4_), channel_id=1, source_target_pairs={{0,8},{8,24},{24,16},{16,0},{1,9},{9,25},{25,17},{17,1},{2,10},{10... | collective-permute-start | bytes 1474568 | tf_op jit(solution)/shard_map/ppermute | solution.py:704
  48.1 17.1 %collective-permute-start.12 = (bf16[240,1024]{1,0:T(8,128)(2,1)S(1)}, bf16[240,1024]{1,0:T(8,128)(2,1)S(1)}, u32[]{:S(2)}, u32[]{:S(2)}) collective-permute-start(bf16[240,1024]{1,0:T(8,128)(2,1)S(1)} %get-tuple-element.84), channel_id=1, source_target_pairs={{8,0},{24,8},{16,24},{0,16},{9,1},{25,9},{17,25},{1,17},{10,2},{26... | collective-permute-start | bytes 1474568 | tf_op jit(solution)/shard_map/ppermute | solution.py:705
  49.6 15.6 %collective-permute-start.11 = (bf16[240,1024]{1,0:T(8,128)(2,1)S(1)}, bf16[240,1024]{1,0:T(8,128)(2,1)S(1)}, u32[]{:S(2)}, u32[]{:S(2)}) collective-permute-start(bf16[240,1024]{1,0:T(8,128)(2,1)S(1)} %get-tuple-element.79.refs_4_), channel_id=1, source_target_pairs={{0,8},{8,24},{24,16},{16,0},{1,9},{9,25},{25,17},{17,1},{2,10},{10... | collective-permute-start | bytes 1474568 | tf_op jit(solution)/shard_map/ppermute | solution.py:704
  54.6 30.8 %copy-start.40 = (bf16[16,256]{1,0:T(8,128)(2,1)}, bf16[16,256]{1,0:T(8,128)(2,1)S(1)}, u32[]{:S(2)}) copy-start(bf16[16,256]{1,0:T(8,128)(2,1)S(1)} %get-tuple-element.97.refs_9_.refs_2_) | copy-start | bytes 24580
  57.4 17.1 %collective-permute-start.14 = (bf16[240,1024]{1,0:T(8,128)(2,1)S(1)}, bf16[240,1024]{1,0:T(8,128)(2,1)S(1)}, u32[]{:S(2)}, u32[]{:S(2)}) collective-permute-start(bf16[240,1024]{1,0:T(8,128)(2,1)S(1)} %get-tuple-element.87), channel_id=1, source_target_pairs={{8,0},{24,8},{16,24},{0,16},{9,1},{25,9},{17,25},{1,17},{10,2},{26... | collective-permute-start | bytes 1474568 | tf_op jit(solution)/shard_map/ppermute | solution.py:705
  58.9 16.0 %collective-permute-start.13 = (bf16[240,1024]{1,0:T(8,128)(2,1)S(1)}, bf16[240,1024]{1,0:T(8,128)(2,1)S(1)}, u32[]{:S(2)}, u32[]{:S(2)}) collective-permute-start(bf16[240,1024]{1,0:T(8,128)(2,1)S(1)} %get-tuple-element.82.refs_4_), channel_id=1, source_target_pairs={{0,8},{8,24},{24,16},{16,0},{1,9},{9,25},{25,17},{17,1},{2,10},{10... | collective-permute-start | bytes 1474568 | tf_op jit(solution)/shard_map/ppermute | solution.py:704
  65.2 20.2 %copy-start.34 = (bf16[16,384]{1,0:T(8,128)(2,1)}, bf16[16,384]{1,0:T(8,128)(2,1)S(1)}, u32[]{:S(2)}) copy-start(bf16[16,384]{1,0:T(8,128)(2,1)S(1)} %get-tuple-element.98.refs_10_.refs_3_) | copy-start | bytes 36868
  68.0 17.4 %collective-permute-start.19 = (bf16[240,1024]{1,0:T(8,128)(2,1)S(1)}, bf16[240,1024]{1,0:T(8,128)(2,1)S(1)}, u32[]{:S(2)}, u32[]{:S(2)}) collective-permute-start(bf16[240,1024]{1,0:T(8,128)(2,1)S(1)} %get-tuple-element.94), channel_id=1, source_target_pairs={{8,0},{24,8},{16,24},{0,16},{9,1},{25,9},{17,25},{1,17},{10,2},{26... | collective-permute-start | bytes 1474568 | tf_op jit(solution)/shard_map/ppermute | solution.py:705
  69.5 15.9 %collective-permute-start.18 = (bf16[240,1024]{1,0:T(8,128)(2,1)S(1)}, bf16[240,1024]{1,0:T(8,128)(2,1)S(1)}, u32[]{:S(2)}, u32[]{:S(2)}) collective-permute-start(bf16[240,1024]{1,0:T(8,128)(2,1)S(1)} %get-tuple-element.85.refs_4_), channel_id=1, source_target_pairs={{0,8},{8,24},{24,16},{16,0},{1,9},{9,25},{25,17},{17,1},{2,10},{10... | collective-permute-start | bytes 1474568 | tf_op jit(solution)/shard_map/ppermute | solution.py:704
  74.5 11.0 %copy-start.42 = (bf16[16,256]{1,0:T(8,128)(2,1)}, bf16[16,256]{1,0:T(8,128)(2,1)S(1)}, u32[]{:S(2)}) copy-start(bf16[16,256]{1,0:T(8,128)(2,1)S(1)} %get-tuple-element.99.refs_11_.refs_4_) | copy-start | bytes 24580
  77.5 17.3 %collective-permute-start.16 = (bf16[240,1024]{1,0:T(8,128)(2,1)S(1)}, bf16[240,1024]{1,0:T(8,128)(2,1)S(1)}, u32[]{:S(2)}, u32[]{:S(2)}) collective-permute-start(bf16[240,1024]{1,0:T(8,128)(2,1)S(1)} %get-tuple-element.90), channel_id=1, source_target_pairs={{8,0},{24,8},{16,24},{0,16},{9,1},{25,9},{17,25},{1,17},{10,2},{26... | collective-permute-start | bytes 1474568 | tf_op jit(solution)/shard_map/ppermute | solution.py:705
  79.1 16.9 %collective-permute-start.15 = (bf16[240,1024]{1,0:T(8,128)(2,1)S(1)}, bf16[240,1024]{1,0:T(8,128)(2,1)S(1)}, u32[]{:S(2)}, u32[]{:S(2)}) collective-permute-start(bf16[240,1024]{1,0:T(8,128)(2,1)S(1)} %get-tuple-element.88.refs_4_), channel_id=1, source_target_pairs={{0,8},{8,24},{24,16},{16,0},{1,9},{9,25},{25,17},{17,1},{2,10},{10... | collective-permute-start | bytes 1474568 | tf_op jit(solution)/shard_map/ppermute | solution.py:704
  88.0 21.3 %collective-permute-start.20 = (bf16[304,1024]{1,0:T(8,128)(2,1)}, bf16[304,1024]{1,0:T(8,128)(2,1)S(1)}, u32[]{:S(2)}, u32[]{:S(2)}) collective-permute-start(bf16[304,1024]{1,0:T(8,128)(2,1)} %get-tuple-element.101), channel_id=1, source_target_pairs={{0,8},{8,24},{24,16},{16,0},{1,9},{9,25},{25,17},{17,1},{2,10},{10... | collective-permute-start | bytes 1867784 | tf_op jit(solution)/shard_map/ppermute | solution.py:704
  89.2 18.3 %collective-permute-start.21 = (bf16[288,1024]{1,0:T(8,128)(2,1)}, bf16[288,1024]{1,0:T(8,128)(2,1)S(1)}, u32[]{:S(2)}, u32[]{:S(2)}) collective-permute-start(bf16[288,1024]{1,0:T(8,128)(2,1)} %get-tuple-element.102), channel_id=1, source_target_pairs={{8,0},{24,8},{16,24},{0,16},{9,1},{25,9},{17,25},{1,17},{10,2},{26... | collective-permute-start | bytes 1769480 | tf_op jit(solution)/shard_map/ppermute | solution.py:705
  98.3 19.9 %collective-permute-start.24 = (bf16[240,1024]{1,0:T(8,128)(2,1)}, bf16[240,1024]{1,0:T(8,128)(2,1)}, u32[]{:S(2)}, u32[]{:S(2)}) collective-permute-start(bf16[240,1024]{1,0:T(8,128)(2,1)} %get-tuple-element.106), channel_id=1, source_target_pairs={{8,0},{24,8},{16,24},{0,16},{9,1},{25,9},{17,25},{1,17},{10,2},{26... | collective-permute-start | bytes 1474568 | tf_op jit(solution)/shard_map/ppermute | solution.py:705
  99.8 20.1 %collective-permute-start.23 = (bf16[240,1024]{1,0:T(8,128)(2,1)}, bf16[240,1024]{1,0:T(8,128)(2,1)}, u32[]{:S(2)}, u32[]{:S(2)}) collective-permute-start(bf16[240,1024]{1,0:T(8,128)(2,1)} %get-tuple-element.91.refs_1_), channel_id=1, source_target_pairs={{0,8},{8,24},{24,16},{16,0},{1,9},{9,25},{25,17},{17,1},{2,10},{10... | collective-permute-start | bytes 1474568 | tf_op jit(solution)/shard_map/ppermute | solution.py:704
  102.0 9.8 %copy-start.29 = (f32[8,4096]{1,0:T(8,128)}, f32[8,4096]{1,0:T(8,128)S(1)}, u32[]{:S(2)}) copy-start(f32[8,4096]{1,0:T(8,128)S(1)} %get-tuple-element.92.refs_6_.refs_0_) | copy-start | bytes 393220
  102.0 11.9 %collective-permute-start.17 = (f32[8,4096]{1,0:T(8,128)}, f32[8,4096]{1,0:T(8,128)}, u32[]{:S(2)}, u32[]{:S(2)}) collective-permute-start(f32[8,4096]{1,0:T(8,128)} %get-tuple-element.93), channel_id=1, source_target_pairs={{0,4},{2,6},{4,0},{6,2},{1,5},{3,7},{5,1},{7,3},{8,12},{10,14},{12... | collective-permute-start | bytes 393224 | tf_op jit(solution)/shard_map/ppermute | solution.py:402
  107.5 29.4 %copy-start.1 = (bf16[288,1024]{1,0:T(8,128)(2,1)}, bf16[288,1024]{1,0:T(8,128)(2,1)S(1)}, u32[]{:S(2)}) copy-start(bf16[288,1024]{1,0:T(8,128)(2,1)S(1)} %collective-permute-done.21.refs_5_.refs_8_.refs_9_) | copy-start | bytes 1769476
  109.3 27.6 %copy-start = (bf16[304,1024]{1,0:T(8,128)(2,1)}, bf16[304,1024]{1,0:T(8,128)(2,1)S(1)}, u32[]{:S(2)}) copy-start(bf16[304,1024]{1,0:T(8,128)(2,1)S(1)} %collective-permute-done.20.refs_4_.refs_6_.refs_8_) | copy-start | bytes 1867780
  111.8 20.7 %collective-permute-start.26 = (bf16[288,1024]{1,0:T(8,128)(2,1)}, bf16[288,1024]{1,0:T(8,128)(2,1)S(1)}, u32[]{:S(2)}, u32[]{:S(2)}) collective-permute-start(bf16[288,1024]{1,0:T(8,128)(2,1)} %get-tuple-element.103.refs_2_), channel_id=1, source_target_pairs={{0,8},{8,24},{24,16},{16,0},{1,9},{9,25},{25,17},{17,1},{2,10},{10... | collective-permute-start | bytes 1769480 | tf_op jit(solution)/shard_map/ppermute | solution.py:704
  112.6 17.9 %collective-permute-start.27 = (bf16[240,1024]{1,0:T(8,128)(2,1)}, bf16[240,1024]{1,0:T(8,128)(2,1)}, u32[]{:S(2)}, u32[]{:S(2)}) collective-permute-start(bf16[240,1024]{1,0:T(8,128)(2,1)} %get-tuple-element.110), channel_id=1, source_target_pairs={{8,0},{24,8},{16,24},{0,16},{9,1},{25,9},{17,25},{1,17},{10,2},{26... | collective-permute-start | bytes 1474568 | tf_op jit(solution)/shard_map/ppermute | solution.py:705
  116.3 5.8 %copy-start.31 = (f32[4,4096]{1,0:T(4,128)}, f32[4,4096]{1,0:T(4,128)S(1)}, u32[]{:S(2)}) copy-start(f32[4,4096]{1,0:T(4,128)S(1)} %get-tuple-element.104.refs_6_.refs_0_) | copy-start | bytes 196612
  122.1 24.1 %collective-permute-start.29 = (bf16[240,1024]{1,0:T(8,128)(2,1)}, bf16[240,1024]{1,0:T(8,128)(2,1)}, u32[]{:S(2)}, u32[]{:S(2)}) collective-permute-start(bf16[240,1024]{1,0:T(8,128)(2,1)} %get-tuple-element.114), channel_id=1, source_target_pairs={{8,0},{24,8},{16,24},{0,16},{9,1},{25,9},{17,25},{1,17},{10,2},{26... | collective-permute-start | bytes 1474568 | tf_op jit(solution)/shard_map/ppermute | solution.py:705
  123.6 22.5 %collective-permute-start.28 = (bf16[240,1024]{1,0:T(8,128)(2,1)}, bf16[240,1024]{1,0:T(8,128)(2,1)}, u32[]{:S(2)}, u32[]{:S(2)}) collective-permute-start(bf16[240,1024]{1,0:T(8,128)(2,1)} %get-tuple-element.107.refs_2_), channel_id=1, source_target_pairs={{0,8},{8,24},{24,16},{16,0},{1,9},{9,25},{25,17},{17,1},{2,10},{10... | collective-permute-start | bytes 1474568 | tf_op jit(solution)/shard_map/ppermute | solution.py:704
  124.1 4.6 %collective-permute-start.22 = (f32[4,4096]{1,0:T(4,128)}, f32[4,4096]{1,0:T(4,128)}, u32[]{:S(2)}, u32[]{:S(2)}) collective-permute-start(f32[4,4096]{1,0:T(4,128)} %get-tuple-element.105), channel_id=1, source_target_pairs={{0,2},{2,0},{4,6},{6,4},{1,3},{3,1},{5,7},{7,5},{8,10},{10,8},{12,... | collective-permute-start | bytes 196616 | tf_op jit(solution)/shard_map/ppermute | solution.py:402
  130.4 15.1 %collective-permute-start.25 = (f32[2,4096]{1,0:T(2,128)S(1)}, f32[2,4096]{1,0:T(2,128)S(1)}, u32[]{:S(2)}, u32[]{:S(2)}) collective-permute-start(f32[2,4096]{1,0:T(2,128)S(1)} %get-tuple-element.109), channel_id=1, source_target_pairs={{0,1},{1,0},{2,3},{3,2},{4,5},{5,4},{6,7},{7,6},{8,9},{9,8},{10,11... | collective-permute-start | bytes 98312 | tf_op jit(solution)/shard_map/ppermute | solution.py:402
  132.5 4.4 %copy-start.37 = (bf16[16,384]{1,0:T(8,128)(2,1)S(1)}, bf16[16,384]{1,0:T(8,128)(2,1)}, u32[]{:S(2)}) copy-start(bf16[16,384]{1,0:T(8,128)(2,1)} %copy-done.36) | copy-start | bytes 36868
  132.5 4.4 %copy-start.39 = (bf16[16,256]{1,0:T(8,128)(2,1)S(1)}, bf16[16,256]{1,0:T(8,128)(2,1)}, u32[]{:S(2)}) copy-start(bf16[16,256]{1,0:T(8,128)(2,1)} %copy-done.38) | copy-start | bytes 24580
  132.5 4.4 %copy-start.41 = (bf16[16,256]{1,0:T(8,128)(2,1)S(1)}, bf16[16,256]{1,0:T(8,128)(2,1)}, u32[]{:S(2)}) copy-start(bf16[16,256]{1,0:T(8,128)(2,1)} %copy-done.40) | copy-start | bytes 24580
  132.5 4.4 %copy-start.43 = (bf16[16,256]{1,0:T(8,128)(2,1)S(1)}, bf16[16,256]{1,0:T(8,128)(2,1)}, u32[]{:S(2)}) copy-start(bf16[16,256]{1,0:T(8,128)(2,1)} %copy-done.42) | copy-start | bytes 24580
  134.8 28.9 %collective-permute-start.33 = (bf16[240,1024]{1,0:T(8,128)(2,1)S(1)}, bf16[240,1024]{1,0:T(8,128)(2,1)S(1)}, u32[]{:S(2)}, u32[]{:S(2)}) collective-permute-start(bf16[240,1024]{1,0:T(8,128)(2,1)S(1)} %get-tuple-element.121), channel_id=1, source_target_pairs={{8,0},{24,8},{16,24},{0,16},{9,1},{25,9},{17,25},{1,17},{10,2},{26... | collective-permute-start | bytes 1474568 | tf_op jit(solution)/shard_map/ppermute | solution.py:705
  136.4 27.4 %collective-permute-start.32 = (bf16[240,1024]{1,0:T(8,128)(2,1)S(1)}, bf16[240,1024]{1,0:T(8,128)(2,1)S(1)}, u32[]{:S(2)}, u32[]{:S(2)}) collective-permute-start(bf16[240,1024]{1,0:T(8,128)(2,1)S(1)} %get-tuple-element.111.refs_2_.refs_9_), channel_id=1, source_target_pairs={{0,8},{8,24},{24,16},{16,0},{1,9},{9,25},{25,17},{17,1},{2,10},{10... | collective-permute-start | bytes 1474568 | tf_op jit(solution)/shard_map/ppermute | solution.py:704
  149.1 17.2 %collective-permute-start.31 = (bf16[240,1024]{1,0:T(8,128)(2,1)S(1)}, bf16[240,1024]{1,0:T(8,128)(2,1)S(1)}, u32[]{:S(2)}, u32[]{:S(2)}) collective-permute-start(bf16[240,1024]{1,0:T(8,128)(2,1)S(1)} %get-tuple-element.120), channel_id=1, source_target_pairs={{8,0},{24,8},{16,24},{0,16},{9,1},{25,9},{17,25},{1,17},{10,2},{26... | collective-permute-start | bytes 1474568 | tf_op jit(solution)/shard_map/ppermute | solution.py:705
  149.2 17.1 %collective-permute-start.30 = (bf16[240,1024]{1,0:T(8,128)(2,1)S(1)}, bf16[240,1024]{1,0:T(8,128)(2,1)S(1)}, u32[]{:S(2)}, u32[]{:S(2)}) collective-permute-start(bf16[240,1024]{1,0:T(8,128)(2,1)S(1)} %get-tuple-element.119.refs_6_), channel_id=1, source_target_pairs={{0,8},{8,24},{24,16},{16,0},{1,9},{9,25},{25,17},{17,1},{2,10},{10... | collective-permute-start | bytes 1474568 | tf_op jit(solution)/shard_map/ppermute | solution.py:704
  (32 other events, 68.3 us)

commit v6 on v3

--- a/solution.py
+++ b/solution.py
@@ -765,7 +765,7 @@
 
     block = largest((b for b in range(TILE, 193, TILE) if rows % b == 0), rows)
     blocks = rows // block
-    early = blocks // 4
+    early = blocks // 2
     ready = parcel_from + LAG * reach[0] + 1
     while len(got) < steps:
         ready_sum = len(got) > parcel_from + SUM_AFTER
@@ -778,7 +778,7 @@
         hidden_t, outs = gathered(sent)
         early = 0
     news = update_part(early, blocks - early, sent)
-    for step in (steps - 2, steps - 1, steps):
+    for step in (steps - 1, steps):
         news = patch_to(step, ())
     while not cotangents.done:
         cotangents.advance(sent)

time: 167 us -> 167 us (level)
  starting transfers between devices: 40.2 us -> 36.9 us
  Pallas kernels: 89.2 us -> 91.1 us
    ppermute x14, starting transfers between devices: 24.8 us -> 20.4 us  [send(): lax.ppermute(sends[-1][1], 'replica', backward)]
    unnamed x86 -> x90, local copies, waits for them, and re-layouts: 3.58 us -> 4.35 us
  transfers between devices with their start and end apart: 34 -> 34, of which waited for: 12 -> 12; matrix products, arithmetic and copies ran while one was open for 0% -> 0% of each run, Pallas kernels for 52% -> 54%
where the time goes in v6:
time: 167 us; the launch traced here: 165 us
  Pallas kernels  91.1 us (55%)
  starting transfers between devices  36.9 us (22%)
  waiting for transfers between devices  30.4 us (18%)
  local copies, waits for them, and re-layouts  4.35 us (3%)
  between operations  2.22 us (1%)
    pallas_call x14, Pallas kernels, pack(): pl.pallas_call(functools.partial(pack_body, n=n, places=places, chunk=chu...  36.3 us
    pallas_call x6, Pallas kernels, layer(): pl.pallas_call(functools.partial(layer_body, resumed=resumed, tile=tile,...  30.4 us
    ppermute x14, starting transfers between devices, send(): lax.ppermute(sends[-1][1], 'replica', backward)  20.4 us
    pallas_call x2, Pallas kernels, update(): pl.pallas_call(functools.partial(update_body, n=n, block=block, first=fir...  19.5 us
    ppermute x14, waiting for transfers between devices, send(): lax.ppermute(sends[-1][1], 'replica', backward)  11.6 us
    ppermute x14, starting transfers between devices, send(): lax.ppermute(sends[-1][0], 'replica', forward)  9.65 us
    ppermute x3, waiting for transfers between devices, per_device(): other = lax.ppermute(both, axis, [(i, i ^ apart) for i in range(size)])  8.85 us
    ppermute x14, waiting for transfers between devices, send(): lax.ppermute(sends[-1][0], 'replica', forward)  6.58 us
  transfers between devices with their start and end apart: 34, of which 12 were waited for; matrix products, arithmetic and copies ran while one was open for 0% of the time, Pallas kernels for 54%

profile of v6, /device:TPU:0, one launch (start us, length us, event | category | flops | bytes accessed | tf_op | source)
XLA Modules:
  0.0 165.0 jit_solution(6388534688910481972)
XLA Ops:
  0.7 2.5 %pack.14 = (bf16[240,1024]{1,0:T(8,128)(2,1)S(1)}, bf16[240,1024]{1,0:T(8,128)(2,1)S(1)}) custom-call(f32[2,1920,1024]{2,1,0:T(8,128)} %refs_0_.31, f32[2,1920,1024]{2,1,0:T(8,128)} %refs_1_.43, f32[2,1920,1024]{2,1,0:T(8,128)} %refs_2_.43), custom_call_target="tpu_custom_call" | custom-call | bytes 2949120 | tf_op jit(solution)/shard_map/pack/pallas_call | solution.py:200
  3.1 3.0 %collective-permute-start.4 = (bf16[240,1024]{1,0:T(8,128)(2,1)S(1)}, bf16[240,1024]{1,0:T(8,128)(2,1)S(1)}, u32[]{:S(2)}, u32[]{:S(2)}) collective-permute-start(bf16[240,1024]{1,0:T(8,128)(2,1)S(1)} %get-tuple-element.69), channel_id=1, source_target_pairs={{8,0},{24,8},{16,24},{0,16},{9,1},{25,9},{17,25},{1,17},{10,2},{26... | collective-permute-start | bytes 1474568 | tf_op jit(solution)/shard_map/ppermute | solution.py:705
  6.2 2.5 %pack.15 = (bf16[240,1024]{1,0:T(8,128)(2,1)S(1)}, bf16[240,1024]{1,0:T(8,128)(2,1)S(1)}) custom-call(f32[2,1920,1024]{2,1,0:T(8,128)} %refs_0_.31, f32[2,1920,1024]{2,1,0:T(8,128)} %refs_1_.43, f32[2,1920,1024]{2,1,0:T(8,128)} %refs_2_.43, bf16[1,2,8192]{2,1,0:T(2,128)(2,1)S(1)} %beside.1.refs_3_.own), custom_call_target="tpu_custom_call" | custom-call | bytes 2949120 | tf_op jit(solution)/shard_map/pack/pallas_call | solution.py:200
  8.7 2.0 %collective-permute-start.6 = (bf16[240,1024]{1,0:T(8,128)(2,1)S(1)}, bf16[240,1024]{1,0:T(8,128)(2,1)S(1)}, u32[]{:S(2)}, u32[]{:S(2)}) collective-permute-start(bf16[240,1024]{1,0:T(8,128)(2,1)S(1)} %get-tuple-element.72), channel_id=1, source_target_pairs={{8,0},{24,8},{16,24},{0,16},{9,1},{25,9},{17,25},{1,17},{10,2},{26... | collective-permute-start | bytes 1474568 | tf_op jit(solution)/shard_map/ppermute | solution.py:705
  10.8 1.2 collective-permute-done.other
  12.0 2.1 %collective-permute-start.1 = (bf16[2,2,8192]{2,1,0:T(2,128)(2,1)S(1)}, bf16[2,2,8192]{2,1,0:T(2,128)(2,1)S(1)}, u32[]{:S(2)}, u32[]{:S(2)}) collective-permute-start(bf16[2,2,8192]{2,1,0:T(2,128)(2,1)S(1)} %join.3.own), channel_id=1, source_target_pairs={{0,2},{2,0},{4,6},{6,4},{1,3},{3,1},{5,7},{7,5},{8,10},{10,8},{12,... | collective-permute-start | bytes 196616 | tf_op jit(solution)/shard_map/ppermute | solution.py:720
  14.1 2.4 %collective-permute-done.1.other = bf16[2,2,8192]{2,1,0:T(2,128)(2,1)S(1)} collective-permute-done((bf16[2,2,8192]{2,1,0:T(2,128)(2,1)S(1)}, bf16[2,2,8192]{2,1,0:T(2,128)(2,1)S(1)}, u32[]{:S(2)}, u32[]{:S(2)}) %collective-permute-start.1) | collective-permute-done | bytes 65568 | tf_op jit(solution)/shard_map/ppermute | solution.py:720
  16.5 2.9 %collective-permute-start.2 = (bf16[4,2,8192]{2,1,0:T(2,128)(2,1)S(1)}, bf16[4,2,8192]{2,1,0:T(2,128)(2,1)S(1)}, u32[]{:S(2)}, u32[]{:S(2)}) collective-permute-start(bf16[4,2,8192]{2,1,0:T(2,128)(2,1)S(1)} %join.4.own), channel_id=1, source_target_pairs={{0,4},{2,6},{4,0},{6,2},{1,5},{3,7},{5,1},{7,3},{8,12},{10,14},{12... | collective-permute-start | bytes 393224 | tf_op jit(solution)/shard_map/ppermute | solution.py:720
  20.1 5.2 %collective-permute-done.2.other = bf16[4,2,8192]{2,1,0:T(2,128)(2,1)S(1)} collective-permute-done((bf16[4,2,8192]{2,1,0:T(2,128)(2,1)S(1)}, bf16[4,2,8192]{2,1,0:T(2,128)(2,1)S(1)}, u32[]{:S(2)}, u32[]{:S(2)}) %collective-permute-start.2) | collective-permute-done | bytes 131104 | tf_op jit(solution)/shard_map/ppermute | solution.py:720
  25.5 2.7 %pack.16 = (bf16[240,1024]{1,0:T(8,128)(2,1)S(1)}, bf16[240,1024]{1,0:T(8,128)(2,1)S(1)}) custom-call(s32[1]{0:T(128)S(6)} %copy.37.refs_0_.failed, f32[2,1920,1024]{2,1,0:T(8,128)} %refs_0_.31, f32[2,1920,1024]{2,1,0:T(8,128)} %refs_1_.43, f32[2,1920,1024]{2,1,0:T(8,128)} %refs_2_.43, bf16[240,1024]{1,0:T(8,128)(2,1)S(1)} %collective-permute-done.3.refs_4_.refs_0_, ...), custom_call_target="tpu_custom_call" | custom-call | bytes 2949120 | tf_op jit(solution)/shard_map/pack/pallas_call | solution.py:200
  28.3 1.5 collective-permute-start.8
  30.4 4.4 %layer.6 = (bf16[16,256]{1,0:T(8,128)(2,1)S(1)}, f32[16,4096]{1,0:T(8,128)S(1)}) custom-call(bf16[16,8192]{1,0:T(8,128)(2,1)S(1)} %join.5.refs_6_.both, bf16[4096,1920]{1,0:T(8,128)(2,1)} %refs_0_.29, bf16[4096,1920]{1,0:T(8,128)(2,1)} %refs_1_.35, bf16[1920,4096]{1,0:T(8,128)(2,1)} %refs_2_.35, bf16[240,1024]{1,0:T(8,128)(2,1)S(1)} %get-tuple-element.70.refs_3_), custom_call_target="tpu_custom_call" | custom-call | flops 167772160 | bytes 6291456 | tf_op jit(solution)/shard_map/layer/pallas_call | solution.py:329
  34.9 2.7 %pack.17 = (bf16[240,1024]{1,0:T(8,128)(2,1)S(1)}, bf16[240,1024]{1,0:T(8,128)(2,1)S(1)}) custom-call(s32[1]{0:T(128)S(6)} %copy.37.refs_0_.failed, f32[2,1920,1024]{2,1,0:T(8,128)} %refs_0_.31, f32[2,1920,1024]{2,1,0:T(8,128)} %refs_1_.43, f32[2,1920,1024]{2,1,0:T(8,128)} %refs_2_.43, bf16[240,1024]{1,0:T(8,128)(2,1)S(1)} %collective-permute-done.5.refs_4_.refs_2_, ...), custom_call_target="tpu_custom_call" | custom-call | bytes 2949120 | tf_op jit(solution)/shard_map/pack/pallas_call | solution.py:200
  37.7 1.4 collective-permute-start.10
  39.7 5.7 %layer.7 = (bf16[16,384]{1,0:T(8,128)(2,1)S(1)}, f32[16,4096]{1,0:T(8,128)S(1)}) custom-call(bf16[16,8192]{1,0:T(8,128)(2,1)S(1)} %join.5.refs_6_.both, bf16[4096,1920]{1,0:T(8,128)(2,1)} %refs_0_.29, bf16[4096,1920]{1,0:T(8,128)(2,1)} %refs_1_.35, bf16[1920,4096]{1,0:T(8,128)(2,1)} %refs_2_.35, f32[16,4096]{1,0:T(8,128)S(1)} %get-tuple-element.71.refs_6_.refs_3_, ...), custom_call_target="tpu_custom_call" | custom-call | flops 251658240 | bytes 9437184 | tf_op jit(solution)/shard_map/layer/pallas_call | solution.py:329
  45.5 2.7 %pack.18 = (bf16[240,1024]{1,0:T(8,128)(2,1)S(1)}, bf16[240,1024]{1,0:T(8,128)(2,1)S(1)}) custom-call(s32[1]{0:T(128)S(6)} %copy.37.refs_0_.failed, f32[2,1920,1024]{2,1,0:T(8,128)} %refs_0_.31, f32[2,1920,1024]{2,1,0:T(8,128)} %refs_1_.43, f32[2,1920,1024]{2,1,0:T(8,128)} %refs_2_.43, bf16[240,1024]{1,0:T(8,128)(2,1)S(1)} %collective-permute-done.7.refs_4_, ...), custom_call_target="tpu_custom_call" | custom-call | bytes 2949120 | tf_op jit(solution)/shard_map/pack/pallas_call | solution.py:200
  48.3 1.3 collective-permute-start.12
  50.4 4.4 %layer.8 = (bf16[16,256]{1,0:T(8,128)(2,1)S(1)}, f32[16,4096]{1,0:T(8,128)S(1)}) custom-call(bf16[16,8192]{1,0:T(8,128)(2,1)S(1)} %join.5.refs_6_.both, bf16[4096,1920]{1,0:T(8,128)(2,1)} %refs_0_.29, bf16[4096,1920]{1,0:T(8,128)(2,1)} %refs_1_.35, bf16[1920,4096]{1,0:T(8,128)(2,1)} %refs_2_.35, f32[16,4096]{1,0:T(8,128)S(1)} %get-tuple-element.74.refs_6_.refs_3_, ...), custom_call_target="tpu_custom_call" | custom-call | flops 167772160 | bytes 6291456 | tf_op jit(solution)/shard_map/layer/pallas_call | solution.py:329
  54.8 2.7 %pack.19 = (bf16[240,1024]{1,0:T(8,128)(2,1)S(1)}, bf16[240,1024]{1,0:T(8,128)(2,1)S(1)}) custom-call(s32[1]{0:T(128)S(6)} %copy.37.refs_0_.failed, f32[2,1920,1024]{2,1,0:T(8,128)} %refs_0_.31, f32[2,1920,1024]{2,1,0:T(8,128)} %refs_1_.43, f32[2,1920,1024]{2,1,0:T(8,128)} %refs_2_.43, bf16[240,1024]{1,0:T(8,128)(2,1)S(1)} %collective-permute-done.9.refs_4_.refs_6_, ...), custom_call_target="tpu_custom_call" | custom-call | bytes 2949120 | tf_op jit(solution)/shard_map/pack/pallas_call | solution.py:200
  57.6 1.3 collective-permute-start.14
  59.7 5.7 %layer.9 = (bf16[16,384]{1,0:T(8,128)(2,1)S(1)}, f32[16,4096]{1,0:T(8,128)S(1)}) custom-call(bf16[16,8192]{1,0:T(8,128)(2,1)S(1)} %join.5.refs_6_.both, bf16[4096,1920]{1,0:T(8,128)(2,1)} %refs_0_.29, bf16[4096,1920]{1,0:T(8,128)(2,1)} %refs_1_.35, bf16[1920,4096]{1,0:T(8,128)(2,1)} %refs_2_.35, f32[16,4096]{1,0:T(8,128)S(1)} %get-tuple-element.77.refs_6_.refs_3_, ...), custom_call_target="tpu_custom_call" | custom-call | flops 251658240 | bytes 9437184 | tf_op jit(solution)/shard_map/layer/pallas_call | solution.py:329
  65.5 2.7 %pack.20 = (bf16[240,1024]{1,0:T(8,128)(2,1)S(1)}, bf16[240,1024]{1,0:T(8,128)(2,1)S(1)}) custom-call(s32[1]{0:T(128)S(6)} %copy.37.refs_0_.failed, f32[2,1920,1024]{2,1,0:T(8,128)} %refs_0_.31, f32[2,1920,1024]{2,1,0:T(8,128)} %refs_1_.43, f32[2,1920,1024]{2,1,0:T(8,128)} %refs_2_.43, bf16[240,1024]{1,0:T(8,128)(2,1)S(1)} %collective-permute-done.11.refs_4_.refs_8_, ...), custom_call_target="tpu_custom_call" | custom-call | bytes 2949120 | tf_op jit(solution)/shard_map/pack/pallas_call | solution.py:200
  68.2 1.2 collective-permute-start.19
  70.3 4.4 %layer.10 = (bf16[16,256]{1,0:T(8,128)(2,1)S(1)}, f32[16,4096]{1,0:T(8,128)S(1)}) custom-call(bf16[16,8192]{1,0:T(8,128)(2,1)S(1)} %join.5.refs_6_.both, bf16[4096,1920]{1,0:T(8,128)(2,1)} %refs_0_.29, bf16[4096,1920]{1,0:T(8,128)(2,1)} %refs_1_.35, bf16[1920,4096]{1,0:T(8,128)(2,1)} %refs_2_.35, f32[16,4096]{1,0:T(8,128)S(1)} %get-tuple-element.80.refs_6_.refs_3_, ...), custom_call_target="tpu_custom_call" | custom-call | flops 167772160 | bytes 6291456 | tf_op jit(solution)/shard_map/layer/pallas_call | solution.py:329
  74.9 2.7 %pack.21 = (bf16[240,1024]{1,0:T(8,128)(2,1)S(1)}, bf16[240,1024]{1,0:T(8,128)(2,1)S(1)}) custom-call(s32[1]{0:T(128)S(6)} %copy.37.refs_0_.failed, f32[2,1920,1024]{2,1,0:T(8,128)} %refs_0_.31, f32[2,1920,1024]{2,1,0:T(8,128)} %refs_1_.43, f32[2,1920,1024]{2,1,0:T(8,128)} %refs_2_.43, bf16[240,1024]{1,0:T(8,128)(2,1)S(1)} %collective-permute-done.13.refs_4_.refs_10_, ...), custom_call_target="tpu_custom_call" | custom-call | bytes 2949120 | tf_op jit(solution)/shard_map/pack/pallas_call | solution.py:200
  77.6 1.5 collective-permute-start.16
  79.7 5.7 %layer.11 = (bf16[16,384]{1,0:T(8,128)(2,1)S(1)}, f32[16,4096]{1,0:T(8,128)S(1)}) custom-call(bf16[16,8192]{1,0:T(8,128)(2,1)S(1)} %join.5.refs_6_.both, bf16[4096,1920]{1,0:T(8,128)(2,1)} %refs_0_.29, bf16[4096,1920]{1,0:T(8,128)(2,1)} %refs_1_.35, bf16[1920,4096]{1,0:T(8,128)(2,1)} %refs_2_.35, f32[16,4096]{1,0:T(8,128)S(1)} %get-tuple-element.83.refs_6_.refs_3_, ...), custom_call_target="tpu_custom_call" | custom-call | flops 251658240 | bytes 9437184 | tf_op jit(solution)/shard_map/layer/pallas_call | solution.py:329
  85.5 2.4 %pack.23 = (bf16[304,1024]{1,0:T(8,128)(2,1)}, bf16[288,1024]{1,0:T(8,128)(2,1)}) custom-call(s32[1]{0:T(128)S(6)} %copy.37.refs_0_.failed, f32[2,1920,1024]{2,1,0:T(8,128)} %refs_0_.31, f32[2,1920,1024]{2,1,0:T(8,128)} %refs_1_.43, f32[2,1920,1024]{2,1,0:T(8,128)} %refs_2_.43, bf16[240,1024]{1,0:T(8,128)(2,1)S(1)} %collective-permute-done.18.refs_4_.refs_0_, ...), custom_call_target="tpu_custom_call" | custom-call | bytes 2949120 | tf_op jit(solution)/shard_map/pack/pallas_call | solution.py:200
  87.9 1.2 collective-permute-start.20
  90.0 4.8 %collective-permute-done.16.refs_5_.refs_3_ = bf16[240,1024]{1,0:T(8,128)(2,1)S(1)} collective-permute-done((bf16[240,1024]{1,0:T(8,128)(2,1)S(1)}, bf16[240,1024]{1,0:T(8,128)(2,1)S(1)}, u32[]{:S(2)}, u32[]{:S(2)}) %collective-permute-start.16) | collective-permute-done | bytes 491552 | tf_op jit(solution)/shard_map/ppermute | solution.py:705
  96.0 2.4 %pack.22 = (bf16[240,1024]{1,0:T(8,128)(2,1)}, bf16[240,1024]{1,0:T(8,128)(2,1)}) custom-call(s32[1]{0:T(128)S(6)} %copy.37.refs_0_.failed, f32[2,1920,1024]{2,1,0:T(8,128)} %refs_0_.31, f32[2,1920,1024]{2,1,0:T(8,128)} %refs_1_.43, f32[2,1920,1024]{2,1,0:T(8,128)} %refs_2_.43, bf16[240,1024]{1,0:T(8,128)(2,1)S(1)} %collective-permute-done.15.refs_4_.refs_2_, ...), custom_call_target="tpu_custom_call" | custom-call | bytes 2949120 | tf_op jit(solution)/shard_map/pack/pallas_call | solution.py:200
  98.4 1.4 collective-permute-start.24
  102.7 4.9 %collective-permute-done.21.refs_5_.refs_8_ = bf16[288,1024]{1,0:T(8,128)(2,1)S(1)} collective-permute-done((bf16[288,1024]{1,0:T(8,128)(2,1)}, bf16[288,1024]{1,0:T(8,128)(2,1)S(1)}, u32[]{:S(2)}, u32[]{:S(2)}) %collective-permute-start.21) | collective-permute-done | bytes 589856 | tf_op jit(solution)/shard_map/ppermute | solution.py:705
  107.5 1.8 %collective-permute-done.20.refs_4_.refs_6_ = bf16[304,1024]{1,0:T(8,128)(2,1)S(1)} collective-permute-done((bf16[304,1024]{1,0:T(8,128)(2,1)}, bf16[304,1024]{1,0:T(8,128)(2,1)S(1)}, u32[]{:S(2)}, u32[]{:S(2)}) %collective-permute-start.20) | collective-permute-done | bytes 622624 | tf_op jit(solution)/shard_map/ppermute | solution.py:704
  109.3 2.5 %pack.24 = (bf16[288,1024]{1,0:T(8,128)(2,1)}, bf16[240,1024]{1,0:T(8,128)(2,1)}) custom-call(s32[1]{0:T(128)S(6)} %copy.37.refs_0_.failed, f32[2,1920,1024]{2,1,0:T(8,128)} %refs_0_.31, f32[2,1920,1024]{2,1,0:T(8,128)} %refs_1_.43, f32[2,1920,1024]{2,1,0:T(8,128)} %refs_2_.43, bf16[304,1024]{1,0:T(8,128)(2,1)S(1)} %collective-permute-done.20.refs_4_.refs_6_, ...), custom_call_target="tpu_custom_call" | custom-call | bytes 2949120 | tf_op jit(solution)/shard_map/pack/pallas_call | solution.py:200
  112.5 1.5 collective-permute-start.27
  114.8 1.5 halve.5
  116.4 1.8 %collective-permute-done.24.refs_5_.refs_7_ = bf16[240,1024]{1,0:T(8,128)(2,1)} collective-permute-done((bf16[240,1024]{1,0:T(8,128)(2,1)}, bf16[240,1024]{1,0:T(8,128)(2,1)}, u32[]{:S(2)}, u32[]{:S(2)}) %collective-permute-start.24) | collective-permute-done | bytes 491552 | tf_op jit(solution)/shard_map/ppermute | solution.py:705
  118.1 1.8 %collective-permute-done.23.refs_4_.refs_6_ = bf16[240,1024]{1,0:T(8,128)(2,1)} collective-permute-done((bf16[240,1024]{1,0:T(8,128)(2,1)}, bf16[240,1024]{1,0:T(8,128)(2,1)}, u32[]{:S(2)}, u32[]{:S(2)}) %collective-permute-start.23) | collective-permute-done | bytes 491552 | tf_op jit(solution)/shard_map/ppermute | solution.py:704
  119.9 2.3 %pack.25 = (bf16[240,1024]{1,0:T(8,128)(2,1)}, bf16[240,1024]{1,0:T(8,128)(2,1)}) custom-call(s32[1]{0:T(128)S(6)} %copy.37.refs_0_.failed, f32[2,1920,1024]{2,1,0:T(8,128)} %refs_0_.31, f32[2,1920,1024]{2,1,0:T(8,128)} %refs_1_.43, f32[2,1920,1024]{2,1,0:T(8,128)} %refs_2_.43, bf16[240,1024]{1,0:T(8,128)(2,1)} %collective-permute-done.23.refs_4_.refs_6_, ...), custom_call_target="tpu_custom_call" | custom-call | bytes 2949120 | tf_op jit(solution)/shard_map/pack/pallas_call | solution.py:200
  122.2 1.4 collective-permute-start.29
  125.5 3.4 %collective-permute-done.22.refs_1_ = f32[4,4096]{1,0:T(4,128)} collective-permute-done((f32[4,4096]{1,0:T(4,128)}, f32[4,4096]{1,0:T(4,128)}, u32[]{:S(2)}, u32[]{:S(2)}) %collective-permute-start.22) | collective-permute-done | bytes 65568 | tf_op jit(solution)/shard_map/ppermute | solution.py:402
  130.7 1.8 %collective-permute-done.26.refs_4_.refs_7_.refs_8_ = bf16[288,1024]{1,0:T(8,128)(2,1)S(1)} collective-permute-done((bf16[288,1024]{1,0:T(8,128)(2,1)}, bf16[288,1024]{1,0:T(8,128)(2,1)S(1)}, u32[]{:S(2)}, u32[]{:S(2)}) %collective-permute-start.26) | collective-permute-done | bytes 589856 | tf_op jit(solution)/shard_map/ppermute | solution.py:704
  132.5 2.7 %pack.26 = (bf16[240,1024]{1,0:T(8,128)(2,1)S(1)}, bf16[240,1024]{1,0:T(8,128)(2,1)S(1)}) custom-call(s32[1]{0:T(128)S(6)} %copy.37.refs_0_.failed, f32[2,1920,1024]{2,1,0:T(8,128)} %refs_0_.31, f32[2,1920,1024]{2,1,0:T(8,128)} %refs_1_.43, f32[2,1920,1024]{2,1,0:T(8,128)} %refs_2_.43, bf16[288,1024]{1,0:T(8,128)(2,1)S(1)} %collective-permute-done.26.refs_4_.refs_7_.refs_8_, ...), custom_call_target="tpu_custom_call" | custom-call | bytes 2949120 | tf_op jit(solution)/shard_map/pack/pallas_call | solution.py:200
  138.1 10.2 %update.2 = (f32[1920,1024]{1,0:T(8,128)}, f32[1920,1024]{1,0:T(8,128)}, f32[1920,1024]{1,0:T(8,128)}) custom-call(s32[1]{0:T(128)S(6)} %copy.37.refs_0_.failed, bf16[1920,64]{1,0:T(8,128)(2,1)S(1)} %get-tuple-element.109.hid_ref.refs_3_, bf16[64,1024]{1,0:T(8,128)(2,1)S(1)} %get-tuple-element.110.out_ref, f32[2,1920,1024]{2,1,0:T(8,128)} %refs_0_.31, ...), custom_call_target="tpu_custom_call" | custom-call | flops 125829120 | bytes 23592960 | tf_op jit(solution)/shard_map/update/pallas_call | solution.py:523
  149.7 2.5 %pack.27 = (bf16[240,1024]{1,0:T(8,128)(2,1)S(1)}, bf16[240,1024]{1,0:T(8,128)(2,1)S(1)}) custom-call(s32[1]{0:T(128)S(6)} %copy.37.refs_0_.failed, f32[2,1920,1024]{2,1,0:T(8,128)} %refs_0_.31, f32[2,1920,1024]{2,1,0:T(8,128)} %refs_1_.43, f32[2,1920,1024]{2,1,0:T(8,128)} %refs_2_.43, bf16[240,1024]{1,0:T(8,128)(2,1)} %collective-permute-done.28.refs_4_.refs_10_, ...), custom_call_target="tpu_custom_call" | custom-call | bytes 2949120 | tf_op jit(solution)/shard_map/pack/pallas_call | solution.py:200
  153.1 1.2 collective-permute-start.30
  154.3 9.3 %update.3 = (f32[1920,1024]{1,0:T(8,128)}, f32[1920,1024]{1,0:T(8,128)}, f32[1920,1024]{1,0:T(8,128)}) custom-call(s32[1]{0:T(128)S(6)} %copy.37.refs_0_.failed, bf16[1920,64]{1,0:T(8,128)(2,1)S(1)} %get-tuple-element.109.hid_ref.refs_3_, ...), custom_call_target="tpu_custom_call", output_to_operand_aliasing={{0}: (6, {}), {1}: (7, {}), {2}: (8, {})} | custom-call | flops 125829120 | bytes 23592960 | tf_op jit(solution)/shard_map/update/pallas_call | solution.py:523
  (144 shorter events, 21.0 us)
Async XLA Ops:
  3.1 22.4 %collective-permute-start.4 = (bf16[240,1024]{1,0:T(8,128)(2,1)S(1)}, bf16[240,1024]{1,0:T(8,128)(2,1)S(1)}, u32[]{:S(2)}, u32[]{:S(2)}) collective-permute-start(bf16[240,1024]{1,0:T(8,128)(2,1)S(1)} %get-tuple-element.69), channel_id=1, source_target_pairs={{8,0},{24,8},{16,24},{0,16},{9,1},{25,9},{17,25},{1,17},{10,2},{26... | collective-permute-start | bytes 1474568 | tf_op jit(solution)/shard_map/ppermute | solution.py:705
  6.2 19.4 %collective-permute-start.3 = (bf16[240,1024]{1,0:T(8,128)(2,1)S(1)}, bf16[240,1024]{1,0:T(8,128)(2,1)S(1)}, u32[]{:S(2)}, u32[]{:S(2)}) collective-permute-start(bf16[240,1024]{1,0:T(8,128)(2,1)S(1)} %get-tuple-element.67.refs_2_), channel_id=1, source_target_pairs={{0,8},{8,24},{24,16},{16,0},{1,9},{9,25},{25,17},{17,1},{2,10},{10... | collective-permute-start | bytes 1474568 | tf_op jit(solution)/shard_map/ppermute | solution.py:704
  8.7 26.2 %collective-permute-start.6 = (bf16[240,1024]{1,0:T(8,128)(2,1)S(1)}, bf16[240,1024]{1,0:T(8,128)(2,1)S(1)}, u32[]{:S(2)}, u32[]{:S(2)}) collective-permute-start(bf16[240,1024]{1,0:T(8,128)(2,1)S(1)} %get-tuple-element.72), channel_id=1, source_target_pairs={{8,0},{24,8},{16,24},{0,16},{9,1},{25,9},{17,25},{1,17},{10,2},{26... | collective-permute-start | bytes 1474568 | tf_op jit(solution)/shard_map/ppermute | solution.py:705
  10.7 24.1 %collective-permute-start.5 = (bf16[240,1024]{1,0:T(8,128)(2,1)S(1)}, bf16[240,1024]{1,0:T(8,128)(2,1)S(1)}, u32[]{:S(2)}, u32[]{:S(2)}) collective-permute-start(bf16[240,1024]{1,0:T(8,128)(2,1)S(1)} %get-tuple-element.68.refs_0_), channel_id=1, source_target_pairs={{0,8},{8,24},{24,16},{16,0},{1,9},{9,25},{25,17},{17,1},{2,10},{10... | collective-permute-start | bytes 1474568 | tf_op jit(solution)/shard_map/ppermute | solution.py:704
  10.8 1.2 collective-permute-start
  12.0 4.5 %collective-permute-start.1 = (bf16[2,2,8192]{2,1,0:T(2,128)(2,1)S(1)}, bf16[2,2,8192]{2,1,0:T(2,128)(2,1)S(1)}, u32[]{:S(2)}, u32[]{:S(2)}) collective-permute-start(bf16[2,2,8192]{2,1,0:T(2,128)(2,1)S(1)} %join.3.own), channel_id=1, source_target_pairs={{0,2},{2,0},{4,6},{6,4},{1,3},{3,1},{5,7},{7,5},{8,10},{10,8},{12,... | collective-permute-start | bytes 196616 | tf_op jit(solution)/shard_map/ppermute | solution.py:720
  16.5 8.8 %collective-permute-start.2 = (bf16[4,2,8192]{2,1,0:T(2,128)(2,1)S(1)}, bf16[4,2,8192]{2,1,0:T(2,128)(2,1)S(1)}, u32[]{:S(2)}, u32[]{:S(2)}) collective-permute-start(bf16[4,2,8192]{2,1,0:T(2,128)(2,1)S(1)} %join.4.own), channel_id=1, source_target_pairs={{0,4},{2,6},{4,0},{6,2},{1,5},{3,7},{5,1},{7,3},{8,12},{10,14},{12... | collective-permute-start | bytes 393224 | tf_op jit(solution)/shard_map/ppermute | solution.py:720
  28.3 17.1 %collective-permute-start.8 = (bf16[240,1024]{1,0:T(8,128)(2,1)S(1)}, bf16[240,1024]{1,0:T(8,128)(2,1)S(1)}, u32[]{:S(2)}, u32[]{:S(2)}) collective-permute-start(bf16[240,1024]{1,0:T(8,128)(2,1)S(1)} %get-tuple-element.75), channel_id=1, source_target_pairs={{8,0},{24,8},{16,24},{0,16},{9,1},{25,9},{17,25},{1,17},{10,2},{26... | collective-permute-start | bytes 1474568 | tf_op jit(solution)/shard_map/ppermute | solution.py:705
  29.8 15.7 %collective-permute-start.7 = (bf16[240,1024]{1,0:T(8,128)(2,1)S(1)}, bf16[240,1024]{1,0:T(8,128)(2,1)S(1)}, u32[]{:S(2)}, u32[]{:S(2)}) collective-permute-start(bf16[240,1024]{1,0:T(8,128)(2,1)S(1)} %get-tuple-element.70.refs_3_), channel_id=1, source_target_pairs={{0,8},{8,24},{24,16},{16,0},{1,9},{9,25},{25,17},{17,1},{2,10},{10... | collective-permute-start | bytes 1474568 | tf_op jit(solution)/shard_map/ppermute | solution.py:704
  34.8 50.6 %copy-start.35 = (bf16[16,256]{1,0:T(8,128)(2,1)}, bf16[16,256]{1,0:T(8,128)(2,1)S(1)}, u32[]{:S(2)}) copy-start(bf16[16,256]{1,0:T(8,128)(2,1)S(1)} %get-tuple-element.92.refs_7_.refs_0_) | copy-start | bytes 24580
  37.7 17.1 %collective-permute-start.10 = (bf16[240,1024]{1,0:T(8,128)(2,1)S(1)}, bf16[240,1024]{1,0:T(8,128)(2,1)S(1)}, u32[]{:S(2)}, u32[]{:S(2)}) collective-permute-start(bf16[240,1024]{1,0:T(8,128)(2,1)S(1)} %get-tuple-element.78), channel_id=1, source_target_pairs={{8,0},{24,8},{16,24},{0,16},{9,1},{25,9},{17,25},{1,17},{10,2},{26... | collective-permute-start | bytes 1474568 | tf_op jit(solution)/shard_map/ppermute | solution.py:705
  39.1 15.8 %collective-permute-start.9 = (bf16[240,1024]{1,0:T(8,128)(2,1)S(1)}, bf16[240,1024]{1,0:T(8,128)(2,1)S(1)}, u32[]{:S(2)}, u32[]{:S(2)}) collective-permute-start(bf16[240,1024]{1,0:T(8,128)(2,1)S(1)} %get-tuple-element.73.refs_4_), channel_id=1, source_target_pairs={{0,8},{8,24},{24,16},{16,0},{1,9},{9,25},{25,17},{17,1},{2,10},{10... | collective-permute-start | bytes 1474568 | tf_op jit(solution)/shard_map/ppermute | solution.py:704
  48.3 17.1 %collective-permute-start.12 = (bf16[240,1024]{1,0:T(8,128)(2,1)S(1)}, bf16[240,1024]{1,0:T(8,128)(2,1)S(1)}, u32[]{:S(2)}, u32[]{:S(2)}) collective-permute-start(bf16[240,1024]{1,0:T(8,128)(2,1)S(1)} %get-tuple-element.81), channel_id=1, source_target_pairs={{8,0},{24,8},{16,24},{0,16},{9,1},{25,9},{17,25},{1,17},{10,2},{26... | collective-permute-start | bytes 1474568 | tf_op jit(solution)/shard_map/ppermute | solution.py:705
  49.6 15.8 %collective-permute-start.11 = (bf16[240,1024]{1,0:T(8,128)(2,1)S(1)}, bf16[240,1024]{1,0:T(8,128)(2,1)S(1)}, u32[]{:S(2)}, u32[]{:S(2)}) collective-permute-start(bf16[240,1024]{1,0:T(8,128)(2,1)S(1)} %get-tuple-element.76.refs_4_), channel_id=1, source_target_pairs={{0,8},{8,24},{24,16},{16,0},{1,9},{9,25},{25,17},{17,1},{2,10},{10... | collective-permute-start | bytes 1474568 | tf_op jit(solution)/shard_map/ppermute | solution.py:704
  54.8 30.7 %copy-start.37 = (bf16[16,256]{1,0:T(8,128)(2,1)}, bf16[16,256]{1,0:T(8,128)(2,1)S(1)}, u32[]{:S(2)}) copy-start(bf16[16,256]{1,0:T(8,128)(2,1)S(1)} %get-tuple-element.94.refs_9_.refs_2_) | copy-start | bytes 24580
  57.6 17.1 %collective-permute-start.14 = (bf16[240,1024]{1,0:T(8,128)(2,1)S(1)}, bf16[240,1024]{1,0:T(8,128)(2,1)S(1)}, u32[]{:S(2)}, u32[]{:S(2)}) collective-permute-start(bf16[240,1024]{1,0:T(8,128)(2,1)S(1)} %get-tuple-element.84), channel_id=1, source_target_pairs={{8,0},{24,8},{16,24},{0,16},{9,1},{25,9},{17,25},{1,17},{10,2},{26... | collective-permute-start | bytes 1474568 | tf_op jit(solution)/shard_map/ppermute | solution.py:705
  58.9 16.0 %collective-permute-start.13 = (bf16[240,1024]{1,0:T(8,128)(2,1)S(1)}, bf16[240,1024]{1,0:T(8,128)(2,1)S(1)}, u32[]{:S(2)}, u32[]{:S(2)}) collective-permute-start(bf16[240,1024]{1,0:T(8,128)(2,1)S(1)} %get-tuple-element.79.refs_4_), channel_id=1, source_target_pairs={{0,8},{8,24},{24,16},{16,0},{1,9},{9,25},{25,17},{17,1},{2,10},{10... | collective-permute-start | bytes 1474568 | tf_op jit(solution)/shard_map/ppermute | solution.py:704
  65.4 20.1 %copy-start.31 = (bf16[16,384]{1,0:T(8,128)(2,1)}, bf16[16,384]{1,0:T(8,128)(2,1)S(1)}, u32[]{:S(2)}) copy-start(bf16[16,384]{1,0:T(8,128)(2,1)S(1)} %get-tuple-element.95.refs_10_.refs_3_) | copy-start | bytes 36868
  68.2 17.2 %collective-permute-start.19 = (bf16[240,1024]{1,0:T(8,128)(2,1)S(1)}, bf16[240,1024]{1,0:T(8,128)(2,1)S(1)}, u32[]{:S(2)}, u32[]{:S(2)}) collective-permute-start(bf16[240,1024]{1,0:T(8,128)(2,1)S(1)} %get-tuple-element.91), channel_id=1, source_target_pairs={{8,0},{24,8},{16,24},{0,16},{9,1},{25,9},{17,25},{1,17},{10,2},{26... | collective-permute-start | bytes 1474568 | tf_op jit(solution)/shard_map/ppermute | solution.py:705
  69.5 16.0 %collective-permute-start.18 = (bf16[240,1024]{1,0:T(8,128)(2,1)S(1)}, bf16[240,1024]{1,0:T(8,128)(2,1)S(1)}, u32[]{:S(2)}, u32[]{:S(2)}) collective-permute-start(bf16[240,1024]{1,0:T(8,128)(2,1)S(1)} %get-tuple-element.82.refs_4_), channel_id=1, source_target_pairs={{0,8},{8,24},{24,16},{16,0},{1,9},{9,25},{25,17},{17,1},{2,10},{10... | collective-permute-start | bytes 1474568 | tf_op jit(solution)/shard_map/ppermute | solution.py:704
  74.7 10.8 %copy-start.39 = (bf16[16,256]{1,0:T(8,128)(2,1)}, bf16[16,256]{1,0:T(8,128)(2,1)S(1)}, u32[]{:S(2)}) copy-start(bf16[16,256]{1,0:T(8,128)(2,1)S(1)} %get-tuple-element.96.refs_11_.refs_4_) | copy-start | bytes 24580
  77.6 17.2 %collective-permute-start.16 = (bf16[240,1024]{1,0:T(8,128)(2,1)S(1)}, bf16[240,1024]{1,0:T(8,128)(2,1)S(1)}, u32[]{:S(2)}, u32[]{:S(2)}) collective-permute-start(bf16[240,1024]{1,0:T(8,128)(2,1)S(1)} %get-tuple-element.87), channel_id=1, source_target_pairs={{8,0},{24,8},{16,24},{0,16},{9,1},{25,9},{17,25},{1,17},{10,2},{26... | collective-permute-start | bytes 1474568 | tf_op jit(solution)/shard_map/ppermute | solution.py:705
  79.1 16.8 %collective-permute-start.15 = (bf16[240,1024]{1,0:T(8,128)(2,1)S(1)}, bf16[240,1024]{1,0:T(8,128)(2,1)S(1)}, u32[]{:S(2)}, u32[]{:S(2)}) collective-permute-start(bf16[240,1024]{1,0:T(8,128)(2,1)S(1)} %get-tuple-element.85.refs_4_), channel_id=1, source_target_pairs={{0,8},{8,24},{24,16},{16,0},{1,9},{9,25},{25,17},{17,1},{2,10},{10... | collective-permute-start | bytes 1474568 | tf_op jit(solution)/shard_map/ppermute | solution.py:704
  87.9 21.4 %collective-permute-start.20 = (bf16[304,1024]{1,0:T(8,128)(2,1)}, bf16[304,1024]{1,0:T(8,128)(2,1)S(1)}, u32[]{:S(2)}, u32[]{:S(2)}) collective-permute-start(bf16[304,1024]{1,0:T(8,128)(2,1)} %get-tuple-element.98), channel_id=1, source_target_pairs={{0,8},{8,24},{24,16},{16,0},{1,9},{9,25},{25,17},{17,1},{2,10},{10... | collective-permute-start | bytes 1867784 | tf_op jit(solution)/shard_map/ppermute | solution.py:704
  89.1 18.4 %collective-permute-start.21 = (bf16[288,1024]{1,0:T(8,128)(2,1)}, bf16[288,1024]{1,0:T(8,128)(2,1)S(1)}, u32[]{:S(2)}, u32[]{:S(2)}) collective-permute-start(bf16[288,1024]{1,0:T(8,128)(2,1)} %get-tuple-element.99), channel_id=1, source_target_pairs={{8,0},{24,8},{16,24},{0,16},{9,1},{25,9},{17,25},{1,17},{10,2},{26... | collective-permute-start | bytes 1769480 | tf_op jit(solution)/shard_map/ppermute | solution.py:705
  98.4 19.7 %collective-permute-start.24 = (bf16[240,1024]{1,0:T(8,128)(2,1)}, bf16[240,1024]{1,0:T(8,128)(2,1)}, u32[]{:S(2)}, u32[]{:S(2)}) collective-permute-start(bf16[240,1024]{1,0:T(8,128)(2,1)} %get-tuple-element.103), channel_id=1, source_target_pairs={{8,0},{24,8},{16,24},{0,16},{9,1},{25,9},{17,25},{1,17},{10,2},{26... | collective-permute-start | bytes 1474568 | tf_op jit(solution)/shard_map/ppermute | solution.py:705
  99.8 20.1 %collective-permute-start.23 = (bf16[240,1024]{1,0:T(8,128)(2,1)}, bf16[240,1024]{1,0:T(8,128)(2,1)}, u32[]{:S(2)}, u32[]{:S(2)}) collective-permute-start(bf16[240,1024]{1,0:T(8,128)(2,1)} %get-tuple-element.88.refs_1_), channel_id=1, source_target_pairs={{0,8},{8,24},{24,16},{16,0},{1,9},{9,25},{25,17},{17,1},{2,10},{10... | collective-permute-start | bytes 1474568 | tf_op jit(solution)/shard_map/ppermute | solution.py:704
  102.1 11.8 %collective-permute-start.17 = (f32[8,4096]{1,0:T(8,128)}, f32[8,4096]{1,0:T(8,128)}, u32[]{:S(2)}, u32[]{:S(2)}) collective-permute-start(f32[8,4096]{1,0:T(8,128)} %get-tuple-element.90), channel_id=1, source_target_pairs={{0,4},{2,6},{4,0},{6,2},{1,5},{3,7},{5,1},{7,3},{8,12},{10,14},{12... | collective-permute-start | bytes 393224 | tf_op jit(solution)/shard_map/ppermute | solution.py:402
  107.5 29.8 %copy-start.1 = (bf16[288,1024]{1,0:T(8,128)(2,1)}, bf16[288,1024]{1,0:T(8,128)(2,1)S(1)}, u32[]{:S(2)}) copy-start(bf16[288,1024]{1,0:T(8,128)(2,1)S(1)} %collective-permute-done.21.refs_5_.refs_8_) | copy-start | bytes 1769476
  109.3 28.0 %copy-start = (bf16[304,1024]{1,0:T(8,128)(2,1)}, bf16[304,1024]{1,0:T(8,128)(2,1)S(1)}, u32[]{:S(2)}) copy-start(bf16[304,1024]{1,0:T(8,128)(2,1)S(1)} %collective-permute-done.20.refs_4_.refs_6_) | copy-start | bytes 1867780
  111.9 20.6 %collective-permute-start.26 = (bf16[288,1024]{1,0:T(8,128)(2,1)}, bf16[288,1024]{1,0:T(8,128)(2,1)S(1)}, u32[]{:S(2)}, u32[]{:S(2)}) collective-permute-start(bf16[288,1024]{1,0:T(8,128)(2,1)} %get-tuple-element.100.refs_2_), channel_id=1, source_target_pairs={{0,8},{8,24},{24,16},{16,0},{1,9},{9,25},{25,17},{17,1},{2,10},{10... | collective-permute-start | bytes 1769480 | tf_op jit(solution)/shard_map/ppermute | solution.py:704
  112.5 18.2 %collective-permute-start.27 = (bf16[240,1024]{1,0:T(8,128)(2,1)}, bf16[240,1024]{1,0:T(8,128)(2,1)}, u32[]{:S(2)}, u32[]{:S(2)}) collective-permute-start(bf16[240,1024]{1,0:T(8,128)(2,1)} %get-tuple-element.107), channel_id=1, source_target_pairs={{8,0},{24,8},{16,24},{0,16},{9,1},{25,9},{17,25},{1,17},{10,2},{26... | collective-permute-start | bytes 1474568 | tf_op jit(solution)/shard_map/ppermute | solution.py:705
  122.2 26.9 %collective-permute-start.29 = (bf16[240,1024]{1,0:T(8,128)(2,1)}, bf16[240,1024]{1,0:T(8,128)(2,1)}, u32[]{:S(2)}, u32[]{:S(2)}) collective-permute-start(bf16[240,1024]{1,0:T(8,128)(2,1)} %get-tuple-element.111), channel_id=1, source_target_pairs={{8,0},{24,8},{16,24},{0,16},{9,1},{25,9},{17,25},{1,17},{10,2},{26... | collective-permute-start | bytes 1474568 | tf_op jit(solution)/shard_map/ppermute | solution.py:705
  123.6 25.5 %collective-permute-start.28 = (bf16[240,1024]{1,0:T(8,128)(2,1)}, bf16[240,1024]{1,0:T(8,128)(2,1)}, u32[]{:S(2)}, u32[]{:S(2)}) collective-permute-start(bf16[240,1024]{1,0:T(8,128)(2,1)} %get-tuple-element.104.refs_2_), channel_id=1, source_target_pairs={{0,8},{8,24},{24,16},{16,0},{1,9},{9,25},{25,17},{17,1},{2,10},{10... | collective-permute-start | bytes 1474568 | tf_op jit(solution)/shard_map/ppermute | solution.py:704
  124.3 4.6 %collective-permute-start.22 = (f32[4,4096]{1,0:T(4,128)}, f32[4,4096]{1,0:T(4,128)}, u32[]{:S(2)}, u32[]{:S(2)}) collective-permute-start(f32[4,4096]{1,0:T(4,128)} %get-tuple-element.102), channel_id=1, source_target_pairs={{0,2},{2,0},{4,6},{6,4},{1,3},{3,1},{5,7},{7,5},{8,10},{10,8},{12,... | collective-permute-start | bytes 196616 | tf_op jit(solution)/shard_map/ppermute | solution.py:402
  130.6 17.7 %collective-permute-start.25 = (f32[2,4096]{1,0:T(2,128)S(1)}, f32[2,4096]{1,0:T(2,128)S(1)}, u32[]{:S(2)}, u32[]{:S(2)}) collective-permute-start(f32[2,4096]{1,0:T(2,128)S(1)} %get-tuple-element.106), channel_id=1, source_target_pairs={{0,1},{1,0},{2,3},{3,2},{4,5},{5,4},{6,7},{7,6},{8,9},{9,8},{10,11... | collective-permute-start | bytes 98312 | tf_op jit(solution)/shard_map/ppermute | solution.py:402
  135.2 28.3 %collective-permute-start.33 = (bf16[240,1024]{1,0:T(8,128)(2,1)S(1)}, bf16[240,1024]{1,0:T(8,128)(2,1)S(1)}, u32[]{:S(2)}, u32[]{:S(2)}) collective-permute-start(bf16[240,1024]{1,0:T(8,128)(2,1)S(1)} %get-tuple-element.118), channel_id=1, source_target_pairs={{8,0},{24,8},{16,24},{0,16},{9,1},{25,9},{17,25},{1,17},{10,2},{26... | collective-permute-start | bytes 1474568 | tf_op jit(solution)/shard_map/ppermute | solution.py:705
  136.4 27.2 %collective-permute-start.32 = (bf16[240,1024]{1,0:T(8,128)(2,1)S(1)}, bf16[240,1024]{1,0:T(8,128)(2,1)S(1)}, u32[]{:S(2)}, u32[]{:S(2)}) collective-permute-start(bf16[240,1024]{1,0:T(8,128)(2,1)S(1)} %get-tuple-element.108.refs_2_.refs_9_), channel_id=1, source_target_pairs={{0,8},{8,24},{24,16},{16,0},{1,9},{9,25},{25,17},{17,1},{2,10},{10... | collective-permute-start | bytes 1474568 | tf_op jit(solution)/shard_map/ppermute | solution.py:704
  138.1 10.9 %copy-start.4 = (bf16[240,1024]{1,0:T(8,128)(2,1)S(1)}, bf16[240,1024]{1,0:T(8,128)(2,1)}, u32[]{:S(2)}) copy-start(bf16[240,1024]{1,0:T(8,128)(2,1)} %copy-done.3) | copy-start | bytes 1474564
  138.1 10.9 %copy-start.6 = (bf16[240,1024]{1,0:T(8,128)(2,1)S(1)}, bf16[240,1024]{1,0:T(8,128)(2,1)}, u32[]{:S(2)}) copy-start(bf16[240,1024]{1,0:T(8,128)(2,1)} %copy-done.5) | copy-start | bytes 1474564
  138.1 10.8 %copy-start.8 = (bf16[240,1024]{1,0:T(8,128)(2,1)S(1)}, bf16[240,1024]{1,0:T(8,128)(2,1)}, u32[]{:S(2)}) copy-start(bf16[240,1024]{1,0:T(8,128)(2,1)} %copy-done.7) | copy-start | bytes 1474564
  138.1 10.8 %copy-start.10 = (bf16[240,1024]{1,0:T(8,128)(2,1)S(1)}, bf16[240,1024]{1,0:T(8,128)(2,1)}, u32[]{:S(2)}) copy-start(bf16[240,1024]{1,0:T(8,128)(2,1)} %copy-done.9) | copy-start | bytes 1474564
  138.1 10.8 %copy-start.12 = (bf16[240,1024]{1,0:T(8,128)(2,1)S(1)}, bf16[240,1024]{1,0:T(8,128)(2,1)}, u32[]{:S(2)}) copy-start(bf16[240,1024]{1,0:T(8,128)(2,1)} %copy-done.11) | copy-start | bytes 1474564
  138.1 10.8 %copy-start.14 = (bf16[240,1024]{1,0:T(8,128)(2,1)S(1)}, bf16[240,1024]{1,0:T(8,128)(2,1)}, u32[]{:S(2)}) copy-start(bf16[240,1024]{1,0:T(8,128)(2,1)} %copy-done.13) | copy-start | bytes 1474564
  138.1 10.8 %copy-start.17 = (bf16[240,1024]{1,0:T(8,128)(2,1)S(1)}, bf16[240,1024]{1,0:T(8,128)(2,1)}, u32[]{:S(2)}) copy-start(bf16[240,1024]{1,0:T(8,128)(2,1)} %copy-done.16) | copy-start | bytes 1474564
  152.2 12.5 %collective-permute-start.31 = (bf16[240,1024]{1,0:T(8,128)(2,1)S(1)}, bf16[240,1024]{1,0:T(8,128)(2,1)S(1)}, u32[]{:S(2)}, u32[]{:S(2)}) collective-permute-start(bf16[240,1024]{1,0:T(8,128)(2,1)S(1)} %get-tuple-element.117), channel_id=1, source_target_pairs={{8,0},{24,8},{16,24},{0,16},{9,1},{25,9},{17,25},{1,17},{10,2},{26... | collective-permute-start | bytes 1474568 | tf_op jit(solution)/shard_map/ppermute | solution.py:705
  153.1 11.6 %collective-permute-start.30 = (bf16[240,1024]{1,0:T(8,128)(2,1)S(1)}, bf16[240,1024]{1,0:T(8,128)(2,1)S(1)}, u32[]{:S(2)}, u32[]{:S(2)}) collective-permute-start(bf16[240,1024]{1,0:T(8,128)(2,1)S(1)} %get-tuple-element.116.refs_6_), channel_id=1, source_target_pairs={{0,8},{8,24},{24,16},{16,0},{1,9},{9,25},{25,17},{17,1},{2,10},{10... | collective-permute-start | bytes 1474568 | tf_op jit(solution)/shard_map/ppermute | solution.py:704
  154.3 10.3 %copy-start.23 = (bf16[240,1024]{1,0:T(8,128)(2,1)S(1)}, bf16[240,1024]{1,0:T(8,128)(2,1)}, u32[]{:S(2)}) copy-start(bf16[240,1024]{1,0:T(8,128)(2,1)} %copy-done.22) | copy-start | bytes 1474564
  (31 other events, 101.9 us)

commit v7 on v6

--- a/solution.py
+++ b/solution.py
@@ -765,7 +765,7 @@
 
     block = largest((b for b in range(TILE, 193, TILE) if rows % b == 0), rows)
     blocks = rows // block
-    early = blocks // 2
+    early = 5 * blocks // 12
     ready = parcel_from + LAG * reach[0] + 1
     while len(got) < steps:
         ready_sum = len(got) > parcel_from + SUM_AFTER
@@ -773,7 +773,7 @@
         if len(got) == ready and early and len(got) < steps:
             hidden_t, outs = gathered(sent)
             news = update_part(0, early, (hidden_t,))
-            news = patch_to(len(got) // 2, ())
+            news = patch_to(len(got) // 2 + 1, ())
     if hidden_t is None:
         hidden_t, outs = gathered(sent)
         early = 0

time: 167 us -> 166 us (level)
  no operation moved by 1% of the time
where the time goes in v7:
time: 166 us
  Pallas kernels  92 us (55%)
  starting transfers between devices  37.1 us (22%)
  waiting for transfers between devices  31 us (19%)
  local copies, waits for them, and re-layouts  3.39 us (2%)
  between operations  2.22 us (1%)
    pallas_call x14, Pallas kernels, pack(): pl.pallas_call(functools.partial(pack_body, n=n, places=places, chunk=chu...  36.4 us
    pallas_call x6, Pallas kernels, layer(): pl.pallas_call(functools.partial(layer_body, resumed=resumed, tile=tile,...  30.4 us
    ppermute x14, starting transfers between devices, send(): lax.ppermute(sends[-1][1], 'replica', backward)  20.9 us
    pallas_call x2, Pallas kernels, update(): pl.pallas_call(functools.partial(update_body, n=n, block=block, first=fir...  20.1 us
    ppermute x14, waiting for transfers between devices, send(): lax.ppermute(sends[-1][1], 'replica', backward)  12 us
    ppermute x14, starting transfers between devices, send(): lax.ppermute(sends[-1][0], 'replica', forward)  9.19 us
    ppermute x3, waiting for transfers between devices, per_device(): other = lax.ppermute(both, axis, [(i, i ^ apart) for i in range(size)])  8.85 us
    ppermute x14, waiting for transfers between devices, send(): lax.ppermute(sends[-1][0], 'replica', forward)  6.67 us
  transfers between devices with their start and end apart: 34, of which 12 were waited for; matrix products, arithmetic and copies ran while one was open for 0% of the time, Pallas kernels for 54%

profile of v7, /device:TPU:0, one launch (start us, length us, event | category | flops | bytes accessed | tf_op | source)
XLA Modules:
  0.0 165.6 jit_solution(11438688563513699299)
XLA Ops:
  0.7 2.5 %pack.14 = (bf16[240,1024]{1,0:T(8,128)(2,1)S(1)}, bf16[240,1024]{1,0:T(8,128)(2,1)S(1)}) custom-call(f32[2,1920,1024]{2,1,0:T(8,128)} %refs_0_.31, f32[2,1920,1024]{2,1,0:T(8,128)} %refs_1_.43, f32[2,1920,1024]{2,1,0:T(8,128)} %refs_2_.43), custom_call_target="tpu_custom_call" | custom-call | bytes 2949120 | tf_op jit(solution)/shard_map/pack/pallas_call | solution.py:200
  3.1 3.0 %collective-permute-start.4 = (bf16[240,1024]{1,0:T(8,128)(2,1)S(1)}, bf16[240,1024]{1,0:T(8,128)(2,1)S(1)}, u32[]{:S(2)}, u32[]{:S(2)}) collective-permute-start(bf16[240,1024]{1,0:T(8,128)(2,1)S(1)} %get-tuple-element.69), channel_id=1, source_target_pairs={{8,0},{24,8},{16,24},{0,16},{9,1},{25,9},{17,25},{1,17},{10,2},{26... | collective-permute-start | bytes 1474568 | tf_op jit(solution)/shard_map/ppermute | solution.py:705
  6.2 2.5 %pack.15 = (bf16[240,1024]{1,0:T(8,128)(2,1)S(1)}, bf16[240,1024]{1,0:T(8,128)(2,1)S(1)}) custom-call(f32[2,1920,1024]{2,1,0:T(8,128)} %refs_0_.31, f32[2,1920,1024]{2,1,0:T(8,128)} %refs_1_.43, f32[2,1920,1024]{2,1,0:T(8,128)} %refs_2_.43, bf16[1,2,8192]{2,1,0:T(2,128)(2,1)S(1)} %beside.1.refs_3_.own), custom_call_target="tpu_custom_call" | custom-call | bytes 2949120 | tf_op jit(solution)/shard_map/pack/pallas_call | solution.py:200
  8.7 2.0 %collective-permute-start.6 = (bf16[240,1024]{1,0:T(8,128)(2,1)S(1)}, bf16[240,1024]{1,0:T(8,128)(2,1)S(1)}, u32[]{:S(2)}, u32[]{:S(2)}) collective-permute-start(bf16[240,1024]{1,0:T(8,128)(2,1)S(1)} %get-tuple-element.72), channel_id=1, source_target_pairs={{8,0},{24,8},{16,24},{0,16},{9,1},{25,9},{17,25},{1,17},{10,2},{26... | collective-permute-start | bytes 1474568 | tf_op jit(solution)/shard_map/ppermute | solution.py:705
  10.8 1.2 collective-permute-done.other
  12.0 2.1 %collective-permute-start.1 = (bf16[2,2,8192]{2,1,0:T(2,128)(2,1)S(1)}, bf16[2,2,8192]{2,1,0:T(2,128)(2,1)S(1)}, u32[]{:S(2)}, u32[]{:S(2)}) collective-permute-start(bf16[2,2,8192]{2,1,0:T(2,128)(2,1)S(1)} %join.3.own), channel_id=1, source_target_pairs={{0,2},{2,0},{4,6},{6,4},{1,3},{3,1},{5,7},{7,5},{8,10},{10,8},{12,... | collective-permute-start | bytes 196616 | tf_op jit(solution)/shard_map/ppermute | solution.py:720
  14.1 2.4 %collective-permute-done.1.other = bf16[2,2,8192]{2,1,0:T(2,128)(2,1)S(1)} collective-permute-done((bf16[2,2,8192]{2,1,0:T(2,128)(2,1)S(1)}, bf16[2,2,8192]{2,1,0:T(2,128)(2,1)S(1)}, u32[]{:S(2)}, u32[]{:S(2)}) %collective-permute-start.1) | collective-permute-done | bytes 65568 | tf_op jit(solution)/shard_map/ppermute | solution.py:720
  16.5 2.9 %collective-permute-start.2 = (bf16[4,2,8192]{2,1,0:T(2,128)(2,1)S(1)}, bf16[4,2,8192]{2,1,0:T(2,128)(2,1)S(1)}, u32[]{:S(2)}, u32[]{:S(2)}) collective-permute-start(bf16[4,2,8192]{2,1,0:T(2,128)(2,1)S(1)} %join.4.own), channel_id=1, source_target_pairs={{0,4},{2,6},{4,0},{6,2},{1,5},{3,7},{5,1},{7,3},{8,12},{10,14},{12... | collective-permute-start | bytes 393224 | tf_op jit(solution)/shard_map/ppermute | solution.py:720
  20.1 5.2 %collective-permute-done.2.other = bf16[4,2,8192]{2,1,0:T(2,128)(2,1)S(1)} collective-permute-done((bf16[4,2,8192]{2,1,0:T(2,128)(2,1)S(1)}, bf16[4,2,8192]{2,1,0:T(2,128)(2,1)S(1)}, u32[]{:S(2)}, u32[]{:S(2)}) %collective-permute-start.2) | collective-permute-done | bytes 131104 | tf_op jit(solution)/shard_map/ppermute | solution.py:720
  25.5 2.7 %pack.16 = (bf16[240,1024]{1,0:T(8,128)(2,1)S(1)}, bf16[240,1024]{1,0:T(8,128)(2,1)S(1)}) custom-call(s32[1]{0:T(128)S(6)} %copy.37.refs_0_.failed, f32[2,1920,1024]{2,1,0:T(8,128)} %refs_0_.31, f32[2,1920,1024]{2,1,0:T(8,128)} %refs_1_.43, f32[2,1920,1024]{2,1,0:T(8,128)} %refs_2_.43, bf16[240,1024]{1,0:T(8,128)(2,1)S(1)} %collective-permute-done.3.refs_4_.refs_0_, ...), custom_call_target="tpu_custom_call" | custom-call | bytes 2949120 | tf_op jit(solution)/shard_map/pack/pallas_call | solution.py:200
  28.3 1.5 collective-permute-start.8
  30.4 4.4 %layer.6 = (bf16[16,256]{1,0:T(8,128)(2,1)S(1)}, f32[16,4096]{1,0:T(8,128)S(1)}) custom-call(bf16[16,8192]{1,0:T(8,128)(2,1)S(1)} %join.5.refs_6_.both, bf16[4096,1920]{1,0:T(8,128)(2,1)} %refs_0_.29, bf16[4096,1920]{1,0:T(8,128)(2,1)} %refs_1_.35, bf16[1920,4096]{1,0:T(8,128)(2,1)} %refs_2_.35, bf16[240,1024]{1,0:T(8,128)(2,1)S(1)} %get-tuple-element.70.refs_3_), custom_call_target="tpu_custom_call" | custom-call | flops 167772160 | bytes 6291456 | tf_op jit(solution)/shard_map/layer/pallas_call | solution.py:329
  34.9 2.7 %pack.17 = (bf16[240,1024]{1,0:T(8,128)(2,1)S(1)}, bf16[240,1024]{1,0:T(8,128)(2,1)S(1)}) custom-call(s32[1]{0:T(128)S(6)} %copy.37.refs_0_.failed, f32[2,1920,1024]{2,1,0:T(8,128)} %refs_0_.31, f32[2,1920,1024]{2,1,0:T(8,128)} %refs_1_.43, f32[2,1920,1024]{2,1,0:T(8,128)} %refs_2_.43, bf16[240,1024]{1,0:T(8,128)(2,1)S(1)} %collective-permute-done.5.refs_4_.refs_2_, ...), custom_call_target="tpu_custom_call" | custom-call | bytes 2949120 | tf_op jit(solution)/shard_map/pack/pallas_call | solution.py:200
  37.7 1.4 collective-permute-start.10
  39.7 5.7 %layer.7 = (bf16[16,384]{1,0:T(8,128)(2,1)S(1)}, f32[16,4096]{1,0:T(8,128)S(1)}) custom-call(bf16[16,8192]{1,0:T(8,128)(2,1)S(1)} %join.5.refs_6_.both, bf16[4096,1920]{1,0:T(8,128)(2,1)} %refs_0_.29, bf16[4096,1920]{1,0:T(8,128)(2,1)} %refs_1_.35, bf16[1920,4096]{1,0:T(8,128)(2,1)} %refs_2_.35, f32[16,4096]{1,0:T(8,128)S(1)} %get-tuple-element.71.refs_6_.refs_3_, ...), custom_call_target="tpu_custom_call" | custom-call | flops 251658240 | bytes 9437184 | tf_op jit(solution)/shard_map/layer/pallas_call | solution.py:329
  45.5 2.7 %pack.18 = (bf16[240,1024]{1,0:T(8,128)(2,1)S(1)}, bf16[240,1024]{1,0:T(8,128)(2,1)S(1)}) custom-call(s32[1]{0:T(128)S(6)} %copy.37.refs_0_.failed, f32[2,1920,1024]{2,1,0:T(8,128)} %refs_0_.31, f32[2,1920,1024]{2,1,0:T(8,128)} %refs_1_.43, f32[2,1920,1024]{2,1,0:T(8,128)} %refs_2_.43, bf16[240,1024]{1,0:T(8,128)(2,1)S(1)} %collective-permute-done.7.refs_4_, ...), custom_call_target="tpu_custom_call" | custom-call | bytes 2949120 | tf_op jit(solution)/shard_map/pack/pallas_call | solution.py:200
  48.3 1.3 collective-permute-start.12
  50.4 4.4 %layer.8 = (bf16[16,256]{1,0:T(8,128)(2,1)S(1)}, f32[16,4096]{1,0:T(8,128)S(1)}) custom-call(bf16[16,8192]{1,0:T(8,128)(2,1)S(1)} %join.5.refs_6_.both, bf16[4096,1920]{1,0:T(8,128)(2,1)} %refs_0_.29, bf16[4096,1920]{1,0:T(8,128)(2,1)} %refs_1_.35, bf16[1920,4096]{1,0:T(8,128)(2,1)} %refs_2_.35, f32[16,4096]{1,0:T(8,128)S(1)} %get-tuple-element.74.refs_6_.refs_3_, ...), custom_call_target="tpu_custom_call" | custom-call | flops 167772160 | bytes 6291456 | tf_op jit(solution)/shard_map/layer/pallas_call | solution.py:329
  54.8 2.7 %pack.19 = (bf16[240,1024]{1,0:T(8,128)(2,1)S(1)}, bf16[240,1024]{1,0:T(8,128)(2,1)S(1)}) custom-call(s32[1]{0:T(128)S(6)} %copy.37.refs_0_.failed, f32[2,1920,1024]{2,1,0:T(8,128)} %refs_0_.31, f32[2,1920,1024]{2,1,0:T(8,128)} %refs_1_.43, f32[2,1920,1024]{2,1,0:T(8,128)} %refs_2_.43, bf16[240,1024]{1,0:T(8,128)(2,1)S(1)} %collective-permute-done.9.refs_4_.refs_6_, ...), custom_call_target="tpu_custom_call" | custom-call | bytes 2949120 | tf_op jit(solution)/shard_map/pack/pallas_call | solution.py:200
  57.6 1.3 collective-permute-start.14
  59.7 5.7 %layer.9 = (bf16[16,384]{1,0:T(8,128)(2,1)S(1)}, f32[16,4096]{1,0:T(8,128)S(1)}) custom-call(bf16[16,8192]{1,0:T(8,128)(2,1)S(1)} %join.5.refs_6_.both, bf16[4096,1920]{1,0:T(8,128)(2,1)} %refs_0_.29, bf16[4096,1920]{1,0:T(8,128)(2,1)} %refs_1_.35, bf16[1920,4096]{1,0:T(8,128)(2,1)} %refs_2_.35, f32[16,4096]{1,0:T(8,128)S(1)} %get-tuple-element.77.refs_6_.refs_3_, ...), custom_call_target="tpu_custom_call" | custom-call | flops 251658240 | bytes 9437184 | tf_op jit(solution)/shard_map/layer/pallas_call | solution.py:329
  65.5 2.7 %pack.20 = (bf16[240,1024]{1,0:T(8,128)(2,1)S(1)}, bf16[240,1024]{1,0:T(8,128)(2,1)S(1)}) custom-call(s32[1]{0:T(128)S(6)} %copy.37.refs_0_.failed, f32[2,1920,1024]{2,1,0:T(8,128)} %refs_0_.31, f32[2,1920,1024]{2,1,0:T(8,128)} %refs_1_.43, f32[2,1920,1024]{2,1,0:T(8,128)} %refs_2_.43, bf16[240,1024]{1,0:T(8,128)(2,1)S(1)} %collective-permute-done.11.refs_4_.refs_8_, ...), custom_call_target="tpu_custom_call" | custom-call | bytes 2949120 | tf_op jit(solution)/shard_map/pack/pallas_call | solution.py:200
  68.2 1.2 collective-permute-start.19
  70.3 4.4 %layer.10 = (bf16[16,256]{1,0:T(8,128)(2,1)S(1)}, f32[16,4096]{1,0:T(8,128)S(1)}) custom-call(bf16[16,8192]{1,0:T(8,128)(2,1)S(1)} %join.5.refs_6_.both, bf16[4096,1920]{1,0:T(8,128)(2,1)} %refs_0_.29, bf16[4096,1920]{1,0:T(8,128)(2,1)} %refs_1_.35, bf16[1920,4096]{1,0:T(8,128)(2,1)} %refs_2_.35, f32[16,4096]{1,0:T(8,128)S(1)} %get-tuple-element.80.refs_6_.refs_3_, ...), custom_call_target="tpu_custom_call" | custom-call | flops 167772160 | bytes 6291456 | tf_op jit(solution)/shard_map/layer/pallas_call | solution.py:329
  74.9 2.7 %pack.21 = (bf16[240,1024]{1,0:T(8,128)(2,1)S(1)}, bf16[240,1024]{1,0:T(8,128)(2,1)S(1)}) custom-call(s32[1]{0:T(128)S(6)} %copy.37.refs_0_.failed, f32[2,1920,1024]{2,1,0:T(8,128)} %refs_0_.31, f32[2,1920,1024]{2,1,0:T(8,128)} %refs_1_.43, f32[2,1920,1024]{2,1,0:T(8,128)} %refs_2_.43, bf16[240,1024]{1,0:T(8,128)(2,1)S(1)} %collective-permute-done.13.refs_4_.refs_10_, ...), custom_call_target="tpu_custom_call" | custom-call | bytes 2949120 | tf_op jit(solution)/shard_map/pack/pallas_call | solution.py:200
  77.6 1.5 collective-permute-start.16
  79.7 5.7 %layer.11 = (bf16[16,384]{1,0:T(8,128)(2,1)S(1)}, f32[16,4096]{1,0:T(8,128)S(1)}) custom-call(bf16[16,8192]{1,0:T(8,128)(2,1)S(1)} %join.5.refs_6_.both, bf16[4096,1920]{1,0:T(8,128)(2,1)} %refs_0_.29, bf16[4096,1920]{1,0:T(8,128)(2,1)} %refs_1_.35, bf16[1920,4096]{1,0:T(8,128)(2,1)} %refs_2_.35, f32[16,4096]{1,0:T(8,128)S(1)} %get-tuple-element.83.refs_6_.refs_3_, ...), custom_call_target="tpu_custom_call" | custom-call | flops 251658240 | bytes 9437184 | tf_op jit(solution)/shard_map/layer/pallas_call | solution.py:329
  85.5 2.7 %pack.23 = (bf16[304,1024]{1,0:T(8,128)(2,1)}, bf16[288,1024]{1,0:T(8,128)(2,1)}) custom-call(s32[1]{0:T(128)S(6)} %copy.37.refs_0_.failed, f32[2,1920,1024]{2,1,0:T(8,128)} %refs_0_.31, f32[2,1920,1024]{2,1,0:T(8,128)} %refs_1_.43, f32[2,1920,1024]{2,1,0:T(8,128)} %refs_2_.43, bf16[240,1024]{1,0:T(8,128)(2,1)S(1)} %collective-permute-done.18.refs_4_.refs_12_, ...), custom_call_target="tpu_custom_call" | custom-call | bytes 2949120 | tf_op jit(solution)/shard_map/pack/pallas_call | solution.py:200
  89.2 1.2 collective-permute-start.21
  90.4 4.5 %collective-permute-done.16.refs_5_.refs_1_ = bf16[240,1024]{1,0:T(8,128)(2,1)S(1)} collective-permute-done((bf16[240,1024]{1,0:T(8,128)(2,1)S(1)}, bf16[240,1024]{1,0:T(8,128)(2,1)S(1)}, u32[]{:S(2)}, u32[]{:S(2)}) %collective-permute-start.16) | collective-permute-done | bytes 491552 | tf_op jit(solution)/shard_map/ppermute | solution.py:705
  96.0 2.3 %pack.22 = (bf16[240,1024]{1,0:T(8,128)(2,1)}, bf16[240,1024]{1,0:T(8,128)(2,1)}) custom-call(s32[1]{0:T(128)S(6)} %copy.37.refs_0_.failed, f32[2,1920,1024]{2,1,0:T(8,128)} %refs_0_.31, f32[2,1920,1024]{2,1,0:T(8,128)} %refs_1_.43, f32[2,1920,1024]{2,1,0:T(8,128)} %refs_2_.43, bf16[240,1024]{1,0:T(8,128)(2,1)S(1)} %collective-permute-done.15.refs_4_.refs_0_, ...), custom_call_target="tpu_custom_call" | custom-call | bytes 2949120 | tf_op jit(solution)/shard_map/pack/pallas_call | solution.py:200
  98.2 1.6 collective-permute-start.24
  101.8 5.8 %collective-permute-done.21.refs_5_.refs_8_.refs_3_ = bf16[288,1024]{1,0:T(8,128)(2,1)S(1)} collective-permute-done((bf16[288,1024]{1,0:T(8,128)(2,1)}, bf16[288,1024]{1,0:T(8,128)(2,1)S(1)}, u32[]{:S(2)}, u32[]{:S(2)}) %collective-permute-start.21) | collective-permute-done | bytes 589856 | tf_op jit(solution)/shard_map/ppermute | solution.py:705
  107.5 1.8 %collective-permute-done.20.refs_4_.refs_6_.refs_2_ = bf16[304,1024]{1,0:T(8,128)(2,1)S(1)} collective-permute-done((bf16[304,1024]{1,0:T(8,128)(2,1)}, bf16[304,1024]{1,0:T(8,128)(2,1)S(1)}, u32[]{:S(2)}, u32[]{:S(2)}) %collective-permute-start.20) | collective-permute-done | bytes 622624 | tf_op jit(solution)/shard_map/ppermute | solution.py:704
  109.3 2.5 %pack.24 = (bf16[288,1024]{1,0:T(8,128)(2,1)}, bf16[240,1024]{1,0:T(8,128)(2,1)}) custom-call(s32[1]{0:T(128)S(6)} %copy.37.refs_0_.failed, f32[2,1920,1024]{2,1,0:T(8,128)} %refs_0_.31, f32[2,1920,1024]{2,1,0:T(8,128)} %refs_1_.43, f32[2,1920,1024]{2,1,0:T(8,128)} %refs_2_.43, bf16[304,1024]{1,0:T(8,128)(2,1)S(1)} %collective-permute-done.20.refs_4_.refs_6_.refs_2_, ...), custom_call_target="tpu_custom_call" | custom-call | bytes 2949120 | tf_op jit(solution)/shard_map/pack/pallas_call | solution.py:200
  112.5 1.5 collective-permute-start.27
  114.8 1.5 halve.5
  116.4 1.7 collective-permute-done.24.refs_5_
  118.0 1.9 %collective-permute-done.23.refs_4_ = bf16[240,1024]{1,0:T(8,128)(2,1)} collective-permute-done((bf16[240,1024]{1,0:T(8,128)(2,1)}, bf16[240,1024]{1,0:T(8,128)(2,1)}, u32[]{:S(2)}, u32[]{:S(2)}) %collective-permute-start.23) | collective-permute-done | bytes 491552 | tf_op jit(solution)/shard_map/ppermute | solution.py:704
  119.9 2.3 %pack.25 = (bf16[240,1024]{1,0:T(8,128)(2,1)}, bf16[240,1024]{1,0:T(8,128)(2,1)}) custom-call(s32[1]{0:T(128)S(6)} %copy.37.refs_0_.failed, f32[2,1920,1024]{2,1,0:T(8,128)} %refs_0_.31, f32[2,1920,1024]{2,1,0:T(8,128)} %refs_1_.43, f32[2,1920,1024]{2,1,0:T(8,128)} %refs_2_.43, bf16[240,1024]{1,0:T(8,128)(2,1)} %collective-permute-done.23.refs_4_, ...), custom_call_target="tpu_custom_call" | custom-call | bytes 2949120 | tf_op jit(solution)/shard_map/pack/pallas_call | solution.py:200
  122.2 1.4 collective-permute-start.29
  125.4 3.5 %collective-permute-done.22.refs_1_ = f32[4,4096]{1,0:T(4,128)} collective-permute-done((f32[4,4096]{1,0:T(4,128)}, f32[4,4096]{1,0:T(4,128)}, u32[]{:S(2)}, u32[]{:S(2)}) %collective-permute-start.22) | collective-permute-done | bytes 65568 | tf_op jit(solution)/shard_map/ppermute | solution.py:402
  130.7 1.8 %collective-permute-done.26.refs_4_.refs_7_.refs_6_ = bf16[288,1024]{1,0:T(8,128)(2,1)S(1)} collective-permute-done((bf16[288,1024]{1,0:T(8,128)(2,1)}, bf16[288,1024]{1,0:T(8,128)(2,1)S(1)}, u32[]{:S(2)}, u32[]{:S(2)}) %collective-permute-start.26) | collective-permute-done | bytes 589856 | tf_op jit(solution)/shard_map/ppermute | solution.py:704
  132.5 2.7 %pack.26 = (bf16[240,1024]{1,0:T(8,128)(2,1)S(1)}, bf16[240,1024]{1,0:T(8,128)(2,1)S(1)}) custom-call(s32[1]{0:T(128)S(6)} %copy.37.refs_0_.failed, f32[2,1920,1024]{2,1,0:T(8,128)} %refs_0_.31, f32[2,1920,1024]{2,1,0:T(8,128)} %refs_1_.43, f32[2,1920,1024]{2,1,0:T(8,128)} %refs_2_.43, bf16[288,1024]{1,0:T(8,128)(2,1)S(1)} %collective-permute-done.26.refs_4_.refs_7_.refs_6_, ...), custom_call_target="tpu_custom_call" | custom-call | bytes 2949120 | tf_op jit(solution)/shard_map/pack/pallas_call | solution.py:200
  138.8 9.4 %update.2 = (f32[1920,1024]{1,0:T(8,128)}, f32[1920,1024]{1,0:T(8,128)}, f32[1920,1024]{1,0:T(8,128)}) custom-call(s32[1]{0:T(128)S(6)} %copy.37.refs_0_.failed, bf16[1920,64]{1,0:T(8,128)(2,1)S(1)} %get-tuple-element.109.hid_ref.refs_3_, bf16[64,1024]{1,0:T(8,128)(2,1)S(1)} %get-tuple-element.110.out_ref, f32[2,1920,1024]{2,1,0:T(8,128)} %refs_0_.31, ...), custom_call_target="tpu_custom_call" | custom-call | flops 100663296 | bytes 18874368 | tf_op jit(solution)/shard_map/update/pallas_call | solution.py:523
  148.9 2.5 %pack.27 = (bf16[240,1024]{1,0:T(8,128)(2,1)S(1)}, bf16[240,1024]{1,0:T(8,128)(2,1)S(1)}) custom-call(s32[1]{0:T(128)S(6)} %copy.37.refs_0_.failed, f32[2,1920,1024]{2,1,0:T(8,128)} %refs_0_.31, f32[2,1920,1024]{2,1,0:T(8,128)} %refs_1_.43, f32[2,1920,1024]{2,1,0:T(8,128)} %refs_2_.43, bf16[240,1024]{1,0:T(8,128)(2,1)} %collective-permute-done.28.refs_4_.refs_8_, ...), custom_call_target="tpu_custom_call" | custom-call | bytes 2949120 | tf_op jit(solution)/shard_map/pack/pallas_call | solution.py:200
  152.3 1.2 collective-permute-start.30
  153.5 10.7 %update.3 = (f32[1920,1024]{1,0:T(8,128)}, f32[1920,1024]{1,0:T(8,128)}, f32[1920,1024]{1,0:T(8,128)}) custom-call(s32[1]{0:T(128)S(6)} %copy.37.refs_0_.failed, bf16[1920,64]{1,0:T(8,128)(2,1)S(1)} %get-tuple-element.109.hid_ref.refs_3_, ...), custom_call_target="tpu_custom_call", output_to_operand_aliasing={{0}: (6, {}), {1}: (7, {}), {2}: (8, {})} | custom-call | flops 150994944 | bytes 28311552 | tf_op jit(solution)/shard_map/update/pallas_call | solution.py:523
  (144 shorter events, 20.1 us)
Async XLA Ops:
  3.1 22.4 %collective-permute-start.4 = (bf16[240,1024]{1,0:T(8,128)(2,1)S(1)}, bf16[240,1024]{1,0:T(8,128)(2,1)S(1)}, u32[]{:S(2)}, u32[]{:S(2)}) collective-permute-start(bf16[240,1024]{1,0:T(8,128)(2,1)S(1)} %get-tuple-element.69), channel_id=1, source_target_pairs={{8,0},{24,8},{16,24},{0,16},{9,1},{25,9},{17,25},{1,17},{10,2},{26... | collective-permute-start | bytes 1474568 | tf_op jit(solution)/shard_map/ppermute | solution.py:705
  6.2 19.4 %collective-permute-start.3 = (bf16[240,1024]{1,0:T(8,128)(2,1)S(1)}, bf16[240,1024]{1,0:T(8,128)(2,1)S(1)}, u32[]{:S(2)}, u32[]{:S(2)}) collective-permute-start(bf16[240,1024]{1,0:T(8,128)(2,1)S(1)} %get-tuple-element.67.refs_2_), channel_id=1, source_target_pairs={{0,8},{8,24},{24,16},{16,0},{1,9},{9,25},{25,17},{17,1},{2,10},{10... | collective-permute-start | bytes 1474568 | tf_op jit(solution)/shard_map/ppermute | solution.py:704
  8.7 26.2 %collective-permute-start.6 = (bf16[240,1024]{1,0:T(8,128)(2,1)S(1)}, bf16[240,1024]{1,0:T(8,128)(2,1)S(1)}, u32[]{:S(2)}, u32[]{:S(2)}) collective-permute-start(bf16[240,1024]{1,0:T(8,128)(2,1)S(1)} %get-tuple-element.72), channel_id=1, source_target_pairs={{8,0},{24,8},{16,24},{0,16},{9,1},{25,9},{17,25},{1,17},{10,2},{26... | collective-permute-start | bytes 1474568 | tf_op jit(solution)/shard_map/ppermute | solution.py:705
  10.7 24.1 %collective-permute-start.5 = (bf16[240,1024]{1,0:T(8,128)(2,1)S(1)}, bf16[240,1024]{1,0:T(8,128)(2,1)S(1)}, u32[]{:S(2)}, u32[]{:S(2)}) collective-permute-start(bf16[240,1024]{1,0:T(8,128)(2,1)S(1)} %get-tuple-element.68.refs_0_), channel_id=1, source_target_pairs={{0,8},{8,24},{24,16},{16,0},{1,9},{9,25},{25,17},{17,1},{2,10},{10... | collective-permute-start | bytes 1474568 | tf_op jit(solution)/shard_map/ppermute | solution.py:704
  10.8 1.2 collective-permute-start
  12.0 4.5 %collective-permute-start.1 = (bf16[2,2,8192]{2,1,0:T(2,128)(2,1)S(1)}, bf16[2,2,8192]{2,1,0:T(2,128)(2,1)S(1)}, u32[]{:S(2)}, u32[]{:S(2)}) collective-permute-start(bf16[2,2,8192]{2,1,0:T(2,128)(2,1)S(1)} %join.3.own), channel_id=1, source_target_pairs={{0,2},{2,0},{4,6},{6,4},{1,3},{3,1},{5,7},{7,5},{8,10},{10,8},{12,... | collective-permute-start | bytes 196616 | tf_op jit(solution)/shard_map/ppermute | solution.py:720
  16.5 8.8 %collective-permute-start.2 = (bf16[4,2,8192]{2,1,0:T(2,128)(2,1)S(1)}, bf16[4,2,8192]{2,1,0:T(2,128)(2,1)S(1)}, u32[]{:S(2)}, u32[]{:S(2)}) collective-permute-start(bf16[4,2,8192]{2,1,0:T(2,128)(2,1)S(1)} %join.4.own), channel_id=1, source_target_pairs={{0,4},{2,6},{4,0},{6,2},{1,5},{3,7},{5,1},{7,3},{8,12},{10,14},{12... | collective-permute-start | bytes 393224 | tf_op jit(solution)/shard_map/ppermute | solution.py:720
  28.3 17.1 %collective-permute-start.8 = (bf16[240,1024]{1,0:T(8,128)(2,1)S(1)}, bf16[240,1024]{1,0:T(8,128)(2,1)S(1)}, u32[]{:S(2)}, u32[]{:S(2)}) collective-permute-start(bf16[240,1024]{1,0:T(8,128)(2,1)S(1)} %get-tuple-element.75), channel_id=1, source_target_pairs={{8,0},{24,8},{16,24},{0,16},{9,1},{25,9},{17,25},{1,17},{10,2},{26... | collective-permute-start | bytes 1474568 | tf_op jit(solution)/shard_map/ppermute | solution.py:705
  29.8 15.7 %collective-permute-start.7 = (bf16[240,1024]{1,0:T(8,128)(2,1)S(1)}, bf16[240,1024]{1,0:T(8,128)(2,1)S(1)}, u32[]{:S(2)}, u32[]{:S(2)}) collective-permute-start(bf16[240,1024]{1,0:T(8,128)(2,1)S(1)} %get-tuple-element.70.refs_3_), channel_id=1, source_target_pairs={{0,8},{8,24},{24,16},{16,0},{1,9},{9,25},{25,17},{17,1},{2,10},{10... | collective-permute-start | bytes 1474568 | tf_op jit(solution)/shard_map/ppermute | solution.py:704
  34.8 50.7 %copy-start.35 = (bf16[16,256]{1,0:T(8,128)(2,1)}, bf16[16,256]{1,0:T(8,128)(2,1)S(1)}, u32[]{:S(2)}) copy-start(bf16[16,256]{1,0:T(8,128)(2,1)S(1)} %get-tuple-element.92.refs_7_.refs_0_) | copy-start | bytes 24580
  37.7 17.1 %collective-permute-start.10 = (bf16[240,1024]{1,0:T(8,128)(2,1)S(1)}, bf16[240,1024]{1,0:T(8,128)(2,1)S(1)}, u32[]{:S(2)}, u32[]{:S(2)}) collective-permute-start(bf16[240,1024]{1,0:T(8,128)(2,1)S(1)} %get-tuple-element.78), channel_id=1, source_target_pairs={{8,0},{24,8},{16,24},{0,16},{9,1},{25,9},{17,25},{1,17},{10,2},{26... | collective-permute-start | bytes 1474568 | tf_op jit(solution)/shard_map/ppermute | solution.py:705
  39.1 15.8 %collective-permute-start.9 = (bf16[240,1024]{1,0:T(8,128)(2,1)S(1)}, bf16[240,1024]{1,0:T(8,128)(2,1)S(1)}, u32[]{:S(2)}, u32[]{:S(2)}) collective-permute-start(bf16[240,1024]{1,0:T(8,128)(2,1)S(1)} %get-tuple-element.73.refs_4_), channel_id=1, source_target_pairs={{0,8},{8,24},{24,16},{16,0},{1,9},{9,25},{25,17},{17,1},{2,10},{10... | collective-permute-start | bytes 1474568 | tf_op jit(solution)/shard_map/ppermute | solution.py:704
  48.3 17.1 %collective-permute-start.12 = (bf16[240,1024]{1,0:T(8,128)(2,1)S(1)}, bf16[240,1024]{1,0:T(8,128)(2,1)S(1)}, u32[]{:S(2)}, u32[]{:S(2)}) collective-permute-start(bf16[240,1024]{1,0:T(8,128)(2,1)S(1)} %get-tuple-element.81), channel_id=1, source_target_pairs={{8,0},{24,8},{16,24},{0,16},{9,1},{25,9},{17,25},{1,17},{10,2},{26... | collective-permute-start | bytes 1474568 | tf_op jit(solution)/shard_map/ppermute | solution.py:705
  49.6 15.8 %collective-permute-start.11 = (bf16[240,1024]{1,0:T(8,128)(2,1)S(1)}, bf16[240,1024]{1,0:T(8,128)(2,1)S(1)}, u32[]{:S(2)}, u32[]{:S(2)}) collective-permute-start(bf16[240,1024]{1,0:T(8,128)(2,1)S(1)} %get-tuple-element.76.refs_4_), channel_id=1, source_target_pairs={{0,8},{8,24},{24,16},{16,0},{1,9},{9,25},{25,17},{17,1},{2,10},{10... | collective-permute-start | bytes 1474568 | tf_op jit(solution)/shard_map/ppermute | solution.py:704
  54.8 30.7 %copy-start.37 = (bf16[16,256]{1,0:T(8,128)(2,1)}, bf16[16,256]{1,0:T(8,128)(2,1)S(1)}, u32[]{:S(2)}) copy-start(bf16[16,256]{1,0:T(8,128)(2,1)S(1)} %get-tuple-element.94.refs_9_.refs_2_) | copy-start | bytes 24580
  57.6 17.1 %collective-permute-start.14 = (bf16[240,1024]{1,0:T(8,128)(2,1)S(1)}, bf16[240,1024]{1,0:T(8,128)(2,1)S(1)}, u32[]{:S(2)}, u32[]{:S(2)}) collective-permute-start(bf16[240,1024]{1,0:T(8,128)(2,1)S(1)} %get-tuple-element.84), channel_id=1, source_target_pairs={{8,0},{24,8},{16,24},{0,16},{9,1},{25,9},{17,25},{1,17},{10,2},{26... | collective-permute-start | bytes 1474568 | tf_op jit(solution)/shard_map/ppermute | solution.py:705
  58.9 16.0 %collective-permute-start.13 = (bf16[240,1024]{1,0:T(8,128)(2,1)S(1)}, bf16[240,1024]{1,0:T(8,128)(2,1)S(1)}, u32[]{:S(2)}, u32[]{:S(2)}) collective-permute-start(bf16[240,1024]{1,0:T(8,128)(2,1)S(1)} %get-tuple-element.79.refs_4_), channel_id=1, source_target_pairs={{0,8},{8,24},{24,16},{16,0},{1,9},{9,25},{25,17},{17,1},{2,10},{10... | collective-permute-start | bytes 1474568 | tf_op jit(solution)/shard_map/ppermute | solution.py:704
  65.4 20.1 %copy-start.31 = (bf16[16,384]{1,0:T(8,128)(2,1)}, bf16[16,384]{1,0:T(8,128)(2,1)S(1)}, u32[]{:S(2)}) copy-start(bf16[16,384]{1,0:T(8,128)(2,1)S(1)} %get-tuple-element.95.refs_10_.refs_3_) | copy-start | bytes 36868
  68.2 17.2 %collective-permute-start.19 = (bf16[240,1024]{1,0:T(8,128)(2,1)S(1)}, bf16[240,1024]{1,0:T(8,128)(2,1)S(1)}, u32[]{:S(2)}, u32[]{:S(2)}) collective-permute-start(bf16[240,1024]{1,0:T(8,128)(2,1)S(1)} %get-tuple-element.91), channel_id=1, source_target_pairs={{8,0},{24,8},{16,24},{0,16},{9,1},{25,9},{17,25},{1,17},{10,2},{26... | collective-permute-start | bytes 1474568 | tf_op jit(solution)/shard_map/ppermute | solution.py:705
  69.5 16.0 %collective-permute-start.18 = (bf16[240,1024]{1,0:T(8,128)(2,1)S(1)}, bf16[240,1024]{1,0:T(8,128)(2,1)S(1)}, u32[]{:S(2)}, u32[]{:S(2)}) collective-permute-start(bf16[240,1024]{1,0:T(8,128)(2,1)S(1)} %get-tuple-element.82.refs_4_), channel_id=1, source_target_pairs={{0,8},{8,24},{24,16},{16,0},{1,9},{9,25},{25,17},{17,1},{2,10},{10... | collective-permute-start | bytes 1474568 | tf_op jit(solution)/shard_map/ppermute | solution.py:704
  74.7 10.8 %copy-start.39 = (bf16[16,256]{1,0:T(8,128)(2,1)}, bf16[16,256]{1,0:T(8,128)(2,1)S(1)}, u32[]{:S(2)}) copy-start(bf16[16,256]{1,0:T(8,128)(2,1)S(1)} %get-tuple-element.96.refs_11_.refs_4_) | copy-start | bytes 24580
  77.6 17.2 %collective-permute-start.16 = (bf16[240,1024]{1,0:T(8,128)(2,1)S(1)}, bf16[240,1024]{1,0:T(8,128)(2,1)S(1)}, u32[]{:S(2)}, u32[]{:S(2)}) collective-permute-start(bf16[240,1024]{1,0:T(8,128)(2,1)S(1)} %get-tuple-element.87), channel_id=1, source_target_pairs={{8,0},{24,8},{16,24},{0,16},{9,1},{25,9},{17,25},{1,17},{10,2},{26... | collective-permute-start | bytes 1474568 | tf_op jit(solution)/shard_map/ppermute | solution.py:705
  79.1 16.8 %collective-permute-start.15 = (bf16[240,1024]{1,0:T(8,128)(2,1)S(1)}, bf16[240,1024]{1,0:T(8,128)(2,1)S(1)}, u32[]{:S(2)}, u32[]{:S(2)}) collective-permute-start(bf16[240,1024]{1,0:T(8,128)(2,1)S(1)} %get-tuple-element.85.refs_4_), channel_id=1, source_target_pairs={{0,8},{8,24},{24,16},{16,0},{1,9},{9,25},{25,17},{17,1},{2,10},{10... | collective-permute-start | bytes 1474568 | tf_op jit(solution)/shard_map/ppermute | solution.py:704
  88.3 21.0 %collective-permute-start.20 = (bf16[304,1024]{1,0:T(8,128)(2,1)}, bf16[304,1024]{1,0:T(8,128)(2,1)S(1)}, u32[]{:S(2)}, u32[]{:S(2)}) collective-permute-start(bf16[304,1024]{1,0:T(8,128)(2,1)} %get-tuple-element.98), channel_id=1, source_target_pairs={{0,8},{8,24},{24,16},{16,0},{1,9},{9,25},{25,17},{17,1},{2,10},{10... | collective-permute-start | bytes 1867784 | tf_op jit(solution)/shard_map/ppermute | solution.py:704
  89.2 11.1 %copy-start.25 = (f32[16,4096]{1,0:T(8,128)S(1)}, f32[16,4096]{1,0:T(8,128)}, u32[]{:S(2)}) copy-start(f32[16,4096]{1,0:T(8,128)} %copy-done.24) | copy-start | bytes 786436
  89.2 18.3 %collective-permute-start.21 = (bf16[288,1024]{1,0:T(8,128)(2,1)}, bf16[288,1024]{1,0:T(8,128)(2,1)S(1)}, u32[]{:S(2)}, u32[]{:S(2)}) collective-permute-start(bf16[288,1024]{1,0:T(8,128)(2,1)} %get-tuple-element.99), channel_id=1, source_target_pairs={{8,0},{24,8},{16,24},{0,16},{9,1},{25,9},{17,25},{1,17},{10,2},{26... | collective-permute-start | bytes 1769480 | tf_op jit(solution)/shard_map/ppermute | solution.py:705
  98.2 19.8 %collective-permute-start.24 = (bf16[240,1024]{1,0:T(8,128)(2,1)}, bf16[240,1024]{1,0:T(8,128)(2,1)S(1)}, u32[]{:S(2)}, u32[]{:S(2)}) collective-permute-start(bf16[240,1024]{1,0:T(8,128)(2,1)} %get-tuple-element.103), channel_id=1, source_target_pairs={{8,0},{24,8},{16,24},{0,16},{9,1},{25,9},{17,25},{1,17},{10,2},{26... | collective-permute-start | bytes 1474568 | tf_op jit(solution)/shard_map/ppermute | solution.py:705
  99.8 20.1 %collective-permute-start.23 = (bf16[240,1024]{1,0:T(8,128)(2,1)}, bf16[240,1024]{1,0:T(8,128)(2,1)}, u32[]{:S(2)}, u32[]{:S(2)}) collective-permute-start(bf16[240,1024]{1,0:T(8,128)(2,1)} %get-tuple-element.88.refs_1_), channel_id=1, source_target_pairs={{0,8},{8,24},{24,16},{16,0},{1,9},{9,25},{25,17},{17,1},{2,10},{10... | collective-permute-start | bytes 1474568 | tf_op jit(solution)/shard_map/ppermute | solution.py:704
  101.0 10.9 %copy-start.26 = (f32[8,4096]{1,0:T(8,128)}, f32[8,4096]{1,0:T(8,128)S(1)}, u32[]{:S(2)}) copy-start(f32[8,4096]{1,0:T(8,128)S(1)} %get-tuple-element.89.refs_6_.refs_0_) | copy-start | bytes 393220
  101.0 13.0 %collective-permute-start.17 = (f32[8,4096]{1,0:T(8,128)}, f32[8,4096]{1,0:T(8,128)}, u32[]{:S(2)}, u32[]{:S(2)}) collective-permute-start(f32[8,4096]{1,0:T(8,128)} %get-tuple-element.90), channel_id=1, source_target_pairs={{0,4},{2,6},{4,0},{6,2},{1,5},{3,7},{5,1},{7,3},{8,12},{10,14},{12... | collective-permute-start | bytes 393224 | tf_op jit(solution)/shard_map/ppermute | solution.py:402
  107.5 29.8 %copy-start.1 = (bf16[288,1024]{1,0:T(8,128)(2,1)}, bf16[288,1024]{1,0:T(8,128)(2,1)S(1)}, u32[]{:S(2)}) copy-start(bf16[288,1024]{1,0:T(8,128)(2,1)S(1)} %collective-permute-done.21.refs_5_.refs_8_.refs_3_) | copy-start | bytes 1769476
  109.3 28.0 %copy-start = (bf16[304,1024]{1,0:T(8,128)(2,1)}, bf16[304,1024]{1,0:T(8,128)(2,1)S(1)}, u32[]{:S(2)}) copy-start(bf16[304,1024]{1,0:T(8,128)(2,1)S(1)} %collective-permute-done.20.refs_4_.refs_6_.refs_2_) | copy-start | bytes 1867780
  111.9 20.6 %collective-permute-start.26 = (bf16[288,1024]{1,0:T(8,128)(2,1)}, bf16[288,1024]{1,0:T(8,128)(2,1)S(1)}, u32[]{:S(2)}, u32[]{:S(2)}) collective-permute-start(bf16[288,1024]{1,0:T(8,128)(2,1)} %get-tuple-element.100.refs_2_), channel_id=1, source_target_pairs={{0,8},{8,24},{24,16},{16,0},{1,9},{9,25},{25,17},{17,1},{2,10},{10... | collective-permute-start | bytes 1769480 | tf_op jit(solution)/shard_map/ppermute | solution.py:704
  112.5 18.2 %collective-permute-start.27 = (bf16[240,1024]{1,0:T(8,128)(2,1)}, bf16[240,1024]{1,0:T(8,128)(2,1)}, u32[]{:S(2)}, u32[]{:S(2)}) collective-permute-start(bf16[240,1024]{1,0:T(8,128)(2,1)} %get-tuple-element.107), channel_id=1, source_target_pairs={{8,0},{24,8},{16,24},{0,16},{9,1},{25,9},{17,25},{1,17},{10,2},{26... | collective-permute-start | bytes 1474568 | tf_op jit(solution)/shard_map/ppermute | solution.py:705
  122.2 26.2 %collective-permute-start.29 = (bf16[240,1024]{1,0:T(8,128)(2,1)}, bf16[240,1024]{1,0:T(8,128)(2,1)}, u32[]{:S(2)}, u32[]{:S(2)}) collective-permute-start(bf16[240,1024]{1,0:T(8,128)(2,1)} %get-tuple-element.111), channel_id=1, source_target_pairs={{8,0},{24,8},{16,24},{0,16},{9,1},{25,9},{17,25},{1,17},{10,2},{26... | collective-permute-start | bytes 1474568 | tf_op jit(solution)/shard_map/ppermute | solution.py:705
  123.6 24.8 %collective-permute-start.28 = (bf16[240,1024]{1,0:T(8,128)(2,1)}, bf16[240,1024]{1,0:T(8,128)(2,1)}, u32[]{:S(2)}, u32[]{:S(2)}) collective-permute-start(bf16[240,1024]{1,0:T(8,128)(2,1)} %get-tuple-element.104.refs_2_), channel_id=1, source_target_pairs={{0,8},{8,24},{24,16},{16,0},{1,9},{9,25},{25,17},{17,1},{2,10},{10... | collective-permute-start | bytes 1474568 | tf_op jit(solution)/shard_map/ppermute | solution.py:704
  124.3 4.6 %collective-permute-start.22 = (f32[4,4096]{1,0:T(4,128)}, f32[4,4096]{1,0:T(4,128)}, u32[]{:S(2)}, u32[]{:S(2)}) collective-permute-start(f32[4,4096]{1,0:T(4,128)} %get-tuple-element.102), channel_id=1, source_target_pairs={{0,2},{2,0},{4,6},{6,4},{1,3},{3,1},{5,7},{7,5},{8,10},{10,8},{12,... | collective-permute-start | bytes 196616 | tf_op jit(solution)/shard_map/ppermute | solution.py:402
  130.6 7.5 %collective-permute-start.25 = (f32[2,4096]{1,0:T(2,128)S(1)}, f32[2,4096]{1,0:T(2,128)S(1)}, u32[]{:S(2)}, u32[]{:S(2)}) collective-permute-start(f32[2,4096]{1,0:T(2,128)S(1)} %get-tuple-element.106), channel_id=1, source_target_pairs={{0,1},{1,0},{2,3},{3,2},{4,5},{5,4},{6,7},{7,6},{8,9},{9,8},{10,11... | collective-permute-start | bytes 98312 | tf_op jit(solution)/shard_map/ppermute | solution.py:402
  135.2 29.0 %collective-permute-start.33 = (bf16[240,1024]{1,0:T(8,128)(2,1)S(1)}, bf16[240,1024]{1,0:T(8,128)(2,1)S(1)}, u32[]{:S(2)}, u32[]{:S(2)}) collective-permute-start(bf16[240,1024]{1,0:T(8,128)(2,1)S(1)} %get-tuple-element.118), channel_id=1, source_target_pairs={{8,0},{24,8},{16,24},{0,16},{9,1},{25,9},{17,25},{1,17},{10,2},{26... | collective-permute-start | bytes 1474568 | tf_op jit(solution)/shard_map/ppermute | solution.py:705
  136.4 27.9 %collective-permute-start.32 = (bf16[240,1024]{1,0:T(8,128)(2,1)S(1)}, bf16[240,1024]{1,0:T(8,128)(2,1)S(1)}, u32[]{:S(2)}, u32[]{:S(2)}) collective-permute-start(bf16[240,1024]{1,0:T(8,128)(2,1)S(1)} %get-tuple-element.108.refs_2_.refs_9_), channel_id=1, source_target_pairs={{0,8},{8,24},{24,16},{16,0},{1,9},{9,25},{25,17},{17,1},{2,10},{10... | collective-permute-start | bytes 1474568 | tf_op jit(solution)/shard_map/ppermute | solution.py:704
  138.7 9.5 %copy-start.6 = (bf16[240,1024]{1,0:T(8,128)(2,1)S(1)}, bf16[240,1024]{1,0:T(8,128)(2,1)}, u32[]{:S(2)}) copy-start(bf16[240,1024]{1,0:T(8,128)(2,1)} %copy-done.5) | copy-start | bytes 1474564
  138.7 9.5 %copy-start.8 = (bf16[240,1024]{1,0:T(8,128)(2,1)S(1)}, bf16[240,1024]{1,0:T(8,128)(2,1)}, u32[]{:S(2)}) copy-start(bf16[240,1024]{1,0:T(8,128)(2,1)} %copy-done.7) | copy-start | bytes 1474564
  138.7 9.5 %copy-start.10 = (bf16[240,1024]{1,0:T(8,128)(2,1)S(1)}, bf16[240,1024]{1,0:T(8,128)(2,1)}, u32[]{:S(2)}) copy-start(bf16[240,1024]{1,0:T(8,128)(2,1)} %copy-done.9) | copy-start | bytes 1474564
  138.7 9.5 %copy-start.12 = (bf16[240,1024]{1,0:T(8,128)(2,1)S(1)}, bf16[240,1024]{1,0:T(8,128)(2,1)}, u32[]{:S(2)}) copy-start(bf16[240,1024]{1,0:T(8,128)(2,1)} %copy-done.11) | copy-start | bytes 1474564
  138.7 9.5 %copy-start.14 = (bf16[240,1024]{1,0:T(8,128)(2,1)S(1)}, bf16[240,1024]{1,0:T(8,128)(2,1)}, u32[]{:S(2)}) copy-start(bf16[240,1024]{1,0:T(8,128)(2,1)} %copy-done.13) | copy-start | bytes 1474564
  138.7 9.5 %copy-start.17 = (bf16[240,1024]{1,0:T(8,128)(2,1)S(1)}, bf16[240,1024]{1,0:T(8,128)(2,1)}, u32[]{:S(2)}) copy-start(bf16[240,1024]{1,0:T(8,128)(2,1)} %copy-done.16) | copy-start | bytes 1474564
  151.4 13.9 %collective-permute-start.31 = (bf16[240,1024]{1,0:T(8,128)(2,1)S(1)}, bf16[240,1024]{1,0:T(8,128)(2,1)S(1)}, u32[]{:S(2)}, u32[]{:S(2)}) collective-permute-start(bf16[240,1024]{1,0:T(8,128)(2,1)S(1)} %get-tuple-element.117), channel_id=1, source_target_pairs={{8,0},{24,8},{16,24},{0,16},{9,1},{25,9},{17,25},{1,17},{10,2},{26... | collective-permute-start | bytes 1474568 | tf_op jit(solution)/shard_map/ppermute | solution.py:705
  152.3 13.0 %collective-permute-start.30 = (bf16[240,1024]{1,0:T(8,128)(2,1)S(1)}, bf16[240,1024]{1,0:T(8,128)(2,1)S(1)}, u32[]{:S(2)}, u32[]{:S(2)}) collective-permute-start(bf16[240,1024]{1,0:T(8,128)(2,1)S(1)} %get-tuple-element.116.refs_6_), channel_id=1, source_target_pairs={{0,8},{8,24},{24,16},{16,0},{1,9},{9,25},{25,17},{17,1},{2,10},{10... | collective-permute-start | bytes 1474568 | tf_op jit(solution)/shard_map/ppermute | solution.py:704
  (31 other events, 104.6 us)
